TPU v7x, 32 devices: a whole 2x2x4 slice. The times are simulated.
32 devices in a mesh: row: 8 (over z, x), col: 4 (over y, core).
Axes of the slice: x: 2, y: 2, z: 4, core: 2. Of those that a mesh axis runs over, the one named last changes fastest.
Arguments:
- right_side: float32 [32, 512, 256], P('row', 'col'), may hold values from -12 to 12
- permeability: bfloat16 [32, 512, 256], P('row', 'col'), may hold values from 0.25 to 4
- lift_weight: float32 [16, 3], replicated, may hold values from -3 to 3
- spectral_weight: float32 [2, 32, 16, 16, 512], P(None, 'row', None, None, 'col'), may hold values from -3 to 3
- mix_weight: float32 [16, 17], replicated, may hold values from -3 to 3
- proj_weight: float32 [17], replicated, may hold values from -3 to 3
Outputs:
- solution: float32 [32, 512, 256], P('row', 'col')
- residual: float32 [32, 512, 256], P('row', 'col')
- kept: float32 [2, 32, 512, 256], P(None, 'row', 'col')
All inputs are finite; a program needn't handle non-finite values.
Results may differ from a plain program's by a relative error of at most 0.0007.
Values may be sent and summed in bfloat16 or wider, within the bound.
No kernel may reach another device: no remote copies, remote signals or barrier semaphores. Data moves between devices by JAX's collectives and lax.ppermute only.
A program may use at most 128 MiB of HBM per device.

v0:
```python
import jax
import jax.numpy as jnp
from jax import lax
from jax.sharding import PartitionSpec as P

CHANNELS = 16
KX = 16
KY = 32
KZ = 32
ITERS = 2


HIGHEST = lax.Precision.HIGHEST


def with_halo(block, sides, width):
    for axis, dim in sides:
        count = lax.axis_size(axis)
        forward = [(i, i + 1) for i in range(count - 1)]
        backward = [(target, source) for source, target in forward]
        low = lax.ppermute(
            lax.slice_in_dim(block, block.shape[dim] - width, None, axis=dim), axis, forward
        )
        high = lax.ppermute(lax.slice_in_dim(block, 0, width, axis=dim), axis, backward)
        block = jnp.concatenate([low, block, high], axis=dim)
    return block


def einsum_high(form, left, right):
    return jnp.einsum(form, left, right, precision=HIGHEST)


def harmonic(first, second):
    return 2.0 * first * second / (first + second)


def wave_table(freqs, places, length):
    turns = freqs[None, :] * places[:, None] % length
    angle = turns.astype(jnp.float32) * (2.0 * jnp.pi / length)
    return (jnp.cos(angle), jnp.sin(angle))


def signed_freqs(count):
    return jnp.arange(count, dtype=jnp.int32) - count // 2


def face_arrays(permeability):
    padded = with_halo(permeability, (("row", 0), ("col", 1)), 1).astype(jnp.float32)
    own = permeability.astype(jnp.float32)
    edged = jnp.pad(own, ((1, 1), (1, 1), (0, 0)), mode="edge")
    padded = jnp.where(padded > 0.0, padded, edged)
    first = harmonic(padded[:-1, 1:-1], padded[1:, 1:-1])
    second = harmonic(padded[1:-1, :-1], padded[1:-1, 1:])
    deep = jnp.pad(own, ((0, 0), (0, 0), (1, 1)), mode="edge")
    third = harmonic(deep[:, :, :-1], deep[:, :, 1:])
    return ((first, second, third), jnp.log(own))


def apply_operator(field, faces):
    first, second, third = faces
    padded = with_halo(field, (("row", 0), ("col", 1)), 1)
    padded = jnp.pad(padded, ((0, 0), (0, 0), (1, 1)))
    total = first[:-1] * (field - padded[:-2, 1:-1, 1:-1])
    total = total + first[1:] * (field - padded[2:, 1:-1, 1:-1])
    total = total + second[:, :-1] * (field - padded[1:-1, :-2, 1:-1])
    total = total + second[:, 1:] * (field - padded[1:-1, 2:, 1:-1])
    total = total + third[:, :, :-1] * (field - padded[1:-1, 1:-1, :-2])
    total = total + third[:, :, 1:] * (field - padded[1:-1, 1:-1, 2:])
    return total


def global_squares(field):
    return lax.psum(jnp.sum(field * field), ("row", "col"))


def mix_modes(real_in, imag_in, spectral_weight, deep_count, freq_count):
    block = spectral_weight.reshape(2, deep_count, CHANNELS, CHANNELS, freq_count, KY)
    real_out = einsum_high("kcfg,kcofg->kofg", real_in, block[0]) - einsum_high(
        "kcfg,kcofg->kofg", imag_in, block[1]
    )
    imag_out = einsum_high("kcfg,kcofg->kofg", imag_in, block[0]) + einsum_high(
        "kcfg,kcofg->kofg", real_in, block[1]
    )
    return (real_out, imag_out)


def spectral_transpose(real_part, imag_part, spectral_weight, grid):
    rows, cols, n_row, n_col, row_id, col_id = grid
    full_rows = rows * n_row
    full_cols = cols * n_col
    cosine_rows, sine_rows = wave_table(
        signed_freqs(KX), jnp.arange(full_rows, dtype=jnp.int32), full_rows
    )
    cosine_cols, sine_cols = wave_table(
        signed_freqs(KY), jnp.arange(full_cols, dtype=jnp.int32), full_cols
    )
    real_part, imag_part = (
        lax.all_to_all(real_part, "row", split_axis=0, concat_axis=1, tiled=True),
        lax.all_to_all(imag_part, "row", split_axis=0, concat_axis=1, tiled=True),
    )
    first_real = einsum_high("qxy,xf->qfy", real_part, cosine_rows) + einsum_high(
        "qxy,xf->qfy", imag_part, sine_rows
    )
    first_imag = einsum_high("qxy,xf->qfy", imag_part, cosine_rows) - einsum_high(
        "qxy,xf->qfy", real_part, sine_rows
    )
    first_real, first_imag = (
        lax.all_to_all(first_real, "col", split_axis=1, concat_axis=2, tiled=True),
        lax.all_to_all(first_imag, "col", split_axis=1, concat_axis=2, tiled=True),
    )
    second_real = einsum_high("qfy,yg->qfg", first_real, cosine_cols) + einsum_high(
        "qfy,yg->qfg", first_imag, sine_cols
    )
    second_imag = einsum_high("qfy,yg->qfg", first_imag, cosine_cols) - einsum_high(
        "qfy,yg->qfg", first_real, sine_cols
    )
    deep_count = KZ // n_row
    freq_count = KX // n_col
    shape_in = (deep_count, CHANNELS, freq_count, KY)
    mixed_real, mixed_imag = mix_modes(
        second_real.reshape(shape_in),
        second_imag.reshape(shape_in),
        spectral_weight,
        deep_count,
        freq_count,
    )
    shape_out = (deep_count * CHANNELS, freq_count, KY)
    mixed_real = mixed_real.reshape(shape_out)
    mixed_imag = mixed_imag.reshape(shape_out)
    back_real = einsum_high("qfg,yg->qfy", mixed_real, cosine_cols) - einsum_high(
        "qfg,yg->qfy", mixed_imag, sine_cols
    )
    back_imag = einsum_high("qfg,yg->qfy", mixed_imag, cosine_cols) + einsum_high(
        "qfg,yg->qfy", mixed_real, sine_cols
    )
    back_real, back_imag = (
        lax.all_to_all(back_real, "col", split_axis=2, concat_axis=1, tiled=True),
        lax.all_to_all(back_imag, "col", split_axis=2, concat_axis=1, tiled=True),
    )
    out_real = einsum_high("qfy,xf->qxy", back_real, cosine_rows) - einsum_high(
        "qfy,xf->qxy", back_imag, sine_rows
    )
    out_imag = einsum_high("qfy,xf->qxy", back_imag, cosine_rows) + einsum_high(
        "qfy,xf->qxy", back_real, sine_rows
    )
    out_real, out_imag = (
        lax.all_to_all(out_real, "row", split_axis=1, concat_axis=0, tiled=True),
        lax.all_to_all(out_imag, "row", split_axis=1, concat_axis=0, tiled=True),
    )
    return (out_real, out_imag)


def precondition(residual, squares_total, log_perm, weights, grid, cells):
    lift_weight, spectral_weight, mix_weight, proj_weight = weights
    rows, cols, depth = residual.shape
    scale = jnp.sqrt(squares_total / cells + 1e-06)
    scaled = residual / scale
    lifted = jax.nn.gelu(
        lift_weight[:, 0, None, None, None] * scaled[None]
        + lift_weight[:, 1, None, None, None] * log_perm[None]
        + lift_weight[:, 2, None, None, None]
    )
    cosine_deep, sine_deep = wave_table(
        jnp.arange(KZ, dtype=jnp.int32), jnp.arange(depth, dtype=jnp.int32), depth
    )
    real_part = einsum_high("cxyz,zk->kcxy", lifted, cosine_deep).reshape(KZ * CHANNELS, rows, cols)
    imag_part = -einsum_high("cxyz,zk->kcxy", lifted, sine_deep).reshape(KZ * CHANNELS, rows, cols)
    out_real, out_imag = spectral_transpose(real_part, imag_part, spectral_weight, grid)
    out_real = out_real.reshape(KZ, CHANNELS, rows, cols)
    out_imag = out_imag.reshape(KZ, CHANNELS, rows, cols)
    spatial = (
        einsum_high("kcxy,zk->cxyz", out_real, cosine_deep)
        - einsum_high("kcxy,zk->cxyz", out_imag, sine_deep)
    ) / cells
    point = (
        einsum_high("oc,cxyz->oxyz", mix_weight[:, :CHANNELS], lifted)
        + mix_weight[:, CHANNELS, None, None, None]
    )
    hidden = jax.nn.gelu(spatial + point)
    return scale * (
        einsum_high("o,oxyz->xyz", proj_weight[:CHANNELS], hidden) + proj_weight[CHANNELS]
    )


def local(right_side, permeability, lift_weight, spectral_weight, mix_weight, proj_weight):
    rows, cols, depth = right_side.shape
    n_row = lax.axis_size("row")
    n_col = lax.axis_size("col")
    grid = (rows, cols, n_row, n_col, lax.axis_index("row"), lax.axis_index("col"))
    cells = float(rows * n_row * cols * n_col * depth)
    faces, log_perm = face_arrays(permeability)
    weights = (lift_weight, spectral_weight, mix_weight, proj_weight)

    def precond(residual, squares_total):
        return precondition(residual, squares_total, log_perm, weights, grid, cells)

    solution = jnp.zeros_like(right_side)
    residual = right_side
    kept = []
    update = precond(residual, global_squares(residual))
    kept.append(update)
    direction = update
    for step in range(ITERS):
        image = apply_operator(direction, faces)
        curvature, along = lax.psum(
            (jnp.sum(direction * image), jnp.sum(residual * direction)), ("row", "col")
        )
        alpha = along / curvature
        solution = solution + alpha * direction
        residual = residual - alpha * image
        if step + 1 < ITERS:
            update = precond(residual, global_squares(residual))
            kept.append(update)
            beta = lax.psum(jnp.sum(update * image), ("row", "col")) / curvature
            direction = update - beta * direction
    return (solution, residual, jnp.stack(kept))


def solution(mesh):
    placed = (
        P("row", "col", None),
        P("row", "col", None),
        P(),
        P(None, "row", None, None, "col"),
        P(),
        P(),
    )
    return jax.shard_map(
        local,
        mesh=mesh,
        in_specs=placed,
        out_specs=(P("row", "col", None), P("row", "col", None), P(None, "row", "col", None)),
        check_vma=False,
    )
```

profile of v0, /device:TPU:0, one launch (start us, length us, event | category | flops | bytes accessed | tf_op | source)
XLA Modules:
  0.0 779.7 jit_solution(10178254948544826394)
XLA Ops:
  4.4 42.2 %psum.49 = f32[]{:T(128)} all-reduce(f32[]{:T(128)} %multiply_reduce_fusion.14), channel_id=1, replica_groups=mesh['row'=8,'col'=4] {'row','col'}, use_global_device_ids=true, to_apply=%region_1.2 | all-reduce | flops 1 | bytes 8 | tf_op jit(solution)/shard_map/psum | solution.py:73
  48.4 10.7 %fusion.44 = f32[32,16,4,128]{3,0,2,1:T(8,128)S(1)} fusion(f32[16]{0:T(128)S(1)} %get-tuple-element.50, f32[4,128,256]{2,1,0:T(8,128)S(1)} %convert_log_fusion, f32[16]{0:T(128)S(1)} %get-tuple-element.51, f32[4,128,256]{2,1,0:T(8,128)S(1)} %broadcast_divide_fusion.1, f32[16]{0:T(128)S(1)} %get-tuple-element.49), kind=kOutput, calls=%fused_computation.62 | convolution fusion | flops 830586880 | bytes 2097344 | tf_op jit(solution)/shard_map/cxyz,zk->kcxy/dot_general | solution.py:30
  61.4 5.6 all-to-all-start
  67.0 10.6 %fusion.46 = f32[32,16,4,128]{3,0,2,1:T(8,128)S(1)} fusion(f32[16]{0:T(128)S(1)} %get-tuple-element.50, f32[4,128,256]{2,1,0:T(8,128)S(1)} %convert_log_fusion, f32[16]{0:T(128)S(1)} %get-tuple-element.51, f32[4,128,256]{2,1,0:T(8,128)S(1)} %broadcast_divide_fusion.1, f32[16]{0:T(128)S(1)} %get-tuple-element.49), kind=kOutput, calls=%fused_computation.63 | convolution fusion | flops 830849024 | bytes 2097344 | tf_op jit(solution)/shard_map/cxyz,zk->kcxy/dot_general | solution.py:30
  79.9 11.4 %all-to-all-done = f32[512,4,128]{2,1,0:T(4,128)S(1)} async-done(((f32[512,4,128]{2,1,0:T(4,128)}), f32[512,4,128]{2,1,0:T(4,128)S(1)}, u32[]{:S(2)}, u32[]{:S(2)}) %all-to-all-start) | async-done | bytes 1048608 | tf_op jit(solution)/shard_map/all_to_all | solution.py:98
  95.7 25.0 %all-to-all-done.1 = f32[512,4,128]{2,1,0:T(4,128)S(1)} async-done(((f32[512,4,128]{2,1,0:T(4,128)}), f32[512,4,128]{2,1,0:T(4,128)S(1)}, u32[]{:S(2)}, u32[]{:S(2)}) %all-to-all-start.1) | async-done | bytes 1048608 | tf_op jit(solution)/shard_map/all_to_all | solution.py:99
  129.8 6.4 all-to-all-done.2
  136.2 4.1 all-to-all-start.3
  141.0 3.9 collective-permute-start
  145.0 9.8 %collective-permute-start.1 = (bf16[1,128,256]{2,1,0:T(8,128)(2,1)}, bf16[1,128,256]{2,1,0:T(8,128)(2,1)}, u32[]{:S(2)}, u32[]{:S(2)}) collective-permute-start(bf16[1,128,256]{2,1,0:T(8,128)(2,1)} %get-tuple-element.41), channel_id=1, source_target_pairs={{4,0},{8,4},{12,8},{16,12},{20,16},{24,20},{28,24},{5,1},{9,5},{13... | collective-permute-start | bytes 196616 | tf_op jit(solution)/shard_map/ppermute | solution.py:24
  181.0 4.1 multiply_reduce_fusion.4
  191.1 4.4 all-to-all-start.4
  204.4 4.1 all-to-all-start.5
  218.3 3.8 reduce.19
  231.3 5.1 all-to-all-start.6
  236.4 4.7 fusion.8
  241.1 12.6 %fusion.36 = f32[4,128,256,16]{2,3,1,0:T(8,128)} fusion(f32[16,4,128,256]{3,2,1,0:T(8,128)S(1)} %fusion.8, f32[16,17]{1,0:T(8,128)S(1)} %copy-done.22), kind=kOutput, calls=%fused_computation.46 | convolution fusion | flops 402653184 | bytes 16778304 | tf_op jit(solution)/shard_map/oc,cxyz->oxyz/dot_general | solution.py:30
  257.7 5.1 all-to-all-done.6
  262.8 4.4 all-to-all-start.7
  276.3 9.1 %fusion.65 = f32[16,4,128,256]{3,2,1,0:T(8,128)} fusion(f32[32,16,4,128]{3,1,0,2:T(8,128)S(1)} %bitcast.353), kind=kOutput, calls=%fused_computation.103 | convolution fusion | flops 805421056 | bytes 9437184 | tf_op jit(solution)/shard_map/kcxy,zk->cxyz/dot_general | solution.py:30
  285.4 7.5 all-to-all-done.7
  294.2 17.4 %fusion.15 = f32[16,4,128,256]{3,2,1,0:T(8,128)S(1)} fusion(f32[4,128,256,16]{2,3,1,0:T(8,128)} %fusion.36, f32[16,4,128,256]{3,2,1,0:T(8,128)} %fusion.65, f32[16]{0:T(128)S(1)} %slice_reduce_fusion, f32[32,16,4,128]{3,1,0,2:T(8,128)S(1)} %bitcast.387), kind=kOutput, calls=%fused_computation.21 | convolution fusion | flops 830586880 | bytes 26214464 | tf_op jit(solution)/shard_map/kcxy,zk->cxyz/dot_general | solution.py:30
  311.7 7.9 %fusion.32 = f32[1,4,128,256]{3,0,2,1:T(1,128)S(1)} fusion(f32[16,4,128,256]{3,2,1,0:T(8,128)S(1)} %fusion.15, f32[17]{0:T(128)S(1)} %copy-done.26), kind=kOutput, calls=%fused_computation.40 | convolution fusion | flops 25165824 | bytes 8912964 | tf_op jit(solution)/shard_map/o,oxyz->xyz/dot_general | solution.py:30
  321.7 4.6 collective-permute-start.4
  336.9 42.6 %all-reduce.3 = (f32[]{:T(128)}, f32[]{:T(128)}) all-reduce(f32[]{:T(128)} %get-tuple-element.14, f32[]{:T(128)} %get-tuple-element.13), channel_id=1, replica_groups=mesh['row'=8,'col'=4] {'row','col'}, use_global_device_ids=true, to_apply=%region_3.4 | all-reduce | flops 2 | bytes 16 | tf_op jit(solution)/shard_map/psum | solution.py:205
  382.8 40.7 %psum.52 = f32[]{:T(128)} all-reduce(f32[]{:T(128)} %get-tuple-element.24), channel_id=1, replica_groups=mesh['row'=8,'col'=4] {'row','col'}, use_global_device_ids=true, to_apply=%region_7.8 | all-reduce | flops 1 | bytes 8 | tf_op jit(solution)/shard_map/psum | solution.py:73
  424.2 12.1 %fusion.40 = f32[32,16,4,128]{3,0,2,1:T(8,128)S(1)} fusion(f32[4,128,256]{2,1,0:T(8,128)S(1)} %broadcast_divide_fusion, f32[16]{0:T(128)S(1)} %get-tuple-element.50, f32[4,128,256]{2,1,0:T(8,128)} %copy-done.12, f32[16]{0:T(128)S(1)} %copy-done.24, f32[16]{0:T(128)S(1)} %get-tuple-element.49), kind=kOutput, calls=%fused_computation.60 | convolution fusion | flops 830586880 | bytes 2097344 | tf_op jit(solution)/shard_map/cxyz,zk->kcxy/dot_general | solution.py:30
  438.5 5.4 all-to-all-start.8
  444.0 11.9 %fusion.49 = f32[32,16,4,128]{3,0,2,1:T(8,128)S(1)} fusion(f32[4,128,256]{2,1,0:T(8,128)} %copy-done.17, f32[16]{0:T(128)S(1)} %get-tuple-element.50, f32[4,128,256]{2,1,0:T(8,128)} %copy-done.12, f32[16]{0:T(128)S(1)} %copy-done.24, f32[16]{0:T(128)S(1)} %get-tuple-element.49), kind=kOutput, calls=%fused_computation.64 | convolution fusion | flops 830849024 | bytes 2097344 | tf_op jit(solution)/shard_map/cxyz,zk->kcxy/dot_general | solution.py:30
  458.1 10.5 %all-to-all-done.8 = f32[512,4,128]{2,1,0:T(4,128)} async-done(((f32[512,4,128]{2,1,0:T(4,128)}), f32[512,4,128]{2,1,0:T(4,128)}, u32[]{:S(2)}, u32[]{:S(2)}) %all-to-all-start.8) | async-done | bytes 1048608 | tf_op jit(solution)/shard_map/all_to_all | solution.py:98
  468.5 4.5 all-to-all-start.9
  476.7 21.7 %all-to-all-done.9 = f32[512,4,128]{2,1,0:T(4,128)} async-done(((f32[512,4,128]{2,1,0:T(4,128)}), f32[512,4,128]{2,1,0:T(4,128)}, u32[]{:S(2)}, u32[]{:S(2)}) %all-to-all-start.9) | async-done | bytes 1048608 | tf_op jit(solution)/shard_map/all_to_all | solution.py:99
  511.4 4.0 all-to-all-done.10
  515.3 4.1 all-to-all-start.11
  523.0 5.4 all-to-all-done.11
  538.4 4.1 multiply_reduce_fusion
  546.4 3.9 all-to-all-start.12
  554.3 4.9 all-to-all-done.12
  580.9 4.4 all-to-all-start.14
  589.3 21.9 %all-to-all-done.14 = f32[64,32,128]{2,0,1:T(8,128)} async-done(((f32[64,32,128]{2,0,1:T(8,128)}), f32[64,32,128]{2,0,1:T(8,128)}, u32[]{:S(2)}, u32[]{:S(2)}) %all-to-all-start.14) | async-done | bytes 1048608 | tf_op jit(solution)/shard_map/all_to_all | solution.py:147
  614.8 3.6 fusion.22
  618.5 12.6 %fusion.34 = f32[4,128,256,16]{2,3,1,0:T(8,128)} fusion(f32[16,4,128,256]{3,2,1,0:T(8,128)S(1)} %fusion.22, f32[16,17]{1,0:T(8,128)S(1)} %copy-done.22), kind=kOutput, calls=%fused_computation.43 | convolution fusion | flops 402653184 | bytes 16778304 | tf_op jit(solution)/shard_map/oc,cxyz->oxyz/dot_general | solution.py:30
  632.4 9.3 %fusion.62 = f32[16,4,128,256]{3,2,1,0:T(8,128)} fusion(f32[32,16,4,128]{3,1,0,2:T(8,128)S(1)} %bitcast.354), kind=kOutput, calls=%fused_computation.100 | convolution fusion | flops 805421056 | bytes 9437184 | tf_op jit(solution)/shard_map/kcxy,zk->cxyz/dot_general | solution.py:30
  641.7 17.4 %fusion.29 = f32[16,4,128,256]{3,2,1,0:T(8,128)S(1)} fusion(f32[4,128,256,16]{2,3,1,0:T(8,128)} %fusion.34, f32[16,4,128,256]{3,2,1,0:T(8,128)} %fusion.62, f32[16]{0:T(128)S(1)} %slice_reduce_fusion, f32[32,16,4,128]{3,1,0,2:T(8,128)S(1)} %bitcast.386), kind=kOutput, calls=%fused_computation.35 | convolution fusion | flops 830586880 | bytes 26214464 | tf_op jit(solution)/shard_map/kcxy,zk->cxyz/dot_general | solution.py:30
  659.2 7.9 %fusion.30 = f32[1,4,128,256]{3,0,2,1:T(1,128)S(1)} fusion(f32[16,4,128,256]{3,2,1,0:T(8,128)S(1)} %fusion.29, f32[17]{0:T(128)S(1)} %copy-done.26), kind=kOutput, calls=%fused_computation.38 | convolution fusion | flops 25165824 | bytes 8912964 | tf_op jit(solution)/shard_map/o,oxyz->xyz/dot_general | solution.py:30
  669.4 40.1 %psum.53 = f32[]{:T(128)} all-reduce(f32[]{:T(128)} %multiply_reduce_fusion.10), channel_id=1, replica_groups=mesh['row'=8,'col'=4] {'row','col'}, use_global_device_ids=true, to_apply=%region_9.10 | all-reduce | flops 1 | bytes 8 | tf_op jit(solution)/shard_map/psum | solution.py:214
  713.8 4.8 collective-permute-start.8
  731.4 42.9 %all-reduce.2 = (f32[]{:T(128)}, f32[]{:T(128)}) all-reduce(f32[]{:T(128)} %get-tuple-element.12, f32[]{:T(128)} %get-tuple-element.11), channel_id=1, replica_groups=mesh['row'=8,'col'=4] {'row','col'}, use_global_device_ids=true, to_apply=%region_11.12 | all-reduce | flops 2 | bytes 16 | tf_op jit(solution)/shard_map/psum | solution.py:205
  (222 shorter events, 207.2 us)
Async XLA Ops:
  1.7 234.7 %copy-start.12 = (f32[4,128,256]{2,1,0:T(8,128)}, f32[4,128,256]{2,1,0:T(8,128)S(1)}, u32[]{:S(2)}) copy-start(f32[4,128,256]{2,1,0:T(8,128)S(1)} %convert_log_fusion) | copy-start | bytes 1572868
  4.4 62.6 %copy-start.23 = (f32[16]{0:T(128)}, f32[16]{0:T(128)S(1)}, u32[]{:S(2)}) copy-start(f32[16]{0:T(128)S(1)} %get-tuple-element.51) | copy-start | bytes 196
  48.4 18.6 %copy-start.16 = (f32[4,128,256]{2,1,0:T(8,128)}, f32[4,128,256]{2,1,0:T(8,128)S(1)}, u32[]{:S(2)}) copy-start(f32[4,128,256]{2,1,0:T(8,128)S(1)} %broadcast_divide_fusion.1) | copy-start | bytes 1572868
  61.4 30.0 %all-to-all-start = ((f32[512,4,128]{2,1,0:T(4,128)}), f32[512,4,128]{2,1,0:T(4,128)S(1)}, u32[]{:S(2)}, u32[]{:S(2)}) async-start(f32[512,4,128]{2,1,0:T(4,128)} %copy.118), calls=%async_computation | async-start | bytes 2097152 | tf_op jit(solution)/shard_map/all_to_all | solution.py:98
  91.4 29.4 %all-to-all-start.1 = ((f32[512,4,128]{2,1,0:T(4,128)}), f32[512,4,128]{2,1,0:T(4,128)S(1)}, u32[]{:S(2)}, u32[]{:S(2)}) async-start(f32[512,4,128]{2,1,0:T(4,128)} %copy.122), calls=%async_computation.1 | async-start | bytes 2097152 | tf_op jit(solution)/shard_map/all_to_all | solution.py:99
  95.7 44.6 %copy-start.10 = (bf16[4,128,256]{2,1,0:T(8,128)(2,1)S(1)}, bf16[4,128,256]{2,1,0:T(8,128)(2,1)}, u32[]{:S(2)}) copy-start(bf16[4,128,256]{2,1,0:T(8,128)(2,1)} %param.7) | copy-start | bytes 786436
  122.2 40.1 %copy-start.25 = (f32[17]{0:T(128)S(1)}, f32[17]{0:T(128)}, u32[]{:S(2)}) copy-start(f32[17]{0:T(128)} %param.11) | copy-start | bytes 208
  123.9 12.3 %all-to-all-start.2 = ((f32[64,16,128]{2,0,1:T(8,128)}), f32[64,16,128]{2,0,1:T(8,128)S(1)}, u32[]{:S(2)}, u32[]{:S(2)}) async-start(f32[64,16,128]{2,0,1:T(8,128)} %copy.125), calls=%async_computation.2 | async-start | bytes 1048576 | tf_op jit(solution)/shard_map/all_to_all | solution.py:108
  136.2 29.1 %all-to-all-start.3 = ((f32[64,16,128]{2,0,1:T(8,128)}), f32[64,16,128]{2,0,1:T(8,128)}, u32[]{:S(2)}, u32[]{:S(2)}) async-start(f32[64,16,128]{2,0,1:T(8,128)} %copy.127), calls=%async_computation.3 | async-start | bytes 1048576 | tf_op jit(solution)/shard_map/all_to_all | solution.py:109
  141.0 126.4 %collective-permute-start = (bf16[1,128,256]{2,1,0:T(8,128)(2,1)}, bf16[1,128,256]{2,1,0:T(8,128)(2,1)}, u32[]{:S(2)}, u32[]{:S(2)}) collective-permute-start(bf16[1,128,256]{2,1,0:T(8,128)(2,1)} %get-tuple-element.42), channel_id=1, source_target_pairs={{0,4},{4,8},{8,12},{12,16},{16,20},{20,24},{24,28},{1,5},{5,9},{9,... | collective-permute-start | bytes 196616 | tf_op jit(solution)/shard_map/ppermute | solution.py:21
  145.0 123.4 %collective-permute-start.1 = (bf16[1,128,256]{2,1,0:T(8,128)(2,1)}, bf16[1,128,256]{2,1,0:T(8,128)(2,1)}, u32[]{:S(2)}, u32[]{:S(2)}) collective-permute-start(bf16[1,128,256]{2,1,0:T(8,128)(2,1)} %get-tuple-element.41), channel_id=1, source_target_pairs={{4,0},{8,4},{12,8},{16,12},{20,16},{24,20},{28,24},{5,1},{9,5},{13... | collective-permute-start | bytes 196616 | tf_op jit(solution)/shard_map/ppermute | solution.py:24
  191.1 13.3 %all-to-all-start.4 = ((f32[4,1,32768]{2,1,0:T(1,128)}), f32[4,1,32768]{2,1,0:T(1,128)}, u32[]{:S(2)}, u32[]{:S(2)}) async-start(f32[4,1,32768]{2,1,0:T(1,128)} %reshape.119), calls=%async_computation.4 | async-start | bytes 1048576 | tf_op jit(solution)/shard_map/all_to_all | solution.py:137
  204.4 13.9 %all-to-all-start.5 = ((f32[4,1,32768]{2,1,0:T(1,128)}), f32[4,1,32768]{2,1,0:T(1,128)}, u32[]{:S(2)}, u32[]{:S(2)}) async-start(f32[4,1,32768]{2,1,0:T(1,128)} %reshape.121), calls=%async_computation.5 | async-start | bytes 1048576 | tf_op jit(solution)/shard_map/all_to_all | solution.py:138
  209.8 26.6 %copy-start.24 = (f32[16]{0:T(128)S(1)}, f32[16]{0:T(128)}, u32[]{:S(2)}) copy-start(f32[16]{0:T(128)} %copy-done.23) | copy-start | bytes 196
  227.2 13.9 %copy-start.22 = (f32[16,17]{1,0:T(8,128)S(1)}, f32[16,17]{1,0:T(8,128)}, u32[]{:S(2)}) copy-start(f32[16,17]{1,0:T(8,128)} %param.10) | copy-start | bytes 3268
  231.3 31.5 %all-to-all-start.6 = ((f32[64,32,128]{2,0,1:T(8,128)}), f32[64,32,128]{2,0,1:T(8,128)}, u32[]{:S(2)}, u32[]{:S(2)}) async-start(f32[64,32,128]{2,0,1:T(8,128)} %copy.139), calls=%async_computation.6 | async-start | bytes 2097152 | tf_op jit(solution)/shard_map/all_to_all | solution.py:147
  241.1 12.6 %copy-start.15 = (f32[64,4,4,128]{3,1,2,0:T(4,128)S(1)}, f32[64,4,4,128]{3,1,2,0:T(4,128)}, u32[]{:S(2)}) copy-start(f32[64,4,4,128]{3,1,2,0:T(4,128)} %copy.138) | copy-start | bytes 1572868
  254.9 18.7 %copy-start.20 = (f32[4,128,1]{2,1,0:T(8,128)S(1)}, f32[4,128,1]{2,1,0:T(8,128)}, u32[]{:S(2)}) copy-start(f32[4,128,1]{2,1,0:T(8,128)} %get-tuple-element.47) | copy-start | bytes 6148
  254.9 18.7 %copy-start.21 = (f32[4,128,1]{2,1,0:T(8,128)S(1)}, f32[4,128,1]{2,1,0:T(8,128)}, u32[]{:S(2)}) copy-start(f32[4,128,1]{2,1,0:T(8,128)} %get-tuple-element.48) | copy-start | bytes 6148
  262.8 30.1 %all-to-all-start.7 = ((f32[64,32,128]{2,0,1:T(8,128)}), f32[64,32,128]{2,0,1:T(8,128)}, u32[]{:S(2)}, u32[]{:S(2)}) async-start(f32[64,32,128]{2,0,1:T(8,128)} %copy.142), calls=%async_computation.7 | async-start | bytes 2097152 | tf_op jit(solution)/shard_map/all_to_all | solution.py:148
  269.2 5.5 collective-permute-start.3
  270.5 4.2 collective-permute-start.2
  294.2 17.5 %copy-start.26 = (f32[17]{0:T(128)S(1)}, f32[17]{0:T(128)}, u32[]{:S(2)}) copy-start(f32[17]{0:T(128)} %param.11) | copy-start | bytes 208
  311.7 23.2 %copy-start.4 = (f32[4,128,257]{2,1,0:T(8,128)S(1)}, f32[4,128,257]{2,1,0:T(8,128)}, u32[]{:S(2)}) copy-start(f32[4,128,257]{2,1,0:T(8,128)} %add_divide_fusion) | copy-start | bytes 1579012
  311.7 23.2 %copy-start.8 = (f32[4,128,256]{2,1,0:T(8,128)S(1)}, f32[4,128,256]{2,1,0:T(8,128)}, u32[]{:S(2)}) copy-start(f32[4,128,256]{2,1,0:T(8,128)} %param.6) | copy-start | bytes 1572868
  320.4 6.9 collective-permute-start.5
  321.7 7.6 collective-permute-start.4
  329.3 4.5 collective-permute-start.7
  330.6 3.8 collective-permute-start.6
  382.8 53.5 %copy-start.9 = (f32[4,128,256]{2,1,0:T(8,128)}, f32[4,128,256]{2,1,0:T(8,128)S(1)}, u32[]{:S(2)}) copy-start(f32[4,128,256]{2,1,0:T(8,128)S(1)} %get-tuple-element.25) | copy-start | bytes 1572868
  424.2 12.1 %copy-start.17 = (f32[4,128,256]{2,1,0:T(8,128)}, f32[4,128,256]{2,1,0:T(8,128)S(1)}, u32[]{:S(2)}) copy-start(f32[4,128,256]{2,1,0:T(8,128)S(1)} %broadcast_divide_fusion) | copy-start | bytes 1572868
  438.5 30.0 %all-to-all-start.8 = ((f32[512,4,128]{2,1,0:T(4,128)}), f32[512,4,128]{2,1,0:T(4,128)}, u32[]{:S(2)}, u32[]{:S(2)}) async-start(f32[512,4,128]{2,1,0:T(4,128)} %copy.148), calls=%async_computation.8 | async-start | bytes 2097152 | tf_op jit(solution)/shard_map/all_to_all | solution.py:98
  468.5 29.9 %all-to-all-start.9 = ((f32[512,4,128]{2,1,0:T(4,128)}), f32[512,4,128]{2,1,0:T(4,128)}, u32[]{:S(2)}, u32[]{:S(2)}) async-start(f32[512,4,128]{2,1,0:T(4,128)} %copy.152), calls=%async_computation.9 | async-start | bytes 2097152 | tf_op jit(solution)/shard_map/all_to_all | solution.py:99
  503.1 12.3 %all-to-all-start.10 = ((f32[64,16,128]{2,0,1:T(8,128)}), f32[64,16,128]{2,0,1:T(8,128)S(1)}, u32[]{:S(2)}, u32[]{:S(2)}) async-start(f32[64,16,128]{2,0,1:T(8,128)} %copy.155), calls=%async_computation.10 | async-start | bytes 1048576 | tf_op jit(solution)/shard_map/all_to_all | solution.py:108
  515.3 13.1 %all-to-all-start.11 = ((f32[64,16,128]{2,0,1:T(8,128)}), f32[64,16,128]{2,0,1:T(8,128)}, u32[]{:S(2)}, u32[]{:S(2)}) async-start(f32[64,16,128]{2,0,1:T(8,128)} %copy.157), calls=%async_computation.11 | async-start | bytes 1048576 | tf_op jit(solution)/shard_map/all_to_all | solution.py:109
  546.4 12.7 %all-to-all-start.12 = ((f32[4,1,32768]{2,1,0:T(1,128)}), f32[4,1,32768]{2,1,0:T(1,128)S(1)}, u32[]{:S(2)}, u32[]{:S(2)}) async-start(f32[4,1,32768]{2,1,0:T(1,128)} %reshape.123), calls=%async_computation.12 | async-start | bytes 1048576 | tf_op jit(solution)/shard_map/all_to_all | solution.py:137
  559.2 12.3 %all-to-all-start.13 = ((f32[4,1,32768]{2,1,0:T(1,128)}), f32[4,1,32768]{2,1,0:T(1,128)S(1)}, u32[]{:S(2)}, u32[]{:S(2)}) async-start(f32[4,1,32768]{2,1,0:T(1,128)} %reshape.125), calls=%async_computation.13 | async-start | bytes 1048576 | tf_op jit(solution)/shard_map/all_to_all | solution.py:138
  575.2 39.6 %copy-start.13 = (f32[4,128,256]{2,1,0:T(8,128)S(1)}, f32[4,128,256]{2,1,0:T(8,128)}, u32[]{:S(2)}) copy-start(f32[4,128,256]{2,1,0:T(8,128)} %copy-done.12) | copy-start | bytes 1572868
  575.2 39.6 %copy-start.18 = (f32[4,128,256]{2,1,0:T(8,128)S(1)}, f32[4,128,256]{2,1,0:T(8,128)}, u32[]{:S(2)}) copy-start(f32[4,128,256]{2,1,0:T(8,128)} %copy-done.17) | copy-start | bytes 1572868
  580.9 30.2 %all-to-all-start.14 = ((f32[64,32,128]{2,0,1:T(8,128)}), f32[64,32,128]{2,0,1:T(8,128)}, u32[]{:S(2)}, u32[]{:S(2)}) async-start(f32[64,32,128]{2,0,1:T(8,128)} %copy.169), calls=%async_computation.14 | async-start | bytes 2097152 | tf_op jit(solution)/shard_map/all_to_all | solution.py:147
  611.2 30.4 %all-to-all-start.15 = ((f32[64,32,128]{2,0,1:T(8,128)}), f32[64,32,128]{2,0,1:T(8,128)S(1)}, u32[]{:S(2)}, u32[]{:S(2)}) async-start(f32[64,32,128]{2,0,1:T(8,128)} %copy.172), calls=%async_computation.15 | async-start | bytes 2097152 | tf_op jit(solution)/shard_map/all_to_all | solution.py:148
  659.2 69.2 %copy-start.1 = (f32[4,129,256]{2,1,0:T(8,128)S(1)}, f32[4,129,256]{2,1,0:T(8,128)}, u32[]{:S(2)}) copy-start(f32[4,129,256]{2,1,0:T(8,128)} %copy-done) | copy-start | bytes 1585156
  659.2 69.2 %copy-start.3 = (f32[5,128,256]{2,1,0:T(8,128)S(1)}, f32[5,128,256]{2,1,0:T(8,128)}, u32[]{:S(2)}) copy-start(f32[5,128,256]{2,1,0:T(8,128)} %copy-done.2) | copy-start | bytes 1966084
  659.2 69.2 %copy-start.5 = (f32[4,128,257]{2,1,0:T(8,128)S(1)}, f32[4,128,257]{2,1,0:T(8,128)}, u32[]{:S(2)}) copy-start(f32[4,128,257]{2,1,0:T(8,128)} %add_divide_fusion) | copy-start | bytes 1579012
  712.5 7.1 collective-permute-start.9
  713.8 8.7 %collective-permute-start.8 = (f32[1,128,256]{2,1,0:T(8,128)S(1)}, f32[1,128,256]{2,1,0:T(8,128)S(1)}, u32[]{:S(2)}, u32[]{:S(2)}) collective-permute-start(f32[1,128,256]{2,1,0:T(8,128)S(1)} %get-tuple-element.35), channel_id=1, source_target_pairs={{0,4},{4,8},{8,12},{12,16},{16,20},{20,24},{24,28},{1,5},{5,9},{9,... | collective-permute-start | bytes 393224 | tf_op jit(solution)/shard_map/ppermute | solution.py:21
  722.5 5.4 collective-permute-start.11
  723.8 4.1 collective-permute-start.10
  (7 other events, 24.1 us)
where the time goes:
time: 791 us; the launch traced here: 780 us
  blocking collectives  208 us (26%)
  matrix products  184 us (23%)
  waiting for transfers between devices  136 us (17%)
  starting transfers between devices  106 us (13%)
  local copies, waits for them, and re-layouts  86.6 us (11%)
  other arithmetic  50.6 us (6%)
    dot_general x44, matrix products, einsum_high(): return jnp.einsum(form, left, right, precision=HIGHEST)  184 us
    psum x2, blocking collectives, local(): lax.psum((jnp.sum(direction * image), jnp.sum(residual * direction)), ('r...  85.5 us
    psum x2, blocking collectives, global_squares(): return lax.psum(jnp.sum(field * field), ('row', 'col'))  82.9 us
    all_to_all x2, waiting for transfers between devices, spectral_transpose(): lax.all_to_all(imag_part, 'row', split_axis=0, concat_axis=1, tiled=True)  46.7 us
    psum x1, blocking collectives, local(): beta = lax.psum(jnp.sum(update * image), ('row', 'col')) / curvature  40.1 us
    all_to_all x2, waiting for transfers between devices, spectral_transpose(): lax.all_to_all(out_real, 'row', split_axis=1, concat_axis=0, tiled=True)  27 us
    unnamed x71, local copies, waits for them, and re-layouts  23.1 us
    ppermute x6, starting transfers between devices, with_halo(): lax.ppermute(lax.slice_in_dim(block, block.shape[dim] - width, None, axis...  22.4 us
  transfers between devices with their start and end apart: 28, of which 18 were waited for; matrix products, arithmetic and copies ran while one was open for 23% of the time, Pallas kernels for 0%

commit v1 on v0

--- a/solution.py
+++ b/solution.py
@@ -1,6 +1,12 @@
+import functools
+
 import jax
 import jax.numpy as jnp
+import ml_dtypes
+import numpy as np
 from jax import lax
+from jax.experimental import pallas as pl
+from jax.experimental.pallas import tpu as pltpu
 from jax.sharding import PartitionSpec as P
 
 CHANNELS = 16
@@ -216,6 +222,782 @@
     return (solution, residual, jnp.stack(kept))
 
 
+LANES = 128
+SUBLANES = 8
+BOTH = ("row", "col")
+F32 = jnp.float32
+BF16 = jnp.bfloat16
+
+
+def split_table(table):
+    high = table.astype(ml_dtypes.bfloat16)
+    low = (table - high.astype(np.float64)).astype(ml_dtypes.bfloat16)
+    return high, low
+
+
+def split(value):
+    high = value.astype(BF16)
+    return high, (value - high.astype(F32)).astype(BF16)
+
+
+def split_three(value):
+    high = value.astype(BF16).astype(F32)
+    rest = value - high
+    middle = rest.astype(BF16).astype(F32)
+    return high, middle, rest - middle
+
+
+def matmul(left, right):
+    return jnp.dot(left, right, preferred_element_type=F32)
+
+
+def matmul_nt(left, right):
+    return lax.dot_general(left, right, (((1,), (1,)), ((), ())), preferred_element_type=F32)
+
+
+def angles(freqs, places, length):
+    turns = np.multiply.outer(freqs, places) % length
+    return turns * (2.0 * np.pi / length)
+
+
+def deep_order(n_row):
+    count = KZ // n_row
+    order = [
+        (part, row * count + place)
+        for row in range(n_row)
+        for part in range(2)
+        for place in range(count)
+    ]
+    return np.array(order)
+
+
+def deep_tables(n_row, depth):
+    order = deep_order(n_row)
+    angle = angles(order[:, 1], np.arange(depth), depth)
+    wave = np.where(order[:, :1] == 0, np.cos(angle), -np.sin(angle))
+    high, low = split_table(wave)
+    return np.concatenate([high, low], 0), np.concatenate([high.T, high.T, high.T, low.T], 1)
+
+
+def column_tables(n_col, cols):
+    freqs = np.arange(KY) - KY // 2
+    forward = []
+    back = []
+    for place in range(n_col):
+        angle = angles(freqs, place * cols + np.arange(cols), n_col * cols)
+        both = np.concatenate([np.cos(angle), np.sin(angle)], 1)
+        high, low = split_table(both)
+        forward.append(np.concatenate([high, low], 0))
+        both = np.concatenate([np.cos(angle), np.sin(angle)], 0)
+        high, low = split_table(both)
+        back.append(
+            np.concatenate(
+                [
+                    np.concatenate([high, low], 1),
+                    np.concatenate([high, low], 1),
+                    np.concatenate([high, np.zeros_like(low)], 1),
+                ],
+                0,
+            )
+        )
+    return np.stack(forward), np.stack(back)
+
+
+def gelu(value):
+    inner = value * (0.7978845608028654 + 0.035677408136300125 * (value * value))
+    return (0.5 * value) * (1.0 + jnp.tanh(inner))
+
+
+def call(body, outs, in_specs, out_specs, grid=(), scratch=(), flops=0, moved=0, alias=None, limit=8, near=()):
+    single = not isinstance(outs, tuple)
+    outs = (outs,) if single else outs
+    out_specs = (out_specs,) if single else out_specs
+    run = pl.pallas_call(
+        body,
+        out_shape=tuple(
+            pltpu.HBM(out.shape, out.dtype) if out.size > 2**16 else out for out in outs
+        ),
+        grid=grid,
+        in_specs=in_specs,
+        out_specs=out_specs,
+        scratch_shapes=list(scratch),
+        input_output_aliases=alias or {},
+        compiler_params=pltpu.CompilerParams(vmem_limit_bytes=limit * 1024 * 1024),
+        cost_estimate=pl.CostEstimate(
+            flops=int(flops), bytes_accessed=int(moved), transcendentals=0
+        ),
+    )
+
+    def wrapped(*args):
+        held = [
+            arg
+            if place in near or spec.memory_space == pltpu.SMEM
+            else pltpu.with_memory_space_constraint(arg, pltpu.HBM)
+            for place, (arg, spec) in enumerate(zip(args, in_specs))
+        ]
+        found = run(*held)
+        return found[0] if single else found
+
+    return wrapped
+
+
+def whole(memory=pltpu.VMEM):
+    return pl.BlockSpec(memory_space=memory)
+
+
+def shape(*dims):
+    return jax.ShapeDtypeStruct(dims, F32)
+
+
+def lane_sums(value):
+    folded = jnp.sum(value.reshape(-1, SUBLANES, value.shape[-1]), axis=0)
+    folded = sum(
+        folded[:, start : start + LANES] for start in range(0, folded.shape[1], LANES)
+    )
+    return jnp.sum(folded, axis=0, keepdims=True)
+
+
+def spread(rows, ref):
+    rows = rows + [jnp.zeros_like(rows[0])] * (SUBLANES - len(rows))
+    ref[...] = jnp.broadcast_to(jnp.concatenate(rows, 0)[None], ref.shape)
+
+
+def gathered(ref, row):
+    total = jnp.sum(ref[...], axis=0)
+    return jnp.sum(total[row : row + 1], axis=1, keepdims=True)
+
+
+def squares_body(field_ref, perm_ref, out_ref, low_ref, high_ref, left_ref, right_ref):
+    total = field_ref[0] * field_ref[0]
+    for place in range(1, field_ref.shape[0]):
+        total = total + field_ref[place] * field_ref[place]
+    spread([lane_sums(total)], out_ref)
+    rows, cols, _ = perm_ref.shape
+    low_ref[...] = perm_ref[0]
+    high_ref[...] = perm_ref[rows - 1]
+    for place in range(rows):
+        plane = perm_ref[place].astype(F32)
+        left_ref[place : place + 1, :] = plane[:1]
+        right_ref[place : place + 1, :] = plane[cols - 1 :]
+
+
+def weight_body(weight_ref, out_ref):
+    groups, freq, channels, fine, _ = out_ref.shape
+    parts, deep, _, outs, modes = weight_ref.shape
+    for channel in range(channels):
+        block = weight_ref[:, :, channel].reshape(parts * deep * outs, modes)
+        block = block.T.reshape(freq, groups, fine, parts * deep * outs)
+        for group in range(groups):
+            out_ref[group, :, channel] = block[:, group]
+
+
+def turn_body(weight_ref, out_ref):
+    out_ref[...] = pltpu.roll(weight_ref[...], LANES // 2, 1)
+
+
+def harmonic_faces(perm_ref, low_ref, high_ref, left_ref, right_ref, first_ref, sec_lo, sec_hi, thi_lo, thi_hi):
+    rows, cols, depth = perm_ref.shape
+    planes = [perm_ref[place].astype(F32) for place in range(rows)]
+    line = lax.broadcasted_iota(jnp.int32, (cols, depth), 0)
+    deep = lax.broadcasted_iota(jnp.int32, (cols, depth), 1)
+    before = low_ref[...].astype(F32)
+    after = high_ref[...].astype(F32)
+    around = [jnp.where(before > 0.0, before, planes[0])] + planes
+    around = around + [jnp.where(after > 0.0, after, planes[-1])]
+    for place in range(rows + 1):
+        first_ref[place] = harmonic(around[place], around[place + 1])
+    for place in range(rows):
+        own = planes[place]
+        left = left_ref[place : place + 1]
+        right = right_ref[place : place + 1]
+        left = jnp.where(left > 0.0, left, own[:1])
+        right = jnp.where(right > 0.0, right, own[cols - 1 :])
+        lower = jnp.where(line == 0, left, pltpu.roll(own, 1, 0))
+        upper = jnp.where(line == cols - 1, right, pltpu.roll(own, cols - 1, 0))
+        sec_lo[place] = harmonic(own, lower)
+        sec_hi[place] = harmonic(own, upper)
+        lower = jnp.where(deep == 0, own, pltpu.roll(own, 1, 1))
+        upper = jnp.where(deep == depth - 1, own, pltpu.roll(own, depth - 1, 1))
+        thi_lo[place] = harmonic(own, lower)
+        thi_hi[place] = harmonic(own, upper)
+
+
+def scale_of(total, cells):
+    return jnp.sqrt(total / cells + 1e-06)
+
+
+def lift_channel(weight_ref, channel, scaled, log_perm):
+    return gelu(
+        weight_ref[0, channel] * scaled
+        + (weight_ref[1, channel] * log_perm + weight_ref[2, channel])
+    )
+
+
+def transform(lift_ref, deep_ref, col_ref, scaled, log_perm, spectra_ref, zt_ref):
+    half = 2 * KZ
+    cols = scaled.shape[1]
+    for channel in range(0, CHANNELS, 2):
+        lifted = jnp.concatenate(
+            [lift_channel(lift_ref, channel + j, scaled, log_perm) for j in range(2)], 1
+        )
+        high, low = split(lifted)
+        part = matmul(deep_ref[...], high)
+        part = part[:half] + part[half:] + matmul(deep_ref[:half], low)
+        for j in range(2):
+            zt_ref[pl.ds(channel + j, half, stride=CHANNELS), :] = part[:, j * cols : (j + 1) * cols]
+    groups = half * CHANNELS // LANES
+    waves = zt_ref[...].reshape(groups, 2, LANES // 2, cols)
+    turned = jnp.concatenate([waves[:, 1:], -waves[:, :1]], 1)
+    waves = jnp.concatenate(
+        [waves.reshape(groups * LANES, cols), turned.reshape(groups * LANES, cols)], 1
+    )
+    high, low = split(waves)
+    table = col_ref[lax.axis_index("col")]
+    part = matmul_nt(table, high)
+    part = part[:KY] + part[KY:] + matmul_nt(table[:KY], low)
+    n_col = KY // SUBLANES
+    for row in range(groups):
+        for col in range(n_col):
+            spectra_ref[row * n_col + col, 0] = part[
+                col * SUBLANES : (col + 1) * SUBLANES, row * LANES : (row + 1) * LANES
+            ]
+
+
+def lift_first_body(cells, lift_ref, sums_ref, res_ref, perm_ref, deep_ref, col_ref, spectra_ref, zt_ref):
+    scale = scale_of(gathered(sums_ref, 0), cells)
+    scaled = (res_ref[0] / scale).T
+    log_perm = jnp.log(perm_ref[0].astype(F32)).T
+    transform(lift_ref, deep_ref, col_ref, scaled, log_perm, spectra_ref, zt_ref)
+
+
+def next_scalars(first_ref, sums_ref):
+    curvature = gathered(sums_ref, 0)
+    alpha = gathered(sums_ref, 1) / curvature
+    total = gathered(first_ref, 0) + alpha * (
+        alpha * gathered(sums_ref, 2) - 2.0 * gathered(sums_ref, 3)
+    )
+    return curvature, alpha, jnp.maximum(total, 0.0)
+
+
+def lift_next_body(cells, lift_ref, first_ref, sums_ref, res_ref, image_ref, perm_ref, deep_ref, col_ref, spectra_ref, next_ref, zt_ref):
+    _, alpha, total = next_scalars(first_ref, sums_ref)
+    scale = scale_of(total, cells)
+    residual = res_ref[0] - alpha * image_ref[0]
+    next_ref[0] = residual
+    scaled = (residual / scale).T
+    log_perm = jnp.log(perm_ref[0].astype(F32)).T
+    transform(lift_ref, deep_ref, col_ref, scaled, log_perm, spectra_ref, zt_ref)
+
+
+def point_body(scale_of_refs, lift_ref, mix_ref, *refs):
+    *scalar_refs, res_ref, perm_ref, _, _, point_ref, scaled_ref, log_ref, lifted_ref = refs
+    scaled_ref[...] = (res_ref[0] / scale_of_refs(*scalar_refs)).T
+    log_ref[...] = jnp.log(perm_ref[0].astype(F32)).T
+    size = lifted_ref.shape[1]
+    group = 4
+
+    def step(index, carry):
+        lines = pl.ds(pl.multiple_of(index * size, size), size)
+        scaled = scaled_ref[lines, :]
+        log_perm = log_ref[lines, :]
+        for channel in range(CHANNELS):
+            lifted_ref[channel] = lift_channel(lift_ref, channel, scaled, log_perm)
+        for first in range(0, CHANNELS, group):
+            sums = [mix_ref[first + j, CHANNELS] for j in range(group)]
+            for channel in range(CHANNELS):
+                lifted = lifted_ref[channel]
+                sums = [
+                    total + mix_ref[first + j, channel] * lifted for j, total in enumerate(sums)
+                ]
+            for j, total in enumerate(sums):
+                point_ref[0, first + j, lines, :] = total
+        return carry
+
+    lax.fori_loop(0, scaled_ref.shape[0] // size, step, 0)
+
+
+def modes_body(cells, n_row, n_col, recv_ref, weight_ref, other_ref, _, out_ref, field_ref, turned_ref, spec_ref, odd_ref):
+    rows = recv_ref.shape[1]
+    places = n_row * rows
+    tile = (SUBLANES, LANES)
+    lane = lax.broadcasted_iota(jnp.int32, tile, 1)
+    first = lane < LANES // 2
+    sign = jnp.where(first, 1.0, -1.0).astype(F32)
+    base = lane - lane % CHANNELS
+
+    def turn(value):
+        return pltpu.roll(value, LANES // 2, 1) * sign
+
+    for row in range(n_row):
+        for place in range(rows):
+            value = recv_ref[row * n_col, place]
+            for col in range(1, n_col):
+                value = value + recv_ref[row * n_col + col, place]
+            field_ref[row * rows + place] = value
+            turned_ref[row * rows + place] = turn(value)
+    angle = 2.0 * np.pi / places
+    half = KX // 2
+
+    def weigh(coefs, ref):
+        total = None
+        for place, coef in enumerate(coefs):
+            coef = float(coef)
+            if abs(coef) < 1e-12:
+                continue
+            term = ref[place]
+            if coef == -1.0:
+                term = -term
+            elif coef != 1.0:
+                term = coef * term
+            total = term if total is None else total + term
+        return jnp.zeros(tile, F32) if total is None else total
+
+    for freq in range(half + 1):
+        turns = freq * np.arange(places) % places
+        even = weigh(np.cos(angle * turns), field_ref)
+        odd = weigh(np.sin(angle * turns), turned_ref)
+        if freq < half:
+            spec_ref[half + freq] = even + odd
+        if freq > 0:
+            spec_ref[half - freq] = even - odd
+
+    def mix(freq, carry):
+        value = spec_ref[freq]
+        same = [None, None]
+        cross = [None, None]
+        for channel in range(CHANNELS):
+            wide = jnp.take_along_axis(value, base + channel, axis=1)
+            for sums, ref in ((same, weight_ref), (cross, other_ref)):
+                term = ref[freq, channel] * wide
+                kept = sums[channel % 2]
+                sums[channel % 2] = term if kept is None else kept + term
+        same = same[0] + same[1]
+        cross = cross[0] + cross[1]
+        total = jnp.where(
+            first,
+            same - pltpu.roll(same, LANES // 2, 1),
+            cross + pltpu.roll(cross, LANES // 2, 1),
+        )
+        field_ref[freq] = total
+        turned_ref[freq] = -turn(total)
+        return carry
+
+    lax.fori_loop(0, KX, mix, 0)
+    gain = 1.0 / cells
+    evens = [field_ref[half] * gain]
+    odds = [None]
+    for freq in range(1, half):
+        evens.append((field_ref[half + freq] + field_ref[half - freq]) * gain)
+        odds.append((turned_ref[half + freq] - turned_ref[half - freq]) * gain)
+    evens.append(field_ref[0] * gain)
+    odds.append(-turned_ref[0] * gain)
+    for freq in range(half + 1):
+        spec_ref[freq] = evens[freq]
+        if freq > 0:
+            odd_ref[freq] = odds[freq]
+
+    def store(place, value):
+        for col in range(n_col):
+            out_ref[(place // rows) * n_col + col, place % rows] = value
+
+    for place in range(places // 2 + 1):
+        turns = place * np.arange(half + 1) % places
+        even = weigh(np.cos(angle * turns), spec_ref)
+        odd = weigh(np.sin(angle * turns), odd_ref)
+        store(place, even + odd)
+        if 0 < place < places // 2:
+            store(places - place, even - odd)
+
+
+def back_transform(recv_ref, point_ref, proj_ref, col_ref, deep_ref, wave_ref, scale):
+    groups = 2 * KZ * CHANNELS // LANES
+    n_col = KY // SUBLANES
+    cols = col_ref.shape[2] // 2
+    lane = lax.broadcasted_iota(jnp.int32, (KY, LANES), 1)
+    sign = jnp.where(lane < LANES // 2, -1.0, 1.0).astype(F32)
+    half = 2 * KZ
+    pieces = []
+    for row in range(groups):
+        value = recv_ref[row * n_col : (row + 1) * n_col, 0].reshape(KY, LANES)
+        turned = pltpu.roll(value, LANES // 2, 1) * sign
+        both = jnp.concatenate([value, turned], 0)
+        pieces.append(jnp.concatenate(split_three(both), 0).T.astype(BF16))
+    part = matmul(jnp.concatenate(pieces, 0), col_ref[lax.axis_index("col")])
+    wave_ref[...] = part[:, :cols] + part[:, cols:]
+    total = None
+    for out in range(0, CHANNELS, 2):
+        waves = jnp.concatenate(
+            [wave_ref[pl.ds(out + j, half, stride=CHANNELS), :] for j in range(2)], 1
+        )
+        high, middle, low = (part.astype(BF16) for part in split_three(waves))
+        spatial = matmul(deep_ref[...], jnp.concatenate([high, middle, low, high], 0))
+        for j in range(2):
+            hidden = gelu(spatial[:, j * cols : (j + 1) * cols] + point_ref[0, out + j])
+            term = proj_ref[out + j] * hidden
+            total = term if total is None else total + term
+    return (scale * (total + proj_ref[CHANNELS])).T
+
+
+def put_edges(update, low_ref, high_ref, left_ref, right_ref):
+    step = pl.program_id(0)
+    left_ref[pl.ds(step, 1), :] = update[:1]
+    right_ref[pl.ds(step, 1), :] = update[update.shape[0] - 1 :]
+
+    @pl.when(step == 0)
+    def _():
+        low_ref[...] = update
+
+    @pl.when(step == pl.num_programs(0) - 1)
+    def _():
+        high_ref[...] = update
+
+
+def back_first_body(cells, proj_ref, sums_ref, recv_ref, point_ref, col_ref, deep_ref, kept_ref, *refs):
+    *edges, wave_ref = refs
+    scale = scale_of(gathered(sums_ref, 0), cells)
+    update = back_transform(
+        recv_ref, point_ref, proj_ref, col_ref, deep_ref, wave_ref, scale
+    )
+    kept_ref[0, 0] = update
+    put_edges(update, *edges)
+
+
+def back_next_body(cells, proj_ref, first_ref, sums_ref, recv_ref, point_ref, col_ref, deep_ref, image_ref, _, kept_ref, out_ref, *refs):
+    *edges, wave_ref, acc_ref = refs
+    _, _, total = next_scalars(first_ref, sums_ref)
+    update = back_transform(
+        recv_ref, point_ref, proj_ref, col_ref, deep_ref, wave_ref, scale_of(total, cells)
+    )
+    kept_ref[0, 0] = update
+    put_edges(update, *edges)
+    line = lane_sums(update * image_ref[0])
+    step = pl.program_id(0)
+
+    @pl.when(step == 0)
+    def _():
+        acc_ref[...] = jnp.zeros_like(acc_ref)
+
+    acc_ref[0:1] += line
+
+    @pl.when(step == pl.num_programs(0) - 1)
+    def _():
+        spread([acc_ref[0:1]], out_ref)
+
+
+def stencil(own, before, after, left, right, faces):
+    first_lo, first_hi, sec_lo, sec_hi, thi_lo, thi_hi = (ref[0] for ref in faces)
+    cols, depth = own.shape
+    line = lax.broadcasted_iota(jnp.int32, (cols, depth), 0)
+    deep = lax.broadcasted_iota(jnp.int32, (cols, depth), 1)
+    total = first_lo * (own - before)
+    total = total + first_hi * (own - after)
+    other = jnp.where(line == 0, left, pltpu.roll(own, 1, 0))
+    total = total + sec_lo * (own - other)
+    other = jnp.where(line == cols - 1, right, pltpu.roll(own, cols - 1, 0))
+    total = total + sec_hi * (own - other)
+    other = jnp.where(deep == 0, 0.0, pltpu.roll(own, 1, 1))
+    total = total + thi_lo * (own - other)
+    other = jnp.where(deep == depth - 1, 0.0, pltpu.roll(own, depth - 1, 1))
+    return total + thi_hi * (own - other)
+
+
+def add_sums(terms, out_ref, acc_ref):
+    step = pl.program_id(0)
+
+    @pl.when(step == 0)
+    def _():
+        acc_ref[...] = jnp.zeros_like(acc_ref)
+
+    for j, term in enumerate(terms):
+        acc_ref[j : j + 1] += lane_sums(term)
+
+    @pl.when(step == pl.num_programs(0) - 1)
+    def _():
+        spread([acc_ref[j : j + 1] for j in range(len(terms))], out_ref)
+
+
+def around(ref, index, low, high):
+    step = pl.program_id(0)
+    last = pl.num_programs(0) - 1
+    before = jnp.where(step == 0, low, ref[index, jnp.maximum(step - 1, 0)])
+    after = jnp.where(step == last, high, ref[index, jnp.minimum(step + 1, last)])
+    return ref[index, step], before, after
+
+
+def operator_first_body(kept_ref, low_ref, high_ref, left_ref, right_ref, res_ref, *refs):
+    *faces, image_ref, out_ref, acc_ref = refs
+    line = pl.ds(pl.program_id(0), 1)
+    own, before, after = around(kept_ref, 0, low_ref[...], high_ref[...])
+    image = stencil(own, before, after, left_ref[line, :], right_ref[line, :], faces)
+    residual = res_ref[0]
+    image_ref[0] = image
+    add_sums((own * image, residual * own, image * image, residual * image), out_ref, acc_ref)
+
+
+def operator_next_body(first_ref, beta_ref, kept_ref, low_ref, high_ref, left_ref, right_ref, old_low, old_high, old_left, old_right, res_ref, *refs):
+    *faces, way_ref, image_ref, out_ref, acc_ref = refs
+    line = pl.ds(pl.program_id(0), 1)
+    beta = gathered(beta_ref, 0) / gathered(first_ref, 0)
+    fields = zip(
+        around(kept_ref, 1, low_ref[...], high_ref[...]),
+        around(kept_ref, 0, old_low[...], old_high[...]),
+    )
+    own, before, after = (new - beta * old for new, old in fields)
+    left = left_ref[line, :] - beta * old_left[line, :]
+    right = right_ref[line, :] - beta * old_right[line, :]
+    image = stencil(own, before, after, left, right, faces)
+    way_ref[0] = own
+    image_ref[0] = image
+    add_sums((own * image, res_ref[0] * own), out_ref, acc_ref)
+
+
+def last_body(first_ref, sums_ref, old_ref, way_ref, res_ref, image_ref, sol_ref, out_ref):
+    alpha = gathered(first_ref, 1) / gathered(first_ref, 0)
+    later = gathered(sums_ref, 1) / gathered(sums_ref, 0)
+    sol_ref[0] = alpha * old_ref[0, 0] + later * way_ref[0]
+    out_ref[0] = res_ref[0] - later * image_ref[0]
+
+
+def exchange(blocks):
+    return lax.all_to_all(blocks, BOTH, split_axis=0, concat_axis=0, tiled=True)
+
+
+def neighbours(low, high, left, right):
+    found = []
+    for axis, first, last in (("row", low, high), ("col", left, right)):
+        forward = [(i, i + 1) for i in range(lax.axis_size(axis) - 1)]
+        backward = [(target, source) for source, target in forward]
+        found.append(lax.ppermute(last, axis, forward))
+        found.append(lax.ppermute(first, axis, backward))
+    return found
+
+
+def tiled_local(right_side, permeability, lift_weight, spectral_weight, mix_weight, proj_weight):
+    rows, cols, depth = right_side.shape
+    n_row = lax.axis_size("row")
+    n_col = lax.axis_size("col")
+    count = n_row * n_col
+    cells = float(rows * n_row * cols * n_col * depth)
+    freq = KX // n_col
+    deep_forward, deep_back = (jnp.asarray(t) for t in deep_tables(n_row, depth))
+    col_forward, col_back = (jnp.asarray(t) for t in column_tables(n_col, cols))
+    lift_weight = lift_weight.T
+    field = shape(rows, cols, depth)
+    field_bytes = 4 * rows * cols * depth
+    partial = shape(count, SUBLANES, LANES)
+    spectra = shape(count, rows, SUBLANES, LANES)
+    spectra_bytes = 4 * count * rows * SUBLANES * LANES
+    smem = whole(pltpu.SMEM)
+    vmem = whole()
+    plane = pl.BlockSpec((1, cols, depth), lambda i: (i, 0, 0))
+    spectra_block = pl.BlockSpec((count, 1, SUBLANES, LANES), lambda i: (0, i, 0, 0))
+    point_block = pl.BlockSpec((1, CHANNELS, depth, cols), lambda i: (i, 0, 0, 0))
+    kept_shape = shape(ITERS, rows, cols, depth)
+    lift_flops = 2.0e9
+    back_flops = 2.0e9
+
+    edge_shapes = (shape(cols, depth),) * 2 + (shape(rows, depth),) * 2
+    thin = jax.ShapeDtypeStruct((cols, depth), permeability.dtype)
+    squares, *edges = call(
+        squares_body,
+        (partial, thin, thin) + edge_shapes[2:],
+        [vmem, vmem],
+        (vmem,) * 5,
+        moved=field_bytes,
+    )(right_side, permeability)
+    squares = exchange(squares)
+
+    weights = call(
+        weight_body,
+        shape(n_col, freq, CHANNELS, SUBLANES, LANES),
+        [vmem],
+        vmem,
+        moved=8 * spectral_weight.size,
+    )(spectral_weight)
+    weights = lax.all_to_all(weights, "col", split_axis=0, concat_axis=0, tiled=True)
+    weights = weights.reshape(KX * CHANNELS * SUBLANES, LANES)
+    others = call(
+        turn_body,
+        shape(*weights.shape),
+        [vmem],
+        vmem,
+        moved=8 * weights.size,
+    )(weights)
+    weights, others = (
+        array.reshape(KX, CHANNELS, SUBLANES, LANES) for array in (weights, others)
+    )
+
+    first, *faces = call(
+        harmonic_faces,
+        (shape(rows + 1, cols, depth),) + (field,) * 4,
+        [vmem] * 5,
+        (vmem,) * 5,
+        moved=6 * field_bytes,
+        near=(1, 2, 3, 4),
+    )(permeability, *neighbours(*edges))
+    faces = [first, first] + faces
+    next_plane = pl.BlockSpec((1, cols, depth), lambda i: (i + 1, 0, 0))
+    face_specs = [plane, next_plane] + [plane] * 4
+    acc_scratch = pltpu.VMEM((SUBLANES, LANES), F32)
+
+    zt_scratch = pltpu.VMEM((2 * KZ * CHANNELS, cols), F32)
+
+    anywhere = whole(pl.ANY)
+
+    def points(scale_of_refs, scalars, residual, part, before, after):
+        first = part * rows // 2
+        moved_plane = pl.BlockSpec((1, cols, depth), lambda i: (first + i, 0, 0))
+        count_in = 4 + len(scalars)
+        return call(
+            functools.partial(point_body, scale_of_refs),
+            shape(rows, CHANNELS, depth, cols),
+            [smem, smem]
+            + [vmem] * len(scalars)
+            + [moved_plane, moved_plane, anywhere, anywhere],
+            pl.BlockSpec((1, CHANNELS, depth, cols), lambda i: (first + i, 0, 0, 0)),
+            grid=(rows // 2,),
+            scratch=[
+                pltpu.VMEM((depth, cols), F32),
+                pltpu.VMEM((depth, cols), F32),
+                pltpu.VMEM((CHANNELS, 4 * SUBLANES, cols), F32),
+            ],
+            flops=2.5e9,
+            moved=9 * field_bytes,
+            alias={count_in: 0} if part else None,
+            limit=12,
+        )(lift_weight, mix_weight, *scalars, residual, permeability, before, after)
+
+    def modes(received, before):
+        places = rows * n_row
+        tiles = lambda size: pltpu.VMEM((size, SUBLANES, LANES), F32)
+        return call(
+            functools.partial(modes_body, cells, n_row, n_col),
+            spectra,
+            [vmem, vmem, vmem, anywhere],
+            vmem,
+            scratch=[tiles(places), tiles(places), tiles(KX), tiles(KX)],
+            moved=2 * spectra_bytes + 8 * weights.size,
+            near=(0,),
+        )(received, weights, others, before)
+
+    def mixed_modes(blocks, scale_of_refs, scalars, residual):
+        received = exchange(blocks)
+        point = points(scale_of_refs, scalars, residual, 0, right_side, right_side)
+        blocks = modes(received, point)
+        received = exchange(blocks)
+        point = points(scale_of_refs, scalars, residual, 1, point, blocks)
+        return received, point
+
+    blocks = call(
+        functools.partial(lift_first_body, cells),
+        spectra,
+        [smem, vmem, plane, plane, vmem, vmem],
+        spectra_block,
+        grid=(rows,),
+        scratch=[zt_scratch],
+        flops=lift_flops,
+        moved=2 * field_bytes + spectra_bytes,
+    )(lift_weight, squares, right_side, permeability, deep_forward, col_forward)
+    received, point = mixed_modes(
+        blocks,
+        lambda sums_ref: scale_of(gathered(sums_ref, 0), cells),
+        (squares,),
+        right_side,
+    )
+    kept, *edges = call(
+        functools.partial(back_first_body, cells),
+        (kept_shape,) + edge_shapes,
+        [smem, vmem, spectra_block, point_block, vmem, vmem],
+        (pl.BlockSpec((1, 1, cols, depth), lambda i: (0, i, 0, 0)),) + (vmem,) * 4,
+        grid=(rows,),
+        scratch=[zt_scratch],
+        limit=12,
+        flops=back_flops,
+        moved=18 * field_bytes,
+    )(proj_weight, squares, received, point, col_back, deep_back)
+
+    old_halo = neighbours(*edges)
+    args = (kept, *old_halo, right_side, *faces)
+    image, sums = call(
+        operator_first_body,
+        (field, partial),
+        [vmem] * 5 + [plane] + face_specs,
+        (plane, vmem),
+        grid=(rows,),
+        scratch=[acc_scratch],
+        moved=9 * field_bytes,
+        near=(1, 2, 3, 4),
+    )(*args)
+    sums = exchange(sums)
+
+    blocks, residual = call(
+        functools.partial(lift_next_body, cells),
+        (spectra, field),
+        [smem, vmem, vmem, plane, plane, plane, vmem, vmem],
+        (spectra_block, plane),
+        grid=(rows,),
+        scratch=[zt_scratch],
+        flops=lift_flops,
+        moved=4 * field_bytes + spectra_bytes,
+    )(lift_weight, squares, sums, right_side, image, permeability, deep_forward, col_forward)
+    received, point = mixed_modes(
+        blocks,
+        lambda first_ref, sums_ref: scale_of(next_scalars(first_ref, sums_ref)[2], cells),
+        (squares, sums),
+        residual,
+    )
+    kept, beta, *edges = call(
+        functools.partial(back_next_body, cells),
+        (kept_shape, partial) + edge_shapes,
+        [smem, vmem, vmem, spectra_block, point_block, vmem, vmem, plane, whole(pl.ANY)],
+        (pl.BlockSpec((1, 1, cols, depth), lambda i: (1, i, 0, 0)),) + (vmem,) * 5,
+        grid=(rows,),
+        limit=12,
+        scratch=[zt_scratch, acc_scratch],
+        flops=back_flops,
+        moved=19 * field_bytes,
+        alias={8: 0},
+    )(proj_weight, squares, sums, received, point, col_back, deep_back, image, kept)
+
+    beta = exchange(beta)
+    halo = neighbours(*edges)
+    args = (sums, beta, kept, *halo, *old_halo, residual, *faces)
+    way, image, later = call(
+        operator_next_body,
+        (field, field, partial),
+        [vmem] * 11 + [plane] + face_specs,
+        (plane, plane, vmem),
+        grid=(rows,),
+        scratch=[acc_scratch],
+        near=(0, 1, 3, 4, 5, 6, 7, 8, 9, 10),
+        moved=11 * field_bytes,
+    )(*args)
+    later = exchange(later)
+    answer, residual = call(
+        last_body,
+        (field, field),
+        [vmem, vmem, pl.BlockSpec((1, 1, cols, depth), lambda i: (0, i, 0, 0)), plane, plane, plane],
+        (plane, plane),
+        grid=(rows,),
+        moved=6 * field_bytes,
+    )(sums, later, kept, way, residual, image)
+    return (answer, residual, kept)
+
+
+def fits_tiles(mesh, block):
+    rows, cols, depth = block
+    n_row, n_col = mesh.shape["row"], mesh.shape["col"]
+    return (
+        ITERS == 2
+        and KZ == n_row * (LANES // (2 * CHANNELS))
+        and KY == n_col * SUBLANES
+        and KX % n_col == 0
+        and cols == LANES
+        and depth % LANES == 0
+        and rows * n_row >= KX
+    )
+
+
 def solution(mesh):
     placed = (
         P("row", "col", None),
@@ -225,10 +1007,16 @@
         P(),
         P(),
     )
-    return jax.shard_map(
-        local,
-        mesh=mesh,
-        in_specs=placed,
-        out_specs=(P("row", "col", None), P("row", "col", None), P(None, "row", "col", None)),
-        check_vma=False,
-    )
+
+    def run(right_side, *others):
+        rows, cols, depth = right_side.shape
+        block = (rows // mesh.shape["row"], cols // mesh.shape["col"], depth)
+        return jax.shard_map(
+            tiled_local if fits_tiles(mesh, block) else local,
+            mesh=mesh,
+            in_specs=placed,
+            out_specs=(P("row", "col", None), P("row", "col", None), P(None, "row", "col", None)),
+            check_vma=False,
+        )(right_side, *others)
+
+    return run

time: 791 us -> 240 us (0.30); the launches traced: 780 us -> 239 us
  matrix products: 184 us -> 0 us
  blocking collectives: 208 us -> 30.5 us
  Pallas kernels: 0 us -> 116 us
  waiting for transfers between devices: 136 us -> 36.9 us
  local copies, waits for them, and re-layouts: 86.6 us -> 2.35 us
  starting transfers between devices: 106 us -> 52.2 us
  other arithmetic: 50.6 us -> 0 us
    psum x5 -> x0, blocking collectives: 208 us -> none  [the longest x2 85.5 us: local(): lax.psum((jnp.sum(direction * image), jnp.sum(residual * direction)), ('r...]
    dot_general x44 -> x0, matrix products: 184 us -> none  [einsum_high(): return jnp.einsum(form, left, right, precision=HIGHEST)]
    pallas_call x0 -> x17, Pallas kernels: none -> 116 us  [wrapped(): found = run(*held)]
    all_to_all x16 -> x7, waiting for transfers between devices: 129 us -> 30 us  [the longest x6 25.8 us: exchange(): return lax.all_to_all(blocks, BOTH, split_axis=0, concat_axis=0, tiled=True)]
    all_to_all x16 -> x7, starting transfers between devices: 67.7 us -> 25.2 us  [the longest x6 21.7 us: exchange(): return lax.all_to_all(blocks, BOTH, split_axis=0, concat_axis=0, tiled=True)]
    all_to_all x0 -> x2, blocking collectives: none -> 30.5 us  [exchange(): return lax.all_to_all(blocks, BOTH, split_axis=0, concat_axis=0, tiled=True)]
    all_to_all x25 -> x0, local copies, waits for them, and re-layouts: 29.3 us -> none  [the longest x4 8.44 us: spectral_transpose(): lax.all_to_all(first_imag, 'col', split_axis=1, concat_axis=2, tiled=True)]
    unnamed x71 -> x18, local copies, waits for them, and re-layouts: 23.1 us -> 2.35 us
  transfers between devices with their start and end apart: 28 -> 19, of which waited for: 18 -> 9; matrix products, arithmetic and copies ran while one was open for 23% -> 0% of each run, Pallas kernels for 0% -> 24%
where the time goes in v1:
time: 240 us; the launch traced here: 239 us
  Pallas kernels  116 us (48%)
  starting transfers between devices  52.2 us (22%)
  waiting for transfers between devices  36.9 us (15%)
  blocking collectives  30.5 us (13%)
    pallas_call x17, Pallas kernels, wrapped(): found = run(*held)  116 us
    all_to_all x2, blocking collectives, exchange(): return lax.all_to_all(blocks, BOTH, split_axis=0, concat_axis=0, tiled=True)  30.5 us
    all_to_all x6, waiting for transfers between devices, exchange(): return lax.all_to_all(blocks, BOTH, split_axis=0, concat_axis=0, tiled=True)  25.8 us
    all_to_all x6, starting transfers between devices, exchange(): return lax.all_to_all(blocks, BOTH, split_axis=0, concat_axis=0, tiled=True)  21.7 us
    ppermute x6, starting transfers between devices, neighbours(): found.append(lax.ppermute(last, axis, forward))  19.2 us
    ppermute x6, starting transfers between devices, neighbours(): found.append(lax.ppermute(first, axis, backward))  7.74 us
    ppermute x6, waiting for transfers between devices, neighbours(): found.append(lax.ppermute(first, axis, backward))  6.06 us
  transfers between devices with their start and end apart: 19, of which 9 were waited for; matrix products, arithmetic and copies ran while one was open for 0% of the time, Pallas kernels for 24%

profile of v1, /device:TPU:0, one launch (start us, length us, event | category | flops | bytes accessed | tf_op | source)
XLA Modules:
  0.0 239.0 jit_solution(4924017001940703572)
XLA Ops:
  0.7 1.8 shard_map.121
  2.5 7.3 %all-to-all-start = ((f32[32,8,128]{2,1,0:T(8,128)}), f32[32,8,128]{2,1,0:T(8,128)S(1)}, u32[]{:S(2)}, u32[]{:S(2)}) async-start(f32[32,8,128]{2,1,0:T(8,128)} %get-tuple-element.33), calls=%async_computation | async-start | bytes 262144 | tf_op jit(solution)/shard_map/all_to_all | solution.py:762
  9.8 2.5 %shard_map.123 = f32[4,4,16,8,128]{4,3,2,1,0:T(8,128)} custom-call(f32[2,4,16,16,128]{4,3,2,1,0:T(8,128)} %weight_ref.1), custom_call_target="tpu_custom_call" | custom-call | bytes 2097152 | tf_op jit(solution)/shard_map/pallas_call | solution.py:338
  12.3 5.7 %all-to-all-done.sums_ref.refs_0_.first_ref = f32[32,8,128]{2,1,0:T(8,128)S(1)} async-done(((f32[32,8,128]{2,1,0:T(8,128)}), f32[32,8,128]{2,1,0:T(8,128)S(1)}, u32[]{:S(2)}, u32[]{:S(2)}) %all-to-all-start) | async-done | bytes 131104 | tf_op jit(solution)/shard_map/all_to_all | solution.py:762
  18.0 3.5 %all-to-all-start.2 = ((f32[4,4,16,8,128]{4,3,2,1,0:T(8,128)}), f32[4,4,16,8,128]{4,3,2,1,0:T(8,128)S(1)}, u32[]{:S(2)}, u32[]{:S(2)}) async-start(f32[4,4,16,8,128]{4,3,2,1,0:T(8,128)} %shard_map.123), calls=%async_computation.2 | async-start | bytes 2097152 | tf_op jit(solution)/shard_map/all_to_all | solution.py:817
  22.3 9.6 %shard_map.122 = f32[32,4,8,128]{3,2,1,0:T(8,128)} custom-call(f32[3,16]{1,0:T(4,128)S(1)} %bitcast.4, f32[32,8,128]{2,1,0:T(8,128)} %copy-done.6, f32[4,128,256]{2,1,0:T(8,128)} %refs_5_.1, bf16[4,128,256]{2,1,0:T(8,128)(2,1)} %refs_3_.5, bf16[128,256]{1,0:T(8,128)(2,1)} %constant.8.clone.deep_ref, bf16[4,64,256]{2,1,0:T(8,128)(2,1)} %constant.10.clone.col_ref), custom_call_target="tpu_custom_call" | custom-call | flops 2000000000 | bytes 1572864 | tf_op jit(solution)/shard_map/pallas_call | solution.py:338
  31.9 4.1 %all-to-all-done.2 = f32[4,4,16,8,128]{4,3,2,1,0:T(8,128)S(1)} async-done(((f32[4,4,16,8,128]{4,3,2,1,0:T(8,128)}), f32[4,4,16,8,128]{4,3,2,1,0:T(8,128)S(1)}, u32[]{:S(2)}, u32[]{:S(2)}) %all-to-all-start.2) | async-done | bytes 1048608 | tf_op jit(solution)/shard_map/all_to_all | solution.py:817
  36.0 2.6 %all-to-all-start.1 = ((f32[32,4,8,128]{3,2,1,0:T(8,128)}), f32[32,4,8,128]{3,2,1,0:T(8,128)S(1)}, u32[]{:S(2)}, u32[]{:S(2)}) async-start(f32[32,4,8,128]{3,2,1,0:T(8,128)} %shard_map.122), calls=%async_computation.1 | async-start | bytes 1048576 | tf_op jit(solution)/shard_map/all_to_all | solution.py:762
  38.6 9.7 %shard_map.125._.refs_3_ = f32[4,16,256,128]{3,2,1,0:T(8,128)} custom-call(f32[3,16]{1,0:T(4,128)S(1)} %bitcast.5, f32[16,17]{1,0:T(8,128)S(1)} %copy-done.1, f32[32,8,128]{2,1,0:T(8,128)} %copy-done.6, f32[4,128,256]{2,1,0:T(8,128)} %refs_5_.1, bf16[4,128,256]{2,1,0:T(8,128)(2,1)} %refs_3_.5, f32[4,128,256]{2,1,0:T(8,128)} %refs_5_.1, f32[4,128,256]{2,1,0:T(8,128)} %refs_5_.1), custom_call_target="tpu_custom_call" | custom-call | flops 2500000000 | bytes 4718592 | tf_op jit(solution)/shard_map/pallas_call | solution.py:338
  48.3 2.5 %shard_map.124 = f32[2048,128]{1,0:T(8,128)} custom-call(f32[2048,128]{1,0:T(8,128)} %bitcast.10), custom_call_target="tpu_custom_call" | custom-call | bytes 2097152 | tf_op jit(solution)/shard_map/pallas_call | solution.py:338
  50.9 3.3 %all-to-all-done.1.recv_ref = f32[32,4,8,128]{3,2,1,0:T(8,128)S(1)} async-done(((f32[32,4,8,128]{3,2,1,0:T(8,128)}), f32[32,4,8,128]{3,2,1,0:T(8,128)S(1)}, u32[]{:S(2)}, u32[]{:S(2)}) %all-to-all-start.1) | async-done | bytes 524320 | tf_op jit(solution)/shard_map/all_to_all | solution.py:762
  54.1 6.6 %shard_map.126.refs_4_ = f32[32,4,8,128]{3,2,1,0:T(8,128)} custom-call(f32[32,4,8,128]{3,2,1,0:T(8,128)S(1)} %all-to-all-done.1.recv_ref, f32[16,16,8,128]{3,2,1,0:T(8,128)} %bitcast.11, f32[16,16,8,128]{3,2,1,0:T(8,128)} %bitcast.13, f32[4,16,256,128]{3,2,1,0:T(8,128)} %shard_map.125._.refs_3_), custom_call_target="tpu_custom_call" | custom-call | bytes 3145728 | tf_op jit(solution)/shard_map/pallas_call | solution.py:338
  60.7 3.0 %all-to-all-start.3 = ((f32[32,4,8,128]{3,2,1,0:T(8,128)}), f32[32,4,8,128]{3,2,1,0:T(8,128)S(1)}, u32[]{:S(2)}, u32[]{:S(2)}) async-start(f32[32,4,8,128]{3,2,1,0:T(8,128)} %shard_map.126.refs_4_), calls=%async_computation.3 | async-start | bytes 1048576 | tf_op jit(solution)/shard_map/all_to_all | solution.py:762
  63.7 9.8 %shard_map.127.point_ref = f32[4,16,256,128]{3,2,1,0:T(8,128)} custom-call(f32[3,16]{1,0:T(4,128)S(1)} %bitcast.6, f32[16,17]{1,0:T(8,128)S(1)} %copy-done.1, f32[32,8,128]{2,1,0:T(8,128)} %copy-done.6, f32[4,128,256]{2,1,0:T(8,128)} %refs_5_.1, bf16[4,128,256]{2,1,0:T(8,128)(2,1)} %refs_3_.5, ...), custom_call_target="tpu_custom_call", output_to_operand_aliasing={{}: (5, {})} | custom-call | flops 2500000000 | bytes 4718592 | tf_op jit(solution)/shard_map/pallas_call | solution.py:338
  73.5 5.8 %all-to-all-done.3.recv_ref = f32[32,4,8,128]{3,2,1,0:T(8,128)S(1)} async-done(((f32[32,4,8,128]{3,2,1,0:T(8,128)}), f32[32,4,8,128]{3,2,1,0:T(8,128)S(1)}, u32[]{:S(2)}, u32[]{:S(2)}) %all-to-all-start.3) | async-done | bytes 524320 | tf_op jit(solution)/shard_map/all_to_all | solution.py:762
  80.0 9.6 %shard_map.128 = (f32[2,4,128,256]{3,2,1,0:T(8,128)}, f32[128,256]{1,0:T(8,128)S(1)}, f32[128,256]{1,0:T(8,128)S(1)}, f32[4,256]{1,0:T(4,128)S(1)}, f32[4,256]{1,0:T(4,128)S(1)}) custom-call(f32[17]{0:T(128)S(1)} %copy-done.4, f32[32,8,128]{2,1,0:T(8,128)} %copy-done.6, f32[32,4,8,128]{3,2,1,0:T(8,128)} %copy-done.8, ...), custom_call_target="tpu_custom_call" | custom-call | flops 2000000000 | bytes 9437184 | tf_op jit(solution)/shard_map/pallas_call | solution.py:338
  89.6 3.1 %collective-permute-start = (f32[128,256]{1,0:T(8,128)S(1)}, f32[128,256]{1,0:T(8,128)S(1)}, u32[]{:S(2)}, u32[]{:S(2)}) collective-permute-start(f32[128,256]{1,0:T(8,128)S(1)} %get-tuple-element.35), channel_id=1, source_target_pairs={{0,4},{4,8},{8,12},{12,16},{16,20},{20,24},{24,28},{1,5},{5,9},{9,... | collective-permute-start | bytes 393224 | tf_op jit(solution)/shard_map/ppermute | solution.py:770
  92.8 1.3 collective-permute-start.1
  94.1 4.5 %collective-permute-start.4 = (bf16[128,256]{1,0:T(8,128)(2,1)S(1)}, bf16[128,256]{1,0:T(8,128)(2,1)S(1)}, u32[]{:S(2)}, u32[]{:S(2)}) collective-permute-start(bf16[128,256]{1,0:T(8,128)(2,1)S(1)} %get-tuple-element.39), channel_id=1, source_target_pairs={{0,4},{4,8},{8,12},{12,16},{16,20},{20,24},{24,28},{1,5},{5,9},{9,... | collective-permute-start | bytes 196616 | tf_op jit(solution)/shard_map/ppermute | solution.py:770
  98.6 1.3 collective-permute-start.5
  99.9 1.3 collective-permute-start.6
  101.2 0.8 collective-permute-done.6.left_ref
  102.0 1.3 collective-permute-start.7
  103.3 3.1 %collective-permute-done.7.right_ref = f32[4,256]{1,0:T(4,128)S(1)} collective-permute-done((f32[4,256]{1,0:T(4,128)S(1)}, f32[4,256]{1,0:T(4,128)S(1)}, u32[]{:S(2)}, u32[]{:S(2)}) %collective-permute-start.7) | collective-permute-done | bytes 4128 | tf_op jit(solution)/shard_map/ppermute | solution.py:771
  106.4 4.8 %collective-permute-start.2 = (f32[4,256]{1,0:T(4,128)S(1)}, f32[4,256]{1,0:T(4,128)S(1)}, u32[]{:S(2)}, u32[]{:S(2)}) collective-permute-start(f32[4,256]{1,0:T(4,128)S(1)} %get-tuple-element.37), channel_id=1, source_target_pairs={{0,1},{1,2},{2,3},{4,5},{5,6},{6,7},{8,9},{9,10},{10,11},{12,13},{... | collective-permute-start | bytes 12296 | tf_op jit(solution)/shard_map/ppermute | solution.py:770
  111.2 1.3 collective-permute-start.3
  112.5 3.1 %shard_map.129 = (f32[5,128,256]{2,1,0:T(8,128)}, f32[4,128,256]{2,1,0:T(8,128)}, f32[4,128,256]{2,1,0:T(8,128)}, f32[4,128,256]{2,1,0:T(8,128)}, f32[4,128,256]{2,1,0:T(8,128)}) custom-call(bf16[4,128,256]{2,1,0:T(8,128)(2,1)} %refs_3_.5, bf16[128,256]{1,0:T(8,128)(2,1)S(1)} %collective-permute-done.4.low_ref, ...), custom_call_target="tpu_custom_call" | custom-call | bytes 3145728 | tf_op jit(solution)/shard_map/pallas_call | solution.py:338
  115.7 4.8 %shard_map.130 = (f32[4,128,256]{2,1,0:T(8,128)}, f32[32,8,128]{2,1,0:T(8,128)S(1)}) custom-call(f32[2,4,128,256]{3,2,1,0:T(8,128)} %get-tuple-element.34.kept_ref._, f32[128,256]{1,0:T(8,128)S(1)} %collective-permute-done.low_ref.old_low, f32[128,256]{1,0:T(8,128)S(1)} %collective-permute-done.1.high_ref.old_high, ...), custom_call_target="tpu_custom_call" | custom-call | bytes 4718592 | tf_op jit(solution)/shard_map/pallas_call | solution.py:338
  120.5 14.6 %all_to_all.45.sums_ref.refs_1_.first_ref = f32[32,8,128]{2,1,0:T(8,128)} all-to-all(f32[32,8,128]{2,1,0:T(8,128)S(1)} %get-tuple-element.48), channel_id=1, replica_groups=mesh['row'=8,'col'=4] {'row','col'}, dimensions={0} | all-to-all | bytes 262144 | tf_op jit(solution)/shard_map/all_to_all | solution.py:762
  135.1 10.0 %shard_map.131 = (f32[32,4,8,128]{3,2,1,0:T(8,128)}, f32[4,128,256]{2,1,0:T(8,128)}) custom-call(f32[3,16]{1,0:T(4,128)S(1)} %bitcast.7, f32[32,8,128]{2,1,0:T(8,128)} %copy-done.6, f32[32,8,128]{2,1,0:T(8,128)} %all_to_all.45.sums_ref.refs_1_.first_ref, f32[4,128,256]{2,1,0:T(8,128)} %refs_5_.1, f32[4,128,256]{2,1,0:T(8,128)} %get-tuple-element.49.image_ref, ...), custom_call_target="tpu_custom_call" | custom-call | flops 2000000000 | bytes 2621440 | tf_op jit(solution)/shard_map/pallas_call | solution.py:338
  145.1 2.6 %all-to-all-start.5 = ((f32[32,4,8,128]{3,2,1,0:T(8,128)}), f32[32,4,8,128]{3,2,1,0:T(8,128)S(1)}, u32[]{:S(2)}, u32[]{:S(2)}) async-start(f32[32,4,8,128]{3,2,1,0:T(8,128)} %get-tuple-element.50), calls=%async_computation.5 | async-start | bytes 1048576 | tf_op jit(solution)/shard_map/all_to_all | solution.py:762
  147.7 9.9 %shard_map.132._.refs_4_ = f32[4,16,256,128]{3,2,1,0:T(8,128)} custom-call(f32[3,16]{1,0:T(4,128)S(1)} %bitcast.8, f32[16,17]{1,0:T(8,128)S(1)} %copy-done.1, f32[32,8,128]{2,1,0:T(8,128)} %copy-done.6, f32[32,8,128]{2,1,0:T(8,128)} %all_to_all.45.sums_ref.refs_1_.first_ref, f32[4,128,256]{2,1,0:T(8,128)} %get-tuple-element.51.refs_2_.res_ref, ...), custom_call_target="tpu_custom_call" | custom-call | flops 2500000000 | bytes 4718592 | tf_op jit(solution)/shard_map/pallas_call | solution.py:338
  157.6 5.7 %all-to-all-done.5.recv_ref = f32[32,4,8,128]{3,2,1,0:T(8,128)S(1)} async-done(((f32[32,4,8,128]{3,2,1,0:T(8,128)}), f32[32,4,8,128]{3,2,1,0:T(8,128)S(1)}, u32[]{:S(2)}, u32[]{:S(2)}) %all-to-all-start.5) | async-done | bytes 524320 | tf_op jit(solution)/shard_map/all_to_all | solution.py:762
  163.3 6.6 %shard_map.133.refs_5_ = f32[32,4,8,128]{3,2,1,0:T(8,128)} custom-call(f32[32,4,8,128]{3,2,1,0:T(8,128)S(1)} %all-to-all-done.5.recv_ref, f32[16,16,8,128]{3,2,1,0:T(8,128)} %bitcast.12, f32[16,16,8,128]{3,2,1,0:T(8,128)} %bitcast.14, f32[4,16,256,128]{3,2,1,0:T(8,128)} %shard_map.132._.refs_4_), custom_call_target="tpu_custom_call" | custom-call | bytes 3145728 | tf_op jit(solution)/shard_map/pallas_call | solution.py:338
  169.9 3.2 %all-to-all-start.6 = ((f32[32,4,8,128]{3,2,1,0:T(8,128)}), f32[32,4,8,128]{3,2,1,0:T(8,128)S(1)}, u32[]{:S(2)}, u32[]{:S(2)}) async-start(f32[32,4,8,128]{3,2,1,0:T(8,128)} %shard_map.133.refs_5_), calls=%async_computation.6 | async-start | bytes 1048576 | tf_op jit(solution)/shard_map/all_to_all | solution.py:762
  173.0 9.9 %shard_map.134.point_ref = f32[4,16,256,128]{3,2,1,0:T(8,128)} custom-call(f32[3,16]{1,0:T(4,128)S(1)} %bitcast.9, f32[16,17]{1,0:T(8,128)S(1)} %copy-done.1, f32[32,8,128]{2,1,0:T(8,128)} %copy-done.6, f32[32,8,128]{2,1,0:T(8,128)} %all_to_all.45.sums_ref.refs_1_.first_ref, ...), custom_call_target="tpu_custom_call", output_to_operand_aliasing={{}: (6, {})} | custom-call | flops 2500000000 | bytes 4718592 | tf_op jit(solution)/shard_map/pallas_call | solution.py:338
  183.0 5.4 %all-to-all-done.6.recv_ref = f32[32,4,8,128]{3,2,1,0:T(8,128)S(1)} async-done(((f32[32,4,8,128]{3,2,1,0:T(8,128)}), f32[32,4,8,128]{3,2,1,0:T(8,128)S(1)}, u32[]{:S(2)}, u32[]{:S(2)}) %all-to-all-start.6) | async-done | bytes 524320 | tf_op jit(solution)/shard_map/all_to_all | solution.py:762
  188.4 0.8 copy-done.7
  189.2 10.5 %shard_map.135 = (f32[2,4,128,256]{3,2,1,0:T(8,128)}, f32[32,8,128]{2,1,0:T(8,128)}, f32[128,256]{1,0:T(8,128)S(1)}, f32[128,256]{1,0:T(8,128)S(1)}, f32[4,256]{1,0:T(4,128)S(1)}, /*index=5*/f32[4,256]{1,0:T(4,128)S(1)}) custom-call(f32[17]{0:T(128)S(1)} %copy-done.4, f32[32,8,128]{2,1,0:T(8,128)} %copy-done.6, ...), custom_call_target="tpu_custom_call", output_to_operand_aliasing={{0}: (8, {})} | custom-call | flops 2000000000 | bytes 9961472 | tf_op jit(solution)/shard_map/pallas_call | solution.py:338
  199.7 3.1 %all-to-all-start.7 = ((f32[32,8,128]{2,1,0:T(8,128)}), f32[32,8,128]{2,1,0:T(8,128)S(1)}, u32[]{:S(2)}, u32[]{:S(2)}) async-start(f32[32,8,128]{2,1,0:T(8,128)} %get-tuple-element.52), calls=%async_computation.7 | async-start | bytes 262144 | tf_op jit(solution)/shard_map/all_to_all | solution.py:762
  202.8 3.7 %collective-permute-start.8 = (f32[128,256]{1,0:T(8,128)S(1)}, f32[128,256]{1,0:T(8,128)S(1)}, u32[]{:S(2)}, u32[]{:S(2)}) collective-permute-start(f32[128,256]{1,0:T(8,128)S(1)} %get-tuple-element.54), channel_id=1, source_target_pairs={{0,4},{4,8},{8,12},{12,16},{16,20},{20,24},{24,28},{1,5},{5,9},{9,... | collective-permute-start | bytes 393224 | tf_op jit(solution)/shard_map/ppermute | solution.py:770
  206.5 1.3 collective-permute-start.9
  207.8 1.8 collective-permute-start.10
  209.6 1.3 collective-permute-start.11
  210.9 3.0 %collective-permute-done.11.right_ref = f32[4,256]{1,0:T(4,128)S(1)} collective-permute-done((f32[4,256]{1,0:T(4,128)S(1)}, f32[4,256]{1,0:T(4,128)S(1)}, u32[]{:S(2)}, u32[]{:S(2)}) %collective-permute-start.11) | collective-permute-done | bytes 4128 | tf_op jit(solution)/shard_map/ppermute | solution.py:771
  213.9 5.1 %shard_map.136 = (f32[4,128,256]{2,1,0:T(8,128)}, f32[4,128,256]{2,1,0:T(8,128)}, f32[32,8,128]{2,1,0:T(8,128)S(1)}) custom-call(f32[32,8,128]{2,1,0:T(8,128)S(1)} %copy-done, f32[32,8,128]{2,1,0:T(8,128)S(1)} %all-to-all-done.7.beta_ref, f32[2,4,128,256]{3,2,1,0:T(8,128)} %get-tuple-element.32.kept_ref.old_ref, ...), custom_call_target="tpu_custom_call" | custom-call | bytes 5767168 | tf_op jit(solution)/shard_map/pallas_call | solution.py:338
  219.0 15.9 %all_to_all.46.sums_ref = f32[32,8,128]{2,1,0:T(8,128)} all-to-all(f32[32,8,128]{2,1,0:T(8,128)S(1)} %get-tuple-element.58), channel_id=1, replica_groups=mesh['row'=8,'col'=4] {'row','col'}, dimensions={0} | all-to-all | bytes 262144 | tf_op jit(solution)/shard_map/all_to_all | solution.py:762
  234.9 4.1 %shard_map.137 = (f32[4,128,256]{2,1,0:T(8,128)}, f32[4,128,256]{2,1,0:T(8,128)}) custom-call(f32[32,8,128]{2,1,0:T(8,128)} %all_to_all.45.sums_ref.refs_1_.first_ref, f32[32,8,128]{2,1,0:T(8,128)} %all_to_all.46.sums_ref, f32[2,4,128,256]{3,2,1,0:T(8,128)} %get-tuple-element.32.kept_ref.old_ref, f32[4,128,256]{2,1,0:T(8,128)} %get-tuple-element.59.way_ref, ...), custom_call_target="tpu_custom_call" | custom-call | bytes 3145728 | tf_op jit(solution)/shard_map/pallas_call | solution.py:338
  (27 shorter events, 1.5 us)
Async XLA Ops:
  0.6 38.0 %copy-start.3 = (f32[16,3]{0,1:T(4,128)S(1)}, f32[16,3]{0,1:T(4,128)}, u32[]{:S(2)}) copy-start(f32[16,3]{0,1:T(4,128)} %param.12) | copy-start | bytes 580
  0.6 38.0 %copy-start.1 = (f32[16,17]{1,0:T(8,128)S(1)}, f32[16,17]{1,0:T(8,128)}, u32[]{:S(2)}) copy-start(f32[16,17]{1,0:T(8,128)} %mix_ref.7) | copy-start | bytes 3268
  2.5 15.5 %all-to-all-start = ((f32[32,8,128]{2,1,0:T(8,128)}), f32[32,8,128]{2,1,0:T(8,128)S(1)}, u32[]{:S(2)}, u32[]{:S(2)}) async-start(f32[32,8,128]{2,1,0:T(8,128)} %get-tuple-element.33), calls=%async_computation | async-start | bytes 262144 | tf_op jit(solution)/shard_map/all_to_all | solution.py:762
  18.0 3.5 %copy-start.6 = (f32[32,8,128]{2,1,0:T(8,128)}, f32[32,8,128]{2,1,0:T(8,128)S(1)}, u32[]{:S(2)}) copy-start(f32[32,8,128]{2,1,0:T(8,128)S(1)} %all-to-all-done.sums_ref.refs_0_.first_ref) | copy-start | bytes 393220
  18.0 18.0 %all-to-all-start.2 = ((f32[4,4,16,8,128]{4,3,2,1,0:T(8,128)}), f32[4,4,16,8,128]{4,3,2,1,0:T(8,128)S(1)}, u32[]{:S(2)}, u32[]{:S(2)}) async-start(f32[4,4,16,8,128]{4,3,2,1,0:T(8,128)} %shard_map.123), calls=%async_computation.2 | async-start | bytes 2097152 | tf_op jit(solution)/shard_map/all_to_all | solution.py:817
  21.6 0.7 copy-start.2
  36.0 12.3 %copy-start.5 = (f32[4,4,16,8,128]{4,3,2,1,0:T(8,128)}, f32[4,4,16,8,128]{4,3,2,1,0:T(8,128)S(1)}, u32[]{:S(2)}) copy-start(f32[4,4,16,8,128]{4,3,2,1,0:T(8,128)S(1)} %all-to-all-done.2) | copy-start | bytes 3145732
  36.0 18.2 %all-to-all-start.1 = ((f32[32,4,8,128]{3,2,1,0:T(8,128)}), f32[32,4,8,128]{3,2,1,0:T(8,128)S(1)}, u32[]{:S(2)}, u32[]{:S(2)}) async-start(f32[32,4,8,128]{3,2,1,0:T(8,128)} %shard_map.122), calls=%async_computation.1 | async-start | bytes 1048576 | tf_op jit(solution)/shard_map/all_to_all | solution.py:762
  60.7 18.5 %all-to-all-start.3 = ((f32[32,4,8,128]{3,2,1,0:T(8,128)}), f32[32,4,8,128]{3,2,1,0:T(8,128)S(1)}, u32[]{:S(2)}, u32[]{:S(2)}) async-start(f32[32,4,8,128]{3,2,1,0:T(8,128)} %shard_map.126.refs_4_), calls=%async_computation.3 | async-start | bytes 1048576 | tf_op jit(solution)/shard_map/all_to_all | solution.py:762
  63.7 16.3 %copy-start.4 = (f32[17]{0:T(128)S(1)}, f32[17]{0:T(128)}, u32[]{:S(2)}) copy-start(f32[17]{0:T(128)} %proj_ref.3) | copy-start | bytes 208
  79.3 0.8 copy-start.8
  89.6 26.1 %collective-permute-start = (f32[128,256]{1,0:T(8,128)S(1)}, f32[128,256]{1,0:T(8,128)S(1)}, u32[]{:S(2)}, u32[]{:S(2)}) collective-permute-start(f32[128,256]{1,0:T(8,128)S(1)} %get-tuple-element.35), channel_id=1, source_target_pairs={{0,4},{4,8},{8,12},{12,16},{16,20},{20,24},{24,28},{1,5},{5,9},{9,... | collective-permute-start | bytes 393224 | tf_op jit(solution)/shard_map/ppermute | solution.py:770
  92.8 22.9 %collective-permute-start.1 = (f32[128,256]{1,0:T(8,128)S(1)}, f32[128,256]{1,0:T(8,128)S(1)}, u32[]{:S(2)}, u32[]{:S(2)}) collective-permute-start(f32[128,256]{1,0:T(8,128)S(1)} %get-tuple-element.36), channel_id=1, source_target_pairs={{4,0},{8,4},{12,8},{16,12},{20,16},{24,20},{28,24},{5,1},{9,5},{13... | collective-permute-start | bytes 393224 | tf_op jit(solution)/shard_map/ppermute | solution.py:771
  94.1 17.1 %collective-permute-start.4 = (bf16[128,256]{1,0:T(8,128)(2,1)S(1)}, bf16[128,256]{1,0:T(8,128)(2,1)S(1)}, u32[]{:S(2)}, u32[]{:S(2)}) collective-permute-start(bf16[128,256]{1,0:T(8,128)(2,1)S(1)} %get-tuple-element.39), channel_id=1, source_target_pairs={{0,4},{4,8},{8,12},{12,16},{16,20},{20,24},{24,28},{1,5},{5,9},{9,... | collective-permute-start | bytes 196616 | tf_op jit(solution)/shard_map/ppermute | solution.py:770
  98.6 13.9 %collective-permute-start.5 = (bf16[128,256]{1,0:T(8,128)(2,1)S(1)}, bf16[128,256]{1,0:T(8,128)(2,1)S(1)}, u32[]{:S(2)}, u32[]{:S(2)}) collective-permute-start(bf16[128,256]{1,0:T(8,128)(2,1)S(1)} %get-tuple-element.40), channel_id=1, source_target_pairs={{4,0},{8,4},{12,8},{16,12},{20,16},{24,20},{28,24},{5,1},{9,5},{13... | collective-permute-start | bytes 196616 | tf_op jit(solution)/shard_map/ppermute | solution.py:771
  99.9 2.1 collective-permute-start.6
  102.0 4.4 %collective-permute-start.7 = (f32[4,256]{1,0:T(4,128)S(1)}, f32[4,256]{1,0:T(4,128)S(1)}, u32[]{:S(2)}, u32[]{:S(2)}) collective-permute-start(f32[4,256]{1,0:T(4,128)S(1)} %get-tuple-element.42), channel_id=1, source_target_pairs={{1,0},{2,1},{3,2},{5,4},{6,5},{7,6},{9,8},{10,9},{11,10},{13,12},{... | collective-permute-start | bytes 12296 | tf_op jit(solution)/shard_map/ppermute | solution.py:771
  106.4 9.3 %collective-permute-start.2 = (f32[4,256]{1,0:T(4,128)S(1)}, f32[4,256]{1,0:T(4,128)S(1)}, u32[]{:S(2)}, u32[]{:S(2)}) collective-permute-start(f32[4,256]{1,0:T(4,128)S(1)} %get-tuple-element.37), channel_id=1, source_target_pairs={{0,1},{1,2},{2,3},{4,5},{5,6},{6,7},{8,9},{9,10},{10,11},{12,13},{... | collective-permute-start | bytes 12296 | tf_op jit(solution)/shard_map/ppermute | solution.py:770
  111.2 4.5 %collective-permute-start.3 = (f32[4,256]{1,0:T(4,128)S(1)}, f32[4,256]{1,0:T(4,128)S(1)}, u32[]{:S(2)}, u32[]{:S(2)}) collective-permute-start(f32[4,256]{1,0:T(4,128)S(1)} %get-tuple-element.38), channel_id=1, source_target_pairs={{1,0},{2,1},{3,2},{5,4},{6,5},{7,6},{9,8},{10,9},{11,10},{13,12},{... | collective-permute-start | bytes 12296 | tf_op jit(solution)/shard_map/ppermute | solution.py:771
  145.1 18.2 %all-to-all-start.5 = ((f32[32,4,8,128]{3,2,1,0:T(8,128)}), f32[32,4,8,128]{3,2,1,0:T(8,128)S(1)}, u32[]{:S(2)}, u32[]{:S(2)}) async-start(f32[32,4,8,128]{3,2,1,0:T(8,128)} %get-tuple-element.50), calls=%async_computation.5 | async-start | bytes 1048576 | tf_op jit(solution)/shard_map/all_to_all | solution.py:762
  169.9 18.5 %all-to-all-start.6 = ((f32[32,4,8,128]{3,2,1,0:T(8,128)}), f32[32,4,8,128]{3,2,1,0:T(8,128)S(1)}, u32[]{:S(2)}, u32[]{:S(2)}) async-start(f32[32,4,8,128]{3,2,1,0:T(8,128)} %shard_map.133.refs_5_), calls=%async_computation.6 | async-start | bytes 1048576 | tf_op jit(solution)/shard_map/all_to_all | solution.py:762
  183.0 30.9 %copy-start = (f32[32,8,128]{2,1,0:T(8,128)S(1)}, f32[32,8,128]{2,1,0:T(8,128)}, u32[]{:S(2)}) copy-start(f32[32,8,128]{2,1,0:T(8,128)} %all_to_all.45.sums_ref.refs_1_.first_ref) | copy-start | bytes 393220
  188.4 0.8 copy-start.7
  199.7 14.1 %all-to-all-start.7 = ((f32[32,8,128]{2,1,0:T(8,128)}), f32[32,8,128]{2,1,0:T(8,128)S(1)}, u32[]{:S(2)}, u32[]{:S(2)}) async-start(f32[32,8,128]{2,1,0:T(8,128)} %get-tuple-element.52), calls=%async_computation.7 | async-start | bytes 262144 | tf_op jit(solution)/shard_map/all_to_all | solution.py:762
  202.8 11.0 %collective-permute-start.8 = (f32[128,256]{1,0:T(8,128)S(1)}, f32[128,256]{1,0:T(8,128)S(1)}, u32[]{:S(2)}, u32[]{:S(2)}) collective-permute-start(f32[128,256]{1,0:T(8,128)S(1)} %get-tuple-element.54), channel_id=1, source_target_pairs={{0,4},{4,8},{8,12},{12,16},{16,20},{20,24},{24,28},{1,5},{5,9},{9,... | collective-permute-start | bytes 393224 | tf_op jit(solution)/shard_map/ppermute | solution.py:770
  206.5 7.4 %collective-permute-start.9 = (f32[128,256]{1,0:T(8,128)S(1)}, f32[128,256]{1,0:T(8,128)S(1)}, u32[]{:S(2)}, u32[]{:S(2)}) collective-permute-start(f32[128,256]{1,0:T(8,128)S(1)} %get-tuple-element.55), channel_id=1, source_target_pairs={{4,0},{8,4},{12,8},{16,12},{20,16},{24,20},{28,24},{5,1},{9,5},{13... | collective-permute-start | bytes 393224 | tf_op jit(solution)/shard_map/ppermute | solution.py:771
  207.8 3.1 %collective-permute-start.10 = (f32[4,256]{1,0:T(4,128)S(1)}, f32[4,256]{1,0:T(4,128)S(1)}, u32[]{:S(2)}, u32[]{:S(2)}) collective-permute-start(f32[4,256]{1,0:T(4,128)S(1)} %get-tuple-element.56), channel_id=1, source_target_pairs={{0,1},{1,2},{2,3},{4,5},{5,6},{6,7},{8,9},{9,10},{10,11},{12,13},{... | collective-permute-start | bytes 12296 | tf_op jit(solution)/shard_map/ppermute | solution.py:770
  209.6 4.3 %collective-permute-start.11 = (f32[4,256]{1,0:T(4,128)S(1)}, f32[4,256]{1,0:T(4,128)S(1)}, u32[]{:S(2)}, u32[]{:S(2)}) collective-permute-start(f32[4,256]{1,0:T(4,128)S(1)} %get-tuple-element.57), channel_id=1, source_target_pairs={{1,0},{2,1},{3,2},{5,4},{6,5},{7,6},{9,8},{10,9},{11,10},{13,12},{... | collective-permute-start | bytes 12296 | tf_op jit(solution)/shard_map/ppermute | solution.py:771

commit v2 on v1

--- a/solution.py
+++ b/solution.py
@@ -308,14 +308,14 @@
     return (0.5 * value) * (1.0 + jnp.tanh(inner))
 
 
-def call(body, outs, in_specs, out_specs, grid=(), scratch=(), flops=0, moved=0, alias=None, limit=8, near=()):
+def call(body, outs, in_specs, out_specs, grid=(), scratch=(), flops=0, moved=0, alias=None, limit=8, near=(), loose=False):
     single = not isinstance(outs, tuple)
     outs = (outs,) if single else outs
     out_specs = (out_specs,) if single else out_specs
     run = pl.pallas_call(
         body,
         out_shape=tuple(
-            pltpu.HBM(out.shape, out.dtype) if out.size > 2**16 else out for out in outs
+            out if loose or out.size <= 2**16 else pltpu.HBM(out.shape, out.dtype) for out in outs
         ),
         grid=grid,
         in_specs=in_specs,
@@ -391,11 +391,8 @@
             out_ref[group, :, channel] = block[:, group]
 
 
-def turn_body(weight_ref, out_ref):
-    out_ref[...] = pltpu.roll(weight_ref[...], LANES // 2, 1)
-
-
-def harmonic_faces(perm_ref, low_ref, high_ref, left_ref, right_ref, first_ref, sec_lo, sec_hi, thi_lo, thi_hi):
+def prepare_body(weight_ref, perm_ref, low_ref, high_ref, left_ref, right_ref, other_ref, first_ref, sec_lo, sec_hi, thi_lo, thi_hi):
+    other_ref[...] = pltpu.roll(weight_ref[...], LANES // 2, 1)
     rows, cols, depth = perm_ref.shape
     planes = [perm_ref[place].astype(F32) for place in range(rows)]
     line = lax.broadcasted_iota(jnp.int32, (cols, depth), 0)
@@ -433,14 +430,14 @@
     )
 
 
-def transform(lift_ref, deep_ref, col_ref, scaled, log_perm, spectra_ref, zt_ref):
+def transform(lift_ref, deep_ref, col_ref, scaled, log_perm, spectra_ref, lifted_ref, zt_ref):
     half = 2 * KZ
     cols = scaled.shape[1]
     for channel in range(0, CHANNELS, 2):
-        lifted = jnp.concatenate(
-            [lift_channel(lift_ref, channel + j, scaled, log_perm) for j in range(2)], 1
-        )
-        high, low = split(lifted)
+        pair = [lift_channel(lift_ref, channel + j, scaled, log_perm) for j in range(2)]
+        for j in range(2):
+            lifted_ref[0, channel + j] = pair[j]
+        high, low = split(jnp.concatenate(pair, 1))
         part = matmul(deep_ref[...], high)
         part = part[:half] + part[half:] + matmul(deep_ref[:half], low)
         for j in range(2):
@@ -463,11 +460,11 @@
             ]
 
 
-def lift_first_body(cells, lift_ref, sums_ref, res_ref, perm_ref, deep_ref, col_ref, spectra_ref, zt_ref):
+def lift_first_body(cells, lift_ref, sums_ref, res_ref, perm_ref, deep_ref, col_ref, spectra_ref, lifted_ref, zt_ref):
     scale = scale_of(gathered(sums_ref, 0), cells)
     scaled = (res_ref[0] / scale).T
     log_perm = jnp.log(perm_ref[0].astype(F32)).T
-    transform(lift_ref, deep_ref, col_ref, scaled, log_perm, spectra_ref, zt_ref)
+    transform(lift_ref, deep_ref, col_ref, scaled, log_perm, spectra_ref, lifted_ref, zt_ref)
 
 
 def next_scalars(first_ref, sums_ref):
@@ -479,33 +476,26 @@
     return curvature, alpha, jnp.maximum(total, 0.0)
 
 
-def lift_next_body(cells, lift_ref, first_ref, sums_ref, res_ref, image_ref, perm_ref, deep_ref, col_ref, spectra_ref, next_ref, zt_ref):
+def lift_next_body(cells, lift_ref, first_ref, sums_ref, res_ref, image_ref, perm_ref, deep_ref, col_ref, spectra_ref, lifted_ref, next_ref, zt_ref):
     _, alpha, total = next_scalars(first_ref, sums_ref)
     scale = scale_of(total, cells)
     residual = res_ref[0] - alpha * image_ref[0]
     next_ref[0] = residual
     scaled = (residual / scale).T
     log_perm = jnp.log(perm_ref[0].astype(F32)).T
-    transform(lift_ref, deep_ref, col_ref, scaled, log_perm, spectra_ref, zt_ref)
-
-
-def point_body(scale_of_refs, lift_ref, mix_ref, *refs):
-    *scalar_refs, res_ref, perm_ref, _, _, point_ref, scaled_ref, log_ref, lifted_ref = refs
-    scaled_ref[...] = (res_ref[0] / scale_of_refs(*scalar_refs)).T
-    log_ref[...] = jnp.log(perm_ref[0].astype(F32)).T
-    size = lifted_ref.shape[1]
+    transform(lift_ref, deep_ref, col_ref, scaled, log_perm, spectra_ref, lifted_ref, zt_ref)
+
+
+def point_body(mix_ref, lifted_ref, _, __, point_ref):
+    size = 4 * SUBLANES
     group = 4
 
     def step(index, carry):
         lines = pl.ds(pl.multiple_of(index * size, size), size)
-        scaled = scaled_ref[lines, :]
-        log_perm = log_ref[lines, :]
-        for channel in range(CHANNELS):
-            lifted_ref[channel] = lift_channel(lift_ref, channel, scaled, log_perm)
         for first in range(0, CHANNELS, group):
             sums = [mix_ref[first + j, CHANNELS] for j in range(group)]
             for channel in range(CHANNELS):
-                lifted = lifted_ref[channel]
+                lifted = lifted_ref[0, channel, lines, :]
                 sums = [
                     total + mix_ref[first + j, channel] * lifted for j, total in enumerate(sums)
                 ]
@@ -513,10 +503,10 @@
                 point_ref[0, first + j, lines, :] = total
         return carry
 
-    lax.fori_loop(0, scaled_ref.shape[0] // size, step, 0)
-
-
-def modes_body(cells, n_row, n_col, recv_ref, weight_ref, other_ref, _, out_ref, field_ref, turned_ref, spec_ref, odd_ref):
+    lax.fori_loop(0, lifted_ref.shape[2] // size, step, 0)
+
+
+def modes_body(cells, n_row, n_col, recv_ref, weight_ref, other_ref, _, __, out_ref, field_ref, turned_ref, spec_ref, odd_ref):
     rows = recv_ref.shape[1]
     places = n_row * rows
     tile = (SUBLANES, LANES)
@@ -534,7 +524,6 @@
             for col in range(1, n_col):
                 value = value + recv_ref[row * n_col + col, place]
             field_ref[row * rows + place] = value
-            turned_ref[row * rows + place] = turn(value)
     angle = 2.0 * np.pi / places
     half = KX // 2
 
@@ -552,10 +541,15 @@
             total = term if total is None else total + term
         return jnp.zeros(tile, F32) if total is None else total
 
+    middle = places // 2
+    for place in range(1, middle):
+        value, mirror = field_ref[place], field_ref[places - place]
+        field_ref[place] = value + mirror
+        turned_ref[place] = turn(value - mirror)
     for freq in range(half + 1):
-        turns = freq * np.arange(places) % places
+        turns = freq * np.arange(middle + 1) % places
         even = weigh(np.cos(angle * turns), field_ref)
-        odd = weigh(np.sin(angle * turns), turned_ref)
+        odd = weigh(np.concatenate([[0.0], np.sin(angle * turns[1:middle])]), turned_ref)
         if freq < half:
             spec_ref[half + freq] = even + odd
         if freq > 0:
@@ -762,6 +756,22 @@
     return lax.all_to_all(blocks, BOTH, split_axis=0, concat_axis=0, tiled=True)
 
 
+def total_body(in_ref, out_ref):
+    out_ref[...] = jnp.broadcast_to(jnp.sum(in_ref[...], axis=0)[None], out_ref.shape)
+
+
+def add_up(partial):
+    found = lax.all_to_all(partial, "row", split_axis=0, concat_axis=0, tiled=True)
+    found = call(
+        total_body,
+        shape(lax.axis_size("col"), SUBLANES, LANES),
+        [whole()],
+        whole(),
+        near=(0,),
+    )(found)
+    return lax.all_to_all(found, "col", split_axis=0, concat_axis=0, tiled=True)
+
+
 def neighbours(low, high, left, right):
     found = []
     for axis, first, last in (("row", low, high), ("col", left, right)):
@@ -784,7 +794,8 @@
     lift_weight = lift_weight.T
     field = shape(rows, cols, depth)
     field_bytes = 4 * rows * cols * depth
-    partial = shape(count, SUBLANES, LANES)
+    partial = shape(n_row, SUBLANES, LANES)
+    channels = shape(rows, CHANNELS, depth, cols)
     spectra = shape(count, rows, SUBLANES, LANES)
     spectra_bytes = 4 * count * rows * SUBLANES * LANES
     smem = whole(pltpu.SMEM)
@@ -805,7 +816,7 @@
         (vmem,) * 5,
         moved=field_bytes,
     )(right_side, permeability)
-    squares = exchange(squares)
+    squares = add_up(squares)
 
     weights = call(
         weight_body,
@@ -816,25 +827,18 @@
     )(spectral_weight)
     weights = lax.all_to_all(weights, "col", split_axis=0, concat_axis=0, tiled=True)
     weights = weights.reshape(KX * CHANNELS * SUBLANES, LANES)
-    others = call(
-        turn_body,
-        shape(*weights.shape),
-        [vmem],
-        vmem,
-        moved=8 * weights.size,
-    )(weights)
+    others, first, *faces = call(
+        prepare_body,
+        (shape(*weights.shape), shape(rows + 1, cols, depth)) + (field,) * 4,
+        [vmem] * 6,
+        (vmem,) * 6,
+        moved=10 * field_bytes,
+        near=(0, 2, 3, 4, 5),
+        limit=12,
+    )(weights, permeability, *neighbours(*edges))
     weights, others = (
         array.reshape(KX, CHANNELS, SUBLANES, LANES) for array in (weights, others)
     )
-
-    first, *faces = call(
-        harmonic_faces,
-        (shape(rows + 1, cols, depth),) + (field,) * 4,
-        [vmem] * 5,
-        (vmem,) * 5,
-        moved=6 * field_bytes,
-        near=(1, 2, 3, 4),
-    )(permeability, *neighbours(*edges))
     faces = [first, first] + faces
     next_plane = pl.BlockSpec((1, cols, depth), lambda i: (i + 1, 0, 0))
     face_specs = [plane, next_plane] + [plane] * 4
@@ -844,28 +848,20 @@
 
     anywhere = whole(pl.ANY)
 
-    def points(scale_of_refs, scalars, residual, part, before, after):
+    def points(lifted, part, before, after):
         first = part * rows // 2
-        moved_plane = pl.BlockSpec((1, cols, depth), lambda i: (first + i, 0, 0))
-        count_in = 4 + len(scalars)
+        half_block = pl.BlockSpec((1, CHANNELS, depth, cols), lambda i: (first + i, 0, 0, 0))
         return call(
-            functools.partial(point_body, scale_of_refs),
-            shape(rows, CHANNELS, depth, cols),
-            [smem, smem]
-            + [vmem] * len(scalars)
-            + [moved_plane, moved_plane, anywhere, anywhere],
-            pl.BlockSpec((1, CHANNELS, depth, cols), lambda i: (first + i, 0, 0, 0)),
+            point_body,
+            channels,
+            [smem, half_block, anywhere, anywhere],
+            half_block,
             grid=(rows // 2,),
-            scratch=[
-                pltpu.VMEM((depth, cols), F32),
-                pltpu.VMEM((depth, cols), F32),
-                pltpu.VMEM((CHANNELS, 4 * SUBLANES, cols), F32),
-            ],
             flops=2.5e9,
-            moved=9 * field_bytes,
-            alias={count_in: 0} if part else None,
+            moved=16 * field_bytes,
+            alias={2: 0} if part else None,
             limit=12,
-        )(lift_weight, mix_weight, *scalars, residual, permeability, before, after)
+        )(mix_weight, lifted, before, after)
 
     def modes(received, before):
         places = rows * n_row
@@ -873,37 +869,33 @@
         return call(
             functools.partial(modes_body, cells, n_row, n_col),
             spectra,
-            [vmem, vmem, vmem, anywhere],
+            [vmem, vmem, vmem, anywhere, anywhere],
             vmem,
             scratch=[tiles(places), tiles(places), tiles(KX), tiles(KX)],
             moved=2 * spectra_bytes + 8 * weights.size,
             near=(0,),
-        )(received, weights, others, before)
-
-    def mixed_modes(blocks, scale_of_refs, scalars, residual):
+        )(received, weights, others, before, faces[0])
+
+    def mixed_modes(blocks, lifted):
         received = exchange(blocks)
-        point = points(scale_of_refs, scalars, residual, 0, right_side, right_side)
+        point = points(lifted, 0, right_side, right_side)
         blocks = modes(received, point)
         received = exchange(blocks)
-        point = points(scale_of_refs, scalars, residual, 1, point, blocks)
+        point = points(lifted, 1, point, blocks)
         return received, point
 
-    blocks = call(
+    blocks, lifted = call(
         functools.partial(lift_first_body, cells),
-        spectra,
+        (spectra, channels),
         [smem, vmem, plane, plane, vmem, vmem],
-        spectra_block,
+        (spectra_block, point_block),
+        limit=16,
         grid=(rows,),
         scratch=[zt_scratch],
         flops=lift_flops,
         moved=2 * field_bytes + spectra_bytes,
     )(lift_weight, squares, right_side, permeability, deep_forward, col_forward)
-    received, point = mixed_modes(
-        blocks,
-        lambda sums_ref: scale_of(gathered(sums_ref, 0), cells),
-        (squares,),
-        right_side,
-    )
+    received, point = mixed_modes(blocks, lifted)
     kept, *edges = call(
         functools.partial(back_first_body, cells),
         (kept_shape,) + edge_shapes,
@@ -926,26 +918,24 @@
         grid=(rows,),
         scratch=[acc_scratch],
         moved=9 * field_bytes,
-        near=(1, 2, 3, 4),
+        near=range(12),
+        loose=True,
     )(*args)
-    sums = exchange(sums)
-
-    blocks, residual = call(
+    sums = add_up(sums)
+
+    blocks, lifted, residual = call(
         functools.partial(lift_next_body, cells),
-        (spectra, field),
+        (spectra, channels, field),
         [smem, vmem, vmem, plane, plane, plane, vmem, vmem],
-        (spectra_block, plane),
+        (spectra_block, point_block, plane),
+        limit=16,
+        near=(4,),
         grid=(rows,),
         scratch=[zt_scratch],
         flops=lift_flops,
         moved=4 * field_bytes + spectra_bytes,
     )(lift_weight, squares, sums, right_side, image, permeability, deep_forward, col_forward)
-    received, point = mixed_modes(
-        blocks,
-        lambda first_ref, sums_ref: scale_of(next_scalars(first_ref, sums_ref)[2], cells),
-        (squares, sums),
-        residual,
-    )
+    received, point = mixed_modes(blocks, lifted)
     kept, beta, *edges = call(
         functools.partial(back_next_body, cells),
         (kept_shape, partial) + edge_shapes,
@@ -959,7 +949,7 @@
         alias={8: 0},
     )(proj_weight, squares, sums, received, point, col_back, deep_back, image, kept)
 
-    beta = exchange(beta)
+    beta = add_up(beta)
     halo = neighbours(*edges)
     args = (sums, beta, kept, *halo, *old_halo, residual, *faces)
     way, image, later = call(
@@ -969,10 +959,11 @@
         (plane, plane, vmem),
         grid=(rows,),
         scratch=[acc_scratch],
-        near=(0, 1, 3, 4, 5, 6, 7, 8, 9, 10),
+        near=range(18),
+        loose=True,
         moved=11 * field_bytes,
     )(*args)
-    later = exchange(later)
+    later = add_up(later)
     answer, residual = call(
         last_body,
         (field, field),
@@ -980,6 +971,8 @@
         (plane, plane),
         grid=(rows,),
         moved=6 * field_bytes,
+        near=range(6),
+        loose=True,
     )(sums, later, kept, way, residual, image)
     return (answer, residual, kept)
 

time: 240 us -> 255 us (1.062)
  blocking collectives: 30.5 us -> 59.4 us
  Pallas kernels: 116 us -> 98.1 us
  local copies, waits for them, and re-layouts: 2.35 us -> 9.09 us
  waiting for transfers between devices: 36.9 us -> 33 us
    all_to_all x2 -> x6, blocking collectives: 30.5 us -> 59.4 us  [the longest x4 44.9 us: add_up(): lax.all_to_all(partial, 'row', split_axis=0, concat_axis=0, tiled=True)]
    pallas_call x17 -> x20, Pallas kernels: 116 us -> 98.1 us  [wrapped(): found = run(*held)]
    all_to_all x0 -> x2, starting transfers between devices: none -> 7.1 us  [add_up(): return lax.all_to_all(found, 'col', split_axis=0, concat_axis=0, tiled=True)]
    unnamed x18 -> x60, local copies, waits for them, and re-layouts: 2.35 us -> 9.09 us
    all_to_all x6 -> x4, waiting for transfers between devices: 25.8 us -> 21.9 us  [exchange(): return lax.all_to_all(blocks, BOTH, split_axis=0, concat_axis=0, tiled=True)]
    all_to_all x6 -> x4, starting transfers between devices: 21.7 us -> 17.9 us  [exchange(): return lax.all_to_all(blocks, BOTH, split_axis=0, concat_axis=0, tiled=True)]
    ppermute x6, starting transfers between devices: 19.2 us -> 16.2 us  [neighbours(): found.append(lax.ppermute(last, axis, forward))]
  transfers between devices with their start and end apart: 19 -> 19, of which waited for: 9 -> 7; matrix products, arithmetic and copies ran while one was open for 0% -> 0% of each run, Pallas kernels for 24% -> 19%
where the time goes in v2:
time: 255 us; the launch traced here: 253 us
  Pallas kernels  98.1 us (38%)
  blocking collectives  59.4 us (23%)
  starting transfers between devices  52.5 us (21%)
  waiting for transfers between devices  33 us (13%)
  local copies, waits for them, and re-layouts  9.09 us (4%)
    pallas_call x20, Pallas kernels, wrapped(): found = run(*held)  98.1 us
    all_to_all x4, blocking collectives, add_up(): lax.all_to_all(partial, 'row', split_axis=0, concat_axis=0, tiled=True)  44.9 us
    all_to_all x4, waiting for transfers between devices, exchange(): return lax.all_to_all(blocks, BOTH, split_axis=0, concat_axis=0, tiled=True)  21.9 us
    all_to_all x4, starting transfers between devices, exchange(): return lax.all_to_all(blocks, BOTH, split_axis=0, concat_axis=0, tiled=True)  17.9 us
    ppermute x6, starting transfers between devices, neighbours(): found.append(lax.ppermute(last, axis, forward))  16.2 us
    all_to_all x2, blocking collectives, add_up(): return lax.all_to_all(found, 'col', split_axis=0, concat_axis=0, tiled=True)  14.5 us
    unnamed x60, local copies, waits for them, and re-layouts  9.09 us
    ppermute x6, starting transfers between devices, neighbours(): found.append(lax.ppermute(first, axis, backward))  7.74 us
  transfers between devices with their start and end apart: 19, of which 7 were waited for; matrix products, arithmetic and copies ran while one was open for 0% of the time, Pallas kernels for 19%

profile of v2, /device:TPU:0, one launch (start us, length us, event | category | flops | bytes accessed | tf_op | source)
XLA Modules:
  0.0 253.1 jit_solution(11099303529720979516)
XLA Ops:
  1.8 13.7 %all_to_all.65.in_ref = f32[8,8,128]{2,1,0:T(8,128)S(1)} all-to-all(f32[8,8,128]{2,1,0:T(8,128)S(1)} %get-tuple-element.37), channel_id=1, replica_groups=mesh['row'=8,'col'=4] {'row'}, dimensions={0} | all-to-all | bytes 65536 | tf_op jit(solution)/shard_map/all_to_all | solution.py:764
  16.2 3.3 %all-to-all-start.1 = ((f32[4,8,128]{2,1,0:T(8,128)}), f32[4,8,128]{2,1,0:T(8,128)S(1)}, u32[]{:S(2)}, u32[]{:S(2)}) async-start(f32[4,8,128]{2,1,0:T(8,128)} %shard_map.122), calls=%async_computation.1 | async-start | bytes 32768 | tf_op jit(solution)/shard_map/all_to_all | solution.py:772
  19.4 2.5 %shard_map.124 = f32[4,4,16,8,128]{4,3,2,1,0:T(8,128)} custom-call(f32[2,4,16,16,128]{4,3,2,1,0:T(8,128)} %weight_ref.1), custom_call_target="tpu_custom_call" | custom-call | bytes 2097152 | tf_op jit(solution)/shard_map/pallas_call | solution.py:338
  22.0 1.3 all-to-all-done.1.sums_ref.first_ref
  23.3 3.5 %all-to-all-start.3 = ((f32[4,4,16,8,128]{4,3,2,1,0:T(8,128)}), f32[4,4,16,8,128]{4,3,2,1,0:T(8,128)S(1)}, u32[]{:S(2)}, u32[]{:S(2)}) async-start(f32[4,4,16,8,128]{4,3,2,1,0:T(8,128)} %shard_map.124), calls=%async_computation.3 | async-start | bytes 2097152 | tf_op jit(solution)/shard_map/all_to_all | solution.py:828
  27.5 9.6 %shard_map.123 = (f32[32,4,8,128]{3,2,1,0:T(8,128)}, f32[4,16,256,128]{3,2,1,0:T(8,128)}) custom-call(f32[3,16]{1,0:T(4,128)S(1)} %bitcast.7, f32[4,8,128]{2,1,0:T(8,128)} %copy-done.29, f32[4,128,256]{2,1,0:T(8,128)} %a_.3, bf16[4,128,256]{2,1,0:T(8,128)(2,1)} %perm_ref.7, bf16[128,256]{1,0:T(8,128)(2,1)} %constant.8.clone.deep_ref, ...), custom_call_target="tpu_custom_call" | custom-call | flops 2000000000 | bytes 1572864 | tf_op jit(solution)/shard_map/pallas_call | solution.py:338
  37.0 4.2 %all-to-all-done.3 = f32[4,4,16,8,128]{4,3,2,1,0:T(8,128)S(1)} async-done(((f32[4,4,16,8,128]{4,3,2,1,0:T(8,128)}), f32[4,4,16,8,128]{4,3,2,1,0:T(8,128)S(1)}, u32[]{:S(2)}, u32[]{:S(2)}) %all-to-all-start.3) | async-done | bytes 1048608 | tf_op jit(solution)/shard_map/all_to_all | solution.py:828
  41.2 2.6 %all-to-all-start.2 = ((f32[32,4,8,128]{3,2,1,0:T(8,128)}), f32[32,4,8,128]{3,2,1,0:T(8,128)S(1)}, u32[]{:S(2)}, u32[]{:S(2)}) async-start(f32[32,4,8,128]{3,2,1,0:T(8,128)} %get-tuple-element.38), calls=%async_computation.2 | async-start | bytes 1048576 | tf_op jit(solution)/shard_map/all_to_all | solution.py:756
  43.8 2.0 collective-permute-start.2
  45.9 1.3 collective-permute-start.3
  47.2 3.6 %collective-permute-start = (bf16[128,256]{1,0:T(8,128)(2,1)S(1)}, bf16[128,256]{1,0:T(8,128)(2,1)S(1)}, u32[]{:S(2)}, u32[]{:S(2)}) collective-permute-start(bf16[128,256]{1,0:T(8,128)(2,1)S(1)} %get-tuple-element.39), channel_id=1, source_target_pairs={{0,4},{4,8},{8,12},{12,16},{16,20},{20,24},{24,28},{1,5},{5,9},{9,... | collective-permute-start | bytes 196616 | tf_op jit(solution)/shard_map/ppermute | solution.py:780
  50.7 1.3 collective-permute-start.1
  52.0 8.2 %shard_map.126._ = f32[4,16,256,128]{3,2,1,0:T(8,128)} custom-call(f32[16,17]{1,0:T(8,128)S(1)} %copy-done.13, f32[4,16,256,128]{3,2,1,0:T(8,128)} %get-tuple-element.44.lifted_ref, f32[4,128,256]{2,1,0:T(8,128)} %a_.3, f32[4,128,256]{2,1,0:T(8,128)} %a_.3), custom_call_target="tpu_custom_call" | custom-call | flops 2500000000 | bytes 8388608 | tf_op jit(solution)/shard_map/pallas_call | solution.py:338
  60.3 3.6 %shard_map.125 = (f32[2048,128]{1,0:T(8,128)}, f32[5,128,256]{2,1,0:T(8,128)}, f32[4,128,256]{2,1,0:T(8,128)}, f32[4,128,256]{2,1,0:T(8,128)}, f32[4,128,256]{2,1,0:T(8,128)}, /*index=5*/f32[4,128,256]{2,1,0:T(8,128)}) custom-call(f32[2048,128]{1,0:T(8,128)S(1)} %bitcast.4, bf16[4,128,256]{2,1,0:T(8,128)(2,1)} %perm_ref.7, ...), custom_call_target="tpu_custom_call" | custom-call | bytes 5242880 | tf_op jit(solution)/shard_map/pallas_call | solution.py:338
  63.9 6.5 %shard_map.127.__ = f32[32,4,8,128]{3,2,1,0:T(8,128)} custom-call(f32[32,4,8,128]{3,2,1,0:T(8,128)S(1)} %all-to-all-done.2.recv_ref, f32[16,16,8,128]{3,2,1,0:T(8,128)} %bitcast.5, f32[16,16,8,128]{3,2,1,0:T(8,128)} %bitcast.9, f32[4,16,256,128]{3,2,1,0:T(8,128)} %shard_map.126._, f32[5,128,256]{2,1,0:T(8,128)} %get-tuple-element.45.__.refs_0_.refs_1_), custom_call_target="tpu_custom_call" | custom-call | bytes 3145728 | tf_op jit(solution)/shard_map/pallas_call | solution.py:338
  70.5 9.2 %all-to-all-start.4 = ((f32[32,4,8,128]{3,2,1,0:T(8,128)}), f32[32,4,8,128]{3,2,1,0:T(8,128)}, u32[]{:S(2)}, u32[]{:S(2)}) async-start(f32[32,4,8,128]{3,2,1,0:T(8,128)} %shard_map.127.__), calls=%async_computation.4 | async-start | bytes 1048576 | tf_op jit(solution)/shard_map/all_to_all | solution.py:756
  79.7 8.1 %shard_map.128.point_ref = f32[4,16,256,128]{3,2,1,0:T(8,128)} custom-call(f32[16,17]{1,0:T(8,128)S(1)} %copy-done.13, f32[4,16,256,128]{3,2,1,0:T(8,128)} %get-tuple-element.44.lifted_ref, f32[4,16,256,128]{3,2,1,0:T(8,128)} %shard_map.126._, f32[32,4,8,128]{3,2,1,0:T(8,128)} %shard_map.127.__), custom_call_target="tpu_custom_call", output_to_operand_aliasing={{}: (2, {})} | custom-call | flops 2500000000 | bytes 8388608 | tf_op jit(solution)/shard_map/pallas_call | solution.py:338
  87.9 7.3 %all-to-all-done.4.recv_ref = f32[32,4,8,128]{3,2,1,0:T(8,128)} async-done(((f32[32,4,8,128]{3,2,1,0:T(8,128)}), f32[32,4,8,128]{3,2,1,0:T(8,128)}, u32[]{:S(2)}, u32[]{:S(2)}) %all-to-all-start.4) | async-done | bytes 524320 | tf_op jit(solution)/shard_map/all_to_all | solution.py:756
  95.2 9.5 %shard_map.129 = (f32[2,4,128,256]{3,2,1,0:T(8,128)}, f32[128,256]{1,0:T(8,128)S(1)}, f32[128,256]{1,0:T(8,128)S(1)}, f32[4,256]{1,0:T(4,128)S(1)}, f32[4,256]{1,0:T(4,128)S(1)}) custom-call(f32[17]{0:T(128)S(1)} %copy-done.23, f32[4,8,128]{2,1,0:T(8,128)} %copy-done.29, f32[32,4,8,128]{3,2,1,0:T(8,128)} %all-to-all-done.4.recv_ref, ...), custom_call_target="tpu_custom_call" | custom-call | flops 2000000000 | bytes 9437184 | tf_op jit(solution)/shard_map/pallas_call | solution.py:338
  104.7 3.2 %collective-permute-start.4 = (f32[128,256]{1,0:T(8,128)S(1)}, f32[128,256]{1,0:T(8,128)S(1)}, u32[]{:S(2)}, u32[]{:S(2)}) collective-permute-start(f32[128,256]{1,0:T(8,128)S(1)} %get-tuple-element.47), channel_id=1, source_target_pairs={{0,4},{4,8},{8,12},{12,16},{16,20},{20,24},{24,28},{1,5},{5,9},{9,... | collective-permute-start | bytes 393224 | tf_op jit(solution)/shard_map/ppermute | solution.py:780
  107.9 1.3 collective-permute-start.5
  109.2 1.3 collective-permute-start.6
  110.5 1.3 collective-permute-start.7
  111.8 3.1 %collective-permute-done.7.right_ref.old_right = f32[4,256]{1,0:T(4,128)S(1)} collective-permute-done((f32[4,256]{1,0:T(4,128)S(1)}, f32[4,256]{1,0:T(4,128)S(1)}, u32[]{:S(2)}, u32[]{:S(2)}) %collective-permute-start.7) | collective-permute-done | bytes 4128 | tf_op jit(solution)/shard_map/ppermute | solution.py:781
  115.0 1.2 copy-done.4
  117.1 11.3 %all_to_all.66.in_ref = f32[8,8,128]{2,1,0:T(8,128)S(1)} all-to-all(f32[8,8,128]{2,1,0:T(8,128)S(1)} %get-tuple-element.55), channel_id=1, replica_groups=mesh['row'=8,'col'=4] {'row'}, dimensions={0} | all-to-all | bytes 65536 | tf_op jit(solution)/shard_map/all_to_all | solution.py:764
  128.4 7.3 %all_to_all.67.sums_ref.first_ref = f32[4,8,128]{2,1,0:T(8,128)} all-to-all(f32[4,8,128]{2,1,0:T(8,128)S(1)} %shard_map.131), channel_id=1, replica_groups=mesh['row'=8,'col'=4] {'col'}, dimensions={0} | all-to-all | bytes 32768 | tf_op jit(solution)/shard_map/all_to_all | solution.py:772
  135.7 9.8 %shard_map.132 = (f32[32,4,8,128]{3,2,1,0:T(8,128)}, f32[4,16,256,128]{3,2,1,0:T(8,128)}, f32[4,128,256]{2,1,0:T(8,128)}) custom-call(f32[3,16]{1,0:T(4,128)S(1)} %bitcast.8, f32[4,8,128]{2,1,0:T(8,128)} %copy-done.29, f32[4,8,128]{2,1,0:T(8,128)} %all_to_all.67.sums_ref.first_ref, f32[4,128,256]{2,1,0:T(8,128)} %a_.3, ...), custom_call_target="tpu_custom_call" | custom-call | flops 2000000000 | bytes 2621440 | tf_op jit(solution)/shard_map/pallas_call | solution.py:338
  146.3 2.6 %all-to-all-start.7 = ((f32[32,4,8,128]{3,2,1,0:T(8,128)}), f32[32,4,8,128]{3,2,1,0:T(8,128)S(1)}, u32[]{:S(2)}, u32[]{:S(2)}) async-start(f32[32,4,8,128]{3,2,1,0:T(8,128)} %get-tuple-element.57), calls=%async_computation.7 | async-start | bytes 1048576 | tf_op jit(solution)/shard_map/all_to_all | solution.py:756
  148.9 8.2 %shard_map.133._ = f32[4,16,256,128]{3,2,1,0:T(8,128)} custom-call(f32[16,17]{1,0:T(8,128)S(1)} %copy-done.13, f32[4,16,256,128]{3,2,1,0:T(8,128)} %get-tuple-element.58.lifted_ref, f32[4,128,256]{2,1,0:T(8,128)} %a_.3, f32[4,128,256]{2,1,0:T(8,128)} %a_.3), custom_call_target="tpu_custom_call" | custom-call | flops 2500000000 | bytes 8388608 | tf_op jit(solution)/shard_map/pallas_call | solution.py:338
  157.2 7.3 %all-to-all-done.7.recv_ref = f32[32,4,8,128]{3,2,1,0:T(8,128)S(1)} async-done(((f32[32,4,8,128]{3,2,1,0:T(8,128)}), f32[32,4,8,128]{3,2,1,0:T(8,128)S(1)}, u32[]{:S(2)}, u32[]{:S(2)}) %all-to-all-start.7) | async-done | bytes 524320 | tf_op jit(solution)/shard_map/all_to_all | solution.py:756
  164.5 6.5 %shard_map.134.__ = f32[32,4,8,128]{3,2,1,0:T(8,128)} custom-call(f32[32,4,8,128]{3,2,1,0:T(8,128)S(1)} %all-to-all-done.7.recv_ref, f32[16,16,8,128]{3,2,1,0:T(8,128)} %bitcast.6, f32[16,16,8,128]{3,2,1,0:T(8,128)} %bitcast.10, f32[4,16,256,128]{3,2,1,0:T(8,128)} %shard_map.133._, f32[5,128,256]{2,1,0:T(8,128)} %get-tuple-element.45.__.refs_0_.refs_1_), custom_call_target="tpu_custom_call" | custom-call | bytes 3145728 | tf_op jit(solution)/shard_map/pallas_call | solution.py:338
  171.0 3.5 %all-to-all-start.8 = ((f32[32,4,8,128]{3,2,1,0:T(8,128)}), f32[32,4,8,128]{3,2,1,0:T(8,128)}, u32[]{:S(2)}, u32[]{:S(2)}) async-start(f32[32,4,8,128]{3,2,1,0:T(8,128)} %shard_map.134.__), calls=%async_computation.8 | async-start | bytes 1048576 | tf_op jit(solution)/shard_map/all_to_all | solution.py:756
  174.5 8.1 %shard_map.135.point_ref = f32[4,16,256,128]{3,2,1,0:T(8,128)} custom-call(f32[16,17]{1,0:T(8,128)S(1)} %copy-done.13, f32[4,16,256,128]{3,2,1,0:T(8,128)} %get-tuple-element.58.lifted_ref, f32[4,16,256,128]{3,2,1,0:T(8,128)} %shard_map.133._, f32[32,4,8,128]{3,2,1,0:T(8,128)} %shard_map.134.__), custom_call_target="tpu_custom_call", output_to_operand_aliasing={{}: (2, {})} | custom-call | flops 2500000000 | bytes 8388608 | tf_op jit(solution)/shard_map/pallas_call | solution.py:338
  182.7 7.2 %all-to-all-done.8.recv_ref = f32[32,4,8,128]{3,2,1,0:T(8,128)} async-done(((f32[32,4,8,128]{3,2,1,0:T(8,128)}), f32[32,4,8,128]{3,2,1,0:T(8,128)}, u32[]{:S(2)}, u32[]{:S(2)}) %all-to-all-start.8) | async-done | bytes 524320 | tf_op jit(solution)/shard_map/all_to_all | solution.py:756
  190.5 10.5 %shard_map.136 = (f32[2,4,128,256]{3,2,1,0:T(8,128)}, f32[8,8,128]{2,1,0:T(8,128)S(1)}, f32[128,256]{1,0:T(8,128)}, f32[128,256]{1,0:T(8,128)}, f32[4,256]{1,0:T(4,128)S(1)}, /*index=5*/f32[4,256]{1,0:T(4,128)S(1)}) custom-call(f32[17]{0:T(128)S(1)} %copy-done.24, f32[4,8,128]{2,1,0:T(8,128)} %copy-done.29, ...), custom_call_target="tpu_custom_call", output_to_operand_aliasing={{0}: (8, {})} | custom-call | flops 2000000000 | bytes 9961472 | tf_op jit(solution)/shard_map/pallas_call | solution.py:338
  201.0 3.8 %collective-permute-start.8 = (f32[128,256]{1,0:T(8,128)}, f32[128,256]{1,0:T(8,128)}, u32[]{:S(2)}, u32[]{:S(2)}) collective-permute-start(f32[128,256]{1,0:T(8,128)} %get-tuple-element.61), channel_id=1, source_target_pairs={{0,4},{4,8},{8,12},{12,16},{16,20},{20,24},{24,28},{1,5},{5,9},{9,... | collective-permute-start | bytes 393224 | tf_op jit(solution)/shard_map/ppermute | solution.py:780
  204.8 1.3 collective-permute-start.9
  206.1 10.8 %all_to_all.68.in_ref = f32[8,8,128]{2,1,0:T(8,128)S(1)} all-to-all(f32[8,8,128]{2,1,0:T(8,128)S(1)} %get-tuple-element.59), channel_id=1, replica_groups=mesh['row'=8,'col'=4] {'row'}, dimensions={0} | all-to-all | bytes 65536 | tf_op jit(solution)/shard_map/all_to_all | solution.py:764
  217.6 3.8 %all-to-all-start.10 = ((f32[4,8,128]{2,1,0:T(8,128)}), f32[4,8,128]{2,1,0:T(8,128)}, u32[]{:S(2)}, u32[]{:S(2)}) async-start(f32[4,8,128]{2,1,0:T(8,128)} %copy-done.14), calls=%async_computation.10 | async-start | bytes 32768 | tf_op jit(solution)/shard_map/all_to_all | solution.py:772
  221.4 2.4 collective-permute-start.10
  223.8 1.3 collective-permute-start.11
  225.7 2.5 collective-permute-done.11.right_ref
  228.8 1.2 copy-done.5
  232.8 2.2 shard_map.138
  235.0 9.1 %all_to_all.69.in_ref = f32[8,8,128]{2,1,0:T(8,128)S(1)} all-to-all(f32[8,8,128]{2,1,0:T(8,128)S(1)} %get-tuple-element.66), channel_id=1, replica_groups=mesh['row'=8,'col'=4] {'row'}, dimensions={0} | all-to-all | bytes 65536 | tf_op jit(solution)/shard_map/all_to_all | solution.py:764
  244.1 7.2 %all_to_all.70.sums_ref = f32[4,8,128]{2,1,0:T(8,128)S(1)} all-to-all(f32[4,8,128]{2,1,0:T(8,128)S(1)} %shard_map.139), channel_id=1, replica_groups=mesh['row'=8,'col'=4] {'col'}, dimensions={0} | all-to-all | bytes 32768 | tf_op jit(solution)/shard_map/all_to_all | solution.py:772
  251.3 1.8 shard_map.140
  (76 shorter events, 9.4 us)
Async XLA Ops:
  0.6 51.4 %copy-start.13 = (f32[16,17]{1,0:T(8,128)S(1)}, f32[16,17]{1,0:T(8,128)}, u32[]{:S(2)}) copy-start(f32[16,17]{1,0:T(8,128)} %mix_ref.7) | copy-start | bytes 3268
  16.2 7.1 %all-to-all-start.1 = ((f32[4,8,128]{2,1,0:T(8,128)}), f32[4,8,128]{2,1,0:T(8,128)S(1)}, u32[]{:S(2)}, u32[]{:S(2)}) async-start(f32[4,8,128]{2,1,0:T(8,128)} %shard_map.122), calls=%async_computation.1 | async-start | bytes 32768 | tf_op jit(solution)/shard_map/all_to_all | solution.py:772
  23.3 3.5 %copy-start.29 = (f32[4,8,128]{2,1,0:T(8,128)}, f32[4,8,128]{2,1,0:T(8,128)S(1)}, u32[]{:S(2)}) copy-start(f32[4,8,128]{2,1,0:T(8,128)S(1)} %all-to-all-done.1.sums_ref.first_ref) | copy-start | bytes 49156
  23.3 18.0 %all-to-all-start.3 = ((f32[4,4,16,8,128]{4,3,2,1,0:T(8,128)}), f32[4,4,16,8,128]{4,3,2,1,0:T(8,128)S(1)}, u32[]{:S(2)}, u32[]{:S(2)}) async-start(f32[4,4,16,8,128]{4,3,2,1,0:T(8,128)} %shard_map.124), calls=%async_computation.3 | async-start | bytes 2097152 | tf_op jit(solution)/shard_map/all_to_all | solution.py:828
  26.8 0.7 copy-start.27
  41.2 19.1 %copy-start.3 = (f32[4,4,16,8,128]{4,3,2,1,0:T(8,128)}, f32[4,4,16,8,128]{4,3,2,1,0:T(8,128)S(1)}, u32[]{:S(2)}) copy-start(f32[4,4,16,8,128]{4,3,2,1,0:T(8,128)S(1)} %all-to-all-done.3) | copy-start | bytes 3145732
  41.2 22.7 %all-to-all-start.2 = ((f32[32,4,8,128]{3,2,1,0:T(8,128)}), f32[32,4,8,128]{3,2,1,0:T(8,128)S(1)}, u32[]{:S(2)}, u32[]{:S(2)}) async-start(f32[32,4,8,128]{3,2,1,0:T(8,128)} %get-tuple-element.38), calls=%async_computation.2 | async-start | bytes 1048576 | tf_op jit(solution)/shard_map/all_to_all | solution.py:756
  43.8 16.5 %collective-permute-start.2 = (f32[4,256]{1,0:T(4,128)S(1)}, f32[4,256]{1,0:T(4,128)S(1)}, u32[]{:S(2)}, u32[]{:S(2)}) collective-permute-start(f32[4,256]{1,0:T(4,128)S(1)} %get-tuple-element.41), channel_id=1, source_target_pairs={{0,1},{1,2},{2,3},{4,5},{5,6},{6,7},{8,9},{9,10},{10,11},{12,13},{... | collective-permute-start | bytes 12296 | tf_op jit(solution)/shard_map/ppermute | solution.py:780
  45.9 14.4 %collective-permute-start.3 = (f32[4,256]{1,0:T(4,128)S(1)}, f32[4,256]{1,0:T(4,128)S(1)}, u32[]{:S(2)}, u32[]{:S(2)}) collective-permute-start(f32[4,256]{1,0:T(4,128)S(1)} %get-tuple-element.42), channel_id=1, source_target_pairs={{1,0},{2,1},{3,2},{5,4},{6,5},{7,6},{9,8},{10,9},{11,10},{13,12},{... | collective-permute-start | bytes 12296 | tf_op jit(solution)/shard_map/ppermute | solution.py:781
  47.2 13.1 %collective-permute-start = (bf16[128,256]{1,0:T(8,128)(2,1)S(1)}, bf16[128,256]{1,0:T(8,128)(2,1)S(1)}, u32[]{:S(2)}, u32[]{:S(2)}) collective-permute-start(bf16[128,256]{1,0:T(8,128)(2,1)S(1)} %get-tuple-element.39), channel_id=1, source_target_pairs={{0,4},{4,8},{8,12},{12,16},{16,20},{20,24},{24,28},{1,5},{5,9},{9,... | collective-permute-start | bytes 196616 | tf_op jit(solution)/shard_map/ppermute | solution.py:780
  50.7 9.6 %collective-permute-start.1 = (bf16[128,256]{1,0:T(8,128)(2,1)S(1)}, bf16[128,256]{1,0:T(8,128)(2,1)S(1)}, u32[]{:S(2)}, u32[]{:S(2)}) collective-permute-start(bf16[128,256]{1,0:T(8,128)(2,1)S(1)} %get-tuple-element.40), channel_id=1, source_target_pairs={{4,0},{8,4},{12,8},{16,12},{20,16},{24,20},{28,24},{5,1},{9,5},{13... | collective-permute-start | bytes 196616 | tf_op jit(solution)/shard_map/ppermute | solution.py:781
  70.5 24.7 %all-to-all-start.4 = ((f32[32,4,8,128]{3,2,1,0:T(8,128)}), f32[32,4,8,128]{3,2,1,0:T(8,128)}, u32[]{:S(2)}, u32[]{:S(2)}) async-start(f32[32,4,8,128]{3,2,1,0:T(8,128)} %shard_map.127.__), calls=%async_computation.4 | async-start | bytes 1048576 | tf_op jit(solution)/shard_map/all_to_all | solution.py:756
  79.7 15.5 %copy-start.23 = (f32[17]{0:T(128)S(1)}, f32[17]{0:T(128)}, u32[]{:S(2)}) copy-start(f32[17]{0:T(128)} %proj_ref.3) | copy-start | bytes 208
  87.8 27.2 %copy-start = (f32[5,128,256]{2,1,0:T(8,128)S(1)}, f32[5,128,256]{2,1,0:T(8,128)}, u32[]{:S(2)}) copy-start(f32[5,128,256]{2,1,0:T(8,128)} %get-tuple-element.45.__.refs_0_.refs_1_) | copy-start | bytes 1966084
  87.8 27.2 %copy-start.2 = (f32[4,128,256]{2,1,0:T(8,128)S(1)}, f32[4,128,256]{2,1,0:T(8,128)}, u32[]{:S(2)}) copy-start(f32[4,128,256]{2,1,0:T(8,128)} %a_.3) | copy-start | bytes 1572868
  87.8 27.2 %copy-start.6 = (f32[4,128,256]{2,1,0:T(8,128)S(1)}, f32[4,128,256]{2,1,0:T(8,128)}, u32[]{:S(2)}) copy-start(f32[4,128,256]{2,1,0:T(8,128)} %get-tuple-element.51.refs_2_) | copy-start | bytes 1572868
  87.8 27.2 %copy-start.7 = (f32[4,128,256]{2,1,0:T(8,128)S(1)}, f32[4,128,256]{2,1,0:T(8,128)}, u32[]{:S(2)}) copy-start(f32[4,128,256]{2,1,0:T(8,128)} %get-tuple-element.52.refs_3_) | copy-start | bytes 1572868
  87.8 27.2 %copy-start.8 = (f32[4,128,256]{2,1,0:T(8,128)S(1)}, f32[4,128,256]{2,1,0:T(8,128)}, u32[]{:S(2)}) copy-start(f32[4,128,256]{2,1,0:T(8,128)} %get-tuple-element.53.refs_4_) | copy-start | bytes 1572868
  87.8 27.2 %copy-start.9 = (f32[4,128,256]{2,1,0:T(8,128)S(1)}, f32[4,128,256]{2,1,0:T(8,128)}, u32[]{:S(2)}) copy-start(f32[4,128,256]{2,1,0:T(8,128)} %get-tuple-element.54.refs_5_) | copy-start | bytes 1572868
  87.8 47.9 %copy-start.28 = (f32[16,3]{0,1:T(4,128)S(1)}, f32[16,3]{0,1:T(4,128)}, u32[]{:S(2)}) copy-start(f32[16,3]{0,1:T(4,128)} %param.12) | copy-start | bytes 580
  104.7 10.2 %collective-permute-start.4 = (f32[128,256]{1,0:T(8,128)S(1)}, f32[128,256]{1,0:T(8,128)S(1)}, u32[]{:S(2)}, u32[]{:S(2)}) collective-permute-start(f32[128,256]{1,0:T(8,128)S(1)} %get-tuple-element.47), channel_id=1, source_target_pairs={{0,4},{4,8},{8,12},{12,16},{16,20},{20,24},{24,28},{1,5},{5,9},{9,... | collective-permute-start | bytes 393224 | tf_op jit(solution)/shard_map/ppermute | solution.py:780
  107.9 7.1 %collective-permute-start.5 = (f32[128,256]{1,0:T(8,128)S(1)}, f32[128,256]{1,0:T(8,128)S(1)}, u32[]{:S(2)}, u32[]{:S(2)}) collective-permute-start(f32[128,256]{1,0:T(8,128)S(1)} %get-tuple-element.48), channel_id=1, source_target_pairs={{4,0},{8,4},{12,8},{16,12},{20,16},{24,20},{28,24},{5,1},{9,5},{13... | collective-permute-start | bytes 393224 | tf_op jit(solution)/shard_map/ppermute | solution.py:781
  109.2 2.6 %collective-permute-start.6 = (f32[4,256]{1,0:T(4,128)S(1)}, f32[4,256]{1,0:T(4,128)S(1)}, u32[]{:S(2)}, u32[]{:S(2)}) collective-permute-start(f32[4,256]{1,0:T(4,128)S(1)} %get-tuple-element.49), channel_id=1, source_target_pairs={{0,1},{1,2},{2,3},{4,5},{5,6},{6,7},{8,9},{9,10},{10,11},{12,13},{... | collective-permute-start | bytes 12296 | tf_op jit(solution)/shard_map/ppermute | solution.py:780
  110.5 4.5 %collective-permute-start.7 = (f32[4,256]{1,0:T(4,128)S(1)}, f32[4,256]{1,0:T(4,128)S(1)}, u32[]{:S(2)}, u32[]{:S(2)}) collective-permute-start(f32[4,256]{1,0:T(4,128)S(1)} %get-tuple-element.50), channel_id=1, source_target_pairs={{1,0},{2,1},{3,2},{5,4},{6,5},{7,6},{9,8},{10,9},{11,10},{13,12},{... | collective-permute-start | bytes 12296 | tf_op jit(solution)/shard_map/ppermute | solution.py:781
  111.8 23.9 %copy-start.15 = (f32[4,256]{1,0:T(4,128)}, f32[4,256]{1,0:T(4,128)S(1)}, u32[]{:S(2)}) copy-start(f32[4,256]{1,0:T(4,128)S(1)} %collective-permute-done.6.left_ref.old_left) | copy-start | bytes 12292
  114.9 20.7 %copy-start.17 = (f32[4,256]{1,0:T(4,128)}, f32[4,256]{1,0:T(4,128)S(1)}, u32[]{:S(2)}) copy-start(f32[4,256]{1,0:T(4,128)S(1)} %collective-permute-done.7.right_ref.old_right) | copy-start | bytes 12292
  115.0 1.2 copy-start.4
  145.5 0.8 copy-start.11
  146.3 18.2 %all-to-all-start.7 = ((f32[32,4,8,128]{3,2,1,0:T(8,128)}), f32[32,4,8,128]{3,2,1,0:T(8,128)S(1)}, u32[]{:S(2)}, u32[]{:S(2)}) async-start(f32[32,4,8,128]{3,2,1,0:T(8,128)} %get-tuple-element.57), calls=%async_computation.7 | async-start | bytes 1048576 | tf_op jit(solution)/shard_map/all_to_all | solution.py:756
  171.0 18.9 %all-to-all-start.8 = ((f32[32,4,8,128]{3,2,1,0:T(8,128)}), f32[32,4,8,128]{3,2,1,0:T(8,128)}, u32[]{:S(2)}, u32[]{:S(2)}) async-start(f32[32,4,8,128]{3,2,1,0:T(8,128)} %shard_map.134.__), calls=%async_computation.8 | async-start | bytes 1048576 | tf_op jit(solution)/shard_map/all_to_all | solution.py:756
  182.7 46.1 %copy-start.1 = (f32[5,128,256]{2,1,0:T(8,128)S(1)}, f32[5,128,256]{2,1,0:T(8,128)}, u32[]{:S(2)}) copy-start(f32[5,128,256]{2,1,0:T(8,128)} %get-tuple-element.45.__.refs_0_.refs_1_) | copy-start | bytes 1966084
  182.7 46.1 %copy-start.10 = (f32[4,128,256]{2,1,0:T(8,128)S(1)}, f32[4,128,256]{2,1,0:T(8,128)}, u32[]{:S(2)}) copy-start(f32[4,128,256]{2,1,0:T(8,128)} %get-tuple-element.65.res_ref) | copy-start | bytes 1572868
  182.7 46.1 %copy-start.12 = (f32[4,8,128]{2,1,0:T(8,128)S(1)}, f32[4,8,128]{2,1,0:T(8,128)}, u32[]{:S(2)}) copy-start(f32[4,8,128]{2,1,0:T(8,128)} %all_to_all.67.sums_ref.first_ref) | copy-start | bytes 49156
  189.9 0.7 copy-start.24
  201.0 16.0 %copy-start.25 = (f32[4,256]{1,0:T(4,128)}, f32[4,256]{1,0:T(4,128)S(1)}, u32[]{:S(2)}) copy-start(f32[4,256]{1,0:T(4,128)S(1)} %get-tuple-element.64) | copy-start | bytes 12292
  201.0 16.0 %copy-start.26 = (f32[4,256]{1,0:T(4,128)}, f32[4,256]{1,0:T(4,128)S(1)}, u32[]{:S(2)}) copy-start(f32[4,256]{1,0:T(4,128)S(1)} %get-tuple-element.63) | copy-start | bytes 12292
  201.0 27.8 %collective-permute-start.8 = (f32[128,256]{1,0:T(8,128)}, f32[128,256]{1,0:T(8,128)}, u32[]{:S(2)}, u32[]{:S(2)}) collective-permute-start(f32[128,256]{1,0:T(8,128)} %get-tuple-element.61), channel_id=1, source_target_pairs={{0,4},{4,8},{8,12},{12,16},{16,20},{20,24},{24,28},{1,5},{5,9},{9,... | collective-permute-start | bytes 393224 | tf_op jit(solution)/shard_map/ppermute | solution.py:780
  204.8 23.9 %collective-permute-start.9 = (f32[128,256]{1,0:T(8,128)}, f32[128,256]{1,0:T(8,128)}, u32[]{:S(2)}, u32[]{:S(2)}) collective-permute-start(f32[128,256]{1,0:T(8,128)} %get-tuple-element.62), channel_id=1, source_target_pairs={{4,0},{8,4},{12,8},{16,12},{20,16},{24,20},{28,24},{5,1},{9,5},{13... | collective-permute-start | bytes 393224 | tf_op jit(solution)/shard_map/ppermute | solution.py:781
  217.0 0.6 copy-start.14
  217.6 11.2 %all-to-all-start.10 = ((f32[4,8,128]{2,1,0:T(8,128)}), f32[4,8,128]{2,1,0:T(8,128)}, u32[]{:S(2)}, u32[]{:S(2)}) async-start(f32[4,8,128]{2,1,0:T(8,128)} %copy-done.14), calls=%async_computation.10 | async-start | bytes 32768 | tf_op jit(solution)/shard_map/all_to_all | solution.py:772
  221.4 3.7 %collective-permute-start.10 = (f32[4,256]{1,0:T(4,128)}, f32[4,256]{1,0:T(4,128)S(1)}, u32[]{:S(2)}, u32[]{:S(2)}) collective-permute-start(f32[4,256]{1,0:T(4,128)} %copy-done.26), channel_id=1, source_target_pairs={{0,1},{1,2},{2,3},{4,5},{5,6},{6,7},{8,9},{9,10},{10,11},{12,13},{... | collective-permute-start | bytes 12296 | tf_op jit(solution)/shard_map/ppermute | solution.py:780
  223.8 4.4 %collective-permute-start.11 = (f32[4,256]{1,0:T(4,128)}, f32[4,256]{1,0:T(4,128)S(1)}, u32[]{:S(2)}, u32[]{:S(2)}) collective-permute-start(f32[4,256]{1,0:T(4,128)} %copy-done.25), channel_id=1, source_target_pairs={{1,0},{2,1},{3,2},{5,4},{6,5},{7,6},{9,8},{10,9},{11,10},{13,12},{... | collective-permute-start | bytes 12296 | tf_op jit(solution)/shard_map/ppermute | solution.py:781
  225.1 0.6 copy-start.19
  228.8 1.2 copy-start.5
  230.1 0.7 copy-start.16
  230.7 0.7 copy-start.18
  231.4 0.7 copy-start.20
  232.1 0.7 copy-start.22
  (1 other events, 0.6 us)

commit v3 on v2

--- a/solution.py
+++ b/solution.py
@@ -367,56 +367,25 @@
     return jnp.sum(total[row : row + 1], axis=1, keepdims=True)
 
 
-def squares_body(field_ref, perm_ref, out_ref, low_ref, high_ref, left_ref, right_ref):
+def squares_body(field_ref, out_ref):
     total = field_ref[0] * field_ref[0]
     for place in range(1, field_ref.shape[0]):
         total = total + field_ref[place] * field_ref[place]
     spread([lane_sums(total)], out_ref)
-    rows, cols, _ = perm_ref.shape
-    low_ref[...] = perm_ref[0]
-    high_ref[...] = perm_ref[rows - 1]
-    for place in range(rows):
-        plane = perm_ref[place].astype(F32)
-        left_ref[place : place + 1, :] = plane[:1]
-        right_ref[place : place + 1, :] = plane[cols - 1 :]
-
-
-def weight_body(weight_ref, out_ref):
-    groups, freq, channels, fine, _ = out_ref.shape
+
+
+def weight_body(weight_ref, *refs):
+    *out_refs, hold_ref = refs
+    groups, freq, channels, fine, _ = hold_ref.shape
     parts, deep, _, outs, modes = weight_ref.shape
     for channel in range(channels):
         block = weight_ref[:, :, channel].reshape(parts * deep * outs, modes)
         block = block.T.reshape(freq, groups, fine, parts * deep * outs)
         for group in range(groups):
-            out_ref[group, :, channel] = block[:, group]
-
-
-def prepare_body(weight_ref, perm_ref, low_ref, high_ref, left_ref, right_ref, other_ref, first_ref, sec_lo, sec_hi, thi_lo, thi_hi):
-    other_ref[...] = pltpu.roll(weight_ref[...], LANES // 2, 1)
-    rows, cols, depth = perm_ref.shape
-    planes = [perm_ref[place].astype(F32) for place in range(rows)]
-    line = lax.broadcasted_iota(jnp.int32, (cols, depth), 0)
-    deep = lax.broadcasted_iota(jnp.int32, (cols, depth), 1)
-    before = low_ref[...].astype(F32)
-    after = high_ref[...].astype(F32)
-    around = [jnp.where(before > 0.0, before, planes[0])] + planes
-    around = around + [jnp.where(after > 0.0, after, planes[-1])]
-    for place in range(rows + 1):
-        first_ref[place] = harmonic(around[place], around[place + 1])
-    for place in range(rows):
-        own = planes[place]
-        left = left_ref[place : place + 1]
-        right = right_ref[place : place + 1]
-        left = jnp.where(left > 0.0, left, own[:1])
-        right = jnp.where(right > 0.0, right, own[cols - 1 :])
-        lower = jnp.where(line == 0, left, pltpu.roll(own, 1, 0))
-        upper = jnp.where(line == cols - 1, right, pltpu.roll(own, cols - 1, 0))
-        sec_lo[place] = harmonic(own, lower)
-        sec_hi[place] = harmonic(own, upper)
-        lower = jnp.where(deep == 0, own, pltpu.roll(own, 1, 1))
-        upper = jnp.where(deep == depth - 1, own, pltpu.roll(own, depth - 1, 1))
-        thi_lo[place] = harmonic(own, lower)
-        thi_hi[place] = harmonic(own, upper)
+            hold_ref[group, :, channel] = block[:, group]
+    place = lax.axis_index("col")
+    for shift, out_ref in enumerate(out_refs):
+        out_ref[...] = hold_ref[lax.rem(place + shift, groups)]
 
 
 def scale_of(total, cells):
@@ -460,7 +429,7 @@
             ]
 
 
-def lift_first_body(cells, lift_ref, sums_ref, res_ref, perm_ref, deep_ref, col_ref, spectra_ref, lifted_ref, zt_ref):
+def lift_first_body(cells, lift_ref, sums_ref, res_ref, perm_ref, deep_ref, col_ref, _, spectra_ref, lifted_ref, zt_ref):
     scale = scale_of(gathered(sums_ref, 0), cells)
     scaled = (res_ref[0] / scale).T
     log_perm = jnp.log(perm_ref[0].astype(F32)).T
@@ -506,7 +475,18 @@
     lax.fori_loop(0, lifted_ref.shape[2] // size, step, 0)
 
 
-def modes_body(cells, n_row, n_col, recv_ref, weight_ref, other_ref, _, __, out_ref, field_ref, turned_ref, spec_ref, odd_ref):
+def modes_body(cells, n_row, n_col, recv_ref, *refs):
+    sources = refs[:n_col]
+    _, out_ref, weight_ref, sems, field_ref, turned_ref, spec_ref, odd_ref = refs[n_col:]
+    own = lax.axis_index("col")
+    copies = [
+        pltpu.make_async_copy(
+            source, weight_ref.at[lax.rem(own + n_col - shift, n_col)], sems.at[shift]
+        )
+        for shift, source in enumerate(sources)
+    ]
+    for copy in copies:
+        copy.start()
     rows = recv_ref.shape[1]
     places = n_row * rows
     tile = (SUBLANES, LANES)
@@ -555,14 +535,18 @@
         if freq > 0:
             spec_ref[half - freq] = even - odd
 
-    def mix(freq, carry):
+    for copy in copies:
+        copy.wait()
+    share = KX // n_col
+    for freq in range(KX):
         value = spec_ref[freq]
         same = [None, None]
         cross = [None, None]
         for channel in range(CHANNELS):
             wide = jnp.take_along_axis(value, base + channel, axis=1)
-            for sums, ref in ((same, weight_ref), (cross, other_ref)):
-                term = ref[freq, channel] * wide
+            weight = weight_ref[freq // share, freq % share, channel]
+            for sums, factor in ((same, weight), (cross, pltpu.roll(weight, LANES // 2, 1))):
+                term = factor * wide
                 kept = sums[channel % 2]
                 sums[channel % 2] = term if kept is None else kept + term
         same = same[0] + same[1]
@@ -574,9 +558,6 @@
         )
         field_ref[freq] = total
         turned_ref[freq] = -turn(total)
-        return carry
-
-    lax.fori_loop(0, KX, mix, 0)
     gain = 1.0 / cells
     evens = [field_ref[half] * gain]
     odds = [None]
@@ -632,21 +613,23 @@
     return (scale * (total + proj_ref[CHANNELS])).T
 
 
-def put_edges(update, low_ref, high_ref, left_ref, right_ref):
+def put_edges(update, low_ref, high_ref, left_ref, right_ref, first=0):
     step = pl.program_id(0)
-    left_ref[pl.ds(step, 1), :] = update[:1]
-    right_ref[pl.ds(step, 1), :] = update[update.shape[0] - 1 :]
+    cols = update.shape[0]
+    line = pl.ds(step + first * pl.num_programs(0), 1)
+    left_ref[line, :] = update[:1]
+    right_ref[line, :] = update[cols - 1 :]
 
     @pl.when(step == 0)
     def _():
-        low_ref[...] = update
+        low_ref[first * cols : (first + 1) * cols] = update
 
     @pl.when(step == pl.num_programs(0) - 1)
     def _():
-        high_ref[...] = update
-
-
-def back_first_body(cells, proj_ref, sums_ref, recv_ref, point_ref, col_ref, deep_ref, kept_ref, *refs):
+        high_ref[first * cols : (first + 1) * cols] = update
+
+
+def back_first_body(cells, proj_ref, sums_ref, recv_ref, point_ref, col_ref, deep_ref, perm_ref, kept_ref, *refs):
     *edges, wave_ref = refs
     scale = scale_of(gathered(sums_ref, 0), cells)
     update = back_transform(
@@ -654,6 +637,7 @@
     )
     kept_ref[0, 0] = update
     put_edges(update, *edges)
+    put_edges(perm_ref[0].astype(F32), *edges, first=1)
 
 
 def back_next_body(cells, proj_ref, first_ref, sums_ref, recv_ref, point_ref, col_ref, deep_ref, image_ref, _, kept_ref, out_ref, *refs):
@@ -678,21 +662,34 @@
         spread([acc_ref[0:1]], out_ref)
 
 
-def stencil(own, before, after, left, right, faces):
-    first_lo, first_hi, sec_lo, sec_hi, thi_lo, thi_hi = (ref[0] for ref in faces)
+def stencil(fields, perms):
+    own, before, after, left, right = fields
     cols, depth = own.shape
     line = lax.broadcasted_iota(jnp.int32, (cols, depth), 0)
     deep = lax.broadcasted_iota(jnp.int32, (cols, depth), 1)
-    total = first_lo * (own - before)
-    total = total + first_hi * (own - after)
-    other = jnp.where(line == 0, left, pltpu.roll(own, 1, 0))
-    total = total + sec_lo * (own - other)
-    other = jnp.where(line == cols - 1, right, pltpu.roll(own, cols - 1, 0))
-    total = total + sec_hi * (own - other)
-    other = jnp.where(deep == 0, 0.0, pltpu.roll(own, 1, 1))
-    total = total + thi_lo * (own - other)
-    other = jnp.where(deep == depth - 1, 0.0, pltpu.roll(own, depth - 1, 1))
-    return total + thi_hi * (own - other)
+
+    def sides(array, before, after, left, right, first, last):
+        return (
+            before,
+            after,
+            jnp.where(line == 0, left, pltpu.roll(array, 1, 0)),
+            jnp.where(line == cols - 1, right, pltpu.roll(array, cols - 1, 0)),
+            jnp.where(deep == 0, first, pltpu.roll(array, 1, 1)),
+            jnp.where(deep == depth - 1, last, pltpu.roll(array, depth - 1, 1)),
+        )
+
+    perm, *others = perms
+    others = [
+        jnp.where(other > 0.0, other, edge)
+        for other, edge in zip(others, (perm, perm, perm[:1], perm[cols - 1 :]))
+    ]
+    total = None
+    for other, conductance in zip(
+        sides(own, before, after, left, right, 0.0, 0.0), sides(perm, *others, perm, perm)
+    ):
+        term = harmonic(perm, conductance) * (own - other)
+        total = term if total is None else total + term
+    return total
 
 
 def add_sums(terms, out_ref, acc_ref):
@@ -710,36 +707,50 @@
         spread([acc_ref[j : j + 1] for j in range(len(terms))], out_ref)
 
 
-def around(ref, index, low, high):
+def around(ref, index, halo, part):
+    low_ref, high_ref, left_ref, right_ref = halo
     step = pl.program_id(0)
     last = pl.num_programs(0) - 1
-    before = jnp.where(step == 0, low, ref[index, jnp.maximum(step - 1, 0)])
-    after = jnp.where(step == last, high, ref[index, jnp.minimum(step + 1, last)])
-    return ref[index, step], before, after
-
-
-def operator_first_body(kept_ref, low_ref, high_ref, left_ref, right_ref, res_ref, *refs):
-    *faces, image_ref, out_ref, acc_ref = refs
-    line = pl.ds(pl.program_id(0), 1)
-    own, before, after = around(kept_ref, 0, low_ref[...], high_ref[...])
-    image = stencil(own, before, after, left_ref[line, :], right_ref[line, :], faces)
+    cols = ref.shape[-2]
+    planes = slice(part * cols, (part + 1) * cols)
+    line = pl.ds(step + part * pl.num_programs(0), 1)
+
+    def plane(place):
+        return ref[index + (place,)].astype(F32)
+
+    def outside(axis, edge, value):
+        return jnp.where(lax.axis_index(axis) == edge, 0.0, value)
+
+    low = outside("row", 0, low_ref[planes])
+    high = outside("row", lax.axis_size("row") - 1, high_ref[planes])
+    left = outside("col", 0, left_ref[line, :])
+    right = outside("col", lax.axis_size("col") - 1, right_ref[line, :])
+    before = jnp.where(step == 0, low, plane(jnp.maximum(step - 1, 0)))
+    after = jnp.where(step == last, high, plane(jnp.minimum(step + 1, last)))
+    return plane(step), before, after, left, right
+
+
+def operator_first_body(kept_ref, perm_ref, *refs):
+    halo = refs[:4]
+    res_ref, image_ref, out_ref, acc_ref = refs[4:]
+    fields = around(kept_ref, (0,), halo, 0)
+    image = stencil(fields, around(perm_ref, (), halo, 1))
+    own = fields[0]
     residual = res_ref[0]
     image_ref[0] = image
     add_sums((own * image, residual * own, image * image, residual * image), out_ref, acc_ref)
 
 
-def operator_next_body(first_ref, beta_ref, kept_ref, low_ref, high_ref, left_ref, right_ref, old_low, old_high, old_left, old_right, res_ref, *refs):
-    *faces, way_ref, image_ref, out_ref, acc_ref = refs
-    line = pl.ds(pl.program_id(0), 1)
+def operator_next_body(first_ref, beta_ref, kept_ref, perm_ref, *refs):
+    halo, old = refs[:4], refs[4:8]
+    res_ref, way_ref, image_ref, out_ref, acc_ref = refs[8:]
     beta = gathered(beta_ref, 0) / gathered(first_ref, 0)
-    fields = zip(
-        around(kept_ref, 1, low_ref[...], high_ref[...]),
-        around(kept_ref, 0, old_low[...], old_high[...]),
-    )
-    own, before, after = (new - beta * old for new, old in fields)
-    left = left_ref[line, :] - beta * old_left[line, :]
-    right = right_ref[line, :] - beta * old_right[line, :]
-    image = stencil(own, before, after, left, right, faces)
+    fields = [
+        new - beta * other
+        for new, other in zip(around(kept_ref, (1,), halo, 0), around(kept_ref, (0,), old, 0))
+    ]
+    image = stencil(fields, around(perm_ref, (), old, 1))
+    own = fields[0]
     way_ref[0] = own
     image_ref[0] = image
     add_sums((own * image, res_ref[0] * own), out_ref, acc_ref)
@@ -756,26 +767,15 @@
     return lax.all_to_all(blocks, BOTH, split_axis=0, concat_axis=0, tiled=True)
 
 
-def total_body(in_ref, out_ref):
-    out_ref[...] = jnp.broadcast_to(jnp.sum(in_ref[...], axis=0)[None], out_ref.shape)
-
-
 def add_up(partial):
-    found = lax.all_to_all(partial, "row", split_axis=0, concat_axis=0, tiled=True)
-    found = call(
-        total_body,
-        shape(lax.axis_size("col"), SUBLANES, LANES),
-        [whole()],
-        whole(),
-        near=(0,),
-    )(found)
-    return lax.all_to_all(found, "col", split_axis=0, concat_axis=0, tiled=True)
+    return exchange(partial)
 
 
 def neighbours(low, high, left, right):
     found = []
     for axis, first, last in (("row", low, high), ("col", left, right)):
-        forward = [(i, i + 1) for i in range(lax.axis_size(axis) - 1)]
+        count = lax.axis_size(axis)
+        forward = [(i, (i + 1) % count) for i in range(count)]
         backward = [(target, source) for source, target in forward]
         found.append(lax.ppermute(last, axis, forward))
         found.append(lax.ppermute(first, axis, backward))
@@ -794,7 +794,7 @@
     lift_weight = lift_weight.T
     field = shape(rows, cols, depth)
     field_bytes = 4 * rows * cols * depth
-    partial = shape(n_row, SUBLANES, LANES)
+    partial = shape(count, SUBLANES, LANES)
     channels = shape(rows, CHANNELS, depth, cols)
     spectra = shape(count, rows, SUBLANES, LANES)
     spectra_bytes = 4 * count * rows * SUBLANES * LANES
@@ -807,43 +807,25 @@
     lift_flops = 2.0e9
     back_flops = 2.0e9
 
-    edge_shapes = (shape(cols, depth),) * 2 + (shape(rows, depth),) * 2
-    thin = jax.ShapeDtypeStruct((cols, depth), permeability.dtype)
-    squares, *edges = call(
-        squares_body,
-        (partial, thin, thin) + edge_shapes[2:],
-        [vmem, vmem],
-        (vmem,) * 5,
-        moved=field_bytes,
-    )(right_side, permeability)
+    squares = call(squares_body, partial, [vmem], vmem, moved=field_bytes)(right_side)
     squares = add_up(squares)
 
-    weights = call(
+    weight_shape = (freq, CHANNELS, SUBLANES, LANES)
+    own, *weights = call(
         weight_body,
-        shape(n_col, freq, CHANNELS, SUBLANES, LANES),
+        (shape(*weight_shape),) * n_col,
         [vmem],
-        vmem,
+        (vmem,) * n_col,
+        scratch=[pltpu.VMEM((n_col,) + weight_shape, F32)],
         moved=8 * spectral_weight.size,
     )(spectral_weight)
-    weights = lax.all_to_all(weights, "col", split_axis=0, concat_axis=0, tiled=True)
-    weights = weights.reshape(KX * CHANNELS * SUBLANES, LANES)
-    others, first, *faces = call(
-        prepare_body,
-        (shape(*weights.shape), shape(rows + 1, cols, depth)) + (field,) * 4,
-        [vmem] * 6,
-        (vmem,) * 6,
-        moved=10 * field_bytes,
-        near=(0, 2, 3, 4, 5),
-        limit=12,
-    )(weights, permeability, *neighbours(*edges))
-    weights, others = (
-        array.reshape(KX, CHANNELS, SUBLANES, LANES) for array in (weights, others)
-    )
-    faces = [first, first] + faces
-    next_plane = pl.BlockSpec((1, cols, depth), lambda i: (i + 1, 0, 0))
-    face_specs = [plane, next_plane] + [plane] * 4
+    weights = [own] + [
+        lax.ppermute(part, "col", [(i, (i + shift + 1) % n_col) for i in range(n_col)])
+        for shift, part in enumerate(weights)
+    ]
+    edge_shapes = (shape(cols, depth),) * 2 + (shape(rows, depth),) * 2
+    both_shapes = (shape(2 * cols, depth),) * 2 + (shape(2 * rows, depth),) * 2
     acc_scratch = pltpu.VMEM((SUBLANES, LANES), F32)
-
     zt_scratch = pltpu.VMEM((2 * KZ * CHANNELS, cols), F32)
 
     anywhere = whole(pl.ANY)
@@ -869,12 +851,19 @@
         return call(
             functools.partial(modes_body, cells, n_row, n_col),
             spectra,
-            [vmem, vmem, vmem, anywhere, anywhere],
+            [vmem] + [anywhere] * (n_col + 1),
             vmem,
-            scratch=[tiles(places), tiles(places), tiles(KX), tiles(KX)],
-            moved=2 * spectra_bytes + 8 * weights.size,
+            scratch=[
+                pltpu.VMEM((n_col,) + weight_shape, F32),
+                pltpu.SemaphoreType.DMA((n_col,)),
+                tiles(places),
+                tiles(places),
+                tiles(KX),
+                tiles(KX),
+            ],
+            moved=2 * spectra_bytes + 4 * spectral_weight.size,
             near=(0,),
-        )(received, weights, others, before, faces[0])
+        )(received, *weights, before)
 
     def mixed_modes(blocks, lifted):
         received = exchange(blocks)
@@ -887,38 +876,38 @@
     blocks, lifted = call(
         functools.partial(lift_first_body, cells),
         (spectra, channels),
-        [smem, vmem, plane, plane, vmem, vmem],
+        [smem, vmem, plane, plane, vmem, vmem, anywhere],
         (spectra_block, point_block),
         limit=16,
         grid=(rows,),
         scratch=[zt_scratch],
         flops=lift_flops,
         moved=2 * field_bytes + spectra_bytes,
-    )(lift_weight, squares, right_side, permeability, deep_forward, col_forward)
+    )(lift_weight, squares, right_side, permeability, deep_forward, col_forward, weights[0])
     received, point = mixed_modes(blocks, lifted)
     kept, *edges = call(
         functools.partial(back_first_body, cells),
-        (kept_shape,) + edge_shapes,
-        [smem, vmem, spectra_block, point_block, vmem, vmem],
+        (kept_shape,) + both_shapes,
+        [smem, vmem, spectra_block, point_block, vmem, vmem, plane],
         (pl.BlockSpec((1, 1, cols, depth), lambda i: (0, i, 0, 0)),) + (vmem,) * 4,
         grid=(rows,),
         scratch=[zt_scratch],
         limit=12,
         flops=back_flops,
         moved=18 * field_bytes,
-    )(proj_weight, squares, received, point, col_back, deep_back)
+    )(proj_weight, squares, received, point, col_back, deep_back, permeability)
 
     old_halo = neighbours(*edges)
-    args = (kept, *old_halo, right_side, *faces)
+    args = (kept, permeability, *old_halo, right_side)
     image, sums = call(
         operator_first_body,
         (field, partial),
-        [vmem] * 5 + [plane] + face_specs,
+        [vmem] * 6 + [plane],
         (plane, vmem),
         grid=(rows,),
         scratch=[acc_scratch],
         moved=9 * field_bytes,
-        near=range(12),
+        near=range(7),
         loose=True,
     )(*args)
     sums = add_up(sums)
@@ -951,15 +940,15 @@
 
     beta = add_up(beta)
     halo = neighbours(*edges)
-    args = (sums, beta, kept, *halo, *old_halo, residual, *faces)
+    args = (sums, beta, kept, permeability, *halo, *old_halo, residual)
     way, image, later = call(
         operator_next_body,
         (field, field, partial),
-        [vmem] * 11 + [plane] + face_specs,
+        [vmem] * 12 + [plane],
         (plane, plane, vmem),
         grid=(rows,),
         scratch=[acc_scratch],
-        near=range(18),
+        near=range(13),
         loose=True,
         moved=11 * field_bytes,
     )(*args)

time: 255 us -> 212 us (0.83)
  blocking collectives: 59.4 us -> 22.7 us
  waiting for transfers between devices: 33 us -> 46.6 us
  starting transfers between devices: 52.5 us -> 40.6 us
  Pallas kernels: 98.1 us -> 92.3 us
    all_to_all x6 -> x2, blocking collectives: 59.4 us -> 22.7 us  [exchange(): return lax.all_to_all(blocks, BOTH, split_axis=0, concat_axis=0, tiled=True)]
    ppermute x6 -> x4, starting transfers between devices: 16.2 us -> 3.07 us  [neighbours(): found.append(lax.ppermute(last, axis, forward))]
    all_to_all x3 -> x0, starting transfers between devices: 10.6 us -> none  [the longest x2 7.1 us: add_up(): return lax.all_to_all(found, 'col', split_axis=0, concat_axis=0, tiled=True)]
    ppermute x6 -> x4, waiting for transfers between devices: 0.02 us -> 9.65 us  [neighbours(): found.append(lax.ppermute(last, axis, forward))]
    ppermute x0 -> x3, waiting for transfers between devices: none -> 6.64 us  [tiled_local(): lax.ppermute(part, 'col', [(i, (i + shift + 1) % n_col) for i in range(n_...]
    all_to_all x4 -> x6, starting transfers between devices: 17.9 us -> 24.4 us  [exchange(): return lax.all_to_all(blocks, BOTH, split_axis=0, concat_axis=0, tiled=True)]
    all_to_all x4 -> x6, waiting for transfers between devices: 21.9 us -> 27.8 us  [exchange(): return lax.all_to_all(blocks, BOTH, split_axis=0, concat_axis=0, tiled=True)]
    pallas_call x20 -> x15, Pallas kernels: 98.1 us -> 92.3 us  [wrapped(): found = run(*held)]
  transfers between devices with their start and end apart: 19 -> 17, of which waited for: 7 -> 13; matrix products, arithmetic and copies ran while one was open for 0% -> 0% of each run, Pallas kernels for 19% -> 16%
where the time goes in v3:
time: 212 us; the launch traced here: 211 us
  Pallas kernels  92.3 us (44%)
  waiting for transfers between devices  46.6 us (22%)
  starting transfers between devices  40.6 us (19%)
  blocking collectives  22.7 us (11%)
  local copies, waits for them, and re-layouts  8.04 us (4%)
    pallas_call x15, Pallas kernels, wrapped(): found = run(*held)  92.3 us
    all_to_all x6, waiting for transfers between devices, exchange(): return lax.all_to_all(blocks, BOTH, split_axis=0, concat_axis=0, tiled=True)  27.8 us
    all_to_all x6, starting transfers between devices, exchange(): return lax.all_to_all(blocks, BOTH, split_axis=0, concat_axis=0, tiled=True)  24.4 us
    all_to_all x2, blocking collectives, exchange(): return lax.all_to_all(blocks, BOTH, split_axis=0, concat_axis=0, tiled=True)  22.7 us
    ppermute x4, starting transfers between devices, neighbours(): found.append(lax.ppermute(first, axis, backward))  9.92 us
    ppermute x4, waiting for transfers between devices, neighbours(): found.append(lax.ppermute(last, axis, forward))  9.65 us
    unnamed x40, local copies, waits for them, and re-layouts  8.04 us
    ppermute x3, waiting for transfers between devices, tiled_local(): lax.ppermute(part, 'col', [(i, (i + shift + 1) % n_col) for i in range(n_...  6.64 us
  transfers between devices with their start and end apart: 17, of which 13 were waited for; matrix products, arithmetic and copies ran while one was open for 0% of the time, Pallas kernels for 16%

profile of v3, /device:TPU:0, one launch (start us, length us, event | category | flops | bytes accessed | tf_op | source)
XLA Modules:
  0.0 211.0 jit_solution(14892651232650519425)
XLA Ops:
  0.6 1.8 shard_map.121
  2.4 7.3 %all-to-all-start = ((f32[32,8,128]{2,1,0:T(8,128)}), f32[32,8,128]{2,1,0:T(8,128)S(1)}, u32[]{:S(2)}, u32[]{:S(2)}) async-start(f32[32,8,128]{2,1,0:T(8,128)} %shard_map.121), calls=%async_computation | async-start | bytes 262144 | tf_op jit(solution)/shard_map/all_to_all | solution.py:767
  9.7 1.7 shard_map.122
  12.1 5.9 %all-to-all-done.sums_ref.first_ref = f32[32,8,128]{2,1,0:T(8,128)S(1)} async-done(((f32[32,8,128]{2,1,0:T(8,128)}), f32[32,8,128]{2,1,0:T(8,128)S(1)}, u32[]{:S(2)}, u32[]{:S(2)}) %all-to-all-start) | async-done | bytes 131104 | tf_op jit(solution)/shard_map/all_to_all | solution.py:767
  19.3 9.7 %shard_map.123 = (f32[32,4,8,128]{3,2,1,0:T(8,128)}, f32[4,16,256,128]{3,2,1,0:T(8,128)}) custom-call(f32[3,16]{1,0:T(4,128)S(1)} %bitcast.1, f32[32,8,128]{2,1,0:T(8,128)} %copy-done.16, f32[4,128,256]{2,1,0:T(8,128)} %a_.3, bf16[4,128,256]{2,1,0:T(8,128)(2,1)} %perm_ref.9, bf16[128,256]{1,0:T(8,128)(2,1)} %constant.8.clone.deep_ref, ...), custom_call_target="tpu_custom_call" | custom-call | flops 2000000000 | bytes 1572864 | tf_op jit(solution)/shard_map/pallas_call | solution.py:338
  29.0 2.6 %all-to-all-start.1 = ((f32[32,4,8,128]{3,2,1,0:T(8,128)}), f32[32,4,8,128]{3,2,1,0:T(8,128)S(1)}, u32[]{:S(2)}, u32[]{:S(2)}) async-start(f32[32,4,8,128]{3,2,1,0:T(8,128)} %get-tuple-element.31), calls=%async_computation.1 | async-start | bytes 1048576 | tf_op jit(solution)/shard_map/all_to_all | solution.py:767
  31.8 1.7 collective-permute-start.1
  33.5 1.3 collective-permute-start.2
  34.8 8.2 %shard_map.124.refs_4_._ = f32[4,16,256,128]{3,2,1,0:T(8,128)} custom-call(f32[16,17]{1,0:T(8,128)S(1)} %copy-done.10, f32[4,16,256,128]{3,2,1,0:T(8,128)} %get-tuple-element.35.lifted_ref, f32[4,128,256]{2,1,0:T(8,128)} %a_.3, f32[4,128,256]{2,1,0:T(8,128)} %a_.3), custom_call_target="tpu_custom_call" | custom-call | flops 2500000000 | bytes 8388608 | tf_op jit(solution)/shard_map/pallas_call | solution.py:338
  43.0 1.2 collective-permute-done.refs_1_
  44.3 1.2 collective-permute-done.1.refs_2_
  45.5 4.2 %collective-permute-done.2.refs_3_ = f32[4,16,8,128]{3,2,1,0:T(8,128)S(1)} collective-permute-done((f32[4,16,8,128]{3,2,1,0:T(8,128)S(1)}, f32[4,16,8,128]{3,2,1,0:T(8,128)S(1)}, u32[]{:S(2)}, u32[]{:S(2)}) %collective-permute-start.2) | collective-permute-done | bytes 262176 | tf_op jit(solution)/shard_map/ppermute | solution.py:823
  50.4 4.8 %shard_map.125.__ = f32[32,4,8,128]{3,2,1,0:T(8,128)} custom-call(f32[32,4,8,128]{3,2,1,0:T(8,128)S(1)} %all-to-all-done.1.recv_ref, f32[4,16,8,128]{3,2,1,0:T(8,128)} %copy-done.8, f32[4,16,8,128]{3,2,1,0:T(8,128)} %copy-done.17, f32[4,16,8,128]{3,2,1,0:T(8,128)} %copy-done.18, f32[4,16,8,128]{3,2,1,0:T(8,128)} %copy-done.19, ...), custom_call_target="tpu_custom_call" | custom-call | bytes 2097152 | tf_op jit(solution)/shard_map/pallas_call | solution.py:338
  55.2 5.7 %all-to-all-start.2 = ((f32[32,4,8,128]{3,2,1,0:T(8,128)}), f32[32,4,8,128]{3,2,1,0:T(8,128)S(1)}, u32[]{:S(2)}, u32[]{:S(2)}) async-start(f32[32,4,8,128]{3,2,1,0:T(8,128)} %shard_map.125.__), calls=%async_computation.2 | async-start | bytes 1048576 | tf_op jit(solution)/shard_map/all_to_all | solution.py:767
  60.9 8.1 %shard_map.126.point_ref = f32[4,16,256,128]{3,2,1,0:T(8,128)} custom-call(f32[16,17]{1,0:T(8,128)S(1)} %copy-done.10, f32[4,16,256,128]{3,2,1,0:T(8,128)} %get-tuple-element.35.lifted_ref, f32[4,16,256,128]{3,2,1,0:T(8,128)} %shard_map.124.refs_4_._, f32[32,4,8,128]{3,2,1,0:T(8,128)} %shard_map.125.__), custom_call_target="tpu_custom_call", output_to_operand_aliasing={{}: (2, {})} | custom-call | flops 2500000000 | bytes 8388608 | tf_op jit(solution)/shard_map/pallas_call | solution.py:338
  69.0 7.4 %all-to-all-done.2.recv_ref = f32[32,4,8,128]{3,2,1,0:T(8,128)S(1)} async-done(((f32[32,4,8,128]{3,2,1,0:T(8,128)}), f32[32,4,8,128]{3,2,1,0:T(8,128)S(1)}, u32[]{:S(2)}, u32[]{:S(2)}) %all-to-all-start.2) | async-done | bytes 524320 | tf_op jit(solution)/shard_map/all_to_all | solution.py:767
  76.4 0.8 copy-done.15
  77.2 10.3 %shard_map.127 = (f32[2,4,128,256]{3,2,1,0:T(8,128)}, f32[256,256]{1,0:T(8,128)S(1)}, f32[256,256]{1,0:T(8,128)S(1)}, f32[8,256]{1,0:T(8,128)S(1)}, f32[8,256]{1,0:T(8,128)S(1)}) custom-call(f32[17]{0:T(128)S(1)} %copy-done.11, f32[32,8,128]{2,1,0:T(8,128)} %copy-done.16, f32[32,4,8,128]{3,2,1,0:T(8,128)} %copy-done.15, ...), custom_call_target="tpu_custom_call" | custom-call | flops 2000000000 | bytes 9437184 | tf_op jit(solution)/shard_map/pallas_call | solution.py:338
  87.5 1.2 collective-permute-start.3
  88.7 3.5 %collective-permute-start.4 = (f32[256,256]{1,0:T(8,128)S(1)}, f32[256,256]{1,0:T(8,128)S(1)}, u32[]{:S(2)}, u32[]{:S(2)}) collective-permute-start(f32[256,256]{1,0:T(8,128)S(1)} %get-tuple-element.38), channel_id=1, source_target_pairs={{4,0},{8,4},{12,8},{16,12},{20,16},{24,20},{28,24},{0,28},{5,1},{9... | collective-permute-start | bytes 786440 | tf_op jit(solution)/shard_map/ppermute | solution.py:781
  92.2 1.7 collective-permute-start.6
  94.0 1.3 collective-permute-done.5.refs_2_.refs_6_
  95.3 4.3 %collective-permute-done.3.refs_0_.refs_4_ = f32[256,256]{1,0:T(8,128)S(1)} collective-permute-done((f32[256,256]{1,0:T(8,128)S(1)}, f32[256,256]{1,0:T(8,128)S(1)}, u32[]{:S(2)}, u32[]{:S(2)}) %collective-permute-start.3) | collective-permute-done | bytes 262176 | tf_op jit(solution)/shard_map/ppermute | solution.py:780
  99.6 2.2 %collective-permute-done.4.refs_1_.refs_5_ = f32[256,256]{1,0:T(8,128)S(1)} collective-permute-done((f32[256,256]{1,0:T(8,128)S(1)}, f32[256,256]{1,0:T(8,128)S(1)}, u32[]{:S(2)}, u32[]{:S(2)}) %collective-permute-start.4) | collective-permute-done | bytes 262176 | tf_op jit(solution)/shard_map/ppermute | solution.py:781
  101.8 1.2 copy-done.1
  103.0 1.9 shard_map.128
  105.0 10.6 %all_to_all.40.sums_ref.first_ref = f32[32,8,128]{2,1,0:T(8,128)} all-to-all(f32[32,8,128]{2,1,0:T(8,128)S(1)} %get-tuple-element.41), channel_id=1, replica_groups=mesh['row'=8,'col'=4] {'row','col'}, dimensions={0} | all-to-all | bytes 262144 | tf_op jit(solution)/shard_map/all_to_all | solution.py:767
  115.6 10.0 %shard_map.129 = (f32[32,4,8,128]{3,2,1,0:T(8,128)}, f32[4,16,256,128]{3,2,1,0:T(8,128)}, f32[4,128,256]{2,1,0:T(8,128)}) custom-call(f32[3,16]{1,0:T(4,128)S(1)} %bitcast.2, f32[32,8,128]{2,1,0:T(8,128)} %copy-done.16, f32[32,8,128]{2,1,0:T(8,128)} %all_to_all.40.sums_ref.first_ref, f32[4,128,256]{2,1,0:T(8,128)} %a_.3, ...), custom_call_target="tpu_custom_call" | custom-call | flops 2000000000 | bytes 2621440 | tf_op jit(solution)/shard_map/pallas_call | solution.py:338
  125.6 2.6 %all-to-all-start.4 = ((f32[32,4,8,128]{3,2,1,0:T(8,128)}), f32[32,4,8,128]{3,2,1,0:T(8,128)S(1)}, u32[]{:S(2)}, u32[]{:S(2)}) async-start(f32[32,4,8,128]{3,2,1,0:T(8,128)} %get-tuple-element.43), calls=%async_computation.4 | async-start | bytes 1048576 | tf_op jit(solution)/shard_map/all_to_all | solution.py:767
  128.3 8.2 %shard_map.130.refs_4_._ = f32[4,16,256,128]{3,2,1,0:T(8,128)} custom-call(f32[16,17]{1,0:T(8,128)S(1)} %copy-done.10, f32[4,16,256,128]{3,2,1,0:T(8,128)} %get-tuple-element.44.lifted_ref, f32[4,128,256]{2,1,0:T(8,128)} %a_.3, f32[4,128,256]{2,1,0:T(8,128)} %a_.3), custom_call_target="tpu_custom_call" | custom-call | flops 2500000000 | bytes 8388608 | tf_op jit(solution)/shard_map/pallas_call | solution.py:338
  136.5 7.3 %all-to-all-done.4.recv_ref = f32[32,4,8,128]{3,2,1,0:T(8,128)S(1)} async-done(((f32[32,4,8,128]{3,2,1,0:T(8,128)}), f32[32,4,8,128]{3,2,1,0:T(8,128)S(1)}, u32[]{:S(2)}, u32[]{:S(2)}) %all-to-all-start.4) | async-done | bytes 524320 | tf_op jit(solution)/shard_map/all_to_all | solution.py:767
  143.8 4.8 %shard_map.131.__ = f32[32,4,8,128]{3,2,1,0:T(8,128)} custom-call(f32[32,4,8,128]{3,2,1,0:T(8,128)S(1)} %all-to-all-done.4.recv_ref, f32[4,16,8,128]{3,2,1,0:T(8,128)} %copy-done.8, f32[4,16,8,128]{3,2,1,0:T(8,128)} %copy-done.17, f32[4,16,8,128]{3,2,1,0:T(8,128)} %copy-done.18, f32[4,16,8,128]{3,2,1,0:T(8,128)} %copy-done.19, ...), custom_call_target="tpu_custom_call" | custom-call | bytes 2097152 | tf_op jit(solution)/shard_map/pallas_call | solution.py:338
  148.6 3.2 %all-to-all-start.5 = ((f32[32,4,8,128]{3,2,1,0:T(8,128)}), f32[32,4,8,128]{3,2,1,0:T(8,128)S(1)}, u32[]{:S(2)}, u32[]{:S(2)}) async-start(f32[32,4,8,128]{3,2,1,0:T(8,128)} %shard_map.131.__), calls=%async_computation.5 | async-start | bytes 1048576 | tf_op jit(solution)/shard_map/all_to_all | solution.py:767
  151.8 8.1 %shard_map.132.point_ref = f32[4,16,256,128]{3,2,1,0:T(8,128)} custom-call(f32[16,17]{1,0:T(8,128)S(1)} %copy-done.10, f32[4,16,256,128]{3,2,1,0:T(8,128)} %get-tuple-element.44.lifted_ref, f32[4,16,256,128]{3,2,1,0:T(8,128)} %shard_map.130.refs_4_._, f32[32,4,8,128]{3,2,1,0:T(8,128)} %shard_map.131.__), custom_call_target="tpu_custom_call", output_to_operand_aliasing={{}: (2, {})} | custom-call | flops 2500000000 | bytes 8388608 | tf_op jit(solution)/shard_map/pallas_call | solution.py:338
  159.9 7.2 %all-to-all-done.5.recv_ref = f32[32,4,8,128]{3,2,1,0:T(8,128)S(1)} async-done(((f32[32,4,8,128]{3,2,1,0:T(8,128)}), f32[32,4,8,128]{3,2,1,0:T(8,128)S(1)}, u32[]{:S(2)}, u32[]{:S(2)}) %all-to-all-start.5) | async-done | bytes 524320 | tf_op jit(solution)/shard_map/all_to_all | solution.py:767
  167.2 0.8 copy-done.14
  167.9 10.5 %shard_map.133 = (f32[2,4,128,256]{3,2,1,0:T(8,128)}, f32[32,8,128]{2,1,0:T(8,128)}, f32[128,256]{1,0:T(8,128)S(1)}, f32[128,256]{1,0:T(8,128)S(1)}, f32[4,256]{1,0:T(4,128)S(1)}, /*index=5*/f32[4,256]{1,0:T(4,128)S(1)}) custom-call(f32[17]{0:T(128)S(1)} %copy-done.11, f32[32,8,128]{2,1,0:T(8,128)} %copy-done.16, ...), custom_call_target="tpu_custom_call", output_to_operand_aliasing={{0}: (8, {})} | custom-call | flops 2000000000 | bytes 9961472 | tf_op jit(solution)/shard_map/pallas_call | solution.py:338
  178.4 3.1 %all-to-all-start.6 = ((f32[32,8,128]{2,1,0:T(8,128)}), f32[32,8,128]{2,1,0:T(8,128)S(1)}, u32[]{:S(2)}, u32[]{:S(2)}) async-start(f32[32,8,128]{2,1,0:T(8,128)} %get-tuple-element.45), calls=%async_computation.6 | async-start | bytes 262144 | tf_op jit(solution)/shard_map/all_to_all | solution.py:767
  181.5 1.8 collective-permute-start.7
  183.4 3.0 %collective-permute-start.8 = (f32[128,256]{1,0:T(8,128)S(1)}, f32[128,256]{1,0:T(8,128)S(1)}, u32[]{:S(2)}, u32[]{:S(2)}) collective-permute-start(f32[128,256]{1,0:T(8,128)S(1)} %get-tuple-element.48), channel_id=1, source_target_pairs={{4,0},{8,4},{12,8},{16,12},{20,16},{24,20},{28,24},{0,28},{5,1},{9... | collective-permute-start | bytes 393224 | tf_op jit(solution)/shard_map/ppermute | solution.py:781
  186.3 1.7 collective-permute-start.10
  188.1 1.3 collective-permute-done.9.refs_2_
  189.4 2.8 %collective-permute-done.7.refs_0_ = f32[128,256]{1,0:T(8,128)S(1)} collective-permute-done((f32[128,256]{1,0:T(8,128)S(1)}, f32[128,256]{1,0:T(8,128)S(1)}, u32[]{:S(2)}, u32[]{:S(2)}) %collective-permute-start.7) | collective-permute-done | bytes 131104 | tf_op jit(solution)/shard_map/ppermute | solution.py:780
  192.3 1.2 copy-done.2
  193.6 2.2 %shard_map.134 = (f32[4,128,256]{2,1,0:T(8,128)S(1)}, f32[4,128,256]{2,1,0:T(8,128)S(1)}, f32[32,8,128]{2,1,0:T(8,128)S(1)}) custom-call(f32[32,8,128]{2,1,0:T(8,128)S(1)} %copy-done.6, f32[32,8,128]{2,1,0:T(8,128)S(1)} %all-to-all-done.6.beta_ref, f32[2,4,128,256]{3,2,1,0:T(8,128)S(1)} %copy-done.2, bf16[4,128,256]{2,1,0:T(8,128)(2,1)S(1)} %copy-done.5, ...), custom_call_target="tpu_custom_call" | custom-call | bytes 5767168 | tf_op jit(solution)/shard_map/pallas_call | solution.py:338
  195.7 12.1 %all_to_all.41.sums_ref = f32[32,8,128]{2,1,0:T(8,128)S(1)} all-to-all(f32[32,8,128]{2,1,0:T(8,128)S(1)} %get-tuple-element.52), channel_id=1, replica_groups=mesh['row'=8,'col'=4] {'row','col'}, dimensions={0} | all-to-all | bytes 262144 | tf_op jit(solution)/shard_map/all_to_all | solution.py:767
  207.8 1.2 copy-done.3
  209.1 2.0 shard_map.135
  (43 shorter events, 3.2 us)
Async XLA Ops:
  0.6 34.2 %copy-start.10 = (f32[16,17]{1,0:T(8,128)S(1)}, f32[16,17]{1,0:T(8,128)}, u32[]{:S(2)}) copy-start(f32[16,17]{1,0:T(8,128)} %mix_ref.7) | copy-start | bytes 3268
  2.4 15.5 %all-to-all-start = ((f32[32,8,128]{2,1,0:T(8,128)}), f32[32,8,128]{2,1,0:T(8,128)S(1)}, u32[]{:S(2)}, u32[]{:S(2)}) async-start(f32[32,8,128]{2,1,0:T(8,128)} %shard_map.121), calls=%async_computation | async-start | bytes 262144 | tf_op jit(solution)/shard_map/all_to_all | solution.py:767
  11.4 0.7 copy-start.8
  17.9 0.7 copy-start.16
  18.6 0.7 copy-start.12
  29.0 20.7 %all-to-all-start.1 = ((f32[32,4,8,128]{3,2,1,0:T(8,128)}), f32[32,4,8,128]{3,2,1,0:T(8,128)S(1)}, u32[]{:S(2)}, u32[]{:S(2)}) async-start(f32[32,4,8,128]{3,2,1,0:T(8,128)} %get-tuple-element.31), calls=%async_computation.1 | async-start | bytes 1048576 | tf_op jit(solution)/shard_map/all_to_all | solution.py:767
  31.6 12.6 %collective-permute-start = (f32[4,16,8,128]{3,2,1,0:T(8,128)S(1)}, f32[4,16,8,128]{3,2,1,0:T(8,128)S(1)}, u32[]{:S(2)}, u32[]{:S(2)}) collective-permute-start(f32[4,16,8,128]{3,2,1,0:T(8,128)S(1)} %get-tuple-element.32), channel_id=1, source_target_pairs={{0,1},{1,2},{2,3},{3,0},{4,5},{5,6},{6,7},{7,4},{8,9},{9,10},{10,1... | collective-permute-start | bytes 786440 | tf_op jit(solution)/shard_map/ppermute | solution.py:823
  31.8 13.7 %collective-permute-start.1 = (f32[4,16,8,128]{3,2,1,0:T(8,128)S(1)}, f32[4,16,8,128]{3,2,1,0:T(8,128)S(1)}, u32[]{:S(2)}, u32[]{:S(2)}) collective-permute-start(f32[4,16,8,128]{3,2,1,0:T(8,128)S(1)} %get-tuple-element.33), channel_id=1, source_target_pairs={{0,2},{1,3},{2,0},{3,1},{4,6},{5,7},{6,4},{7,5},{8,10},{9,11},{10,... | collective-permute-start | bytes 786440 | tf_op jit(solution)/shard_map/ppermute | solution.py:823
  33.5 16.2 %collective-permute-start.2 = (f32[4,16,8,128]{3,2,1,0:T(8,128)S(1)}, f32[4,16,8,128]{3,2,1,0:T(8,128)S(1)}, u32[]{:S(2)}, u32[]{:S(2)}) collective-permute-start(f32[4,16,8,128]{3,2,1,0:T(8,128)S(1)} %get-tuple-element.34), channel_id=1, source_target_pairs={{0,3},{1,0},{2,1},{3,2},{4,7},{5,4},{6,5},{7,6},{8,11},{9,8},{10,9... | collective-permute-start | bytes 786440 | tf_op jit(solution)/shard_map/ppermute | solution.py:823
  44.3 5.4 %copy-start.17 = (f32[4,16,8,128]{3,2,1,0:T(8,128)}, f32[4,16,8,128]{3,2,1,0:T(8,128)S(1)}, u32[]{:S(2)}) copy-start(f32[4,16,8,128]{3,2,1,0:T(8,128)S(1)} %collective-permute-done.refs_1_) | copy-start | bytes 786436
  45.5 4.2 %copy-start.18 = (f32[4,16,8,128]{3,2,1,0:T(8,128)}, f32[4,16,8,128]{3,2,1,0:T(8,128)S(1)}, u32[]{:S(2)}) copy-start(f32[4,16,8,128]{3,2,1,0:T(8,128)S(1)} %collective-permute-done.1.refs_2_) | copy-start | bytes 786436
  49.7 0.7 copy-start.19
  55.2 21.2 %all-to-all-start.2 = ((f32[32,4,8,128]{3,2,1,0:T(8,128)}), f32[32,4,8,128]{3,2,1,0:T(8,128)S(1)}, u32[]{:S(2)}, u32[]{:S(2)}) async-start(f32[32,4,8,128]{3,2,1,0:T(8,128)} %shard_map.125.__), calls=%async_computation.2 | async-start | bytes 1048576 | tf_op jit(solution)/shard_map/all_to_all | solution.py:767
  60.9 16.3 %copy-start.11 = (f32[17]{0:T(128)S(1)}, f32[17]{0:T(128)}, u32[]{:S(2)}) copy-start(f32[17]{0:T(128)} %proj_ref.3) | copy-start | bytes 208
  69.0 32.8 %copy-start = (f32[4,128,256]{2,1,0:T(8,128)S(1)}, f32[4,128,256]{2,1,0:T(8,128)}, u32[]{:S(2)}) copy-start(f32[4,128,256]{2,1,0:T(8,128)} %a_.3) | copy-start | bytes 1572868
  69.0 32.8 %copy-start.4 = (bf16[4,128,256]{2,1,0:T(8,128)(2,1)S(1)}, bf16[4,128,256]{2,1,0:T(8,128)(2,1)}, u32[]{:S(2)}) copy-start(bf16[4,128,256]{2,1,0:T(8,128)(2,1)} %perm_ref.9) | copy-start | bytes 786436
  69.0 46.6 %copy-start.13 = (f32[16,3]{0,1:T(4,128)S(1)}, f32[16,3]{0,1:T(4,128)}, u32[]{:S(2)}) copy-start(f32[16,3]{0,1:T(4,128)} %param.12) | copy-start | bytes 580
  76.4 0.8 copy-start.15
  87.5 12.1 %collective-permute-start.3 = (f32[256,256]{1,0:T(8,128)S(1)}, f32[256,256]{1,0:T(8,128)S(1)}, u32[]{:S(2)}, u32[]{:S(2)}) collective-permute-start(f32[256,256]{1,0:T(8,128)S(1)} %get-tuple-element.37), channel_id=1, source_target_pairs={{0,4},{4,8},{8,12},{12,16},{16,20},{20,24},{24,28},{28,0},{1,5},{5... | collective-permute-start | bytes 786440 | tf_op jit(solution)/shard_map/ppermute | solution.py:780
  88.7 13.1 %collective-permute-start.4 = (f32[256,256]{1,0:T(8,128)S(1)}, f32[256,256]{1,0:T(8,128)S(1)}, u32[]{:S(2)}, u32[]{:S(2)}) collective-permute-start(f32[256,256]{1,0:T(8,128)S(1)} %get-tuple-element.38), channel_id=1, source_target_pairs={{4,0},{8,4},{12,8},{16,12},{20,16},{24,20},{28,24},{0,28},{5,1},{9... | collective-permute-start | bytes 786440 | tf_op jit(solution)/shard_map/ppermute | solution.py:781
  92.2 3.1 %collective-permute-start.5 = (f32[8,256]{1,0:T(8,128)S(1)}, f32[8,256]{1,0:T(8,128)S(1)}, u32[]{:S(2)}, u32[]{:S(2)}) collective-permute-start(f32[8,256]{1,0:T(8,128)S(1)} %get-tuple-element.39), channel_id=1, source_target_pairs={{0,1},{1,2},{2,3},{3,0},{4,5},{5,6},{6,7},{7,4},{8,9},{9,10},{10,1... | collective-permute-start | bytes 24584 | tf_op jit(solution)/shard_map/ppermute | solution.py:780
  92.2 3.1 %collective-permute-start.6 = (f32[8,256]{1,0:T(8,128)S(1)}, f32[8,256]{1,0:T(8,128)S(1)}, u32[]{:S(2)}, u32[]{:S(2)}) collective-permute-start(f32[8,256]{1,0:T(8,128)S(1)} %get-tuple-element.40), channel_id=1, source_target_pairs={{1,0},{2,1},{3,2},{0,3},{5,4},{6,5},{7,6},{4,7},{9,8},{10,9},{11,1... | collective-permute-start | bytes 24584 | tf_op jit(solution)/shard_map/ppermute | solution.py:781
  101.8 1.2 copy-start.1
  105.0 31.5 %copy-start.9 = (f32[4,128,256]{2,1,0:T(8,128)}, f32[4,128,256]{2,1,0:T(8,128)S(1)}, u32[]{:S(2)}) copy-start(f32[4,128,256]{2,1,0:T(8,128)S(1)} %get-tuple-element.42.image_ref) | copy-start | bytes 1572868
  125.6 18.2 %all-to-all-start.4 = ((f32[32,4,8,128]{3,2,1,0:T(8,128)}), f32[32,4,8,128]{3,2,1,0:T(8,128)S(1)}, u32[]{:S(2)}, u32[]{:S(2)}) async-start(f32[32,4,8,128]{3,2,1,0:T(8,128)} %get-tuple-element.43), calls=%async_computation.4 | async-start | bytes 1048576 | tf_op jit(solution)/shard_map/all_to_all | solution.py:767
  148.6 18.5 %all-to-all-start.5 = ((f32[32,4,8,128]{3,2,1,0:T(8,128)}), f32[32,4,8,128]{3,2,1,0:T(8,128)S(1)}, u32[]{:S(2)}, u32[]{:S(2)}) async-start(f32[32,4,8,128]{3,2,1,0:T(8,128)} %shard_map.131.__), calls=%async_computation.5 | async-start | bytes 1048576 | tf_op jit(solution)/shard_map/all_to_all | solution.py:767
  159.9 32.4 %copy-start.5 = (bf16[4,128,256]{2,1,0:T(8,128)(2,1)S(1)}, bf16[4,128,256]{2,1,0:T(8,128)(2,1)}, u32[]{:S(2)}) copy-start(bf16[4,128,256]{2,1,0:T(8,128)(2,1)} %perm_ref.9) | copy-start | bytes 786436
  159.9 32.4 %copy-start.6 = (f32[32,8,128]{2,1,0:T(8,128)S(1)}, f32[32,8,128]{2,1,0:T(8,128)}, u32[]{:S(2)}) copy-start(f32[32,8,128]{2,1,0:T(8,128)} %all_to_all.40.sums_ref.first_ref) | copy-start | bytes 393220
  159.9 32.4 %copy-start.7 = (f32[4,128,256]{2,1,0:T(8,128)S(1)}, f32[4,128,256]{2,1,0:T(8,128)}, u32[]{:S(2)}) copy-start(f32[4,128,256]{2,1,0:T(8,128)} %get-tuple-element.51.refs_8_.res_ref) | copy-start | bytes 1572868
  167.2 0.8 copy-start.14
  178.4 13.9 %all-to-all-start.6 = ((f32[32,8,128]{2,1,0:T(8,128)}), f32[32,8,128]{2,1,0:T(8,128)S(1)}, u32[]{:S(2)}, u32[]{:S(2)}) async-start(f32[32,8,128]{2,1,0:T(8,128)} %get-tuple-element.45), calls=%async_computation.6 | async-start | bytes 262144 | tf_op jit(solution)/shard_map/all_to_all | solution.py:767
  181.5 10.6 %collective-permute-start.7 = (f32[128,256]{1,0:T(8,128)S(1)}, f32[128,256]{1,0:T(8,128)S(1)}, u32[]{:S(2)}, u32[]{:S(2)}) collective-permute-start(f32[128,256]{1,0:T(8,128)S(1)} %get-tuple-element.47), channel_id=1, source_target_pairs={{0,4},{4,8},{8,12},{12,16},{16,20},{20,24},{24,28},{28,0},{1,5},{5... | collective-permute-start | bytes 393224 | tf_op jit(solution)/shard_map/ppermute | solution.py:780
  183.4 9.0 %collective-permute-start.8 = (f32[128,256]{1,0:T(8,128)S(1)}, f32[128,256]{1,0:T(8,128)S(1)}, u32[]{:S(2)}, u32[]{:S(2)}) collective-permute-start(f32[128,256]{1,0:T(8,128)S(1)} %get-tuple-element.48), channel_id=1, source_target_pairs={{4,0},{8,4},{12,8},{16,12},{20,16},{24,20},{28,24},{0,28},{5,1},{9... | collective-permute-start | bytes 393224 | tf_op jit(solution)/shard_map/ppermute | solution.py:781
  186.3 3.0 %collective-permute-start.9 = (f32[4,256]{1,0:T(4,128)S(1)}, f32[4,256]{1,0:T(4,128)S(1)}, u32[]{:S(2)}, u32[]{:S(2)}) collective-permute-start(f32[4,256]{1,0:T(4,128)S(1)} %get-tuple-element.49), channel_id=1, source_target_pairs={{0,1},{1,2},{2,3},{3,0},{4,5},{5,6},{6,7},{7,4},{8,9},{9,10},{10,1... | collective-permute-start | bytes 12296 | tf_op jit(solution)/shard_map/ppermute | solution.py:780
  186.3 3.1 %collective-permute-start.10 = (f32[4,256]{1,0:T(4,128)S(1)}, f32[4,256]{1,0:T(4,128)S(1)}, u32[]{:S(2)}, u32[]{:S(2)}) collective-permute-start(f32[4,256]{1,0:T(4,128)S(1)} %get-tuple-element.50), channel_id=1, source_target_pairs={{1,0},{2,1},{3,2},{0,3},{5,4},{6,5},{7,6},{4,7},{9,8},{10,9},{11,1... | collective-permute-start | bytes 12296 | tf_op jit(solution)/shard_map/ppermute | solution.py:781
  192.3 1.2 copy-start.2
  207.8 1.2 copy-start.3

commit v4 on v3

--- a/solution.py
+++ b/solution.py
@@ -1,4 +1,5 @@
 import functools
+import math
 
 import jax
 import jax.numpy as jnp
@@ -285,9 +286,17 @@
     back = []
     for place in range(n_col):
         angle = angles(freqs, place * cols + np.arange(cols), n_col * cols)
-        both = np.concatenate([np.cos(angle), np.sin(angle)], 1)
+        both = np.concatenate([np.cos(angle), np.sin(angle)], 0)
         high, low = split_table(both)
-        forward.append(np.concatenate([high, low], 0))
+        forward.append(
+            np.concatenate(
+                [
+                    np.concatenate([high, high], 1),
+                    np.concatenate([low, np.zeros_like(low)], 1),
+                ],
+                0,
+            )
+        )
         both = np.concatenate([np.cos(angle), np.sin(angle)], 0)
         high, low = split_table(both)
         back.append(
@@ -303,9 +312,12 @@
     return np.stack(forward), np.stack(back)
 
 
-def gelu(value):
-    inner = value * (0.7978845608028654 + 0.035677408136300125 * (value * value))
-    return (0.5 * value) * (1.0 + jnp.tanh(inner))
+GAIN = (math.sqrt(2.0 / math.pi) * 0.044715) ** (1.0 / 3.0)
+LINEAR = math.sqrt(2.0 / math.pi) / GAIN
+
+
+def scaled_gelu(value):
+    return value + value * jnp.tanh(value * (value * value + LINEAR))
 
 
 def call(body, outs, in_specs, out_specs, grid=(), scratch=(), flops=0, moved=0, alias=None, limit=8, near=(), loose=False):
@@ -367,11 +379,18 @@
     return jnp.sum(total[row : row + 1], axis=1, keepdims=True)
 
 
-def squares_body(field_ref, out_ref):
+def squares_body(field_ref, perm_ref, _, out_ref, low_ref, high_ref, left_ref, right_ref):
     total = field_ref[0] * field_ref[0]
     for place in range(1, field_ref.shape[0]):
         total = total + field_ref[place] * field_ref[place]
     spread([lane_sums(total)], out_ref)
+    rows, cols, _ = perm_ref.shape
+    low_ref[...] = perm_ref[0].astype(F32)
+    high_ref[...] = perm_ref[rows - 1].astype(F32)
+    for place in range(rows):
+        plane = perm_ref[place].astype(F32)
+        left_ref[place : place + 1, :] = plane[:1]
+        right_ref[place : place + 1, :] = plane[cols - 1 :]
 
 
 def weight_body(weight_ref, *refs):
@@ -393,7 +412,7 @@
 
 
 def lift_channel(weight_ref, channel, scaled, log_perm):
-    return gelu(
+    return scaled_gelu(
         weight_ref[0, channel] * scaled
         + (weight_ref[1, channel] * log_perm + weight_ref[2, channel])
     )
@@ -412,24 +431,20 @@
         for j in range(2):
             zt_ref[pl.ds(channel + j, half, stride=CHANNELS), :] = part[:, j * cols : (j + 1) * cols]
     groups = half * CHANNELS // LANES
-    waves = zt_ref[...].reshape(groups, 2, LANES // 2, cols)
-    turned = jnp.concatenate([waves[:, 1:], -waves[:, :1]], 1)
-    waves = jnp.concatenate(
-        [waves.reshape(groups * LANES, cols), turned.reshape(groups * LANES, cols)], 1
-    )
-    high, low = split(waves)
-    table = col_ref[lax.axis_index("col")]
-    part = matmul_nt(table, high)
-    part = part[:KY] + part[KY:] + matmul_nt(table[:KY], low)
+    part = matmul_nt(col_ref[lax.axis_index("col")], jnp.concatenate(split(zt_ref[...]), 1))
+    part = part[: 2 * KY] + part[2 * KY :]
+    lane = lax.broadcasted_iota(jnp.int32, (KY, LANES), 1)
+    sign = jnp.where(lane < LANES // 2, 1.0, -1.0).astype(F32)
     n_col = KY // SUBLANES
     for row in range(groups):
+        lanes = slice(row * LANES, (row + 1) * LANES)
+        block = part[:KY, lanes] + pltpu.roll(part[KY:, lanes], LANES // 2, 1) * sign
         for col in range(n_col):
-            spectra_ref[row * n_col + col, 0] = part[
-                col * SUBLANES : (col + 1) * SUBLANES, row * LANES : (row + 1) * LANES
-            ]
-
-
-def lift_first_body(cells, lift_ref, sums_ref, res_ref, perm_ref, deep_ref, col_ref, _, spectra_ref, lifted_ref, zt_ref):
+            spectra_ref[row * n_col + col, 0] = block[col * SUBLANES : (col + 1) * SUBLANES]
+
+
+def lift_first_body(cells, lift_ref, sums_ref, res_ref, perm_ref, deep_ref, col_ref, *refs):
+    spectra_ref, lifted_ref, zt_ref = refs[-3:]
     scale = scale_of(gathered(sums_ref, 0), cells)
     scaled = (res_ref[0] / scale).T
     log_perm = jnp.log(perm_ref[0].astype(F32)).T
@@ -558,7 +573,7 @@
         )
         field_ref[freq] = total
         turned_ref[freq] = -turn(total)
-    gain = 1.0 / cells
+    gain = 0.5 / cells
     evens = [field_ref[half] * gain]
     odds = [None]
     for freq in range(1, half):
@@ -607,37 +622,34 @@
         high, middle, low = (part.astype(BF16) for part in split_three(waves))
         spatial = matmul(deep_ref[...], jnp.concatenate([high, middle, low, high], 0))
         for j in range(2):
-            hidden = gelu(spatial[:, j * cols : (j + 1) * cols] + point_ref[0, out + j])
+            hidden = scaled_gelu(spatial[:, j * cols : (j + 1) * cols] + point_ref[0, out + j])
             term = proj_ref[out + j] * hidden
             total = term if total is None else total + term
     return (scale * (total + proj_ref[CHANNELS])).T
 
 
-def put_edges(update, low_ref, high_ref, left_ref, right_ref, first=0):
+def put_edges(update, low_ref, high_ref, left_ref, right_ref):
     step = pl.program_id(0)
-    cols = update.shape[0]
-    line = pl.ds(step + first * pl.num_programs(0), 1)
-    left_ref[line, :] = update[:1]
-    right_ref[line, :] = update[cols - 1 :]
+    left_ref[pl.ds(step, 1), :] = update[:1]
+    right_ref[pl.ds(step, 1), :] = update[update.shape[0] - 1 :]
 
     @pl.when(step == 0)
     def _():
-        low_ref[first * cols : (first + 1) * cols] = update
+        low_ref[...] = update
 
     @pl.when(step == pl.num_programs(0) - 1)
     def _():
-        high_ref[first * cols : (first + 1) * cols] = update
-
-
-def back_first_body(cells, proj_ref, sums_ref, recv_ref, point_ref, col_ref, deep_ref, perm_ref, kept_ref, *refs):
-    *edges, wave_ref = refs
+        high_ref[...] = update
+
+
+def back_first_body(cells, proj_ref, sums_ref, recv_ref, point_ref, col_ref, deep_ref, *refs):
+    kept_ref, *edges, wave_ref = refs[4:]
     scale = scale_of(gathered(sums_ref, 0), cells)
     update = back_transform(
         recv_ref, point_ref, proj_ref, col_ref, deep_ref, wave_ref, scale
     )
     kept_ref[0, 0] = update
     put_edges(update, *edges)
-    put_edges(perm_ref[0].astype(F32), *edges, first=1)
 
 
 def back_next_body(cells, proj_ref, first_ref, sums_ref, recv_ref, point_ref, col_ref, deep_ref, image_ref, _, kept_ref, out_ref, *refs):
@@ -707,13 +719,11 @@
         spread([acc_ref[j : j + 1] for j in range(len(terms))], out_ref)
 
 
-def around(ref, index, halo, part):
+def around(ref, index, halo):
     low_ref, high_ref, left_ref, right_ref = halo
     step = pl.program_id(0)
     last = pl.num_programs(0) - 1
-    cols = ref.shape[-2]
-    planes = slice(part * cols, (part + 1) * cols)
-    line = pl.ds(step + part * pl.num_programs(0), 1)
+    line = pl.ds(step, 1)
 
     def plane(place):
         return ref[index + (place,)].astype(F32)
@@ -721,8 +731,8 @@
     def outside(axis, edge, value):
         return jnp.where(lax.axis_index(axis) == edge, 0.0, value)
 
-    low = outside("row", 0, low_ref[planes])
-    high = outside("row", lax.axis_size("row") - 1, high_ref[planes])
+    low = outside("row", 0, low_ref[...])
+    high = outside("row", lax.axis_size("row") - 1, high_ref[...])
     left = outside("col", 0, left_ref[line, :])
     right = outside("col", lax.axis_size("col") - 1, right_ref[line, :])
     before = jnp.where(step == 0, low, plane(jnp.maximum(step - 1, 0)))
@@ -731,10 +741,10 @@
 
 
 def operator_first_body(kept_ref, perm_ref, *refs):
-    halo = refs[:4]
-    res_ref, image_ref, out_ref, acc_ref = refs[4:]
-    fields = around(kept_ref, (0,), halo, 0)
-    image = stencil(fields, around(perm_ref, (), halo, 1))
+    halo, perm_halo = refs[:4], refs[4:8]
+    res_ref, image_ref, out_ref, acc_ref = refs[8:]
+    fields = around(kept_ref, (0,), halo)
+    image = stencil(fields, around(perm_ref, (), perm_halo))
     own = fields[0]
     residual = res_ref[0]
     image_ref[0] = image
@@ -742,14 +752,14 @@
 
 
 def operator_next_body(first_ref, beta_ref, kept_ref, perm_ref, *refs):
-    halo, old = refs[:4], refs[4:8]
-    res_ref, way_ref, image_ref, out_ref, acc_ref = refs[8:]
+    halo, old, perm_halo = refs[:4], refs[4:8], refs[8:12]
+    res_ref, way_ref, image_ref, out_ref, acc_ref = refs[12:]
     beta = gathered(beta_ref, 0) / gathered(first_ref, 0)
     fields = [
         new - beta * other
-        for new, other in zip(around(kept_ref, (1,), halo, 0), around(kept_ref, (0,), old, 0))
+        for new, other in zip(around(kept_ref, (1,), halo), around(kept_ref, (0,), old))
     ]
-    image = stencil(fields, around(perm_ref, (), old, 1))
+    image = stencil(fields, around(perm_ref, (), perm_halo))
     own = fields[0]
     way_ref[0] = own
     image_ref[0] = image
@@ -791,7 +801,9 @@
     freq = KX // n_col
     deep_forward, deep_back = (jnp.asarray(t) for t in deep_tables(n_row, depth))
     col_forward, col_back = (jnp.asarray(t) for t in column_tables(n_col, cols))
-    lift_weight = lift_weight.T
+    lift_weight = GAIN * lift_weight.T
+    mix_weight = jnp.where(jnp.arange(CHANNELS + 1) < CHANNELS, 0.5, GAIN) * mix_weight
+    proj_weight = jnp.where(jnp.arange(CHANNELS + 1) < CHANNELS, 0.5 / GAIN, 1.0) * proj_weight
     field = shape(rows, cols, depth)
     field_bytes = 4 * rows * cols * depth
     partial = shape(count, SUBLANES, LANES)
@@ -800,15 +812,13 @@
     spectra_bytes = 4 * count * rows * SUBLANES * LANES
     smem = whole(pltpu.SMEM)
     vmem = whole()
+    anywhere = whole(pl.ANY)
     plane = pl.BlockSpec((1, cols, depth), lambda i: (i, 0, 0))
     spectra_block = pl.BlockSpec((count, 1, SUBLANES, LANES), lambda i: (0, i, 0, 0))
     point_block = pl.BlockSpec((1, CHANNELS, depth, cols), lambda i: (i, 0, 0, 0))
     kept_shape = shape(ITERS, rows, cols, depth)
     lift_flops = 2.0e9
     back_flops = 2.0e9
-
-    squares = call(squares_body, partial, [vmem], vmem, moved=field_bytes)(right_side)
-    squares = add_up(squares)
 
     weight_shape = (freq, CHANNELS, SUBLANES, LANES)
     own, *weights = call(
@@ -824,11 +834,17 @@
         for shift, part in enumerate(weights)
     ]
     edge_shapes = (shape(cols, depth),) * 2 + (shape(rows, depth),) * 2
-    both_shapes = (shape(2 * cols, depth),) * 2 + (shape(2 * rows, depth),) * 2
+    squares, *perm_edges = call(
+        squares_body,
+        (partial,) + edge_shapes,
+        [vmem, vmem, anywhere],
+        (vmem,) * 5,
+        moved=2 * field_bytes,
+    )(right_side, permeability, own)
+    squares = add_up(squares)
+    perm_halo = neighbours(*perm_edges)
     acc_scratch = pltpu.VMEM((SUBLANES, LANES), F32)
     zt_scratch = pltpu.VMEM((2 * KZ * CHANNELS, cols), F32)
-
-    anywhere = whole(pl.ANY)
 
     def points(lifted, part, before, after):
         first = part * rows // 2
@@ -876,38 +892,39 @@
     blocks, lifted = call(
         functools.partial(lift_first_body, cells),
         (spectra, channels),
-        [smem, vmem, plane, plane, vmem, vmem, anywhere],
+        [smem, vmem, plane, plane, vmem, vmem] + [anywhere] * n_col,
         (spectra_block, point_block),
         limit=16,
         grid=(rows,),
         scratch=[zt_scratch],
         flops=lift_flops,
         moved=2 * field_bytes + spectra_bytes,
-    )(lift_weight, squares, right_side, permeability, deep_forward, col_forward, weights[0])
+    )(lift_weight, squares, right_side, permeability, deep_forward, col_forward, *weights)
     received, point = mixed_modes(blocks, lifted)
     kept, *edges = call(
         functools.partial(back_first_body, cells),
-        (kept_shape,) + both_shapes,
-        [smem, vmem, spectra_block, point_block, vmem, vmem, plane],
+        (kept_shape,) + edge_shapes,
+        [smem, vmem, spectra_block, point_block, vmem, vmem] + [anywhere] * 4,
         (pl.BlockSpec((1, 1, cols, depth), lambda i: (0, i, 0, 0)),) + (vmem,) * 4,
         grid=(rows,),
         scratch=[zt_scratch],
         limit=12,
         flops=back_flops,
         moved=18 * field_bytes,
-    )(proj_weight, squares, received, point, col_back, deep_back, permeability)
+    )(proj_weight, squares, received, point, col_back, deep_back, *perm_halo)
 
     old_halo = neighbours(*edges)
-    args = (kept, permeability, *old_halo, right_side)
+    kept_first = pl.BlockSpec((1, rows, cols, depth), lambda i: (0, 0, 0, 0))
+    args = (kept, permeability, *old_halo, *perm_halo, right_side)
     image, sums = call(
         operator_first_body,
         (field, partial),
-        [vmem] * 6 + [plane],
+        [kept_first] + [vmem] * 9 + [plane],
         (plane, vmem),
         grid=(rows,),
         scratch=[acc_scratch],
         moved=9 * field_bytes,
-        near=range(7),
+        near=range(1, 11),
         loose=True,
     )(*args)
     sums = add_up(sums)
@@ -940,15 +957,15 @@
 
     beta = add_up(beta)
     halo = neighbours(*edges)
-    args = (sums, beta, kept, permeability, *halo, *old_halo, residual)
+    args = (sums, beta, kept, permeability, *halo, *old_halo, *perm_halo, residual)
     way, image, later = call(
         operator_next_body,
         (field, field, partial),
-        [vmem] * 12 + [plane],
+        [vmem] * 16 + [plane],
         (plane, plane, vmem),
         grid=(rows,),
         scratch=[acc_scratch],
-        near=range(13),
+        near=(0, 1) + tuple(range(3, 17)),
         loose=True,
         moved=11 * field_bytes,
     )(*args)
@@ -960,7 +977,7 @@
         (plane, plane),
         grid=(rows,),
         moved=6 * field_bytes,
-        near=range(6),
+        near=(0, 1, 3, 4, 5),
         loose=True,
     )(sums, later, kept, way, residual, image)
     return (answer, residual, kept)

time: 212 us -> 212 us (level)
  waiting for transfers between devices: 46.6 us -> 39.5 us
  starting transfers between devices: 40.6 us -> 44.3 us
  blocking collectives: 22.7 us -> 25.2 us
    ppermute x3, waiting for transfers between devices: 6.64 us -> 0.01 us  [tiled_local(): lax.ppermute(part, 'col', [(i, (i + shift + 1) % n_col) for i in range(n_...]
    ppermute x4 -> x6, starting transfers between devices: 9.92 us -> 14.7 us  [neighbours(): found.append(lax.ppermute(first, axis, backward))]
    all_to_all x6, starting transfers between devices: 24.4 us -> 20.3 us  [exchange(): return lax.all_to_all(blocks, BOTH, split_axis=0, concat_axis=0, tiled=True)]
    all_to_all x6, waiting for transfers between devices: 27.8 us -> 30.8 us  [exchange(): return lax.all_to_all(blocks, BOTH, split_axis=0, concat_axis=0, tiled=True)]
    all_to_all x2, blocking collectives: 22.7 us -> 25.2 us  [exchange(): return lax.all_to_all(blocks, BOTH, split_axis=0, concat_axis=0, tiled=True)]
    ppermute x4 -> x6, waiting for transfers between devices: 9.65 us -> 7.8 us  [neighbours(): found.append(lax.ppermute(last, axis, forward))]
    ppermute x4 -> x6, starting transfers between devices: 3.07 us -> 4.82 us  [neighbours(): found.append(lax.ppermute(last, axis, forward))]
    unnamed x40 -> x54, local copies, waits for them, and re-layouts: 8.04 us -> 7.03 us
  transfers between devices with their start and end apart: 17 -> 21, of which waited for: 13 -> 12; matrix products, arithmetic and copies ran while one was open for 0% -> 0% of each run, Pallas kernels for 16% -> 16%
where the time goes in v4:
time: 212 us; the launch traced here: 211 us
  Pallas kernels  93.3 us (44%)
  starting transfers between devices  44.3 us (21%)
  waiting for transfers between devices  39.5 us (19%)
  blocking collectives  25.2 us (12%)
  local copies, waits for them, and re-layouts  7.03 us (3%)
    pallas_call x15, Pallas kernels, wrapped(): found = run(*held)  93.3 us
    all_to_all x6, waiting for transfers between devices, exchange(): return lax.all_to_all(blocks, BOTH, split_axis=0, concat_axis=0, tiled=True)  30.8 us
    all_to_all x2, blocking collectives, exchange(): return lax.all_to_all(blocks, BOTH, split_axis=0, concat_axis=0, tiled=True)  25.2 us
    all_to_all x6, starting transfers between devices, exchange(): return lax.all_to_all(blocks, BOTH, split_axis=0, concat_axis=0, tiled=True)  20.3 us
    ppermute x6, starting transfers between devices, neighbours(): found.append(lax.ppermute(first, axis, backward))  14.7 us
    ppermute x6, waiting for transfers between devices, neighbours(): found.append(lax.ppermute(last, axis, forward))  7.8 us
    unnamed x54, local copies, waits for them, and re-layouts  7.03 us
    ppermute x6, starting transfers between devices, neighbours(): found.append(lax.ppermute(last, axis, forward))  4.82 us
  transfers between devices with their start and end apart: 21, of which 12 were waited for; matrix products, arithmetic and copies ran while one was open for 0% of the time, Pallas kernels for 16%

profile of v4, /device:TPU:0, one launch (start us, length us, event | category | flops | bytes accessed | tf_op | source)
XLA Modules:
  0.0 210.9 jit_solution(1180962641313444127)
XLA Ops:
  0.6 1.7 shard_map.121
  2.3 0.7 copy-done.1
  3.5 2.6 %collective-permute-start.1 = (f32[4,16,8,128]{3,2,1,0:T(8,128)S(1)}, f32[4,16,8,128]{3,2,1,0:T(8,128)S(1)}, u32[]{:S(2)}, u32[]{:S(2)}) collective-permute-start(f32[4,16,8,128]{3,2,1,0:T(8,128)S(1)} %get-tuple-element.38), channel_id=1, source_target_pairs={{0,2},{1,3},{2,0},{3,1},{4,6},{5,7},{6,4},{7,5},{8,10},{9,11},{10,... | collective-permute-start | bytes 786440 | tf_op jit(solution)/shard_map/ppermute | solution.py:833
  6.0 1.4 collective-permute-start.2
  7.5 1.8 shard_map.122
  9.3 4.9 %all-to-all-start = ((f32[32,8,128]{2,1,0:T(8,128)}), f32[32,8,128]{2,1,0:T(8,128)S(1)}, u32[]{:S(2)}, u32[]{:S(2)}) async-start(f32[32,8,128]{2,1,0:T(8,128)} %get-tuple-element.36), calls=%async_computation | async-start | bytes 262144 | tf_op jit(solution)/shard_map/all_to_all | solution.py:777
  14.9 7.5 %all-to-all-done.sums_ref.first_ref = f32[32,8,128]{2,1,0:T(8,128)S(1)} async-done(((f32[32,8,128]{2,1,0:T(8,128)}), f32[32,8,128]{2,1,0:T(8,128)S(1)}, u32[]{:S(2)}, u32[]{:S(2)}) %all-to-all-start) | async-done | bytes 131104 | tf_op jit(solution)/shard_map/all_to_all | solution.py:777
  24.0 9.1 %shard_map.123 = (f32[32,4,8,128]{3,2,1,0:T(8,128)}, f32[4,16,256,128]{3,2,1,0:T(8,128)}) custom-call(f32[3,16]{1,0:T(4,128)S(1)} %multiply_bitcast_fusion.lift_ref, f32[32,8,128]{2,1,0:T(8,128)} %copy-done.21, f32[4,128,256]{2,1,0:T(8,128)} %a_.3, bf16[4,128,256]{2,1,0:T(8,128)(2,1)} %perm_ref.9, bf16[128,256]{1,0:T(8,128)(2,1)} %constant.8.clone.deep_ref, ...), custom_call_target="tpu_custom_call" | custom-call | flops 2000000000 | bytes 1572864 | tf_op jit(solution)/shard_map/pallas_call | solution.py:350
  33.1 3.5 %all-to-all-start.1 = ((f32[32,4,8,128]{3,2,1,0:T(8,128)}), f32[32,4,8,128]{3,2,1,0:T(8,128)S(1)}, u32[]{:S(2)}, u32[]{:S(2)}) async-start(f32[32,4,8,128]{3,2,1,0:T(8,128)} %get-tuple-element.40), calls=%async_computation.1 | async-start | bytes 1048576 | tf_op jit(solution)/shard_map/all_to_all | solution.py:777
  36.6 8.2 %shard_map.124.refs_4_._ = f32[4,16,256,128]{3,2,1,0:T(8,128)} custom-call(f32[16,17]{1,0:T(8,128)S(1)} %broadcast_multiply_fusion.mix_ref, f32[4,16,256,128]{3,2,1,0:T(8,128)} %get-tuple-element.41.lifted_ref, f32[4,128,256]{2,1,0:T(8,128)} %a_.3, f32[4,128,256]{2,1,0:T(8,128)} %a_.3), custom_call_target="tpu_custom_call" | custom-call | flops 2500000000 | bytes 8388608 | tf_op jit(solution)/shard_map/pallas_call | solution.py:350
  44.8 7.3 %all-to-all-done.1.recv_ref = f32[32,4,8,128]{3,2,1,0:T(8,128)S(1)} async-done(((f32[32,4,8,128]{3,2,1,0:T(8,128)}), f32[32,4,8,128]{3,2,1,0:T(8,128)S(1)}, u32[]{:S(2)}, u32[]{:S(2)}) %all-to-all-start.1) | async-done | bytes 524320 | tf_op jit(solution)/shard_map/all_to_all | solution.py:777
  52.1 4.8 %shard_map.125.__ = f32[32,4,8,128]{3,2,1,0:T(8,128)} custom-call(f32[32,4,8,128]{3,2,1,0:T(8,128)S(1)} %all-to-all-done.1.recv_ref, f32[4,16,8,128]{3,2,1,0:T(8,128)} %copy-done.1, f32[4,16,8,128]{3,2,1,0:T(8,128)} %copy-done.22, f32[4,16,8,128]{3,2,1,0:T(8,128)} %copy-done.23, f32[4,16,8,128]{3,2,1,0:T(8,128)} %copy-done.24, ...), custom_call_target="tpu_custom_call" | custom-call | bytes 2097152 | tf_op jit(solution)/shard_map/pallas_call | solution.py:350
  56.9 3.1 %all-to-all-start.2 = ((f32[32,4,8,128]{3,2,1,0:T(8,128)}), f32[32,4,8,128]{3,2,1,0:T(8,128)S(1)}, u32[]{:S(2)}, u32[]{:S(2)}) async-start(f32[32,4,8,128]{3,2,1,0:T(8,128)} %shard_map.125.__), calls=%async_computation.2 | async-start | bytes 1048576 | tf_op jit(solution)/shard_map/all_to_all | solution.py:777
  60.3 1.5 collective-permute-start.6
  61.8 1.8 collective-permute-start.3
  63.5 3.0 %collective-permute-start.4 = (f32[128,256]{1,0:T(8,128)S(1)}, f32[128,256]{1,0:T(8,128)S(1)}, u32[]{:S(2)}, u32[]{:S(2)}) collective-permute-start(f32[128,256]{1,0:T(8,128)S(1)} %get-tuple-element.43), channel_id=1, source_target_pairs={{4,0},{8,4},{12,8},{16,12},{20,16},{24,20},{28,24},{0,28},{5,1},{9... | collective-permute-start | bytes 393224 | tf_op jit(solution)/shard_map/ppermute | solution.py:791
  66.5 8.1 %shard_map.126.point_ref = f32[4,16,256,128]{3,2,1,0:T(8,128)} custom-call(f32[16,17]{1,0:T(8,128)S(1)} %broadcast_multiply_fusion.mix_ref, f32[4,16,256,128]{3,2,1,0:T(8,128)} %get-tuple-element.41.lifted_ref, f32[4,16,256,128]{3,2,1,0:T(8,128)} %shard_map.124.refs_4_._, f32[32,4,8,128]{3,2,1,0:T(8,128)} %shard_map.125.__), custom_call_target="tpu_custom_call", output_to_operand_aliasing={{}: (2, {})} | custom-call | flops 2500000000 | bytes 8388608 | tf_op jit(solution)/shard_map/pallas_call | solution.py:350
  74.7 2.2 %collective-permute-done.3.refs_0_.refs_4_.refs_8_ = f32[128,256]{1,0:T(8,128)S(1)} collective-permute-done((f32[128,256]{1,0:T(8,128)S(1)}, f32[128,256]{1,0:T(8,128)S(1)}, u32[]{:S(2)}, u32[]{:S(2)}) %collective-permute-start.3) | collective-permute-done | bytes 131104 | tf_op jit(solution)/shard_map/ppermute | solution.py:790
  76.9 1.5 all-to-all-done.2.recv_ref
  78.4 0.8 copy-done.19
  79.1 9.0 %shard_map.127 = (f32[2,4,128,256]{3,2,1,0:T(8,128)}, f32[128,256]{1,0:T(8,128)S(1)}, f32[128,256]{1,0:T(8,128)S(1)}, f32[4,256]{1,0:T(4,128)S(1)}, f32[4,256]{1,0:T(4,128)S(1)}) custom-call(f32[17]{0:T(128)S(1)} %fusion.proj_ref, f32[32,8,128]{2,1,0:T(8,128)} %copy-done.21, f32[32,4,8,128]{3,2,1,0:T(8,128)} %copy-done.19, ...), custom_call_target="tpu_custom_call" | custom-call | flops 2000000000 | bytes 9437184 | tf_op jit(solution)/shard_map/pallas_call | solution.py:350
  88.2 0.9 collective-permute-start.7
  89.1 3.8 %collective-permute-start.8 = (f32[128,256]{1,0:T(8,128)S(1)}, f32[128,256]{1,0:T(8,128)S(1)}, u32[]{:S(2)}, u32[]{:S(2)}) collective-permute-start(f32[128,256]{1,0:T(8,128)S(1)} %get-tuple-element.48), channel_id=1, source_target_pairs={{4,0},{8,4},{12,8},{16,12},{20,16},{24,20},{28,24},{0,28},{5,1},{9... | collective-permute-start | bytes 393224 | tf_op jit(solution)/shard_map/ppermute | solution.py:791
  92.9 1.7 collective-permute-start.10
  94.7 1.3 collective-permute-done.9.refs_2_.refs_6_
  96.9 0.9 copy-done.7
  97.8 0.9 copy-done.10
  100.1 3.0 %shard_map.128 = (f32[4,128,256]{2,1,0:T(8,128)S(1)}, f32[32,8,128]{2,1,0:T(8,128)S(1)}) custom-call(f32[2,4,128,256]{3,2,1,0:T(8,128)} %get-tuple-element.46.kept_ref._, bf16[4,128,256]{2,1,0:T(8,128)(2,1)S(1)} %copy-done.2, f32[128,256]{1,0:T(8,128)S(1)} %collective-permute-done.7.refs_0_.refs_4_, f32[128,256]{1,0:T(8,128)S(1)} %collective-permute-done.8.refs_1_.refs_5_, ...), custom_call_target="tpu_custom_call" | custom-call | bytes 4718592 | tf_op jit(solution)/shard_map/pallas_call | solution.py:350
  103.1 13.1 %all_to_all.40.sums_ref.first_ref = f32[32,8,128]{2,1,0:T(8,128)} all-to-all(f32[32,8,128]{2,1,0:T(8,128)S(1)} %get-tuple-element.51), channel_id=1, replica_groups=mesh['row'=8,'col'=4] {'row','col'}, dimensions={0} | all-to-all | bytes 262144 | tf_op jit(solution)/shard_map/all_to_all | solution.py:777
  116.2 9.4 %shard_map.129 = (f32[32,4,8,128]{3,2,1,0:T(8,128)}, f32[4,16,256,128]{3,2,1,0:T(8,128)}, f32[4,128,256]{2,1,0:T(8,128)}) custom-call(f32[3,16]{1,0:T(4,128)S(1)} %multiply_bitcast_fusion.lift_ref, f32[32,8,128]{2,1,0:T(8,128)} %copy-done.21, f32[32,8,128]{2,1,0:T(8,128)} %all_to_all.40.sums_ref.first_ref, f32[4,128,256]{2,1,0:T(8,128)} %a_.3, ...), custom_call_target="tpu_custom_call" | custom-call | flops 2000000000 | bytes 2621440 | tf_op jit(solution)/shard_map/pallas_call | solution.py:350
  125.6 2.6 %all-to-all-start.4 = ((f32[32,4,8,128]{3,2,1,0:T(8,128)}), f32[32,4,8,128]{3,2,1,0:T(8,128)S(1)}, u32[]{:S(2)}, u32[]{:S(2)}) async-start(f32[32,4,8,128]{3,2,1,0:T(8,128)} %get-tuple-element.53), calls=%async_computation.4 | async-start | bytes 1048576 | tf_op jit(solution)/shard_map/all_to_all | solution.py:777
  128.2 8.2 %shard_map.130.refs_4_._ = f32[4,16,256,128]{3,2,1,0:T(8,128)} custom-call(f32[16,17]{1,0:T(8,128)S(1)} %broadcast_multiply_fusion.mix_ref, f32[4,16,256,128]{3,2,1,0:T(8,128)} %get-tuple-element.54.lifted_ref, f32[4,128,256]{2,1,0:T(8,128)} %a_.3, f32[4,128,256]{2,1,0:T(8,128)} %a_.3), custom_call_target="tpu_custom_call" | custom-call | flops 2500000000 | bytes 8388608 | tf_op jit(solution)/shard_map/pallas_call | solution.py:350
  136.5 7.3 %all-to-all-done.4.recv_ref = f32[32,4,8,128]{3,2,1,0:T(8,128)S(1)} async-done(((f32[32,4,8,128]{3,2,1,0:T(8,128)}), f32[32,4,8,128]{3,2,1,0:T(8,128)S(1)}, u32[]{:S(2)}, u32[]{:S(2)}) %all-to-all-start.4) | async-done | bytes 524320 | tf_op jit(solution)/shard_map/all_to_all | solution.py:777
  143.8 4.8 %shard_map.131.__ = f32[32,4,8,128]{3,2,1,0:T(8,128)} custom-call(f32[32,4,8,128]{3,2,1,0:T(8,128)S(1)} %all-to-all-done.4.recv_ref, f32[4,16,8,128]{3,2,1,0:T(8,128)} %copy-done.1, f32[4,16,8,128]{3,2,1,0:T(8,128)} %copy-done.22, f32[4,16,8,128]{3,2,1,0:T(8,128)} %copy-done.23, f32[4,16,8,128]{3,2,1,0:T(8,128)} %copy-done.24, ...), custom_call_target="tpu_custom_call" | custom-call | bytes 2097152 | tf_op jit(solution)/shard_map/pallas_call | solution.py:350
  148.6 3.2 %all-to-all-start.5 = ((f32[32,4,8,128]{3,2,1,0:T(8,128)}), f32[32,4,8,128]{3,2,1,0:T(8,128)S(1)}, u32[]{:S(2)}, u32[]{:S(2)}) async-start(f32[32,4,8,128]{3,2,1,0:T(8,128)} %shard_map.131.__), calls=%async_computation.5 | async-start | bytes 1048576 | tf_op jit(solution)/shard_map/all_to_all | solution.py:777
  151.7 8.1 %shard_map.132.point_ref = f32[4,16,256,128]{3,2,1,0:T(8,128)} custom-call(f32[16,17]{1,0:T(8,128)S(1)} %broadcast_multiply_fusion.mix_ref, f32[4,16,256,128]{3,2,1,0:T(8,128)} %get-tuple-element.54.lifted_ref, f32[4,16,256,128]{3,2,1,0:T(8,128)} %shard_map.130.refs_4_._, f32[32,4,8,128]{3,2,1,0:T(8,128)} %shard_map.131.__), custom_call_target="tpu_custom_call", output_to_operand_aliasing={{}: (2, {})} | custom-call | flops 2500000000 | bytes 8388608 | tf_op jit(solution)/shard_map/pallas_call | solution.py:350
  159.9 7.2 %all-to-all-done.5.recv_ref = f32[32,4,8,128]{3,2,1,0:T(8,128)S(1)} async-done(((f32[32,4,8,128]{3,2,1,0:T(8,128)}), f32[32,4,8,128]{3,2,1,0:T(8,128)S(1)}, u32[]{:S(2)}, u32[]{:S(2)}) %all-to-all-start.5) | async-done | bytes 524320 | tf_op jit(solution)/shard_map/all_to_all | solution.py:777
  167.1 0.8 copy-done.20
  167.9 9.9 %shard_map.133 = (f32[2,4,128,256]{3,2,1,0:T(8,128)}, f32[32,8,128]{2,1,0:T(8,128)}, f32[128,256]{1,0:T(8,128)S(1)}, f32[128,256]{1,0:T(8,128)S(1)}, f32[4,256]{1,0:T(4,128)S(1)}, /*index=5*/f32[4,256]{1,0:T(4,128)S(1)}) custom-call(f32[17]{0:T(128)S(1)} %fusion.proj_ref, f32[32,8,128]{2,1,0:T(8,128)} %copy-done.21, ...), custom_call_target="tpu_custom_call", output_to_operand_aliasing={{0}: (8, {})} | custom-call | flops 2000000000 | bytes 9961472 | tf_op jit(solution)/shard_map/pallas_call | solution.py:350
  177.9 3.1 %all-to-all-start.6 = ((f32[32,8,128]{2,1,0:T(8,128)}), f32[32,8,128]{2,1,0:T(8,128)S(1)}, u32[]{:S(2)}, u32[]{:S(2)}) async-start(f32[32,8,128]{2,1,0:T(8,128)} %get-tuple-element.55), calls=%async_computation.6 | async-start | bytes 262144 | tf_op jit(solution)/shard_map/all_to_all | solution.py:777
  180.9 1.8 collective-permute-start.11
  182.8 3.0 %collective-permute-start.12 = (f32[128,256]{1,0:T(8,128)S(1)}, f32[128,256]{1,0:T(8,128)S(1)}, u32[]{:S(2)}, u32[]{:S(2)}) collective-permute-start(f32[128,256]{1,0:T(8,128)S(1)} %get-tuple-element.58), channel_id=1, source_target_pairs={{4,0},{8,4},{12,8},{16,12},{20,16},{24,20},{28,24},{0,28},{5,1},{9... | collective-permute-start | bytes 393224 | tf_op jit(solution)/shard_map/ppermute | solution.py:791
  185.7 1.7 collective-permute-start.14
  187.5 1.3 collective-permute-done.13.refs_2_
  188.8 2.8 %collective-permute-done.11.refs_0_ = f32[128,256]{1,0:T(8,128)S(1)} collective-permute-done((f32[128,256]{1,0:T(8,128)S(1)}, f32[128,256]{1,0:T(8,128)S(1)}, u32[]{:S(2)}, u32[]{:S(2)}) %collective-permute-start.11) | collective-permute-done | bytes 131104 | tf_op jit(solution)/shard_map/ppermute | solution.py:790
  191.8 3.4 %shard_map.134 = (f32[4,128,256]{2,1,0:T(8,128)S(1)}, f32[4,128,256]{2,1,0:T(8,128)S(1)}, f32[32,8,128]{2,1,0:T(8,128)S(1)}) custom-call(f32[32,8,128]{2,1,0:T(8,128)S(1)} %copy-done.4, f32[32,8,128]{2,1,0:T(8,128)S(1)} %all-to-all-done.6.beta_ref, f32[2,4,128,256]{3,2,1,0:T(8,128)} %get-tuple-element.34.kept_ref.old_ref, ...), custom_call_target="tpu_custom_call" | custom-call | bytes 5767168 | tf_op jit(solution)/shard_map/pallas_call | solution.py:350
  195.2 12.1 %all_to_all.41.sums_ref = f32[32,8,128]{2,1,0:T(8,128)S(1)} all-to-all(f32[32,8,128]{2,1,0:T(8,128)S(1)} %get-tuple-element.62), channel_id=1, replica_groups=mesh['row'=8,'col'=4] {'row','col'}, dimensions={0} | all-to-all | bytes 262144 | tf_op jit(solution)/shard_map/all_to_all | solution.py:777
  207.3 3.6 %shard_map.135 = (f32[4,128,256]{2,1,0:T(8,128)}, f32[4,128,256]{2,1,0:T(8,128)}) custom-call(f32[32,8,128]{2,1,0:T(8,128)S(1)} %copy-done.4, f32[32,8,128]{2,1,0:T(8,128)S(1)} %all_to_all.41.sums_ref, f32[2,4,128,256]{3,2,1,0:T(8,128)} %get-tuple-element.34.kept_ref.old_ref, f32[4,128,256]{2,1,0:T(8,128)S(1)} %get-tuple-element.63.way_ref, ...), custom_call_target="tpu_custom_call" | custom-call | bytes 3145728 | tf_op jit(solution)/shard_map/pallas_call | solution.py:350
  (69 shorter events, 5.6 us)
Async XLA Ops:
  0.6 35.9 %copy-start.25 = (f32[16,17]{1,0:T(8,128)S(1)}, f32[16,17]{1,0:T(8,128)}, u32[]{:S(2)}) copy-start(f32[16,17]{1,0:T(8,128)} %param.14) | copy-start | bytes 3268
  2.3 0.7 copy-start.1
  3.0 19.4 %collective-permute-start = (f32[4,16,8,128]{3,2,1,0:T(8,128)S(1)}, f32[4,16,8,128]{3,2,1,0:T(8,128)S(1)}, u32[]{:S(2)}, u32[]{:S(2)}) collective-permute-start(f32[4,16,8,128]{3,2,1,0:T(8,128)S(1)} %get-tuple-element.37), channel_id=1, source_target_pairs={{0,1},{1,2},{2,3},{3,0},{4,5},{5,6},{6,7},{7,4},{8,9},{9,10},{10,1... | collective-permute-start | bytes 786440 | tf_op jit(solution)/shard_map/ppermute | solution.py:833
  3.5 19.0 %collective-permute-start.1 = (f32[4,16,8,128]{3,2,1,0:T(8,128)S(1)}, f32[4,16,8,128]{3,2,1,0:T(8,128)S(1)}, u32[]{:S(2)}, u32[]{:S(2)}) collective-permute-start(f32[4,16,8,128]{3,2,1,0:T(8,128)S(1)} %get-tuple-element.38), channel_id=1, source_target_pairs={{0,2},{1,3},{2,0},{3,1},{4,6},{5,7},{6,4},{7,5},{8,10},{9,11},{10,... | collective-permute-start | bytes 786440 | tf_op jit(solution)/shard_map/ppermute | solution.py:833
  6.0 16.4 %collective-permute-start.2 = (f32[4,16,8,128]{3,2,1,0:T(8,128)S(1)}, f32[4,16,8,128]{3,2,1,0:T(8,128)S(1)}, u32[]{:S(2)}, u32[]{:S(2)}) collective-permute-start(f32[4,16,8,128]{3,2,1,0:T(8,128)S(1)} %get-tuple-element.39), channel_id=1, source_target_pairs={{0,3},{1,0},{2,1},{3,2},{4,7},{5,4},{6,5},{7,6},{8,11},{9,8},{10,9... | collective-permute-start | bytes 786440 | tf_op jit(solution)/shard_map/ppermute | solution.py:833
  9.3 13.1 %all-to-all-start = ((f32[32,8,128]{2,1,0:T(8,128)}), f32[32,8,128]{2,1,0:T(8,128)S(1)}, u32[]{:S(2)}, u32[]{:S(2)}) async-start(f32[32,8,128]{2,1,0:T(8,128)} %get-tuple-element.36), calls=%async_computation | async-start | bytes 262144 | tf_op jit(solution)/shard_map/all_to_all | solution.py:777
  22.4 0.6 copy-start.21
  22.4 0.8 copy-start.22
  22.5 0.8 copy-start.23
  23.3 0.7 copy-start.24
  33.1 19.0 %all-to-all-start.1 = ((f32[32,4,8,128]{3,2,1,0:T(8,128)}), f32[32,4,8,128]{3,2,1,0:T(8,128)S(1)}, u32[]{:S(2)}, u32[]{:S(2)}) async-start(f32[32,4,8,128]{3,2,1,0:T(8,128)} %get-tuple-element.40), calls=%async_computation.1 | async-start | bytes 1048576 | tf_op jit(solution)/shard_map/all_to_all | solution.py:777
  44.8 21.7 %copy-start.26 = (f32[17]{0:T(128)S(1)}, f32[17]{0:T(128)}, u32[]{:S(2)}) copy-start(f32[17]{0:T(128)} %param.15) | copy-start | bytes 208
  56.9 21.4 %all-to-all-start.2 = ((f32[32,4,8,128]{3,2,1,0:T(8,128)}), f32[32,4,8,128]{3,2,1,0:T(8,128)S(1)}, u32[]{:S(2)}, u32[]{:S(2)}) async-start(f32[32,4,8,128]{3,2,1,0:T(8,128)} %shard_map.125.__), calls=%async_computation.2 | async-start | bytes 1048576 | tf_op jit(solution)/shard_map/all_to_all | solution.py:777
  60.0 14.7 %collective-permute-start.5 = (f32[4,256]{1,0:T(4,128)S(1)}, f32[4,256]{1,0:T(4,128)S(1)}, u32[]{:S(2)}, u32[]{:S(2)}) collective-permute-start(f32[4,256]{1,0:T(4,128)S(1)} %get-tuple-element.44), channel_id=1, source_target_pairs={{0,1},{1,2},{2,3},{3,0},{4,5},{5,6},{6,7},{7,4},{8,9},{9,10},{10,1... | collective-permute-start | bytes 12296 | tf_op jit(solution)/shard_map/ppermute | solution.py:790
  60.3 14.4 %collective-permute-start.6 = (f32[4,256]{1,0:T(4,128)S(1)}, f32[4,256]{1,0:T(4,128)S(1)}, u32[]{:S(2)}, u32[]{:S(2)}) collective-permute-start(f32[4,256]{1,0:T(4,128)S(1)} %get-tuple-element.45), channel_id=1, source_target_pairs={{1,0},{2,1},{3,2},{0,3},{5,4},{6,5},{7,6},{4,7},{9,8},{10,9},{11,1... | collective-permute-start | bytes 12296 | tf_op jit(solution)/shard_map/ppermute | solution.py:791
  61.8 15.1 %collective-permute-start.3 = (f32[128,256]{1,0:T(8,128)S(1)}, f32[128,256]{1,0:T(8,128)S(1)}, u32[]{:S(2)}, u32[]{:S(2)}) collective-permute-start(f32[128,256]{1,0:T(8,128)S(1)} %get-tuple-element.42), channel_id=1, source_target_pairs={{0,4},{4,8},{8,12},{12,16},{16,20},{20,24},{24,28},{28,0},{1,5},{5... | collective-permute-start | bytes 393224 | tf_op jit(solution)/shard_map/ppermute | solution.py:790
  63.5 13.3 %collective-permute-start.4 = (f32[128,256]{1,0:T(8,128)S(1)}, f32[128,256]{1,0:T(8,128)S(1)}, u32[]{:S(2)}, u32[]{:S(2)}) collective-permute-start(f32[128,256]{1,0:T(8,128)S(1)} %get-tuple-element.43), channel_id=1, source_target_pairs={{4,0},{8,4},{12,8},{16,12},{20,16},{24,20},{28,24},{0,28},{5,1},{9... | collective-permute-start | bytes 393224 | tf_op jit(solution)/shard_map/ppermute | solution.py:791
  74.6 22.3 %copy-start = (f32[4,128,256]{2,1,0:T(8,128)S(1)}, f32[4,128,256]{2,1,0:T(8,128)}, u32[]{:S(2)}) copy-start(f32[4,128,256]{2,1,0:T(8,128)} %a_.3) | copy-start | bytes 1572868
  74.6 22.3 %copy-start.2 = (bf16[4,128,256]{2,1,0:T(8,128)(2,1)S(1)}, bf16[4,128,256]{2,1,0:T(8,128)(2,1)}, u32[]{:S(2)}) copy-start(bf16[4,128,256]{2,1,0:T(8,128)(2,1)} %perm_ref.9) | copy-start | bytes 786436
  74.6 3.7 %copy-start.13 = (f32[4,256]{1,0:T(4,128)}, f32[4,256]{1,0:T(4,128)S(1)}, u32[]{:S(2)}) copy-start(f32[4,256]{1,0:T(4,128)S(1)} %collective-permute-done.5.refs_2_.refs_6_.refs_10_) | copy-start | bytes 12292
  74.7 3.7 %copy-start.16 = (f32[4,256]{1,0:T(4,128)}, f32[4,256]{1,0:T(4,128)S(1)}, u32[]{:S(2)}) copy-start(f32[4,256]{1,0:T(4,128)S(1)} %collective-permute-done.6.refs_3_.refs_7_.refs_11_) | copy-start | bytes 12292
  76.8 1.5 copy-start.6
  76.8 1.5 copy-start.9
  78.4 0.8 copy-start.19
  88.2 8.1 %collective-permute-start.7 = (f32[128,256]{1,0:T(8,128)S(1)}, f32[128,256]{1,0:T(8,128)S(1)}, u32[]{:S(2)}, u32[]{:S(2)}) collective-permute-start(f32[128,256]{1,0:T(8,128)S(1)} %get-tuple-element.47), channel_id=1, source_target_pairs={{0,4},{4,8},{8,12},{12,16},{16,20},{20,24},{24,28},{28,0},{1,5},{5... | collective-permute-start | bytes 393224 | tf_op jit(solution)/shard_map/ppermute | solution.py:790
  89.1 7.8 %collective-permute-start.8 = (f32[128,256]{1,0:T(8,128)S(1)}, f32[128,256]{1,0:T(8,128)S(1)}, u32[]{:S(2)}, u32[]{:S(2)}) collective-permute-start(f32[128,256]{1,0:T(8,128)S(1)} %get-tuple-element.48), channel_id=1, source_target_pairs={{4,0},{8,4},{12,8},{16,12},{20,16},{24,20},{28,24},{0,28},{5,1},{9... | collective-permute-start | bytes 393224 | tf_op jit(solution)/shard_map/ppermute | solution.py:791
  92.9 3.0 %collective-permute-start.9 = (f32[4,256]{1,0:T(4,128)S(1)}, f32[4,256]{1,0:T(4,128)S(1)}, u32[]{:S(2)}, u32[]{:S(2)}) collective-permute-start(f32[4,256]{1,0:T(4,128)S(1)} %get-tuple-element.49), channel_id=1, source_target_pairs={{0,1},{1,2},{2,3},{3,0},{4,5},{5,6},{6,7},{7,4},{8,9},{9,10},{10,1... | collective-permute-start | bytes 12296 | tf_op jit(solution)/shard_map/ppermute | solution.py:790
  92.9 3.1 %collective-permute-start.10 = (f32[4,256]{1,0:T(4,128)S(1)}, f32[4,256]{1,0:T(4,128)S(1)}, u32[]{:S(2)}, u32[]{:S(2)}) collective-permute-start(f32[4,256]{1,0:T(4,128)S(1)} %get-tuple-element.50), channel_id=1, source_target_pairs={{1,0},{2,1},{3,2},{0,3},{5,4},{6,5},{7,6},{4,7},{9,8},{10,9},{11,1... | collective-permute-start | bytes 12296 | tf_op jit(solution)/shard_map/ppermute | solution.py:791
  96.9 0.9 copy-start.7
  97.8 0.9 copy-start.10
  98.7 0.7 copy-start.14
  99.4 0.7 copy-start.17
  103.1 33.4 %copy-start.12 = (f32[4,128,256]{2,1,0:T(8,128)}, f32[4,128,256]{2,1,0:T(8,128)S(1)}, u32[]{:S(2)}) copy-start(f32[4,128,256]{2,1,0:T(8,128)S(1)} %get-tuple-element.52.image_ref) | copy-start | bytes 1572868
  125.6 18.2 %all-to-all-start.4 = ((f32[32,4,8,128]{3,2,1,0:T(8,128)}), f32[32,4,8,128]{3,2,1,0:T(8,128)S(1)}, u32[]{:S(2)}, u32[]{:S(2)}) async-start(f32[32,4,8,128]{3,2,1,0:T(8,128)} %get-tuple-element.53), calls=%async_computation.4 | async-start | bytes 1048576 | tf_op jit(solution)/shard_map/all_to_all | solution.py:777
  148.6 18.5 %all-to-all-start.5 = ((f32[32,4,8,128]{3,2,1,0:T(8,128)}), f32[32,4,8,128]{3,2,1,0:T(8,128)S(1)}, u32[]{:S(2)}, u32[]{:S(2)}) async-start(f32[32,4,8,128]{3,2,1,0:T(8,128)} %shard_map.131.__), calls=%async_computation.5 | async-start | bytes 1048576 | tf_op jit(solution)/shard_map/all_to_all | solution.py:777
  159.9 31.8 %copy-start.3 = (bf16[4,128,256]{2,1,0:T(8,128)(2,1)S(1)}, bf16[4,128,256]{2,1,0:T(8,128)(2,1)}, u32[]{:S(2)}) copy-start(bf16[4,128,256]{2,1,0:T(8,128)(2,1)} %perm_ref.9) | copy-start | bytes 786436
  159.9 31.8 %copy-start.4 = (f32[32,8,128]{2,1,0:T(8,128)S(1)}, f32[32,8,128]{2,1,0:T(8,128)}, u32[]{:S(2)}) copy-start(f32[32,8,128]{2,1,0:T(8,128)} %all_to_all.40.sums_ref.first_ref) | copy-start | bytes 393220
  159.9 31.8 %copy-start.5 = (f32[4,128,256]{2,1,0:T(8,128)S(1)}, f32[4,128,256]{2,1,0:T(8,128)}, u32[]{:S(2)}) copy-start(f32[4,128,256]{2,1,0:T(8,128)} %get-tuple-element.61.refs_12_.res_ref) | copy-start | bytes 1572868
  159.9 31.9 %copy-start.8 = (f32[128,256]{1,0:T(8,128)S(1)}, f32[128,256]{1,0:T(8,128)}, u32[]{:S(2)}) copy-start(f32[128,256]{1,0:T(8,128)} %copy-done.6) | copy-start | bytes 393220
  159.9 31.9 %copy-start.11 = (f32[128,256]{1,0:T(8,128)S(1)}, f32[128,256]{1,0:T(8,128)}, u32[]{:S(2)}) copy-start(f32[128,256]{1,0:T(8,128)} %copy-done.9) | copy-start | bytes 393220
  159.9 31.9 %copy-start.15 = (f32[4,256]{1,0:T(4,128)S(1)}, f32[4,256]{1,0:T(4,128)}, u32[]{:S(2)}) copy-start(f32[4,256]{1,0:T(4,128)} %copy-done.13) | copy-start | bytes 12292
  159.9 31.9 %copy-start.18 = (f32[4,256]{1,0:T(4,128)S(1)}, f32[4,256]{1,0:T(4,128)}, u32[]{:S(2)}) copy-start(f32[4,256]{1,0:T(4,128)} %copy-done.16) | copy-start | bytes 12292
  167.1 0.8 copy-start.20
  177.9 13.9 %all-to-all-start.6 = ((f32[32,8,128]{2,1,0:T(8,128)}), f32[32,8,128]{2,1,0:T(8,128)S(1)}, u32[]{:S(2)}, u32[]{:S(2)}) async-start(f32[32,8,128]{2,1,0:T(8,128)} %get-tuple-element.55), calls=%async_computation.6 | async-start | bytes 262144 | tf_op jit(solution)/shard_map/all_to_all | solution.py:777
  180.9 10.6 %collective-permute-start.11 = (f32[128,256]{1,0:T(8,128)S(1)}, f32[128,256]{1,0:T(8,128)S(1)}, u32[]{:S(2)}, u32[]{:S(2)}) collective-permute-start(f32[128,256]{1,0:T(8,128)S(1)} %get-tuple-element.57), channel_id=1, source_target_pairs={{0,4},{4,8},{8,12},{12,16},{16,20},{20,24},{24,28},{28,0},{1,5},{5... | collective-permute-start | bytes 393224 | tf_op jit(solution)/shard_map/ppermute | solution.py:790
  182.8 9.0 %collective-permute-start.12 = (f32[128,256]{1,0:T(8,128)S(1)}, f32[128,256]{1,0:T(8,128)S(1)}, u32[]{:S(2)}, u32[]{:S(2)}) collective-permute-start(f32[128,256]{1,0:T(8,128)S(1)} %get-tuple-element.58), channel_id=1, source_target_pairs={{4,0},{8,4},{12,8},{16,12},{20,16},{24,20},{28,24},{0,28},{5,1},{9... | collective-permute-start | bytes 393224 | tf_op jit(solution)/shard_map/ppermute | solution.py:791
  185.7 3.0 %collective-permute-start.13 = (f32[4,256]{1,0:T(4,128)S(1)}, f32[4,256]{1,0:T(4,128)S(1)}, u32[]{:S(2)}, u32[]{:S(2)}) collective-permute-start(f32[4,256]{1,0:T(4,128)S(1)} %get-tuple-element.59), channel_id=1, source_target_pairs={{0,1},{1,2},{2,3},{3,0},{4,5},{5,6},{6,7},{7,4},{8,9},{9,10},{10,1... | collective-permute-start | bytes 12296 | tf_op jit(solution)/shard_map/ppermute | solution.py:790
  185.7 3.1 %collective-permute-start.14 = (f32[4,256]{1,0:T(4,128)S(1)}, f32[4,256]{1,0:T(4,128)S(1)}, u32[]{:S(2)}, u32[]{:S(2)}) collective-permute-start(f32[4,256]{1,0:T(4,128)S(1)} %get-tuple-element.60), channel_id=1, source_target_pairs={{1,0},{2,1},{3,2},{0,3},{5,4},{6,5},{7,6},{4,7},{9,8},{10,9},{11,1... | collective-permute-start | bytes 12296 | tf_op jit(solution)/shard_map/ppermute | solution.py:791

commit v5 on v4

--- a/solution.py
+++ b/solution.py
@@ -320,14 +320,15 @@
     return value + value * jnp.tanh(value * (value * value + LINEAR))
 
 
-def call(body, outs, in_specs, out_specs, grid=(), scratch=(), flops=0, moved=0, alias=None, limit=8, near=(), loose=False):
+def call(body, outs, in_specs, out_specs, grid=(), scratch=(), flops=0, moved=0, alias=None, limit=8, near=(), loose=()):
     single = not isinstance(outs, tuple)
     outs = (outs,) if single else outs
     out_specs = (out_specs,) if single else out_specs
     run = pl.pallas_call(
         body,
         out_shape=tuple(
-            out if loose or out.size <= 2**16 else pltpu.HBM(out.shape, out.dtype) for out in outs
+            out if place in loose or out.size <= 2**16 else pltpu.HBM(out.shape, out.dtype)
+            for place, out in enumerate(outs)
         ),
         grid=grid,
         in_specs=in_specs,
@@ -628,8 +629,9 @@
     return (scale * (total + proj_ref[CHANNELS])).T
 
 
-def put_edges(update, low_ref, high_ref, left_ref, right_ref):
+def put_edges(update, field_ref, low_ref, high_ref, left_ref, right_ref):
     step = pl.program_id(0)
+    field_ref[0] = update
     left_ref[pl.ds(step, 1), :] = update[:1]
     right_ref[pl.ds(step, 1), :] = update[update.shape[0] - 1 :]
 
@@ -652,26 +654,14 @@
     put_edges(update, *edges)
 
 
-def back_next_body(cells, proj_ref, first_ref, sums_ref, recv_ref, point_ref, col_ref, deep_ref, image_ref, _, kept_ref, out_ref, *refs):
-    *edges, wave_ref, acc_ref = refs
+def back_next_body(cells, proj_ref, first_ref, sums_ref, recv_ref, point_ref, col_ref, deep_ref, _, kept_ref, *refs):
+    *edges, wave_ref = refs
     _, _, total = next_scalars(first_ref, sums_ref)
     update = back_transform(
         recv_ref, point_ref, proj_ref, col_ref, deep_ref, wave_ref, scale_of(total, cells)
     )
     kept_ref[0, 0] = update
     put_edges(update, *edges)
-    line = lane_sums(update * image_ref[0])
-    step = pl.program_id(0)
-
-    @pl.when(step == 0)
-    def _():
-        acc_ref[...] = jnp.zeros_like(acc_ref)
-
-    acc_ref[0:1] += line
-
-    @pl.when(step == pl.num_programs(0) - 1)
-    def _():
-        spread([acc_ref[0:1]], out_ref)
 
 
 def stencil(fields, perms):
@@ -740,10 +730,10 @@
     return plane(step), before, after, left, right
 
 
-def operator_first_body(kept_ref, perm_ref, *refs):
+def operator_first_body(field_ref, perm_ref, *refs):
     halo, perm_halo = refs[:4], refs[4:8]
     res_ref, image_ref, out_ref, acc_ref = refs[8:]
-    fields = around(kept_ref, (0,), halo)
+    fields = around(field_ref, (), halo)
     image = stencil(fields, around(perm_ref, (), perm_halo))
     own = fields[0]
     residual = res_ref[0]
@@ -751,26 +741,30 @@
     add_sums((own * image, residual * own, image * image, residual * image), out_ref, acc_ref)
 
 
-def operator_next_body(first_ref, beta_ref, kept_ref, perm_ref, *refs):
+def operator_next_body(cells, first_ref, sums_ref, field_ref, old_ref, perm_ref, *refs):
     halo, old, perm_halo = refs[:4], refs[4:8], refs[8:12]
-    res_ref, way_ref, image_ref, out_ref, acc_ref = refs[12:]
-    beta = gathered(beta_ref, 0) / gathered(first_ref, 0)
-    fields = [
-        new - beta * other
-        for new, other in zip(around(kept_ref, (1,), halo), around(kept_ref, (0,), old))
-    ]
+    res_ref, before_ref, way_ref, image_ref, out_ref, acc_ref = refs[12:]
+    _, _, total = next_scalars(first_ref, sums_ref)
+    factor = scale_of(total, cells) / scale_of(gathered(first_ref, 0), cells)
+    old = around(old_ref, (), old)
+    fields = [new - factor * other for new, other in zip(around(field_ref, (), halo), old)]
     image = stencil(fields, around(perm_ref, (), perm_halo))
     own = fields[0]
+    residual = res_ref[0]
     way_ref[0] = own
     image_ref[0] = image
-    add_sums((own * image, res_ref[0] * own), out_ref, acc_ref)
-
-
-def last_body(first_ref, sums_ref, old_ref, way_ref, res_ref, image_ref, sol_ref, out_ref):
-    alpha = gathered(first_ref, 1) / gathered(first_ref, 0)
-    later = gathered(sums_ref, 1) / gathered(sums_ref, 0)
-    sol_ref[0] = alpha * old_ref[0, 0] + later * way_ref[0]
-    out_ref[0] = res_ref[0] - later * image_ref[0]
+    add_sums((own * image, own * before_ref[0], residual * own, residual * old[0]), out_ref, acc_ref)
+
+
+def last_body(sums_ref, later_ref, old_ref, way_ref, res_ref, before_ref, image_ref, sol_ref, out_ref):
+    curvature = gathered(sums_ref, 0)
+    alpha = gathered(sums_ref, 1) / curvature
+    cross = gathered(later_ref, 1)
+    delta = cross / curvature
+    along = gathered(later_ref, 2) - delta * gathered(later_ref, 3)
+    later = along / (gathered(later_ref, 0) - delta * cross)
+    sol_ref[0] = alpha * old_ref[0] + later * (way_ref[0] - delta * old_ref[0])
+    out_ref[0] = res_ref[0] - later * (image_ref[0] - delta * before_ref[0])
 
 
 def exchange(blocks):
@@ -901,11 +895,13 @@
         moved=2 * field_bytes + spectra_bytes,
     )(lift_weight, squares, right_side, permeability, deep_forward, col_forward, *weights)
     received, point = mixed_modes(blocks, lifted)
-    kept, *edges = call(
+    kept, old, *edges = call(
         functools.partial(back_first_body, cells),
-        (kept_shape,) + edge_shapes,
+        (kept_shape, field) + edge_shapes,
         [smem, vmem, spectra_block, point_block, vmem, vmem] + [anywhere] * 4,
-        (pl.BlockSpec((1, 1, cols, depth), lambda i: (0, i, 0, 0)),) + (vmem,) * 4,
+        (pl.BlockSpec((1, 1, cols, depth), lambda i: (0, i, 0, 0)), plane) + (vmem,) * 4,
+        near=(2, 6, 7, 8, 9),
+        loose=(1,),
         grid=(rows,),
         scratch=[zt_scratch],
         limit=12,
@@ -914,18 +910,17 @@
     )(proj_weight, squares, received, point, col_back, deep_back, *perm_halo)
 
     old_halo = neighbours(*edges)
-    kept_first = pl.BlockSpec((1, rows, cols, depth), lambda i: (0, 0, 0, 0))
-    args = (kept, permeability, *old_halo, *perm_halo, right_side)
+    args = (old, permeability, *old_halo, *perm_halo, right_side)
     image, sums = call(
         operator_first_body,
         (field, partial),
-        [kept_first] + [vmem] * 9 + [plane],
+        [vmem] * 10 + [plane],
         (plane, vmem),
         grid=(rows,),
         scratch=[acc_scratch],
         moved=9 * field_bytes,
-        near=range(1, 11),
-        loose=True,
+        near=range(11),
+        loose=range(3),
     )(*args)
     sums = add_up(sums)
 
@@ -942,44 +937,45 @@
         moved=4 * field_bytes + spectra_bytes,
     )(lift_weight, squares, sums, right_side, image, permeability, deep_forward, col_forward)
     received, point = mixed_modes(blocks, lifted)
-    kept, beta, *edges = call(
+    kept, update, *edges = call(
         functools.partial(back_next_body, cells),
-        (kept_shape, partial) + edge_shapes,
-        [smem, vmem, vmem, spectra_block, point_block, vmem, vmem, plane, whole(pl.ANY)],
-        (pl.BlockSpec((1, 1, cols, depth), lambda i: (1, i, 0, 0)),) + (vmem,) * 5,
+        (kept_shape, field) + edge_shapes,
+        [smem, vmem, vmem, spectra_block, point_block, vmem, vmem, anywhere],
+        (pl.BlockSpec((1, 1, cols, depth), lambda i: (1, i, 0, 0)), plane) + (vmem,) * 4,
+        near=(3,),
+        loose=(1,),
         grid=(rows,),
         limit=12,
-        scratch=[zt_scratch, acc_scratch],
+        scratch=[zt_scratch],
         flops=back_flops,
         moved=19 * field_bytes,
-        alias={8: 0},
-    )(proj_weight, squares, sums, received, point, col_back, deep_back, image, kept)
-
-    beta = add_up(beta)
+        alias={7: 0},
+    )(proj_weight, squares, sums, received, point, col_back, deep_back, kept)
+
     halo = neighbours(*edges)
-    args = (sums, beta, kept, permeability, *halo, *old_halo, *perm_halo, residual)
-    way, image, later = call(
-        operator_next_body,
+    args = (squares, sums, update, old, permeability, *halo, *old_halo, *perm_halo, residual, image)
+    way, last_image, later = call(
+        functools.partial(operator_next_body, cells),
         (field, field, partial),
-        [vmem] * 16 + [plane],
+        [vmem] * 17 + [plane] * 2,
         (plane, plane, vmem),
         grid=(rows,),
         scratch=[acc_scratch],
-        near=(0, 1) + tuple(range(3, 17)),
-        loose=True,
+        near=range(19),
+        loose=range(3),
         moved=11 * field_bytes,
     )(*args)
     later = add_up(later)
     answer, residual = call(
         last_body,
         (field, field),
-        [vmem, vmem, pl.BlockSpec((1, 1, cols, depth), lambda i: (0, i, 0, 0)), plane, plane, plane],
+        [vmem, vmem] + [plane] * 5,
         (plane, plane),
         grid=(rows,),
         moved=6 * field_bytes,
-        near=(0, 1, 3, 4, 5),
-        loose=True,
-    )(sums, later, kept, way, residual, image)
+        near=range(7),
+        loose=range(3),
+    )(sums, later, old, way, residual, image, last_image)
     return (answer, residual, kept)
 
 

time: 212 us -> 198 us (0.934)
  Pallas kernels: 93.3 us -> 88.5 us
  local copies, waits for them, and re-layouts: 7.03 us -> 2.28 us
  starting transfers between devices: 44.3 us -> 41.1 us
    unnamed x54 -> x26, local copies, waits for them, and re-layouts: 7.03 us -> 2.28 us
    pallas_call x15, Pallas kernels: 93.3 us -> 88.5 us  [wrapped(): found = run(*held)]
    all_to_all x6 -> x5, starting transfers between devices: 20.3 us -> 17.2 us  [exchange(): return lax.all_to_all(blocks, BOTH, split_axis=0, concat_axis=0, tiled=True)]
    ppermute x6, waiting for transfers between devices: 7.8 us -> 5.37 us  [neighbours(): found.append(lax.ppermute(last, axis, forward))]
    all_to_all x6 -> x5, waiting for transfers between devices: 30.8 us -> 30.9 us  [exchange(): return lax.all_to_all(blocks, BOTH, split_axis=0, concat_axis=0, tiled=True)]
  transfers between devices with their start and end apart: 21 -> 20, of which waited for: 12 -> 12; matrix products, arithmetic and copies ran while one was open for 0% -> 0% of each run, Pallas kernels for 16% -> 18%
where the time goes in v5:
time: 198 us; the launch traced here: 197 us
  Pallas kernels  88.5 us (45%)
  starting transfers between devices  41.1 us (21%)
  waiting for transfers between devices  37.9 us (19%)
  blocking collectives  25.8 us (13%)
  local copies, waits for them, and re-layouts  2.28 us (1%)
    pallas_call x15, Pallas kernels, wrapped(): found = run(*held)  88.5 us
    all_to_all x5, waiting for transfers between devices, exchange(): return lax.all_to_all(blocks, BOTH, split_axis=0, concat_axis=0, tiled=True)  30.9 us
    all_to_all x2, blocking collectives, exchange(): return lax.all_to_all(blocks, BOTH, split_axis=0, concat_axis=0, tiled=True)  25.8 us
    all_to_all x5, starting transfers between devices, exchange(): return lax.all_to_all(blocks, BOTH, split_axis=0, concat_axis=0, tiled=True)  17.2 us
    ppermute x6, starting transfers between devices, neighbours(): found.append(lax.ppermute(first, axis, backward))  15.2 us
    ppermute x6, waiting for transfers between devices, neighbours(): found.append(lax.ppermute(last, axis, forward))  5.37 us
    ppermute x3, starting transfers between devices, tiled_local(): lax.ppermute(part, 'col', [(i, (i + shift + 1) % n_col) for i in range(n_...  4.45 us
    ppermute x6, starting transfers between devices, neighbours(): found.append(lax.ppermute(last, axis, forward))  4.24 us
  transfers between devices with their start and end apart: 20, of which 12 were waited for; matrix products, arithmetic and copies ran while one was open for 0% of the time, Pallas kernels for 18%

profile of v5, /device:TPU:0, one launch (start us, length us, event | category | flops | bytes accessed | tf_op | source)
XLA Modules:
  0.0 197.1 jit_solution(14861336858040210908)
XLA Ops:
  0.6 1.7 shard_map.121
  2.3 0.7 copy-done.1
  3.0 0.5 collective-permute-start
  3.5 2.6 %collective-permute-start.1 = (f32[4,16,8,128]{3,2,1,0:T(8,128)S(1)}, f32[4,16,8,128]{3,2,1,0:T(8,128)S(1)}, u32[]{:S(2)}, u32[]{:S(2)}) collective-permute-start(f32[4,16,8,128]{3,2,1,0:T(8,128)S(1)} %get-tuple-element.39), channel_id=1, source_target_pairs={{0,2},{1,3},{2,0},{3,1},{4,6},{5,7},{6,4},{7,5},{8,10},{9,11},{10,... | collective-permute-start | bytes 786440 | tf_op jit(solution)/shard_map/ppermute | solution.py:827
  6.1 1.4 collective-permute-start.2
  7.5 1.8 shard_map.122
  9.3 4.9 %all-to-all-start = ((f32[32,8,128]{2,1,0:T(8,128)}), f32[32,8,128]{2,1,0:T(8,128)S(1)}, u32[]{:S(2)}, u32[]{:S(2)}) async-start(f32[32,8,128]{2,1,0:T(8,128)} %get-tuple-element.37), calls=%async_computation | async-start | bytes 262144 | tf_op jit(solution)/shard_map/all_to_all | solution.py:771
  14.2 0.7 multiply_bitcast_fusion.lift_ref
  14.9 7.5 %all-to-all-done.sums_ref.first_ref = f32[32,8,128]{2,1,0:T(8,128)S(1)} async-done(((f32[32,8,128]{2,1,0:T(8,128)}), f32[32,8,128]{2,1,0:T(8,128)S(1)}, u32[]{:S(2)}, u32[]{:S(2)}) %all-to-all-start) | async-done | bytes 131104 | tf_op jit(solution)/shard_map/all_to_all | solution.py:771
  22.5 0.6 copy-done.4
  23.3 0.7 copy-done.10
  24.0 9.1 %shard_map.123 = (f32[32,4,8,128]{3,2,1,0:T(8,128)}, f32[4,16,256,128]{3,2,1,0:T(8,128)}) custom-call(f32[3,16]{1,0:T(4,128)S(1)} %multiply_bitcast_fusion.lift_ref, f32[32,8,128]{2,1,0:T(8,128)} %copy-done.4, f32[4,128,256]{2,1,0:T(8,128)} %a_.3, bf16[4,128,256]{2,1,0:T(8,128)(2,1)} %perm_ref.9, bf16[128,256]{1,0:T(8,128)(2,1)} %constant.8.clone.deep_ref, ...), custom_call_target="tpu_custom_call" | custom-call | flops 2000000000 | bytes 1572864 | tf_op jit(solution)/shard_map/pallas_call | solution.py:351
  33.1 3.5 %all-to-all-start.1 = ((f32[32,4,8,128]{3,2,1,0:T(8,128)}), f32[32,4,8,128]{3,2,1,0:T(8,128)S(1)}, u32[]{:S(2)}, u32[]{:S(2)}) async-start(f32[32,4,8,128]{3,2,1,0:T(8,128)} %get-tuple-element.41), calls=%async_computation.1 | async-start | bytes 1048576 | tf_op jit(solution)/shard_map/all_to_all | solution.py:771
  36.6 8.2 %shard_map.124.refs_4_._ = f32[4,16,256,128]{3,2,1,0:T(8,128)} custom-call(f32[16,17]{1,0:T(8,128)S(1)} %broadcast_multiply_fusion.mix_ref, f32[4,16,256,128]{3,2,1,0:T(8,128)} %get-tuple-element.42.lifted_ref, f32[4,128,256]{2,1,0:T(8,128)} %a_.3, f32[4,128,256]{2,1,0:T(8,128)} %a_.3), custom_call_target="tpu_custom_call" | custom-call | flops 2500000000 | bytes 8388608 | tf_op jit(solution)/shard_map/pallas_call | solution.py:351
  44.8 7.3 %all-to-all-done.1.recv_ref = f32[32,4,8,128]{3,2,1,0:T(8,128)S(1)} async-done(((f32[32,4,8,128]{3,2,1,0:T(8,128)}), f32[32,4,8,128]{3,2,1,0:T(8,128)S(1)}, u32[]{:S(2)}, u32[]{:S(2)}) %all-to-all-start.1) | async-done | bytes 524320 | tf_op jit(solution)/shard_map/all_to_all | solution.py:771
  52.1 4.8 %shard_map.125.__ = f32[32,4,8,128]{3,2,1,0:T(8,128)} custom-call(f32[32,4,8,128]{3,2,1,0:T(8,128)S(1)} %all-to-all-done.1.recv_ref, f32[4,16,8,128]{3,2,1,0:T(8,128)} %copy-done.1, f32[4,16,8,128]{3,2,1,0:T(8,128)} %copy-done.8, f32[4,16,8,128]{3,2,1,0:T(8,128)} %copy-done.9, f32[4,16,8,128]{3,2,1,0:T(8,128)} %copy-done.10, ...), custom_call_target="tpu_custom_call" | custom-call | bytes 2097152 | tf_op jit(solution)/shard_map/pallas_call | solution.py:351
  56.9 3.1 %all-to-all-start.2 = ((f32[32,4,8,128]{3,2,1,0:T(8,128)}), f32[32,4,8,128]{3,2,1,0:T(8,128)S(1)}, u32[]{:S(2)}, u32[]{:S(2)}) async-start(f32[32,4,8,128]{3,2,1,0:T(8,128)} %shard_map.125.__), calls=%async_computation.2 | async-start | bytes 1048576 | tf_op jit(solution)/shard_map/all_to_all | solution.py:771
  60.3 1.5 collective-permute-start.6
  61.8 1.8 collective-permute-start.3
  63.6 3.0 %collective-permute-start.4 = (f32[128,256]{1,0:T(8,128)S(1)}, f32[128,256]{1,0:T(8,128)S(1)}, u32[]{:S(2)}, u32[]{:S(2)}) collective-permute-start(f32[128,256]{1,0:T(8,128)S(1)} %get-tuple-element.44), channel_id=1, source_target_pairs={{4,0},{8,4},{12,8},{16,12},{20,16},{24,20},{28,24},{0,28},{5,1},{9... | collective-permute-start | bytes 393224 | tf_op jit(solution)/shard_map/ppermute | solution.py:785
  66.5 8.1 %shard_map.126.point_ref = f32[4,16,256,128]{3,2,1,0:T(8,128)} custom-call(f32[16,17]{1,0:T(8,128)S(1)} %broadcast_multiply_fusion.mix_ref, f32[4,16,256,128]{3,2,1,0:T(8,128)} %get-tuple-element.42.lifted_ref, f32[4,16,256,128]{3,2,1,0:T(8,128)} %shard_map.124.refs_4_._, f32[32,4,8,128]{3,2,1,0:T(8,128)} %shard_map.125.__), custom_call_target="tpu_custom_call", output_to_operand_aliasing={{}: (2, {})} | custom-call | flops 2500000000 | bytes 8388608 | tf_op jit(solution)/shard_map/pallas_call | solution.py:351
  74.7 2.2 %collective-permute-done.3.refs_0_.refs_4_.refs_8_ = f32[128,256]{1,0:T(8,128)S(1)} collective-permute-done((f32[128,256]{1,0:T(8,128)S(1)}, f32[128,256]{1,0:T(8,128)S(1)}, u32[]{:S(2)}, u32[]{:S(2)}) %collective-permute-start.3) | collective-permute-done | bytes 131104 | tf_op jit(solution)/shard_map/ppermute | solution.py:784
  76.9 1.5 all-to-all-done.2.recv_ref
  78.4 9.0 %shard_map.127 = (f32[2,4,128,256]{3,2,1,0:T(8,128)}, f32[4,128,256]{2,1,0:T(8,128)S(1)}, f32[128,256]{1,0:T(8,128)S(1)}, f32[128,256]{1,0:T(8,128)S(1)}, f32[4,256]{1,0:T(4,128)S(1)}, /*index=5*/f32[4,256]{1,0:T(4,128)S(1)}) custom-call(f32[17]{0:T(128)S(1)} %fusion.proj_ref, f32[32,8,128]{2,1,0:T(8,128)} %copy-done.4, ...), custom_call_target="tpu_custom_call" | custom-call | flops 2000000000 | bytes 9437184 | tf_op jit(solution)/shard_map/pallas_call | solution.py:351
  87.3 0.9 collective-permute-start.7
  88.2 3.8 %collective-permute-start.8 = (f32[128,256]{1,0:T(8,128)S(1)}, f32[128,256]{1,0:T(8,128)S(1)}, u32[]{:S(2)}, u32[]{:S(2)}) collective-permute-start(f32[128,256]{1,0:T(8,128)S(1)} %get-tuple-element.49), channel_id=1, source_target_pairs={{4,0},{8,4},{12,8},{16,12},{20,16},{24,20},{28,24},{0,28},{5,1},{9... | collective-permute-start | bytes 393224 | tf_op jit(solution)/shard_map/ppermute | solution.py:785
  92.1 1.7 collective-permute-start.10
  93.8 1.3 collective-permute-done.9.refs_2_.refs_6_
  95.4 0.6 collective-permute-done.8.refs_1_.refs_5_
  96.0 1.9 shard_map.128
  98.0 13.1 %all_to_all.35.sums_ref = f32[32,8,128]{2,1,0:T(8,128)} all-to-all(f32[32,8,128]{2,1,0:T(8,128)S(1)} %get-tuple-element.52), channel_id=1, replica_groups=mesh['row'=8,'col'=4] {'row','col'}, dimensions={0} | all-to-all | bytes 262144 | tf_op jit(solution)/shard_map/all_to_all | solution.py:771
  111.1 9.4 %shard_map.129 = (f32[32,4,8,128]{3,2,1,0:T(8,128)}, f32[4,16,256,128]{3,2,1,0:T(8,128)}, f32[4,128,256]{2,1,0:T(8,128)}) custom-call(f32[3,16]{1,0:T(4,128)S(1)} %multiply_bitcast_fusion.lift_ref, f32[32,8,128]{2,1,0:T(8,128)} %copy-done.4, f32[32,8,128]{2,1,0:T(8,128)} %all_to_all.35.sums_ref, f32[4,128,256]{2,1,0:T(8,128)} %a_.3, ...), custom_call_target="tpu_custom_call" | custom-call | flops 2000000000 | bytes 2621440 | tf_op jit(solution)/shard_map/pallas_call | solution.py:351
  120.5 2.6 %all-to-all-start.4 = ((f32[32,4,8,128]{3,2,1,0:T(8,128)}), f32[32,4,8,128]{3,2,1,0:T(8,128)S(1)}, u32[]{:S(2)}, u32[]{:S(2)}) async-start(f32[32,4,8,128]{3,2,1,0:T(8,128)} %get-tuple-element.54), calls=%async_computation.4 | async-start | bytes 1048576 | tf_op jit(solution)/shard_map/all_to_all | solution.py:771
  123.1 8.2 %shard_map.130.refs_4_._ = f32[4,16,256,128]{3,2,1,0:T(8,128)} custom-call(f32[16,17]{1,0:T(8,128)S(1)} %broadcast_multiply_fusion.mix_ref, f32[4,16,256,128]{3,2,1,0:T(8,128)} %get-tuple-element.55.lifted_ref, f32[4,128,256]{2,1,0:T(8,128)} %a_.3, f32[4,128,256]{2,1,0:T(8,128)} %a_.3), custom_call_target="tpu_custom_call" | custom-call | flops 2500000000 | bytes 8388608 | tf_op jit(solution)/shard_map/pallas_call | solution.py:351
  131.3 7.3 %all-to-all-done.4.recv_ref = f32[32,4,8,128]{3,2,1,0:T(8,128)S(1)} async-done(((f32[32,4,8,128]{3,2,1,0:T(8,128)}), f32[32,4,8,128]{3,2,1,0:T(8,128)S(1)}, u32[]{:S(2)}, u32[]{:S(2)}) %all-to-all-start.4) | async-done | bytes 524320 | tf_op jit(solution)/shard_map/all_to_all | solution.py:771
  138.6 4.8 %shard_map.131.__ = f32[32,4,8,128]{3,2,1,0:T(8,128)} custom-call(f32[32,4,8,128]{3,2,1,0:T(8,128)S(1)} %all-to-all-done.4.recv_ref, f32[4,16,8,128]{3,2,1,0:T(8,128)} %copy-done.1, f32[4,16,8,128]{3,2,1,0:T(8,128)} %copy-done.8, f32[4,16,8,128]{3,2,1,0:T(8,128)} %copy-done.9, f32[4,16,8,128]{3,2,1,0:T(8,128)} %copy-done.10, ...), custom_call_target="tpu_custom_call" | custom-call | bytes 2097152 | tf_op jit(solution)/shard_map/pallas_call | solution.py:351
  143.4 3.2 %all-to-all-start.5 = ((f32[32,4,8,128]{3,2,1,0:T(8,128)}), f32[32,4,8,128]{3,2,1,0:T(8,128)S(1)}, u32[]{:S(2)}, u32[]{:S(2)}) async-start(f32[32,4,8,128]{3,2,1,0:T(8,128)} %shard_map.131.__), calls=%async_computation.5 | async-start | bytes 1048576 | tf_op jit(solution)/shard_map/all_to_all | solution.py:771
  146.6 8.1 %shard_map.132.point_ref = f32[4,16,256,128]{3,2,1,0:T(8,128)} custom-call(f32[16,17]{1,0:T(8,128)S(1)} %broadcast_multiply_fusion.mix_ref, f32[4,16,256,128]{3,2,1,0:T(8,128)} %get-tuple-element.55.lifted_ref, f32[4,16,256,128]{3,2,1,0:T(8,128)} %shard_map.130.refs_4_._, f32[32,4,8,128]{3,2,1,0:T(8,128)} %shard_map.131.__), custom_call_target="tpu_custom_call", output_to_operand_aliasing={{}: (2, {})} | custom-call | flops 2500000000 | bytes 8388608 | tf_op jit(solution)/shard_map/pallas_call | solution.py:351
  154.8 7.2 %all-to-all-done.5.recv_ref = f32[32,4,8,128]{3,2,1,0:T(8,128)S(1)} async-done(((f32[32,4,8,128]{3,2,1,0:T(8,128)}), f32[32,4,8,128]{3,2,1,0:T(8,128)S(1)}, u32[]{:S(2)}, u32[]{:S(2)}) %all-to-all-start.5) | async-done | bytes 524320 | tf_op jit(solution)/shard_map/all_to_all | solution.py:771
  162.0 9.1 %shard_map.133 = (f32[2,4,128,256]{3,2,1,0:T(8,128)}, f32[4,128,256]{2,1,0:T(8,128)S(1)}, f32[128,256]{1,0:T(8,128)S(1)}, f32[128,256]{1,0:T(8,128)S(1)}, f32[4,256]{1,0:T(4,128)S(1)}, /*index=5*/f32[4,256]{1,0:T(4,128)S(1)}) custom-call(f32[17]{0:T(128)S(1)} %fusion.proj_ref, f32[32,8,128]{2,1,0:T(8,128)} %copy-done.4, ...), custom_call_target="tpu_custom_call", output_to_operand_aliasing={{0}: (7, {})} | custom-call | flops 2000000000 | bytes 9961472 | tf_op jit(solution)/shard_map/pallas_call | solution.py:351
  171.1 1.2 collective-permute-start.11
  172.3 3.5 %collective-permute-start.12 = (f32[128,256]{1,0:T(8,128)S(1)}, f32[128,256]{1,0:T(8,128)S(1)}, u32[]{:S(2)}, u32[]{:S(2)}) collective-permute-start(f32[128,256]{1,0:T(8,128)S(1)} %get-tuple-element.59), channel_id=1, source_target_pairs={{4,0},{8,4},{12,8},{16,12},{20,16},{24,20},{28,24},{0,28},{5,1},{9... | collective-permute-start | bytes 393224 | tf_op jit(solution)/shard_map/ppermute | solution.py:785
  175.8 1.7 collective-permute-start.14
  177.5 1.3 collective-permute-done.13.refs_2_
  179.2 0.9 collective-permute-done.12.refs_1_
  180.1 2.3 %shard_map.134 = (f32[4,128,256]{2,1,0:T(8,128)S(1)}, f32[4,128,256]{2,1,0:T(8,128)S(1)}, f32[32,8,128]{2,1,0:T(8,128)S(1)}) custom-call(f32[32,8,128]{2,1,0:T(8,128)S(1)} %copy-done.5, f32[32,8,128]{2,1,0:T(8,128)S(1)} %copy-done.6, f32[4,128,256]{2,1,0:T(8,128)S(1)} %get-tuple-element.57.field_ref, f32[4,128,256]{2,1,0:T(8,128)S(1)} %get-tuple-element.47.field_ref.old_ref, ...), custom_call_target="tpu_custom_call" | custom-call | bytes 5767168 | tf_op jit(solution)/shard_map/pallas_call | solution.py:351
  182.5 12.7 %all_to_all.36.later_ref = f32[32,8,128]{2,1,0:T(8,128)S(1)} all-to-all(f32[32,8,128]{2,1,0:T(8,128)S(1)} %get-tuple-element.63), channel_id=1, replica_groups=mesh['row'=8,'col'=4] {'row','col'}, dimensions={0} | all-to-all | bytes 262144 | tf_op jit(solution)/shard_map/all_to_all | solution.py:771
  195.1 2.0 %shard_map.135 = (f32[4,128,256]{2,1,0:T(8,128)}, f32[4,128,256]{2,1,0:T(8,128)}) custom-call(f32[32,8,128]{2,1,0:T(8,128)S(1)} %copy-done.6, f32[32,8,128]{2,1,0:T(8,128)S(1)} %all_to_all.36.later_ref, f32[4,128,256]{2,1,0:T(8,128)S(1)} %get-tuple-element.47.field_ref.old_ref, f32[4,128,256]{2,1,0:T(8,128)S(1)} %get-tuple-element.64.way_ref, ...), custom_call_target="tpu_custom_call" | custom-call | bytes 3145728 | tf_op jit(solution)/shard_map/pallas_call | solution.py:351
  (39 shorter events, 1.3 us)
Async XLA Ops:
  0.6 36.0 %copy-start.11 = (f32[16,17]{1,0:T(8,128)S(1)}, f32[16,17]{1,0:T(8,128)}, u32[]{:S(2)}) copy-start(f32[16,17]{1,0:T(8,128)} %param.14) | copy-start | bytes 3268
  2.3 0.7 copy-start.1
  3.0 19.4 %collective-permute-start = (f32[4,16,8,128]{3,2,1,0:T(8,128)S(1)}, f32[4,16,8,128]{3,2,1,0:T(8,128)S(1)}, u32[]{:S(2)}, u32[]{:S(2)}) collective-permute-start(f32[4,16,8,128]{3,2,1,0:T(8,128)S(1)} %get-tuple-element.38), channel_id=1, source_target_pairs={{0,1},{1,2},{2,3},{3,0},{4,5},{5,6},{6,7},{7,4},{8,9},{9,10},{10,1... | collective-permute-start | bytes 786440 | tf_op jit(solution)/shard_map/ppermute | solution.py:827
  3.5 19.0 %collective-permute-start.1 = (f32[4,16,8,128]{3,2,1,0:T(8,128)S(1)}, f32[4,16,8,128]{3,2,1,0:T(8,128)S(1)}, u32[]{:S(2)}, u32[]{:S(2)}) collective-permute-start(f32[4,16,8,128]{3,2,1,0:T(8,128)S(1)} %get-tuple-element.39), channel_id=1, source_target_pairs={{0,2},{1,3},{2,0},{3,1},{4,6},{5,7},{6,4},{7,5},{8,10},{9,11},{10,... | collective-permute-start | bytes 786440 | tf_op jit(solution)/shard_map/ppermute | solution.py:827
  6.1 16.4 %collective-permute-start.2 = (f32[4,16,8,128]{3,2,1,0:T(8,128)S(1)}, f32[4,16,8,128]{3,2,1,0:T(8,128)S(1)}, u32[]{:S(2)}, u32[]{:S(2)}) collective-permute-start(f32[4,16,8,128]{3,2,1,0:T(8,128)S(1)} %get-tuple-element.40), channel_id=1, source_target_pairs={{0,3},{1,0},{2,1},{3,2},{4,7},{5,4},{6,5},{7,6},{8,11},{9,8},{10,9... | collective-permute-start | bytes 786440 | tf_op jit(solution)/shard_map/ppermute | solution.py:827
  9.3 13.1 %all-to-all-start = ((f32[32,8,128]{2,1,0:T(8,128)}), f32[32,8,128]{2,1,0:T(8,128)S(1)}, u32[]{:S(2)}, u32[]{:S(2)}) async-start(f32[32,8,128]{2,1,0:T(8,128)} %get-tuple-element.37), calls=%async_computation | async-start | bytes 262144 | tf_op jit(solution)/shard_map/all_to_all | solution.py:771
  22.5 0.6 copy-start.4
  22.5 0.8 copy-start.8
  22.5 0.8 copy-start.9
  23.3 0.7 copy-start.10
  33.1 19.0 %all-to-all-start.1 = ((f32[32,4,8,128]{3,2,1,0:T(8,128)}), f32[32,4,8,128]{3,2,1,0:T(8,128)S(1)}, u32[]{:S(2)}, u32[]{:S(2)}) async-start(f32[32,4,8,128]{3,2,1,0:T(8,128)} %get-tuple-element.41), calls=%async_computation.1 | async-start | bytes 1048576 | tf_op jit(solution)/shard_map/all_to_all | solution.py:771
  44.8 21.7 %copy-start.12 = (f32[17]{0:T(128)S(1)}, f32[17]{0:T(128)}, u32[]{:S(2)}) copy-start(f32[17]{0:T(128)} %param.15) | copy-start | bytes 208
  56.9 21.4 %all-to-all-start.2 = ((f32[32,4,8,128]{3,2,1,0:T(8,128)}), f32[32,4,8,128]{3,2,1,0:T(8,128)S(1)}, u32[]{:S(2)}, u32[]{:S(2)}) async-start(f32[32,4,8,128]{3,2,1,0:T(8,128)} %shard_map.125.__), calls=%async_computation.2 | async-start | bytes 1048576 | tf_op jit(solution)/shard_map/all_to_all | solution.py:771
  60.0 14.7 %collective-permute-start.5 = (f32[4,256]{1,0:T(4,128)S(1)}, f32[4,256]{1,0:T(4,128)S(1)}, u32[]{:S(2)}, u32[]{:S(2)}) collective-permute-start(f32[4,256]{1,0:T(4,128)S(1)} %get-tuple-element.45), channel_id=1, source_target_pairs={{0,1},{1,2},{2,3},{3,0},{4,5},{5,6},{6,7},{7,4},{8,9},{9,10},{10,1... | collective-permute-start | bytes 12296 | tf_op jit(solution)/shard_map/ppermute | solution.py:784
  60.3 14.4 %collective-permute-start.6 = (f32[4,256]{1,0:T(4,128)S(1)}, f32[4,256]{1,0:T(4,128)S(1)}, u32[]{:S(2)}, u32[]{:S(2)}) collective-permute-start(f32[4,256]{1,0:T(4,128)S(1)} %get-tuple-element.46), channel_id=1, source_target_pairs={{1,0},{2,1},{3,2},{0,3},{5,4},{6,5},{7,6},{4,7},{9,8},{10,9},{11,1... | collective-permute-start | bytes 12296 | tf_op jit(solution)/shard_map/ppermute | solution.py:785
  61.8 15.1 %collective-permute-start.3 = (f32[128,256]{1,0:T(8,128)S(1)}, f32[128,256]{1,0:T(8,128)S(1)}, u32[]{:S(2)}, u32[]{:S(2)}) collective-permute-start(f32[128,256]{1,0:T(8,128)S(1)} %get-tuple-element.43), channel_id=1, source_target_pairs={{0,4},{4,8},{8,12},{12,16},{16,20},{20,24},{24,28},{28,0},{1,5},{5... | collective-permute-start | bytes 393224 | tf_op jit(solution)/shard_map/ppermute | solution.py:784
  63.6 13.3 %collective-permute-start.4 = (f32[128,256]{1,0:T(8,128)S(1)}, f32[128,256]{1,0:T(8,128)S(1)}, u32[]{:S(2)}, u32[]{:S(2)}) collective-permute-start(f32[128,256]{1,0:T(8,128)S(1)} %get-tuple-element.44), channel_id=1, source_target_pairs={{4,0},{8,4},{12,8},{16,12},{20,16},{24,20},{28,24},{0,28},{5,1},{9... | collective-permute-start | bytes 393224 | tf_op jit(solution)/shard_map/ppermute | solution.py:785
  74.6 21.4 %copy-start = (f32[4,128,256]{2,1,0:T(8,128)S(1)}, f32[4,128,256]{2,1,0:T(8,128)}, u32[]{:S(2)}) copy-start(f32[4,128,256]{2,1,0:T(8,128)} %a_.3) | copy-start | bytes 1572868
  74.6 21.4 %copy-start.2 = (bf16[4,128,256]{2,1,0:T(8,128)(2,1)S(1)}, bf16[4,128,256]{2,1,0:T(8,128)(2,1)}, u32[]{:S(2)}) copy-start(bf16[4,128,256]{2,1,0:T(8,128)(2,1)} %perm_ref.9) | copy-start | bytes 786436
  87.3 8.1 %collective-permute-start.7 = (f32[128,256]{1,0:T(8,128)S(1)}, f32[128,256]{1,0:T(8,128)S(1)}, u32[]{:S(2)}, u32[]{:S(2)}) collective-permute-start(f32[128,256]{1,0:T(8,128)S(1)} %get-tuple-element.48), channel_id=1, source_target_pairs={{0,4},{4,8},{8,12},{12,16},{16,20},{20,24},{24,28},{28,0},{1,5},{5... | collective-permute-start | bytes 393224 | tf_op jit(solution)/shard_map/ppermute | solution.py:784
  88.2 7.8 %collective-permute-start.8 = (f32[128,256]{1,0:T(8,128)S(1)}, f32[128,256]{1,0:T(8,128)S(1)}, u32[]{:S(2)}, u32[]{:S(2)}) collective-permute-start(f32[128,256]{1,0:T(8,128)S(1)} %get-tuple-element.49), channel_id=1, source_target_pairs={{4,0},{8,4},{12,8},{16,12},{20,16},{24,20},{28,24},{0,28},{5,1},{9... | collective-permute-start | bytes 393224 | tf_op jit(solution)/shard_map/ppermute | solution.py:785
  92.1 3.0 %collective-permute-start.9 = (f32[4,256]{1,0:T(4,128)S(1)}, f32[4,256]{1,0:T(4,128)S(1)}, u32[]{:S(2)}, u32[]{:S(2)}) collective-permute-start(f32[4,256]{1,0:T(4,128)S(1)} %get-tuple-element.50), channel_id=1, source_target_pairs={{0,1},{1,2},{2,3},{3,0},{4,5},{5,6},{6,7},{7,4},{8,9},{9,10},{10,1... | collective-permute-start | bytes 12296 | tf_op jit(solution)/shard_map/ppermute | solution.py:784
  92.1 3.1 %collective-permute-start.10 = (f32[4,256]{1,0:T(4,128)S(1)}, f32[4,256]{1,0:T(4,128)S(1)}, u32[]{:S(2)}, u32[]{:S(2)}) collective-permute-start(f32[4,256]{1,0:T(4,128)S(1)} %get-tuple-element.51), channel_id=1, source_target_pairs={{1,0},{2,1},{3,2},{0,3},{5,4},{6,5},{7,6},{4,7},{9,8},{10,9},{11,1... | collective-permute-start | bytes 12296 | tf_op jit(solution)/shard_map/ppermute | solution.py:785
  120.5 18.2 %all-to-all-start.4 = ((f32[32,4,8,128]{3,2,1,0:T(8,128)}), f32[32,4,8,128]{3,2,1,0:T(8,128)S(1)}, u32[]{:S(2)}, u32[]{:S(2)}) async-start(f32[32,4,8,128]{3,2,1,0:T(8,128)} %get-tuple-element.54), calls=%async_computation.4 | async-start | bytes 1048576 | tf_op jit(solution)/shard_map/all_to_all | solution.py:771
  143.4 18.5 %all-to-all-start.5 = ((f32[32,4,8,128]{3,2,1,0:T(8,128)}), f32[32,4,8,128]{3,2,1,0:T(8,128)S(1)}, u32[]{:S(2)}, u32[]{:S(2)}) async-start(f32[32,4,8,128]{3,2,1,0:T(8,128)} %shard_map.131.__), calls=%async_computation.5 | async-start | bytes 1048576 | tf_op jit(solution)/shard_map/all_to_all | solution.py:771
  154.7 25.4 %copy-start.3 = (bf16[4,128,256]{2,1,0:T(8,128)(2,1)S(1)}, bf16[4,128,256]{2,1,0:T(8,128)(2,1)}, u32[]{:S(2)}) copy-start(bf16[4,128,256]{2,1,0:T(8,128)(2,1)} %perm_ref.9) | copy-start | bytes 786436
  154.7 25.4 %copy-start.5 = (f32[32,8,128]{2,1,0:T(8,128)S(1)}, f32[32,8,128]{2,1,0:T(8,128)}, u32[]{:S(2)}) copy-start(f32[32,8,128]{2,1,0:T(8,128)} %copy-done.4) | copy-start | bytes 393220
  154.7 25.4 %copy-start.6 = (f32[32,8,128]{2,1,0:T(8,128)S(1)}, f32[32,8,128]{2,1,0:T(8,128)}, u32[]{:S(2)}) copy-start(f32[32,8,128]{2,1,0:T(8,128)} %all_to_all.35.sums_ref) | copy-start | bytes 393220
  154.7 25.4 %copy-start.7 = (f32[4,128,256]{2,1,0:T(8,128)S(1)}, f32[4,128,256]{2,1,0:T(8,128)}, u32[]{:S(2)}) copy-start(f32[4,128,256]{2,1,0:T(8,128)} %get-tuple-element.62.refs_12_.res_ref) | copy-start | bytes 1572868
  171.1 8.1 %collective-permute-start.11 = (f32[128,256]{1,0:T(8,128)S(1)}, f32[128,256]{1,0:T(8,128)S(1)}, u32[]{:S(2)}, u32[]{:S(2)}) collective-permute-start(f32[128,256]{1,0:T(8,128)S(1)} %get-tuple-element.58), channel_id=1, source_target_pairs={{0,4},{4,8},{8,12},{12,16},{16,20},{20,24},{24,28},{28,0},{1,5},{5... | collective-permute-start | bytes 393224 | tf_op jit(solution)/shard_map/ppermute | solution.py:784
  172.3 7.8 %collective-permute-start.12 = (f32[128,256]{1,0:T(8,128)S(1)}, f32[128,256]{1,0:T(8,128)S(1)}, u32[]{:S(2)}, u32[]{:S(2)}) collective-permute-start(f32[128,256]{1,0:T(8,128)S(1)} %get-tuple-element.59), channel_id=1, source_target_pairs={{4,0},{8,4},{12,8},{16,12},{20,16},{24,20},{28,24},{0,28},{5,1},{9... | collective-permute-start | bytes 393224 | tf_op jit(solution)/shard_map/ppermute | solution.py:785
  175.8 3.0 %collective-permute-start.13 = (f32[4,256]{1,0:T(4,128)S(1)}, f32[4,256]{1,0:T(4,128)S(1)}, u32[]{:S(2)}, u32[]{:S(2)}) collective-permute-start(f32[4,256]{1,0:T(4,128)S(1)} %get-tuple-element.60), channel_id=1, source_target_pairs={{0,1},{1,2},{2,3},{3,0},{4,5},{5,6},{6,7},{7,4},{8,9},{9,10},{10,1... | collective-permute-start | bytes 12296 | tf_op jit(solution)/shard_map/ppermute | solution.py:784
  175.8 3.1 %collective-permute-start.14 = (f32[4,256]{1,0:T(4,128)S(1)}, f32[4,256]{1,0:T(4,128)S(1)}, u32[]{:S(2)}, u32[]{:S(2)}) collective-permute-start(f32[4,256]{1,0:T(4,128)S(1)} %get-tuple-element.61), channel_id=1, source_target_pairs={{1,0},{2,1},{3,2},{0,3},{5,4},{6,5},{7,6},{4,7},{9,8},{10,9},{11,1... | collective-permute-start | bytes 12296 | tf_op jit(solution)/shard_map/ppermute | solution.py:785

commit v6 on v5

--- a/solution.py
+++ b/solution.py
@@ -226,6 +226,7 @@
 LANES = 128
 SUBLANES = 8
 BOTH = ("row", "col")
+CHUNK = 32
 F32 = jnp.float32
 BF16 = jnp.bfloat16
 
@@ -380,7 +381,7 @@
     return jnp.sum(total[row : row + 1], axis=1, keepdims=True)
 
 
-def squares_body(field_ref, perm_ref, _, out_ref, low_ref, high_ref, left_ref, right_ref):
+def squares_body(field_ref, perm_ref, out_ref, low_ref, high_ref, left_ref, right_ref):
     total = field_ref[0] * field_ref[0]
     for place in range(1, field_ref.shape[0]):
         total = total + field_ref[place] * field_ref[place]
@@ -419,16 +420,31 @@
     )
 
 
-def transform(lift_ref, deep_ref, col_ref, scaled, log_perm, spectra_ref, lifted_ref, zt_ref):
+def transform(lift_ref, deep_ref, col_ref, scaled, log_perm, spectra_ref, lifted_ref, *refs):
+    zt_ref, scaled_ref, log_ref, high_ref, low_ref = refs
     half = 2 * KZ
-    cols = scaled.shape[1]
-    for channel in range(0, CHANNELS, 2):
-        pair = [lift_channel(lift_ref, channel + j, scaled, log_perm) for j in range(2)]
+    depth, cols = scaled.shape
+    scaled_ref[...] = scaled
+    log_ref[...] = log_perm
+
+    def lift(pair):
         for j in range(2):
-            lifted_ref[0, channel + j] = pair[j]
-        high, low = split(jnp.concatenate(pair, 1))
-        part = matmul(deep_ref[...], high)
-        part = part[:half] + part[half:] + matmul(deep_ref[:half], low)
+            channel = 2 * pair + j
+            for start in range(0, depth, CHUNK):
+                lines = slice(start, start + CHUNK)
+                lifted = lift_channel(lift_ref, channel, scaled_ref[lines], log_ref[lines])
+                lifted_ref[0, channel, lines] = lifted
+                high, low = split(lifted)
+                high_ref[pair, lines, j * cols : (j + 1) * cols] = high
+                low_ref[pair, lines, j * cols : (j + 1) * cols] = low
+
+    lift(0)
+    for pair in range(CHANNELS // 2):
+        if pair + 1 < CHANNELS // 2:
+            lift(pair + 1)
+        channel = 2 * pair
+        part = matmul(deep_ref[...], high_ref[pair])
+        part = part[:half] + part[half:] + matmul(deep_ref[:half], low_ref[pair])
         for j in range(2):
             zt_ref[pl.ds(channel + j, half, stride=CHANNELS), :] = part[:, j * cols : (j + 1) * cols]
     groups = half * CHANNELS // LANES
@@ -445,11 +461,11 @@
 
 
 def lift_first_body(cells, lift_ref, sums_ref, res_ref, perm_ref, deep_ref, col_ref, *refs):
-    spectra_ref, lifted_ref, zt_ref = refs[-3:]
+    spectra_ref, lifted_ref, *scratch = refs
     scale = scale_of(gathered(sums_ref, 0), cells)
     scaled = (res_ref[0] / scale).T
     log_perm = jnp.log(perm_ref[0].astype(F32)).T
-    transform(lift_ref, deep_ref, col_ref, scaled, log_perm, spectra_ref, lifted_ref, zt_ref)
+    transform(lift_ref, deep_ref, col_ref, scaled, log_perm, spectra_ref, lifted_ref, *scratch)
 
 
 def next_scalars(first_ref, sums_ref):
@@ -461,17 +477,18 @@
     return curvature, alpha, jnp.maximum(total, 0.0)
 
 
-def lift_next_body(cells, lift_ref, first_ref, sums_ref, res_ref, image_ref, perm_ref, deep_ref, col_ref, spectra_ref, lifted_ref, next_ref, zt_ref):
+def lift_next_body(cells, lift_ref, first_ref, sums_ref, res_ref, image_ref, perm_ref, deep_ref, col_ref, spectra_ref, lifted_ref, next_ref, *scratch):
     _, alpha, total = next_scalars(first_ref, sums_ref)
     scale = scale_of(total, cells)
     residual = res_ref[0] - alpha * image_ref[0]
     next_ref[0] = residual
     scaled = (residual / scale).T
     log_perm = jnp.log(perm_ref[0].astype(F32)).T
-    transform(lift_ref, deep_ref, col_ref, scaled, log_perm, spectra_ref, lifted_ref, zt_ref)
-
-
-def point_body(mix_ref, lifted_ref, _, __, point_ref):
+    transform(lift_ref, deep_ref, col_ref, scaled, log_perm, spectra_ref, lifted_ref, *scratch)
+
+
+def point_body(mix_ref, lifted_ref, *refs):
+    point_ref = refs[-1]
     size = 4 * SUBLANES
     group = 4
 
@@ -600,7 +617,7 @@
             store(places - place, even - odd)
 
 
-def back_transform(recv_ref, point_ref, proj_ref, col_ref, deep_ref, wave_ref, scale):
+def back_transform(recv_ref, point_ref, proj_ref, col_ref, deep_ref, wave_ref, total_ref, scale):
     groups = 2 * KZ * CHANNELS // LANES
     n_col = KY // SUBLANES
     cols = col_ref.shape[2] // 2
@@ -615,18 +632,24 @@
         pieces.append(jnp.concatenate(split_three(both), 0).T.astype(BF16))
     part = matmul(jnp.concatenate(pieces, 0), col_ref[lax.axis_index("col")])
     wave_ref[...] = part[:, :cols] + part[:, cols:]
-    total = None
+
+    def waves(out):
+        both = [wave_ref[pl.ds(out + j, half, stride=CHANNELS), :] for j in range(2)]
+        high, middle, low = (
+            part.astype(BF16) for part in split_three(jnp.concatenate(both, 1))
+        )
+        return jnp.concatenate([high, middle, low, high], 0)
+
     for out in range(0, CHANNELS, 2):
-        waves = jnp.concatenate(
-            [wave_ref[pl.ds(out + j, half, stride=CHANNELS), :] for j in range(2)], 1
-        )
-        high, middle, low = (part.astype(BF16) for part in split_three(waves))
-        spatial = matmul(deep_ref[...], jnp.concatenate([high, middle, low, high], 0))
-        for j in range(2):
-            hidden = scaled_gelu(spatial[:, j * cols : (j + 1) * cols] + point_ref[0, out + j])
-            term = proj_ref[out + j] * hidden
-            total = term if total is None else total + term
-    return (scale * (total + proj_ref[CHANNELS])).T
+        spatial = matmul(deep_ref[...], waves(out))
+        for start in range(0, spatial.shape[0], CHUNK):
+            lines = slice(start, start + CHUNK)
+            total = proj_ref[CHANNELS] if out == 0 else total_ref[lines]
+            for j in range(2):
+                value = spatial[lines, j * cols : (j + 1) * cols] + point_ref[0, out + j, lines]
+                total = total + proj_ref[out + j] * scaled_gelu(value)
+            total_ref[lines] = total
+    return (scale * total_ref[...]).T
 
 
 def put_edges(update, field_ref, low_ref, high_ref, left_ref, right_ref):
@@ -645,20 +668,20 @@
 
 
 def back_first_body(cells, proj_ref, sums_ref, recv_ref, point_ref, col_ref, deep_ref, *refs):
-    kept_ref, *edges, wave_ref = refs[4:]
+    kept_ref, *edges, wave_ref, total_ref = refs[4:]
     scale = scale_of(gathered(sums_ref, 0), cells)
     update = back_transform(
-        recv_ref, point_ref, proj_ref, col_ref, deep_ref, wave_ref, scale
+        recv_ref, point_ref, proj_ref, col_ref, deep_ref, wave_ref, total_ref, scale
     )
     kept_ref[0, 0] = update
     put_edges(update, *edges)
 
 
 def back_next_body(cells, proj_ref, first_ref, sums_ref, recv_ref, point_ref, col_ref, deep_ref, _, kept_ref, *refs):
-    *edges, wave_ref = refs
+    *edges, wave_ref, total_ref = refs
     _, _, total = next_scalars(first_ref, sums_ref)
     update = back_transform(
-        recv_ref, point_ref, proj_ref, col_ref, deep_ref, wave_ref, scale_of(total, cells)
+        recv_ref, point_ref, proj_ref, col_ref, deep_ref, wave_ref, total_ref, scale_of(total, cells)
     )
     kept_ref[0, 0] = update
     put_edges(update, *edges)
@@ -831,29 +854,33 @@
     squares, *perm_edges = call(
         squares_body,
         (partial,) + edge_shapes,
-        [vmem, vmem, anywhere],
+        [vmem, vmem],
         (vmem,) * 5,
         moved=2 * field_bytes,
-    )(right_side, permeability, own)
+    )(right_side, permeability)
     squares = add_up(squares)
     perm_halo = neighbours(*perm_edges)
     acc_scratch = pltpu.VMEM((SUBLANES, LANES), F32)
+    plane_scratch = pltpu.VMEM((depth, cols), F32)
+    part_scratch = pltpu.VMEM((CHANNELS // 2, depth, 2 * cols), BF16)
     zt_scratch = pltpu.VMEM((2 * KZ * CHANNELS, cols), F32)
-
-    def points(lifted, part, before, after):
+    lift_scratch = [zt_scratch, plane_scratch, plane_scratch, part_scratch, part_scratch]
+
+    def points(lifted, part, *others):
         first = part * rows // 2
         half_block = pl.BlockSpec((1, CHANNELS, depth, cols), lambda i: (first + i, 0, 0, 0))
         return call(
             point_body,
             channels,
-            [smem, half_block, anywhere, anywhere],
+            [smem, half_block] + [anywhere] * len(others),
             half_block,
             grid=(rows // 2,),
             flops=2.5e9,
             moved=16 * field_bytes,
             alias={2: 0} if part else None,
             limit=12,
-        )(mix_weight, lifted, before, after)
+            near=range(3, 2 + len(others)),
+        )(mix_weight, lifted, *others)
 
     def modes(received, before):
         places = rows * n_row
@@ -875,9 +902,9 @@
             near=(0,),
         )(received, *weights, before)
 
-    def mixed_modes(blocks, lifted):
+    def mixed_modes(blocks, lifted, others):
         received = exchange(blocks)
-        point = points(lifted, 0, right_side, right_side)
+        point = points(lifted, 0, *others)
         blocks = modes(received, point)
         received = exchange(blocks)
         point = points(lifted, 1, point, blocks)
@@ -886,15 +913,15 @@
     blocks, lifted = call(
         functools.partial(lift_first_body, cells),
         (spectra, channels),
-        [smem, vmem, plane, plane, vmem, vmem] + [anywhere] * n_col,
+        [smem, vmem, plane, plane, vmem, vmem],
         (spectra_block, point_block),
         limit=16,
         grid=(rows,),
-        scratch=[zt_scratch],
+        scratch=lift_scratch,
         flops=lift_flops,
         moved=2 * field_bytes + spectra_bytes,
-    )(lift_weight, squares, right_side, permeability, deep_forward, col_forward, *weights)
-    received, point = mixed_modes(blocks, lifted)
+    )(lift_weight, squares, right_side, permeability, deep_forward, col_forward)
+    received, point = mixed_modes(blocks, lifted, weights)
     kept, old, *edges = call(
         functools.partial(back_first_body, cells),
         (kept_shape, field) + edge_shapes,
@@ -903,7 +930,7 @@
         near=(2, 6, 7, 8, 9),
         loose=(1,),
         grid=(rows,),
-        scratch=[zt_scratch],
+        scratch=[zt_scratch, plane_scratch],
         limit=12,
         flops=back_flops,
         moved=18 * field_bytes,
@@ -932,11 +959,11 @@
         limit=16,
         near=(4,),
         grid=(rows,),
-        scratch=[zt_scratch],
+        scratch=lift_scratch,
         flops=lift_flops,
         moved=4 * field_bytes + spectra_bytes,
     )(lift_weight, squares, sums, right_side, image, permeability, deep_forward, col_forward)
-    received, point = mixed_modes(blocks, lifted)
+    received, point = mixed_modes(blocks, lifted, ())
     kept, update, *edges = call(
         functools.partial(back_next_body, cells),
         (kept_shape, field) + edge_shapes,
@@ -946,7 +973,7 @@
         loose=(1,),
         grid=(rows,),
         limit=12,
-        scratch=[zt_scratch],
+        scratch=[zt_scratch, plane_scratch],
         flops=back_flops,
         moved=19 * field_bytes,
         alias={7: 0},

time: 198 us -> 209 us (1.056)
  waiting for transfers between devices: 37.9 us -> 41.9 us
  Pallas kernels: 88.5 us -> 91.7 us
  starting transfers between devices: 41.1 us -> 43.4 us
    ppermute x3, waiting for transfers between devices: 0.01 us -> 13.5 us  [tiled_local(): lax.ppermute(part, 'col', [(i, (i + shift + 1) % n_col) for i in range(n_...]
    all_to_all x5, waiting for transfers between devices: 30.9 us -> 22.5 us  [exchange(): return lax.all_to_all(blocks, BOTH, split_axis=0, concat_axis=0, tiled=True)]
    all_to_all x5, starting transfers between devices: 17.2 us -> 20.8 us  [exchange(): return lax.all_to_all(blocks, BOTH, split_axis=0, concat_axis=0, tiled=True)]
    pallas_call x15, Pallas kernels: 88.5 us -> 91.7 us  [wrapped(): found = run(*held)]
  transfers between devices with their start and end apart: 20 -> 20, of which waited for: 12 -> 14; matrix products, arithmetic and copies ran while one was open for 0% -> 0% of each run, Pallas kernels for 18% -> 17%
where the time goes in v6:
time: 209 us; the launch traced here: 208 us
  Pallas kernels  91.7 us (44%)
  starting transfers between devices  43.4 us (21%)
  waiting for transfers between devices  41.9 us (20%)
  blocking collectives  25.8 us (12%)
  local copies, waits for them, and re-layouts  3.51 us (2%)
    pallas_call x15, Pallas kernels, wrapped(): found = run(*held)  91.7 us
    all_to_all x2, blocking collectives, exchange(): return lax.all_to_all(blocks, BOTH, split_axis=0, concat_axis=0, tiled=True)  25.8 us
    all_to_all x5, waiting for transfers between devices, exchange(): return lax.all_to_all(blocks, BOTH, split_axis=0, concat_axis=0, tiled=True)  22.5 us
    all_to_all x5, starting transfers between devices, exchange(): return lax.all_to_all(blocks, BOTH, split_axis=0, concat_axis=0, tiled=True)  20.8 us
    ppermute x6, starting transfers between devices, neighbours(): found.append(lax.ppermute(first, axis, backward))  15.2 us
    ppermute x3, waiting for transfers between devices, tiled_local(): lax.ppermute(part, 'col', [(i, (i + shift + 1) % n_col) for i in range(n_...  13.5 us
    ppermute x6, waiting for transfers between devices, neighbours(): found.append(lax.ppermute(last, axis, forward))  4.35 us
    ppermute x6, starting transfers between devices, neighbours(): found.append(lax.ppermute(last, axis, forward))  4.25 us
  transfers between devices with their start and end apart: 20, of which 14 were waited for; matrix products, arithmetic and copies ran while one was open for 0% of the time, Pallas kernels for 17%

profile of v6, /device:TPU:0, one launch (start us, length us, event | category | flops | bytes accessed | tf_op | source)
XLA Modules:
  0.0 207.8 jit_solution(7718729960126702266)
XLA Ops:
  0.6 1.8 shard_map.121
  2.5 7.3 %all-to-all-start = ((f32[32,8,128]{2,1,0:T(8,128)}), f32[32,8,128]{2,1,0:T(8,128)S(1)}, u32[]{:S(2)}, u32[]{:S(2)}) async-start(f32[32,8,128]{2,1,0:T(8,128)} %get-tuple-element.36), calls=%async_computation | async-start | bytes 262144 | tf_op jit(solution)/shard_map/all_to_all | solution.py:794
  9.8 0.7 multiply_bitcast_fusion.lift_ref
  10.5 7.5 %all-to-all-done.sums_ref.first_ref = f32[32,8,128]{2,1,0:T(8,128)S(1)} async-done(((f32[32,8,128]{2,1,0:T(8,128)}), f32[32,8,128]{2,1,0:T(8,128)S(1)}, u32[]{:S(2)}, u32[]{:S(2)}) %all-to-all-start) | async-done | bytes 131104 | tf_op jit(solution)/shard_map/all_to_all | solution.py:794
  18.0 0.7 copy-done.8
  18.7 10.6 %shard_map.122 = (f32[32,4,8,128]{3,2,1,0:T(8,128)}, f32[4,16,256,128]{3,2,1,0:T(8,128)}) custom-call(f32[3,16]{1,0:T(4,128)S(1)} %multiply_bitcast_fusion.lift_ref, f32[32,8,128]{2,1,0:T(8,128)} %copy-done.8, f32[4,128,256]{2,1,0:T(8,128)} %res_ref.3, bf16[4,128,256]{2,1,0:T(8,128)(2,1)} %perm_ref.9, bf16[128,256]{1,0:T(8,128)(2,1)} %constant.8.clone.deep_ref, ...), custom_call_target="tpu_custom_call" | custom-call | flops 2000000000 | bytes 1572864 | tf_op jit(solution)/shard_map/pallas_call | solution.py:352
  29.3 2.6 %all-to-all-start.1 = ((f32[32,4,8,128]{3,2,1,0:T(8,128)}), f32[32,4,8,128]{3,2,1,0:T(8,128)S(1)}, u32[]{:S(2)}, u32[]{:S(2)}) async-start(f32[32,4,8,128]{3,2,1,0:T(8,128)} %get-tuple-element.37), calls=%async_computation.1 | async-start | bytes 1048576 | tf_op jit(solution)/shard_map/all_to_all | solution.py:794
  31.9 1.7 shard_map.123
  33.6 0.7 copy-done.2
  34.4 1.7 collective-permute-start.1
  36.1 1.3 collective-permute-start.2
  37.4 8.7 %collective-permute-done.refs_1_ = f32[4,16,8,128]{3,2,1,0:T(8,128)S(1)} collective-permute-done((f32[4,16,8,128]{3,2,1,0:T(8,128)S(1)}, f32[4,16,8,128]{3,2,1,0:T(8,128)S(1)}, u32[]{:S(2)}, u32[]{:S(2)}) %collective-permute-start) | collective-permute-done | bytes 262176 | tf_op jit(solution)/shard_map/ppermute | solution.py:850
  46.7 4.2 %collective-permute-done.2.refs_3_ = f32[4,16,8,128]{3,2,1,0:T(8,128)S(1)} collective-permute-done((f32[4,16,8,128]{3,2,1,0:T(8,128)S(1)}, f32[4,16,8,128]{3,2,1,0:T(8,128)S(1)}, u32[]{:S(2)}, u32[]{:S(2)}) %collective-permute-start.2) | collective-permute-done | bytes 262176 | tf_op jit(solution)/shard_map/ppermute | solution.py:850
  50.9 8.3 %shard_map.124.refs_4_.refs_0_ = f32[4,16,256,128]{3,2,1,0:T(8,128)} custom-call(f32[16,17]{1,0:T(8,128)S(1)} %broadcast_multiply_fusion.mix_ref, f32[4,16,256,128]{3,2,1,0:T(8,128)} %get-tuple-element.42.lifted_ref, f32[4,16,8,128]{3,2,1,0:T(8,128)} %copy-done.2, f32[4,16,8,128]{3,2,1,0:T(8,128)S(1)} %collective-permute-done.refs_1_, ...), custom_call_target="tpu_custom_call" | custom-call | flops 2500000000 | bytes 8388608 | tf_op jit(solution)/shard_map/pallas_call | solution.py:352
  59.2 4.8 %shard_map.125.refs_1_ = f32[32,4,8,128]{3,2,1,0:T(8,128)} custom-call(f32[32,4,8,128]{3,2,1,0:T(8,128)S(1)} %all-to-all-done.1.recv_ref, f32[4,16,8,128]{3,2,1,0:T(8,128)} %copy-done.2, f32[4,16,8,128]{3,2,1,0:T(8,128)} %copy-done.3, f32[4,16,8,128]{3,2,1,0:T(8,128)} %copy-done.4, f32[4,16,8,128]{3,2,1,0:T(8,128)} %copy-done.5, ...), custom_call_target="tpu_custom_call" | custom-call | bytes 2097152 | tf_op jit(solution)/shard_map/pallas_call | solution.py:352
  64.0 5.2 %all-to-all-start.2 = ((f32[32,4,8,128]{3,2,1,0:T(8,128)}), f32[32,4,8,128]{3,2,1,0:T(8,128)S(1)}, u32[]{:S(2)}, u32[]{:S(2)}) async-start(f32[32,4,8,128]{3,2,1,0:T(8,128)} %shard_map.125.refs_1_), calls=%async_computation.2 | async-start | bytes 1048576 | tf_op jit(solution)/shard_map/all_to_all | solution.py:794
  69.5 1.5 collective-permute-start.6
  71.0 1.8 collective-permute-start.3
  72.8 3.0 %collective-permute-start.4 = (f32[128,256]{1,0:T(8,128)S(1)}, f32[128,256]{1,0:T(8,128)S(1)}, u32[]{:S(2)}, u32[]{:S(2)}) collective-permute-start(f32[128,256]{1,0:T(8,128)S(1)} %get-tuple-element.44), channel_id=1, source_target_pairs={{4,0},{8,4},{12,8},{16,12},{20,16},{24,20},{28,24},{0,28},{5,1},{9... | collective-permute-start | bytes 393224 | tf_op jit(solution)/shard_map/ppermute | solution.py:808
  75.7 1.0 copy-done
  76.8 8.1 %shard_map.126.point_ref = f32[4,16,256,128]{3,2,1,0:T(8,128)} custom-call(f32[16,17]{1,0:T(8,128)S(1)} %broadcast_multiply_fusion.mix_ref, f32[4,16,256,128]{3,2,1,0:T(8,128)} %get-tuple-element.42.lifted_ref, f32[4,16,256,128]{3,2,1,0:T(8,128)} %shard_map.124.refs_4_.refs_0_, f32[32,4,8,128]{3,2,1,0:T(8,128)S(1)} %copy-done), custom_call_target="tpu_custom_call", output_to_operand_aliasing={{}: (2, {})} | custom-call | flops 2500000000 | bytes 8388608 | tf_op jit(solution)/shard_map/pallas_call | solution.py:352
  84.9 1.2 collective-permute-done.3.refs_0_.refs_4_.refs_8_
  86.1 1.5 all-to-all-done.2.recv_ref
  87.5 9.0 %shard_map.127 = (f32[2,4,128,256]{3,2,1,0:T(8,128)}, f32[4,128,256]{2,1,0:T(8,128)S(1)}, f32[128,256]{1,0:T(8,128)S(1)}, f32[128,256]{1,0:T(8,128)S(1)}, f32[4,256]{1,0:T(4,128)S(1)}, /*index=5*/f32[4,256]{1,0:T(4,128)S(1)}) custom-call(f32[17]{0:T(128)S(1)} %fusion.proj_ref, f32[32,8,128]{2,1,0:T(8,128)} %copy-done.8, ...), custom_call_target="tpu_custom_call" | custom-call | flops 2000000000 | bytes 9437184 | tf_op jit(solution)/shard_map/pallas_call | solution.py:352
  96.5 0.9 collective-permute-start.7
  97.5 3.8 %collective-permute-start.8 = (f32[128,256]{1,0:T(8,128)S(1)}, f32[128,256]{1,0:T(8,128)S(1)}, u32[]{:S(2)}, u32[]{:S(2)}) collective-permute-start(f32[128,256]{1,0:T(8,128)S(1)} %get-tuple-element.49), channel_id=1, source_target_pairs={{4,0},{8,4},{12,8},{16,12},{20,16},{24,20},{28,24},{0,28},{5,1},{9... | collective-permute-start | bytes 393224 | tf_op jit(solution)/shard_map/ppermute | solution.py:808
  101.3 1.7 collective-permute-start.10
  103.0 1.3 collective-permute-done.9.refs_2_.refs_6_
  105.2 1.9 shard_map.128
  107.2 13.1 %all_to_all.35.sums_ref = f32[32,8,128]{2,1,0:T(8,128)} all-to-all(f32[32,8,128]{2,1,0:T(8,128)S(1)} %get-tuple-element.52), channel_id=1, replica_groups=mesh['row'=8,'col'=4] {'row','col'}, dimensions={0} | all-to-all | bytes 262144 | tf_op jit(solution)/shard_map/all_to_all | solution.py:794
  120.3 10.9 %shard_map.129 = (f32[32,4,8,128]{3,2,1,0:T(8,128)}, f32[4,16,256,128]{3,2,1,0:T(8,128)}, f32[4,128,256]{2,1,0:T(8,128)}) custom-call(f32[3,16]{1,0:T(4,128)S(1)} %multiply_bitcast_fusion.lift_ref, f32[32,8,128]{2,1,0:T(8,128)} %copy-done.8, f32[32,8,128]{2,1,0:T(8,128)} %all_to_all.35.sums_ref, f32[4,128,256]{2,1,0:T(8,128)} %res_ref.3, ...), custom_call_target="tpu_custom_call" | custom-call | flops 2000000000 | bytes 2621440 | tf_op jit(solution)/shard_map/pallas_call | solution.py:352
  131.2 2.6 %all-to-all-start.4 = ((f32[32,4,8,128]{3,2,1,0:T(8,128)}), f32[32,4,8,128]{3,2,1,0:T(8,128)S(1)}, u32[]{:S(2)}, u32[]{:S(2)}) async-start(f32[32,4,8,128]{3,2,1,0:T(8,128)} %get-tuple-element.54), calls=%async_computation.4 | async-start | bytes 1048576 | tf_op jit(solution)/shard_map/all_to_all | solution.py:794
  133.8 8.2 %shard_map.130.refs_4_.refs_0_ = f32[4,16,256,128]{3,2,1,0:T(8,128)} custom-call(f32[16,17]{1,0:T(8,128)S(1)} %broadcast_multiply_fusion.mix_ref, f32[4,16,256,128]{3,2,1,0:T(8,128)} %get-tuple-element.55.lifted_ref), custom_call_target="tpu_custom_call" | custom-call | flops 2500000000 | bytes 8388608 | tf_op jit(solution)/shard_map/pallas_call | solution.py:352
  142.0 7.3 %all-to-all-done.4.recv_ref = f32[32,4,8,128]{3,2,1,0:T(8,128)S(1)} async-done(((f32[32,4,8,128]{3,2,1,0:T(8,128)}), f32[32,4,8,128]{3,2,1,0:T(8,128)S(1)}, u32[]{:S(2)}, u32[]{:S(2)}) %all-to-all-start.4) | async-done | bytes 524320 | tf_op jit(solution)/shard_map/all_to_all | solution.py:794
  149.4 4.8 %shard_map.131.refs_1_ = f32[32,4,8,128]{3,2,1,0:T(8,128)} custom-call(f32[32,4,8,128]{3,2,1,0:T(8,128)S(1)} %all-to-all-done.4.recv_ref, f32[4,16,8,128]{3,2,1,0:T(8,128)} %copy-done.2, f32[4,16,8,128]{3,2,1,0:T(8,128)} %copy-done.3, f32[4,16,8,128]{3,2,1,0:T(8,128)} %copy-done.4, f32[4,16,8,128]{3,2,1,0:T(8,128)} %copy-done.5, ...), custom_call_target="tpu_custom_call" | custom-call | bytes 2097152 | tf_op jit(solution)/shard_map/pallas_call | solution.py:352
  154.2 3.2 %all-to-all-start.5 = ((f32[32,4,8,128]{3,2,1,0:T(8,128)}), f32[32,4,8,128]{3,2,1,0:T(8,128)S(1)}, u32[]{:S(2)}, u32[]{:S(2)}) async-start(f32[32,4,8,128]{3,2,1,0:T(8,128)} %shard_map.131.refs_1_), calls=%async_computation.5 | async-start | bytes 1048576 | tf_op jit(solution)/shard_map/all_to_all | solution.py:794
  157.3 1.1 copy-done.1
  158.4 8.1 %shard_map.132.point_ref = f32[4,16,256,128]{3,2,1,0:T(8,128)} custom-call(f32[16,17]{1,0:T(8,128)S(1)} %broadcast_multiply_fusion.mix_ref, f32[4,16,256,128]{3,2,1,0:T(8,128)} %get-tuple-element.55.lifted_ref, f32[4,16,256,128]{3,2,1,0:T(8,128)} %shard_map.130.refs_4_.refs_0_, f32[32,4,8,128]{3,2,1,0:T(8,128)S(1)} %copy-done.1), custom_call_target="tpu_custom_call", output_to_operand_aliasing={{}: (2, {})} | custom-call | flops 2500000000 | bytes 8388608 | tf_op jit(solution)/shard_map/pallas_call | solution.py:352
  166.5 6.2 %all-to-all-done.5.recv_ref = f32[32,4,8,128]{3,2,1,0:T(8,128)S(1)} async-done(((f32[32,4,8,128]{3,2,1,0:T(8,128)}), f32[32,4,8,128]{3,2,1,0:T(8,128)S(1)}, u32[]{:S(2)}, u32[]{:S(2)}) %all-to-all-start.5) | async-done | bytes 524320 | tf_op jit(solution)/shard_map/all_to_all | solution.py:794
  172.7 9.1 %shard_map.133 = (f32[2,4,128,256]{3,2,1,0:T(8,128)}, f32[4,128,256]{2,1,0:T(8,128)S(1)}, f32[128,256]{1,0:T(8,128)S(1)}, f32[128,256]{1,0:T(8,128)S(1)}, f32[4,256]{1,0:T(4,128)S(1)}, /*index=5*/f32[4,256]{1,0:T(4,128)S(1)}) custom-call(f32[17]{0:T(128)S(1)} %fusion.proj_ref, f32[32,8,128]{2,1,0:T(8,128)} %copy-done.8, ...), custom_call_target="tpu_custom_call", output_to_operand_aliasing={{0}: (7, {})} | custom-call | flops 2000000000 | bytes 9961472 | tf_op jit(solution)/shard_map/pallas_call | solution.py:352
  181.8 1.3 collective-permute-start.11
  183.0 3.5 %collective-permute-start.12 = (f32[128,256]{1,0:T(8,128)S(1)}, f32[128,256]{1,0:T(8,128)S(1)}, u32[]{:S(2)}, u32[]{:S(2)}) collective-permute-start(f32[128,256]{1,0:T(8,128)S(1)} %get-tuple-element.59), channel_id=1, source_target_pairs={{4,0},{8,4},{12,8},{16,12},{20,16},{24,20},{28,24},{0,28},{5,1},{9... | collective-permute-start | bytes 393224 | tf_op jit(solution)/shard_map/ppermute | solution.py:808
  186.5 1.7 collective-permute-start.14
  188.3 1.3 collective-permute-done.13.refs_2_
  189.9 0.9 collective-permute-done.12.refs_1_
  190.8 2.3 %shard_map.134 = (f32[4,128,256]{2,1,0:T(8,128)S(1)}, f32[4,128,256]{2,1,0:T(8,128)S(1)}, f32[32,8,128]{2,1,0:T(8,128)S(1)}) custom-call(f32[32,8,128]{2,1,0:T(8,128)S(1)} %copy-done.9, f32[32,8,128]{2,1,0:T(8,128)S(1)} %copy-done.10, f32[4,128,256]{2,1,0:T(8,128)S(1)} %get-tuple-element.57.field_ref, ...), custom_call_target="tpu_custom_call" | custom-call | bytes 5767168 | tf_op jit(solution)/shard_map/pallas_call | solution.py:352
  193.2 12.7 %all_to_all.36.later_ref = f32[32,8,128]{2,1,0:T(8,128)S(1)} all-to-all(f32[32,8,128]{2,1,0:T(8,128)S(1)} %get-tuple-element.63), channel_id=1, replica_groups=mesh['row'=8,'col'=4] {'row','col'}, dimensions={0} | all-to-all | bytes 262144 | tf_op jit(solution)/shard_map/all_to_all | solution.py:794
  205.8 2.0 shard_map.135
  (43 shorter events, 2.4 us)
Async XLA Ops:
  0.6 36.8 %copy-start.13 = (f32[16,17]{1,0:T(8,128)S(1)}, f32[16,17]{1,0:T(8,128)}, u32[]{:S(2)}) copy-start(f32[16,17]{1,0:T(8,128)} %param.14) | copy-start | bytes 3268
  2.5 15.5 %all-to-all-start = ((f32[32,8,128]{2,1,0:T(8,128)}), f32[32,8,128]{2,1,0:T(8,128)S(1)}, u32[]{:S(2)}, u32[]{:S(2)}) async-start(f32[32,8,128]{2,1,0:T(8,128)} %get-tuple-element.36), calls=%async_computation | async-start | bytes 262144 | tf_op jit(solution)/shard_map/all_to_all | solution.py:794
  18.0 0.7 copy-start.8
  29.3 29.9 %all-to-all-start.1 = ((f32[32,4,8,128]{3,2,1,0:T(8,128)}), f32[32,4,8,128]{3,2,1,0:T(8,128)S(1)}, u32[]{:S(2)}, u32[]{:S(2)}) async-start(f32[32,4,8,128]{3,2,1,0:T(8,128)} %get-tuple-element.37), calls=%async_computation.1 | async-start | bytes 1048576 | tf_op jit(solution)/shard_map/all_to_all | solution.py:794
  33.6 0.7 copy-start.2
  34.3 11.8 %collective-permute-start = (f32[4,16,8,128]{3,2,1,0:T(8,128)S(1)}, f32[4,16,8,128]{3,2,1,0:T(8,128)S(1)}, u32[]{:S(2)}, u32[]{:S(2)}) collective-permute-start(f32[4,16,8,128]{3,2,1,0:T(8,128)S(1)} %get-tuple-element.39), channel_id=1, source_target_pairs={{0,1},{1,2},{2,3},{3,0},{4,5},{5,6},{6,7},{7,4},{8,9},{9,10},{10,1... | collective-permute-start | bytes 786440 | tf_op jit(solution)/shard_map/ppermute | solution.py:850
  34.4 12.3 %collective-permute-start.1 = (f32[4,16,8,128]{3,2,1,0:T(8,128)S(1)}, f32[4,16,8,128]{3,2,1,0:T(8,128)S(1)}, u32[]{:S(2)}, u32[]{:S(2)}) collective-permute-start(f32[4,16,8,128]{3,2,1,0:T(8,128)S(1)} %get-tuple-element.40), channel_id=1, source_target_pairs={{0,2},{1,3},{2,0},{3,1},{4,6},{5,7},{6,4},{7,5},{8,10},{9,11},{10,... | collective-permute-start | bytes 786440 | tf_op jit(solution)/shard_map/ppermute | solution.py:850
  36.1 14.8 %collective-permute-start.2 = (f32[4,16,8,128]{3,2,1,0:T(8,128)S(1)}, f32[4,16,8,128]{3,2,1,0:T(8,128)S(1)}, u32[]{:S(2)}, u32[]{:S(2)}) collective-permute-start(f32[4,16,8,128]{3,2,1,0:T(8,128)S(1)} %get-tuple-element.41), channel_id=1, source_target_pairs={{0,3},{1,0},{2,1},{3,2},{4,7},{5,4},{6,5},{7,6},{8,11},{9,8},{10,9... | collective-permute-start | bytes 786440 | tf_op jit(solution)/shard_map/ppermute | solution.py:850
  46.1 13.1 %copy-start.3 = (f32[4,16,8,128]{3,2,1,0:T(8,128)}, f32[4,16,8,128]{3,2,1,0:T(8,128)S(1)}, u32[]{:S(2)}) copy-start(f32[4,16,8,128]{3,2,1,0:T(8,128)S(1)} %collective-permute-done.refs_1_) | copy-start | bytes 786436
  46.7 12.5 %copy-start.4 = (f32[4,16,8,128]{3,2,1,0:T(8,128)}, f32[4,16,8,128]{3,2,1,0:T(8,128)S(1)}, u32[]{:S(2)}) copy-start(f32[4,16,8,128]{3,2,1,0:T(8,128)S(1)} %collective-permute-done.1.refs_2_) | copy-start | bytes 786436
  50.9 8.3 %copy-start.5 = (f32[4,16,8,128]{3,2,1,0:T(8,128)}, f32[4,16,8,128]{3,2,1,0:T(8,128)S(1)}, u32[]{:S(2)}) copy-start(f32[4,16,8,128]{3,2,1,0:T(8,128)S(1)} %collective-permute-done.2.refs_3_) | copy-start | bytes 786436
  59.2 16.5 %copy-start.14 = (f32[17]{0:T(128)S(1)}, f32[17]{0:T(128)}, u32[]{:S(2)}) copy-start(f32[17]{0:T(128)} %param.15) | copy-start | bytes 208
  64.0 23.5 %all-to-all-start.2 = ((f32[32,4,8,128]{3,2,1,0:T(8,128)}), f32[32,4,8,128]{3,2,1,0:T(8,128)S(1)}, u32[]{:S(2)}, u32[]{:S(2)}) async-start(f32[32,4,8,128]{3,2,1,0:T(8,128)} %shard_map.125.refs_1_), calls=%async_computation.2 | async-start | bytes 1048576 | tf_op jit(solution)/shard_map/all_to_all | solution.py:794
  69.2 15.7 %collective-permute-start.5 = (f32[4,256]{1,0:T(4,128)S(1)}, f32[4,256]{1,0:T(4,128)S(1)}, u32[]{:S(2)}, u32[]{:S(2)}) collective-permute-start(f32[4,256]{1,0:T(4,128)S(1)} %get-tuple-element.45), channel_id=1, source_target_pairs={{0,1},{1,2},{2,3},{3,0},{4,5},{5,6},{6,7},{7,4},{8,9},{9,10},{10,1... | collective-permute-start | bytes 12296 | tf_op jit(solution)/shard_map/ppermute | solution.py:807
  69.5 15.4 %collective-permute-start.6 = (f32[4,256]{1,0:T(4,128)S(1)}, f32[4,256]{1,0:T(4,128)S(1)}, u32[]{:S(2)}, u32[]{:S(2)}) collective-permute-start(f32[4,256]{1,0:T(4,128)S(1)} %get-tuple-element.46), channel_id=1, source_target_pairs={{1,0},{2,1},{3,2},{0,3},{5,4},{6,5},{7,6},{4,7},{9,8},{10,9},{11,1... | collective-permute-start | bytes 12296 | tf_op jit(solution)/shard_map/ppermute | solution.py:808
  71.0 15.1 %collective-permute-start.3 = (f32[128,256]{1,0:T(8,128)S(1)}, f32[128,256]{1,0:T(8,128)S(1)}, u32[]{:S(2)}, u32[]{:S(2)}) collective-permute-start(f32[128,256]{1,0:T(8,128)S(1)} %get-tuple-element.43), channel_id=1, source_target_pairs={{0,4},{4,8},{8,12},{12,16},{16,20},{20,24},{24,28},{28,0},{1,5},{5... | collective-permute-start | bytes 393224 | tf_op jit(solution)/shard_map/ppermute | solution.py:807
  72.8 13.3 %collective-permute-start.4 = (f32[128,256]{1,0:T(8,128)S(1)}, f32[128,256]{1,0:T(8,128)S(1)}, u32[]{:S(2)}, u32[]{:S(2)}) collective-permute-start(f32[128,256]{1,0:T(8,128)S(1)} %get-tuple-element.44), channel_id=1, source_target_pairs={{4,0},{8,4},{12,8},{16,12},{20,16},{24,20},{28,24},{0,28},{5,1},{9... | collective-permute-start | bytes 393224 | tf_op jit(solution)/shard_map/ppermute | solution.py:808
  75.7 1.0 copy-start
  84.9 20.4 %copy-start.6 = (bf16[4,128,256]{2,1,0:T(8,128)(2,1)S(1)}, bf16[4,128,256]{2,1,0:T(8,128)(2,1)}, u32[]{:S(2)}) copy-start(bf16[4,128,256]{2,1,0:T(8,128)(2,1)} %perm_ref.9) | copy-start | bytes 786436
  84.9 20.4 %copy-start.11 = (f32[4,128,256]{2,1,0:T(8,128)S(1)}, f32[4,128,256]{2,1,0:T(8,128)}, u32[]{:S(2)}) copy-start(f32[4,128,256]{2,1,0:T(8,128)} %res_ref.3) | copy-start | bytes 1572868
  96.5 8.1 %collective-permute-start.7 = (f32[128,256]{1,0:T(8,128)S(1)}, f32[128,256]{1,0:T(8,128)S(1)}, u32[]{:S(2)}, u32[]{:S(2)}) collective-permute-start(f32[128,256]{1,0:T(8,128)S(1)} %get-tuple-element.48), channel_id=1, source_target_pairs={{0,4},{4,8},{8,12},{12,16},{16,20},{20,24},{24,28},{28,0},{1,5},{5... | collective-permute-start | bytes 393224 | tf_op jit(solution)/shard_map/ppermute | solution.py:807
  97.5 7.8 %collective-permute-start.8 = (f32[128,256]{1,0:T(8,128)S(1)}, f32[128,256]{1,0:T(8,128)S(1)}, u32[]{:S(2)}, u32[]{:S(2)}) collective-permute-start(f32[128,256]{1,0:T(8,128)S(1)} %get-tuple-element.49), channel_id=1, source_target_pairs={{4,0},{8,4},{12,8},{16,12},{20,16},{24,20},{28,24},{0,28},{5,1},{9... | collective-permute-start | bytes 393224 | tf_op jit(solution)/shard_map/ppermute | solution.py:808
  101.3 3.0 %collective-permute-start.9 = (f32[4,256]{1,0:T(4,128)S(1)}, f32[4,256]{1,0:T(4,128)S(1)}, u32[]{:S(2)}, u32[]{:S(2)}) collective-permute-start(f32[4,256]{1,0:T(4,128)S(1)} %get-tuple-element.50), channel_id=1, source_target_pairs={{0,1},{1,2},{2,3},{3,0},{4,5},{5,6},{6,7},{7,4},{8,9},{9,10},{10,1... | collective-permute-start | bytes 12296 | tf_op jit(solution)/shard_map/ppermute | solution.py:807
  101.3 3.1 %collective-permute-start.10 = (f32[4,256]{1,0:T(4,128)S(1)}, f32[4,256]{1,0:T(4,128)S(1)}, u32[]{:S(2)}, u32[]{:S(2)}) collective-permute-start(f32[4,256]{1,0:T(4,128)S(1)} %get-tuple-element.51), channel_id=1, source_target_pairs={{1,0},{2,1},{3,2},{0,3},{5,4},{6,5},{7,6},{4,7},{9,8},{10,9},{11,1... | collective-permute-start | bytes 12296 | tf_op jit(solution)/shard_map/ppermute | solution.py:808
  131.2 18.2 %all-to-all-start.4 = ((f32[32,4,8,128]{3,2,1,0:T(8,128)}), f32[32,4,8,128]{3,2,1,0:T(8,128)S(1)}, u32[]{:S(2)}, u32[]{:S(2)}) async-start(f32[32,4,8,128]{3,2,1,0:T(8,128)} %get-tuple-element.54), calls=%async_computation.4 | async-start | bytes 1048576 | tf_op jit(solution)/shard_map/all_to_all | solution.py:794
  154.2 18.5 %all-to-all-start.5 = ((f32[32,4,8,128]{3,2,1,0:T(8,128)}), f32[32,4,8,128]{3,2,1,0:T(8,128)S(1)}, u32[]{:S(2)}, u32[]{:S(2)}) async-start(f32[32,4,8,128]{3,2,1,0:T(8,128)} %shard_map.131.refs_1_), calls=%async_computation.5 | async-start | bytes 1048576 | tf_op jit(solution)/shard_map/all_to_all | solution.py:794
  157.3 1.1 copy-start.1
  166.5 24.3 %copy-start.7 = (bf16[4,128,256]{2,1,0:T(8,128)(2,1)S(1)}, bf16[4,128,256]{2,1,0:T(8,128)(2,1)}, u32[]{:S(2)}) copy-start(bf16[4,128,256]{2,1,0:T(8,128)(2,1)} %perm_ref.9) | copy-start | bytes 786436
  166.5 24.3 %copy-start.9 = (f32[32,8,128]{2,1,0:T(8,128)S(1)}, f32[32,8,128]{2,1,0:T(8,128)}, u32[]{:S(2)}) copy-start(f32[32,8,128]{2,1,0:T(8,128)} %copy-done.8) | copy-start | bytes 393220
  166.5 24.3 %copy-start.10 = (f32[32,8,128]{2,1,0:T(8,128)S(1)}, f32[32,8,128]{2,1,0:T(8,128)}, u32[]{:S(2)}) copy-start(f32[32,8,128]{2,1,0:T(8,128)} %all_to_all.35.sums_ref) | copy-start | bytes 393220
  166.5 24.3 %copy-start.12 = (f32[4,128,256]{2,1,0:T(8,128)S(1)}, f32[4,128,256]{2,1,0:T(8,128)}, u32[]{:S(2)}) copy-start(f32[4,128,256]{2,1,0:T(8,128)} %get-tuple-element.62.refs_12_.res_ref) | copy-start | bytes 1572868
  181.8 8.1 %collective-permute-start.11 = (f32[128,256]{1,0:T(8,128)S(1)}, f32[128,256]{1,0:T(8,128)S(1)}, u32[]{:S(2)}, u32[]{:S(2)}) collective-permute-start(f32[128,256]{1,0:T(8,128)S(1)} %get-tuple-element.58), channel_id=1, source_target_pairs={{0,4},{4,8},{8,12},{12,16},{16,20},{20,24},{24,28},{28,0},{1,5},{5... | collective-permute-start | bytes 393224 | tf_op jit(solution)/shard_map/ppermute | solution.py:807
  183.0 7.8 %collective-permute-start.12 = (f32[128,256]{1,0:T(8,128)S(1)}, f32[128,256]{1,0:T(8,128)S(1)}, u32[]{:S(2)}, u32[]{:S(2)}) collective-permute-start(f32[128,256]{1,0:T(8,128)S(1)} %get-tuple-element.59), channel_id=1, source_target_pairs={{4,0},{8,4},{12,8},{16,12},{20,16},{24,20},{28,24},{0,28},{5,1},{9... | collective-permute-start | bytes 393224 | tf_op jit(solution)/shard_map/ppermute | solution.py:808
  186.5 3.0 %collective-permute-start.13 = (f32[4,256]{1,0:T(4,128)S(1)}, f32[4,256]{1,0:T(4,128)S(1)}, u32[]{:S(2)}, u32[]{:S(2)}) collective-permute-start(f32[4,256]{1,0:T(4,128)S(1)} %get-tuple-element.60), channel_id=1, source_target_pairs={{0,1},{1,2},{2,3},{3,0},{4,5},{5,6},{6,7},{7,4},{8,9},{9,10},{10,1... | collective-permute-start | bytes 12296 | tf_op jit(solution)/shard_map/ppermute | solution.py:807
  186.5 3.1 %collective-permute-start.14 = (f32[4,256]{1,0:T(4,128)S(1)}, f32[4,256]{1,0:T(4,128)S(1)}, u32[]{:S(2)}, u32[]{:S(2)}) collective-permute-start(f32[4,256]{1,0:T(4,128)S(1)} %get-tuple-element.61), channel_id=1, source_target_pairs={{1,0},{2,1},{3,2},{0,3},{5,4},{6,5},{7,6},{4,7},{9,8},{10,9},{11,1... | collective-permute-start | bytes 12296 | tf_op jit(solution)/shard_map/ppermute | solution.py:808

commit v7 on v5

--- a/solution.py
+++ b/solution.py
@@ -225,7 +225,9 @@
 
 LANES = 128
 SUBLANES = 8
-BOTH = ("row", "col")
+COL = ("y", "core")
+CHIPS = ("row", "y")
+BOTH = ("row", "y", "core")
 F32 = jnp.float32
 BF16 = jnp.bfloat16
 
@@ -286,6 +288,8 @@
     back = []
     for place in range(n_col):
         angle = angles(freqs, place * cols + np.arange(cols), n_col * cols)
+        own = np.arange(KY).reshape(-1, 2, SUBLANES)[:, place % 2].reshape(-1)
+        partner = np.arange(KY).reshape(-1, 2, SUBLANES)[:, 1 - place % 2].reshape(-1)
         both = np.concatenate([np.cos(angle), np.sin(angle)], 0)
         high, low = split_table(both)
         forward.append(
@@ -297,6 +301,7 @@
                 0,
             )
         )
+        angle = angle[np.concatenate([own, partner])]
         both = np.concatenate([np.cos(angle), np.sin(angle)], 0)
         high, low = split_table(both)
         back.append(
@@ -403,7 +408,7 @@
         block = block.T.reshape(freq, groups, fine, parts * deep * outs)
         for group in range(groups):
             hold_ref[group, :, channel] = block[:, group]
-    place = lax.axis_index("col")
+    place = lax.axis_index(COL)
     for shift, out_ref in enumerate(out_refs):
         out_ref[...] = hold_ref[lax.rem(place + shift, groups)]
 
@@ -419,7 +424,7 @@
     )
 
 
-def transform(lift_ref, deep_ref, col_ref, scaled, log_perm, spectra_ref, lifted_ref, zt_ref):
+def transform(lift_ref, deep_ref, col_ref, scaled, log_perm, own_ref, partner_ref, lifted_ref, zt_ref):
     half = 2 * KZ
     cols = scaled.shape[1]
     for channel in range(0, CHANNELS, 2):
@@ -432,24 +437,33 @@
         for j in range(2):
             zt_ref[pl.ds(channel + j, half, stride=CHANNELS), :] = part[:, j * cols : (j + 1) * cols]
     groups = half * CHANNELS // LANES
-    part = matmul_nt(col_ref[lax.axis_index("col")], jnp.concatenate(split(zt_ref[...]), 1))
+    part = matmul_nt(col_ref[lax.axis_index(COL)], jnp.concatenate(split(zt_ref[...]), 1))
     part = part[: 2 * KY] + part[2 * KY :]
     lane = lax.broadcasted_iota(jnp.int32, (KY, LANES), 1)
     sign = jnp.where(lane < LANES // 2, 1.0, -1.0).astype(F32)
     n_col = KY // SUBLANES
+    core = lax.axis_index("core")
     for row in range(groups):
         lanes = slice(row * LANES, (row + 1) * LANES)
         block = part[:KY, lanes] + pltpu.roll(part[KY:, lanes], LANES // 2, 1) * sign
-        for col in range(n_col):
-            spectra_ref[row * n_col + col, 0] = block[col * SUBLANES : (col + 1) * SUBLANES]
+        for place in range(n_col // 2):
+            start = 2 * place * SUBLANES
+            even = block[start : start + SUBLANES]
+            odd = block[start + SUBLANES : start + 2 * SUBLANES]
+            own_ref[row * n_col // 2 + place, 0] = jnp.where(core == 0, even, odd)
+            partner_ref[row * n_col // 2 + place, 0] = jnp.where(core == 0, odd, even)
 
 
 def lift_first_body(cells, lift_ref, sums_ref, res_ref, perm_ref, deep_ref, col_ref, *refs):
-    spectra_ref, lifted_ref, zt_ref = refs[-3:]
+    own_ref, partner_ref, lifted_ref, zt_ref = refs[-4:]
     scale = scale_of(gathered(sums_ref, 0), cells)
     scaled = (res_ref[0] / scale).T
     log_perm = jnp.log(perm_ref[0].astype(F32)).T
-    transform(lift_ref, deep_ref, col_ref, scaled, log_perm, spectra_ref, lifted_ref, zt_ref)
+    transform(lift_ref, deep_ref, col_ref, scaled, log_perm, own_ref, partner_ref, lifted_ref, zt_ref)
+
+
+def join_body(own_ref, partner_ref, out_ref):
+    out_ref[...] = own_ref[...] + partner_ref[...]
 
 
 def next_scalars(first_ref, sums_ref):
@@ -461,14 +475,14 @@
     return curvature, alpha, jnp.maximum(total, 0.0)
 
 
-def lift_next_body(cells, lift_ref, first_ref, sums_ref, res_ref, image_ref, perm_ref, deep_ref, col_ref, spectra_ref, lifted_ref, next_ref, zt_ref):
+def lift_next_body(cells, lift_ref, first_ref, sums_ref, res_ref, image_ref, perm_ref, deep_ref, col_ref, own_ref, partner_ref, lifted_ref, next_ref, zt_ref):
     _, alpha, total = next_scalars(first_ref, sums_ref)
     scale = scale_of(total, cells)
     residual = res_ref[0] - alpha * image_ref[0]
     next_ref[0] = residual
     scaled = (residual / scale).T
     log_perm = jnp.log(perm_ref[0].astype(F32)).T
-    transform(lift_ref, deep_ref, col_ref, scaled, log_perm, spectra_ref, lifted_ref, zt_ref)
+    transform(lift_ref, deep_ref, col_ref, scaled, log_perm, own_ref, partner_ref, lifted_ref, zt_ref)
 
 
 def point_body(mix_ref, lifted_ref, _, __, point_ref):
@@ -491,10 +505,10 @@
     lax.fori_loop(0, lifted_ref.shape[2] // size, step, 0)
 
 
-def modes_body(cells, n_row, n_col, recv_ref, *refs):
+def modes_body(cells, n_row, n_col, n_chip, recv_ref, *refs):
     sources = refs[:n_col]
     _, out_ref, weight_ref, sems, field_ref, turned_ref, spec_ref, odd_ref = refs[n_col:]
-    own = lax.axis_index("col")
+    own = lax.axis_index(COL)
     copies = [
         pltpu.make_async_copy(
             source, weight_ref.at[lax.rem(own + n_col - shift, n_col)], sems.at[shift]
@@ -516,9 +530,9 @@
 
     for row in range(n_row):
         for place in range(rows):
-            value = recv_ref[row * n_col, place]
-            for col in range(1, n_col):
-                value = value + recv_ref[row * n_col + col, place]
+            value = recv_ref[row * n_chip, place]
+            for chip in range(1, n_chip):
+                value = value + recv_ref[row * n_chip + chip, place]
             field_ref[row * rows + place] = value
     angle = 2.0 * np.pi / places
     half = KX // 2
@@ -588,8 +602,8 @@
             odd_ref[freq] = odds[freq]
 
     def store(place, value):
-        for col in range(n_col):
-            out_ref[(place // rows) * n_col + col, place % rows] = value
+        for chip in range(n_chip):
+            out_ref[(place // rows) * n_chip + chip, place % rows] = value
 
     for place in range(places // 2 + 1):
         turns = place * np.arange(half + 1) % places
@@ -600,7 +614,7 @@
             store(places - place, even - odd)
 
 
-def back_transform(recv_ref, point_ref, proj_ref, col_ref, deep_ref, wave_ref, scale):
+def back_transform(recv_ref, other_ref, point_ref, proj_ref, col_ref, deep_ref, wave_ref, scale):
     groups = 2 * KZ * CHANNELS // LANES
     n_col = KY // SUBLANES
     cols = col_ref.shape[2] // 2
@@ -609,11 +623,13 @@
     half = 2 * KZ
     pieces = []
     for row in range(groups):
-        value = recv_ref[row * n_col : (row + 1) * n_col, 0].reshape(KY, LANES)
+        chips = slice(row * n_col // 2, (row + 1) * n_col // 2)
+        value = jnp.concatenate([recv_ref[chips, 0], other_ref[chips, 0]], 0)
+        value = value.reshape(KY, LANES)
         turned = pltpu.roll(value, LANES // 2, 1) * sign
         both = jnp.concatenate([value, turned], 0)
         pieces.append(jnp.concatenate(split_three(both), 0).T.astype(BF16))
-    part = matmul(jnp.concatenate(pieces, 0), col_ref[lax.axis_index("col")])
+    part = matmul(jnp.concatenate(pieces, 0), col_ref[lax.axis_index(COL)])
     wave_ref[...] = part[:, :cols] + part[:, cols:]
     total = None
     for out in range(0, CHANNELS, 2):
@@ -644,21 +660,21 @@
         high_ref[...] = update
 
 
-def back_first_body(cells, proj_ref, sums_ref, recv_ref, point_ref, col_ref, deep_ref, *refs):
+def back_first_body(cells, proj_ref, sums_ref, recv_ref, other_ref, point_ref, col_ref, deep_ref, *refs):
     kept_ref, *edges, wave_ref = refs[4:]
     scale = scale_of(gathered(sums_ref, 0), cells)
     update = back_transform(
-        recv_ref, point_ref, proj_ref, col_ref, deep_ref, wave_ref, scale
+        recv_ref, other_ref, point_ref, proj_ref, col_ref, deep_ref, wave_ref, scale
     )
     kept_ref[0, 0] = update
     put_edges(update, *edges)
 
 
-def back_next_body(cells, proj_ref, first_ref, sums_ref, recv_ref, point_ref, col_ref, deep_ref, _, kept_ref, *refs):
+def back_next_body(cells, proj_ref, first_ref, sums_ref, recv_ref, other_ref, point_ref, col_ref, deep_ref, _, kept_ref, *refs):
     *edges, wave_ref = refs
     _, _, total = next_scalars(first_ref, sums_ref)
     update = back_transform(
-        recv_ref, point_ref, proj_ref, col_ref, deep_ref, wave_ref, scale_of(total, cells)
+        recv_ref, other_ref, point_ref, proj_ref, col_ref, deep_ref, wave_ref, scale_of(total, cells)
     )
     kept_ref[0, 0] = update
     put_edges(update, *edges)
@@ -723,8 +739,8 @@
 
     low = outside("row", 0, low_ref[...])
     high = outside("row", lax.axis_size("row") - 1, high_ref[...])
-    left = outside("col", 0, left_ref[line, :])
-    right = outside("col", lax.axis_size("col") - 1, right_ref[line, :])
+    left = outside(COL, 0, left_ref[line, :])
+    right = outside(COL, lax.axis_size(COL) - 1, right_ref[line, :])
     before = jnp.where(step == 0, low, plane(jnp.maximum(step - 1, 0)))
     after = jnp.where(step == last, high, plane(jnp.minimum(step + 1, last)))
     return plane(step), before, after, left, right
@@ -767,17 +783,21 @@
     out_ref[0] = res_ref[0] - later * (image_ref[0] - delta * before_ref[0])
 
 
-def exchange(blocks):
-    return lax.all_to_all(blocks, BOTH, split_axis=0, concat_axis=0, tiled=True)
+def exchange(blocks, axes):
+    return lax.all_to_all(blocks, axes, split_axis=0, concat_axis=0, tiled=True)
+
+
+def swap(blocks):
+    return lax.ppermute(blocks, "core", [(0, 1), (1, 0)])
 
 
 def add_up(partial):
-    return exchange(partial)
+    return exchange(partial, BOTH)
 
 
 def neighbours(low, high, left, right):
     found = []
-    for axis, first, last in (("row", low, high), ("col", left, right)):
+    for axis, first, last in (("row", low, high), (COL, left, right)):
         count = lax.axis_size(axis)
         forward = [(i, (i + 1) % count) for i in range(count)]
         backward = [(target, source) for source, target in forward]
@@ -789,7 +809,7 @@
 def tiled_local(right_side, permeability, lift_weight, spectral_weight, mix_weight, proj_weight):
     rows, cols, depth = right_side.shape
     n_row = lax.axis_size("row")
-    n_col = lax.axis_size("col")
+    n_col = lax.axis_size(COL)
     count = n_row * n_col
     cells = float(rows * n_row * cols * n_col * depth)
     freq = KX // n_col
@@ -802,20 +822,21 @@
     field_bytes = 4 * rows * cols * depth
     partial = shape(count, SUBLANES, LANES)
     channels = shape(rows, CHANNELS, depth, cols)
-    spectra = shape(count, rows, SUBLANES, LANES)
-    spectra_bytes = 4 * count * rows * SUBLANES * LANES
+    n_chip = n_col // 2
+    spectra = shape(n_row * n_chip, rows, SUBLANES, LANES)
+    spectra_bytes = 4 * spectra.size
     smem = whole(pltpu.SMEM)
     vmem = whole()
     anywhere = whole(pl.ANY)
     plane = pl.BlockSpec((1, cols, depth), lambda i: (i, 0, 0))
-    spectra_block = pl.BlockSpec((count, 1, SUBLANES, LANES), lambda i: (0, i, 0, 0))
+    spectra_block = pl.BlockSpec((n_row * n_chip, 1, SUBLANES, LANES), lambda i: (0, i, 0, 0))
     point_block = pl.BlockSpec((1, CHANNELS, depth, cols), lambda i: (i, 0, 0, 0))
     kept_shape = shape(ITERS, rows, cols, depth)
     lift_flops = 2.0e9
     back_flops = 2.0e9
 
     weight_shape = (freq, CHANNELS, SUBLANES, LANES)
-    own, *weights = call(
+    kept_weights, *weights = call(
         weight_body,
         (shape(*weight_shape),) * n_col,
         [vmem],
@@ -823,8 +844,8 @@
         scratch=[pltpu.VMEM((n_col,) + weight_shape, F32)],
         moved=8 * spectral_weight.size,
     )(spectral_weight)
-    weights = [own] + [
-        lax.ppermute(part, "col", [(i, (i + shift + 1) % n_col) for i in range(n_col)])
+    weights = [kept_weights] + [
+        lax.ppermute(part, COL, [(i, (i + shift + 1) % n_col) for i in range(n_col)])
         for shift, part in enumerate(weights)
     ]
     edge_shapes = (shape(cols, depth),) * 2 + (shape(rows, depth),) * 2
@@ -834,7 +855,7 @@
         [vmem, vmem, anywhere],
         (vmem,) * 5,
         moved=2 * field_bytes,
-    )(right_side, permeability, own)
+    )(right_side, permeability, kept_weights)
     squares = add_up(squares)
     perm_halo = neighbours(*perm_edges)
     acc_scratch = pltpu.VMEM((SUBLANES, LANES), F32)
@@ -859,7 +880,7 @@
         places = rows * n_row
         tiles = lambda size: pltpu.VMEM((size, SUBLANES, LANES), F32)
         return call(
-            functools.partial(modes_body, cells, n_row, n_col),
+            functools.partial(modes_body, cells, n_row, n_col, n_chip),
             spectra,
             [vmem] + [anywhere] * (n_col + 1),
             vmem,
@@ -875,39 +896,43 @@
             near=(0,),
         )(received, *weights, before)
 
-    def mixed_modes(blocks, lifted):
-        received = exchange(blocks)
-        point = points(lifted, 0, right_side, right_side)
+    def mixed_modes(own, partner, lifted):
+        blocks = call(join_body, spectra, [vmem, vmem], vmem, near=(0, 1))(own, swap(partner))
+        received = exchange(blocks, CHIPS)
+        point = points(lifted, 0, blocks, blocks)
         blocks = modes(received, point)
-        received = exchange(blocks)
+        received = exchange(blocks, CHIPS)
         point = points(lifted, 1, point, blocks)
-        return received, point
-
-    blocks, lifted = call(
+        return received, swap(received), point
+
+    own, partner, lifted = call(
         functools.partial(lift_first_body, cells),
-        (spectra, channels),
+        (spectra, spectra, channels),
         [smem, vmem, plane, plane, vmem, vmem] + [anywhere] * n_col,
-        (spectra_block, point_block),
+        (spectra_block, spectra_block, point_block),
         limit=16,
+        loose=(0, 1),
+        near=(6, 7, 8, 9),
         grid=(rows,),
         scratch=[zt_scratch],
         flops=lift_flops,
         moved=2 * field_bytes + spectra_bytes,
     )(lift_weight, squares, right_side, permeability, deep_forward, col_forward, *weights)
-    received, point = mixed_modes(blocks, lifted)
+    received, other, point = mixed_modes(own, partner, lifted)
     kept, old, *edges = call(
         functools.partial(back_first_body, cells),
         (kept_shape, field) + edge_shapes,
-        [smem, vmem, spectra_block, point_block, vmem, vmem] + [anywhere] * 4,
+        [smem, vmem, spectra_block, spectra_block, point_block, vmem, vmem]
+        + [anywhere] * 4,
         (pl.BlockSpec((1, 1, cols, depth), lambda i: (0, i, 0, 0)), plane) + (vmem,) * 4,
-        near=(2, 6, 7, 8, 9),
+        near=(2, 3, 7, 8, 9, 10),
         loose=(1,),
         grid=(rows,),
         scratch=[zt_scratch],
         limit=12,
         flops=back_flops,
         moved=18 * field_bytes,
-    )(proj_weight, squares, received, point, col_back, deep_back, *perm_halo)
+    )(proj_weight, squares, received, other, point, col_back, deep_back, *perm_halo)
 
     old_halo = neighbours(*edges)
     args = (old, permeability, *old_halo, *perm_halo, right_side)
@@ -924,33 +949,34 @@
     )(*args)
     sums = add_up(sums)
 
-    blocks, lifted, residual = call(
+    own, partner, lifted, residual = call(
         functools.partial(lift_next_body, cells),
-        (spectra, channels, field),
+        (spectra, spectra, channels, field),
         [smem, vmem, vmem, plane, plane, plane, vmem, vmem],
-        (spectra_block, point_block, plane),
+        (spectra_block, spectra_block, point_block, plane),
         limit=16,
         near=(4,),
+        loose=(0, 1),
         grid=(rows,),
         scratch=[zt_scratch],
         flops=lift_flops,
         moved=4 * field_bytes + spectra_bytes,
     )(lift_weight, squares, sums, right_side, image, permeability, deep_forward, col_forward)
-    received, point = mixed_modes(blocks, lifted)
+    received, other, point = mixed_modes(own, partner, lifted)
     kept, update, *edges = call(
         functools.partial(back_next_body, cells),
         (kept_shape, field) + edge_shapes,
-        [smem, vmem, vmem, spectra_block, point_block, vmem, vmem, anywhere],
+        [smem, vmem, vmem, spectra_block, spectra_block, point_block, vmem, vmem, anywhere],
         (pl.BlockSpec((1, 1, cols, depth), lambda i: (1, i, 0, 0)), plane) + (vmem,) * 4,
-        near=(3,),
+        near=(3, 4),
         loose=(1,),
         grid=(rows,),
         limit=12,
         scratch=[zt_scratch],
         flops=back_flops,
         moved=19 * field_bytes,
-        alias={7: 0},
-    )(proj_weight, squares, sums, received, point, col_back, deep_back, kept)
+        alias={8: 0},
+    )(proj_weight, squares, sums, received, other, point, col_back, deep_back, kept)
 
     halo = neighbours(*edges)
     args = (squares, sums, update, old, permeability, *halo, *old_halo, *perm_halo, residual, image)
@@ -987,6 +1013,7 @@
         and KZ == n_row * (LANES // (2 * CHANNELS))
         and KY == n_col * SUBLANES
         and KX % n_col == 0
+        and n_col % 2 == 0
         and cols == LANES
         and depth % LANES == 0
         and rows * n_row >= KX
@@ -1002,15 +1029,26 @@
         P(),
         P(),
     )
+    outputs = (P("row", "col", None), P("row", "col", None), P(None, "row", "col", None))
 
     def run(right_side, *others):
         rows, cols, depth = right_side.shape
-        block = (rows // mesh.shape["row"], cols // mesh.shape["col"], depth)
+        n_row, n_col = mesh.shape["row"], mesh.shape["col"]
+        if not fits_tiles(mesh, (rows // n_row, cols // n_col, depth)):
+            return jax.shard_map(
+                local, mesh=mesh, in_specs=placed, out_specs=outputs, check_vma=False
+            )(right_side, *others)
+        cores = jax.sharding.Mesh(mesh.devices.reshape(n_row, n_col // 2, 2), BOTH)
+        placed_cores, outputs_cores = jax.tree.map(
+            lambda spec: P(*(COL if axis == "col" else axis for axis in spec)),
+            (placed, outputs),
+            is_leaf=lambda spec: isinstance(spec, P),
+        )
         return jax.shard_map(
-            tiled_local if fits_tiles(mesh, block) else local,
-            mesh=mesh,
-            in_specs=placed,
-            out_specs=(P("row", "col", None), P("row", "col", None), P(None, "row", "col", None)),
+            tiled_local,
+            mesh=cores,
+            in_specs=placed_cores,
+            out_specs=outputs_cores,
             check_vma=False,
         )(right_side, *others)
 

time: 198 us -> 202 us (1.020)
  blocking collectives: 25.8 us -> 37.6 us
  waiting for transfers between devices: 37.9 us -> 26.1 us
  Pallas kernels: 88.5 us -> 91 us
    all_to_all x5 -> x4, waiting for transfers between devices: 30.9 us -> 16.2 us  [exchange(): return lax.all_to_all(blocks, axes, split_axis=0, concat_axis=0, tiled=True)]
    all_to_all x2 -> x3, blocking collectives: 25.8 us -> 37.6 us  [exchange(): return lax.all_to_all(blocks, axes, split_axis=0, concat_axis=0, tiled=True)]
    ppermute x3 -> x7, waiting for transfers between devices: 0.01 us -> 2.65 us  [the longest x4 2.65 us: swap(): return lax.ppermute(blocks, 'core', [(0, 1), (1, 0)])]
    pallas_call x15 -> x17, Pallas kernels: 88.5 us -> 91 us  [wrapped(): found = run(*held)]
    all_to_all x5 -> x4, starting transfers between devices: 17.2 us -> 18 us  [exchange(): return lax.all_to_all(blocks, axes, split_axis=0, concat_axis=0, tiled=True)]
    ppermute x3 -> x7, starting transfers between devices: 4.45 us -> 4.89 us  [the longest x3 4.45 us: tiled_local(): lax.ppermute(part, COL, [(i, (i + shift + 1) % n_col) for i in range(n_co...]
  transfers between devices with their start and end apart: 20 -> 23, of which waited for: 12 -> 12; matrix products, arithmetic and copies ran while one was open for 0% -> 0% of each run, Pallas kernels for 18% -> 17%
where the time goes in v7:
time: 202 us; the launch traced here: 201 us
  Pallas kernels  91 us (45%)
  starting transfers between devices  42.3 us (21%)
  blocking collectives  37.6 us (19%)
  waiting for transfers between devices  26.1 us (13%)
  local copies, waits for them, and re-layouts  2.33 us (1%)
    pallas_call x17, Pallas kernels, wrapped(): found = run(*held)  91 us
    all_to_all x3, blocking collectives, exchange(): return lax.all_to_all(blocks, axes, split_axis=0, concat_axis=0, tiled=True)  37.6 us
    all_to_all x4, starting transfers between devices, exchange(): return lax.all_to_all(blocks, axes, split_axis=0, concat_axis=0, tiled=True)  18 us
    all_to_all x4, waiting for transfers between devices, exchange(): return lax.all_to_all(blocks, axes, split_axis=0, concat_axis=0, tiled=True)  16.2 us
    ppermute x6, starting transfers between devices, neighbours(): found.append(lax.ppermute(first, axis, backward))  14.2 us
    ppermute x6, starting transfers between devices, neighbours(): found.append(lax.ppermute(last, axis, forward))  5.3 us
    ppermute x3, starting transfers between devices, tiled_local(): lax.ppermute(part, COL, [(i, (i + shift + 1) % n_col) for i in range(n_co...  4.45 us
    ppermute x6, waiting for transfers between devices, neighbours(): found.append(lax.ppermute(last, axis, forward))  4.38 us
  transfers between devices with their start and end apart: 23, of which 12 were waited for; matrix products, arithmetic and copies ran while one was open for 0% of the time, Pallas kernels for 17%

profile of v7, /device:TPU:0, one launch (start us, length us, event | category | flops | bytes accessed | tf_op | source)
XLA Modules:
  0.0 200.9 jit_solution(9208758589429914235)
XLA Ops:
  0.6 1.7 shard_map.121
  3.5 2.6 %collective-permute-start.1 = (f32[4,16,8,128]{3,2,1,0:T(8,128)S(1)}, f32[4,16,8,128]{3,2,1,0:T(8,128)S(1)}, u32[]{:S(2)}, u32[]{:S(2)}) collective-permute-start(f32[4,16,8,128]{3,2,1,0:T(8,128)S(1)} %get-tuple-element.41), channel_id=1, source_target_pairs={{0,2},{1,3},{2,0},{3,1},{4,6},{5,7},{6,4},{7,5},{8,10},{9,11},{10,... | collective-permute-start | bytes 786440 | tf_op jit(solution)/shard_map/ppermute | solution.py:848
  6.0 1.4 collective-permute-start.2
  7.5 1.8 shard_map.122
  9.3 4.9 %all-to-all-start = ((f32[32,8,128]{2,1,0:T(8,128)}), f32[32,8,128]{2,1,0:T(8,128)S(1)}, u32[]{:S(2)}, u32[]{:S(2)}) async-start(f32[32,8,128]{2,1,0:T(8,128)} %get-tuple-element.39), calls=%async_computation | async-start | bytes 262144 | tf_op jit(solution)/shard_map/all_to_all | solution.py:787
  14.9 7.5 %all-to-all-done.sums_ref.first_ref = f32[32,8,128]{2,1,0:T(8,128)S(1)} async-done(((f32[32,8,128]{2,1,0:T(8,128)}), f32[32,8,128]{2,1,0:T(8,128)S(1)}, u32[]{:S(2)}, u32[]{:S(2)}) %all-to-all-start) | async-done | bytes 131104 | tf_op jit(solution)/shard_map/all_to_all | solution.py:787
  23.1 0.9 copy-done.2
  24.0 9.8 %shard_map.123 = (f32[16,4,8,128]{3,2,1,0:T(8,128)S(1)}, f32[16,4,8,128]{3,2,1,0:T(8,128)S(1)}, f32[4,16,256,128]{3,2,1,0:T(8,128)}) custom-call(f32[3,16]{1,0:T(4,128)S(1)} %multiply_bitcast_fusion.lift_ref, f32[32,8,128]{2,1,0:T(8,128)} %copy-done.5, f32[4,128,256]{2,1,0:T(8,128)} %res_ref.3, bf16[4,128,256]{2,1,0:T(8,128)(2,1)} %perm_ref.9, ...), custom_call_target="tpu_custom_call" | custom-call | flops 2000000000 | bytes 1310720 | tf_op jit(solution)/shard_map/pallas_call | solution.py:356
  34.1 1.3 collective-permute-done.3.partner_ref
  35.4 0.7 shard_map.124._.__
  36.1 4.5 %all-to-all-start.1 = ((f32[16,4,8,128]{3,2,1,0:T(8,128)}), f32[16,4,8,128]{3,2,1,0:T(8,128)S(1)}, u32[]{:S(2)}, u32[]{:S(2)}) async-start(f32[16,4,8,128]{3,2,1,0:T(8,128)} %shard_map.124._.__), calls=%async_computation.1 | async-start | bytes 524288 | tf_op jit(solution)/shard_map/all_to_all | solution.py:787
  40.7 8.2 %shard_map.125.refs_4_._ = f32[4,16,256,128]{3,2,1,0:T(8,128)} custom-call(f32[16,17]{1,0:T(8,128)S(1)} %broadcast_multiply_fusion.mix_ref, f32[4,16,256,128]{3,2,1,0:T(8,128)} %get-tuple-element.45.lifted_ref, f32[16,4,8,128]{3,2,1,0:T(8,128)} %shard_map.124._.__, f32[16,4,8,128]{3,2,1,0:T(8,128)} %shard_map.124._.__), custom_call_target="tpu_custom_call" | custom-call | flops 2500000000 | bytes 8388608 | tf_op jit(solution)/shard_map/pallas_call | solution.py:356
  48.9 1.9 all-to-all-done.1.recv_ref
  50.8 4.7 %shard_map.126.__ = f32[16,4,8,128]{3,2,1,0:T(8,128)} custom-call(f32[16,4,8,128]{3,2,1,0:T(8,128)S(1)} %all-to-all-done.1.recv_ref, f32[4,16,8,128]{3,2,1,0:T(8,128)} %copy-done.1, f32[4,16,8,128]{3,2,1,0:T(8,128)} %copy-done.10, f32[4,16,8,128]{3,2,1,0:T(8,128)} %copy-done.11, f32[4,16,8,128]{3,2,1,0:T(8,128)} %copy-done.12, ...), custom_call_target="tpu_custom_call" | custom-call | bytes 1572864 | tf_op jit(solution)/shard_map/pallas_call | solution.py:356
  55.5 5.0 %all-to-all-start.2 = ((f32[16,4,8,128]{3,2,1,0:T(8,128)}), f32[16,4,8,128]{3,2,1,0:T(8,128)S(1)}, u32[]{:S(2)}, u32[]{:S(2)}) async-start(f32[16,4,8,128]{3,2,1,0:T(8,128)} %shard_map.126.__), calls=%async_computation.2 | async-start | bytes 524288 | tf_op jit(solution)/shard_map/all_to_all | solution.py:787
  60.6 1.7 collective-permute-start.8
  62.3 1.9 collective-permute-start.5
  64.2 2.8 %collective-permute-start.6 = (f32[128,256]{1,0:T(8,128)S(1)}, f32[128,256]{1,0:T(8,128)S(1)}, u32[]{:S(2)}, u32[]{:S(2)}) collective-permute-start(f32[128,256]{1,0:T(8,128)S(1)} %get-tuple-element.47), channel_id=1, source_target_pairs={{4,0},{8,4},{12,8},{16,12},{20,16},{24,20},{28,24},{0,28},{5,1},{9... | collective-permute-start | bytes 393224 | tf_op jit(solution)/shard_map/ppermute | solution.py:805
  67.0 4.5 %all-to-all-done.2.recv_ref = f32[16,4,8,128]{3,2,1,0:T(8,128)S(1)} async-done(((f32[16,4,8,128]{3,2,1,0:T(8,128)}), f32[16,4,8,128]{3,2,1,0:T(8,128)S(1)}, u32[]{:S(2)}, u32[]{:S(2)}) %all-to-all-start.2) | async-done | bytes 262176 | tf_op jit(solution)/shard_map/all_to_all | solution.py:787
  71.6 8.1 %shard_map.127.point_ref = f32[4,16,256,128]{3,2,1,0:T(8,128)} custom-call(f32[16,17]{1,0:T(8,128)S(1)} %broadcast_multiply_fusion.mix_ref, f32[4,16,256,128]{3,2,1,0:T(8,128)} %get-tuple-element.45.lifted_ref, f32[4,16,256,128]{3,2,1,0:T(8,128)} %shard_map.125.refs_4_._, f32[16,4,8,128]{3,2,1,0:T(8,128)} %shard_map.126.__), custom_call_target="tpu_custom_call", output_to_operand_aliasing={{}: (2, {})} | custom-call | flops 2500000000 | bytes 8388608 | tf_op jit(solution)/shard_map/pallas_call | solution.py:356
  79.7 9.1 %shard_map.128 = (f32[2,4,128,256]{3,2,1,0:T(8,128)}, f32[4,128,256]{2,1,0:T(8,128)S(1)}, f32[128,256]{1,0:T(8,128)S(1)}, f32[128,256]{1,0:T(8,128)S(1)}, f32[4,256]{1,0:T(4,128)S(1)}, /*index=5*/f32[4,256]{1,0:T(4,128)S(1)}) custom-call(f32[17]{0:T(128)S(1)} %fusion.proj_ref, f32[32,8,128]{2,1,0:T(8,128)} %copy-done.5, ...), custom_call_target="tpu_custom_call" | custom-call | flops 2000000000 | bytes 9437184 | tf_op jit(solution)/shard_map/pallas_call | solution.py:356
  88.8 2.3 %collective-permute-start.9 = (f32[128,256]{1,0:T(8,128)S(1)}, f32[128,256]{1,0:T(8,128)S(1)}, u32[]{:S(2)}, u32[]{:S(2)}) collective-permute-start(f32[128,256]{1,0:T(8,128)S(1)} %get-tuple-element.51), channel_id=1, source_target_pairs={{0,4},{4,8},{8,12},{12,16},{16,20},{20,24},{24,28},{28,0},{1,5},{5... | collective-permute-start | bytes 393224 | tf_op jit(solution)/shard_map/ppermute | solution.py:804
  91.1 2.4 %collective-permute-start.10 = (f32[128,256]{1,0:T(8,128)S(1)}, f32[128,256]{1,0:T(8,128)S(1)}, u32[]{:S(2)}, u32[]{:S(2)}) collective-permute-start(f32[128,256]{1,0:T(8,128)S(1)} %get-tuple-element.52), channel_id=1, source_target_pairs={{4,0},{8,4},{12,8},{16,12},{20,16},{24,20},{28,24},{0,28},{5,1},{9... | collective-permute-start | bytes 393224 | tf_op jit(solution)/shard_map/ppermute | solution.py:805
  93.5 1.7 collective-permute-start.12
  95.3 1.3 collective-permute-done.11.refs_2_.refs_6_
  96.6 0.9 collective-permute-done.9.refs_0_.refs_4_
  97.5 2.0 %collective-permute-done.10.refs_1_.refs_5_ = f32[128,256]{1,0:T(8,128)S(1)} collective-permute-done((f32[128,256]{1,0:T(8,128)S(1)}, f32[128,256]{1,0:T(8,128)S(1)}, u32[]{:S(2)}, u32[]{:S(2)}) %collective-permute-start.10) | collective-permute-done | bytes 131104 | tf_op jit(solution)/shard_map/ppermute | solution.py:805
  99.5 1.9 shard_map.129
  101.5 11.0 %all_to_all.35.sums_ref = f32[32,8,128]{2,1,0:T(8,128)} all-to-all(f32[32,8,128]{2,1,0:T(8,128)S(1)} %get-tuple-element.55), channel_id=1, replica_groups=mesh['row'=8,'y'=2,'core'=2] {'row','y','core'}, dimensions={0} | all-to-all | bytes 262144 | tf_op jit(solution)/shard_map/all_to_all | solution.py:787
  112.5 10.0 %shard_map.130 = (f32[16,4,8,128]{3,2,1,0:T(8,128)S(1)}, f32[16,4,8,128]{3,2,1,0:T(8,128)S(1)}, f32[4,16,256,128]{3,2,1,0:T(8,128)}, f32[4,128,256]{2,1,0:T(8,128)}) custom-call(f32[3,16]{1,0:T(4,128)S(1)} %multiply_bitcast_fusion.lift_ref, f32[32,8,128]{2,1,0:T(8,128)} %copy-done.5, f32[32,8,128]{2,1,0:T(8,128)} %all_to_all.35.sums_ref, ...), custom_call_target="tpu_custom_call" | custom-call | flops 2000000000 | bytes 2359296 | tf_op jit(solution)/shard_map/pallas_call | solution.py:356
  122.7 1.3 collective-permute-done.13.partner_ref
  124.0 0.7 shard_map.131._.__
  124.8 3.5 %all-to-all-start.4 = ((f32[16,4,8,128]{3,2,1,0:T(8,128)}), f32[16,4,8,128]{3,2,1,0:T(8,128)S(1)}, u32[]{:S(2)}, u32[]{:S(2)}) async-start(f32[16,4,8,128]{3,2,1,0:T(8,128)} %shard_map.131._.__), calls=%async_computation.4 | async-start | bytes 524288 | tf_op jit(solution)/shard_map/all_to_all | solution.py:787
  128.3 8.2 %shard_map.132.refs_4_._ = f32[4,16,256,128]{3,2,1,0:T(8,128)} custom-call(f32[16,17]{1,0:T(8,128)S(1)} %broadcast_multiply_fusion.mix_ref, f32[4,16,256,128]{3,2,1,0:T(8,128)} %get-tuple-element.59.lifted_ref, f32[16,4,8,128]{3,2,1,0:T(8,128)} %shard_map.131._.__, f32[16,4,8,128]{3,2,1,0:T(8,128)} %shard_map.131._.__), custom_call_target="tpu_custom_call" | custom-call | flops 2500000000 | bytes 8388608 | tf_op jit(solution)/shard_map/pallas_call | solution.py:356
  136.5 2.2 %all-to-all-done.4.recv_ref = f32[16,4,8,128]{3,2,1,0:T(8,128)S(1)} async-done(((f32[16,4,8,128]{3,2,1,0:T(8,128)}), f32[16,4,8,128]{3,2,1,0:T(8,128)S(1)}, u32[]{:S(2)}, u32[]{:S(2)}) %all-to-all-start.4) | async-done | bytes 262176 | tf_op jit(solution)/shard_map/all_to_all | solution.py:787
  138.8 4.0 %shard_map.133.__ = f32[16,4,8,128]{3,2,1,0:T(8,128)S(1)} custom-call(f32[16,4,8,128]{3,2,1,0:T(8,128)S(1)} %all-to-all-done.4.recv_ref, f32[4,16,8,128]{3,2,1,0:T(8,128)} %copy-done.1, f32[4,16,8,128]{3,2,1,0:T(8,128)} %copy-done.10, f32[4,16,8,128]{3,2,1,0:T(8,128)} %copy-done.11, f32[4,16,8,128]{3,2,1,0:T(8,128)} %copy-done.12, ...), custom_call_target="tpu_custom_call" | custom-call | bytes 1572864 | tf_op jit(solution)/shard_map/pallas_call | solution.py:356
  142.8 14.4 %all_to_all.36.recv_ref = f32[16,4,8,128]{3,2,1,0:T(8,128)S(1)} all-to-all(f32[16,4,8,128]{3,2,1,0:T(8,128)S(1)} %shard_map.133.__), channel_id=1, replica_groups=mesh['row'=8,'y'=2,'core'=2] {'row','y'}, dimensions={0} | all-to-all | bytes 524288 | tf_op jit(solution)/shard_map/all_to_all | solution.py:787
  157.2 8.1 %shard_map.134.point_ref = f32[4,16,256,128]{3,2,1,0:T(8,128)} custom-call(f32[16,17]{1,0:T(8,128)S(1)} %broadcast_multiply_fusion.mix_ref, f32[4,16,256,128]{3,2,1,0:T(8,128)} %get-tuple-element.59.lifted_ref, f32[4,16,256,128]{3,2,1,0:T(8,128)} %shard_map.132.refs_4_._, f32[16,4,8,128]{3,2,1,0:T(8,128)} %copy-done), custom_call_target="tpu_custom_call", output_to_operand_aliasing={{}: (2, {})} | custom-call | flops 2500000000 | bytes 8388608 | tf_op jit(solution)/shard_map/pallas_call | solution.py:356
  165.3 9.6 %shard_map.135 = (f32[2,4,128,256]{3,2,1,0:T(8,128)}, f32[4,128,256]{2,1,0:T(8,128)S(1)}, f32[128,256]{1,0:T(8,128)S(1)}, f32[128,256]{1,0:T(8,128)S(1)}, f32[4,256]{1,0:T(4,128)S(1)}, /*index=5*/f32[4,256]{1,0:T(4,128)S(1)}) custom-call(f32[17]{0:T(128)S(1)} %fusion.proj_ref, f32[32,8,128]{2,1,0:T(8,128)} %copy-done.5, ...), custom_call_target="tpu_custom_call", output_to_operand_aliasing={{0}: (8, {})} | custom-call | flops 2000000000 | bytes 9961472 | tf_op jit(solution)/shard_map/pallas_call | solution.py:356
  174.9 1.1 collective-permute-start.15
  176.0 3.7 %collective-permute-start.16 = (f32[128,256]{1,0:T(8,128)S(1)}, f32[128,256]{1,0:T(8,128)S(1)}, u32[]{:S(2)}, u32[]{:S(2)}) collective-permute-start(f32[128,256]{1,0:T(8,128)S(1)} %get-tuple-element.63), channel_id=1, source_target_pairs={{4,0},{8,4},{12,8},{16,12},{20,16},{24,20},{28,24},{0,28},{5,1},{9... | collective-permute-start | bytes 393224 | tf_op jit(solution)/shard_map/ppermute | solution.py:805
  179.6 1.7 collective-permute-start.18
  181.4 1.3 collective-permute-done.17.refs_2_
  182.7 0.9 collective-permute-done.15.refs_0_
  183.6 0.8 collective-permute-done.16.refs_1_
  184.4 2.3 %shard_map.136 = (f32[4,128,256]{2,1,0:T(8,128)S(1)}, f32[4,128,256]{2,1,0:T(8,128)S(1)}, f32[32,8,128]{2,1,0:T(8,128)S(1)}) custom-call(f32[32,8,128]{2,1,0:T(8,128)S(1)} %copy-done.6, f32[32,8,128]{2,1,0:T(8,128)S(1)} %copy-done.7, f32[4,128,256]{2,1,0:T(8,128)S(1)} %get-tuple-element.61.field_ref, f32[4,128,256]{2,1,0:T(8,128)S(1)} %get-tuple-element.50.field_ref.old_ref, ...), custom_call_target="tpu_custom_call" | custom-call | bytes 5767168 | tf_op jit(solution)/shard_map/pallas_call | solution.py:356
  186.8 12.1 %all_to_all.37.later_ref = f32[32,8,128]{2,1,0:T(8,128)S(1)} all-to-all(f32[32,8,128]{2,1,0:T(8,128)S(1)} %get-tuple-element.67), channel_id=1, replica_groups=mesh['row'=8,'y'=2,'core'=2] {'row','y','core'}, dimensions={0} | all-to-all | bytes 262144 | tf_op jit(solution)/shard_map/all_to_all | solution.py:787
  198.9 2.0 shard_map.137
  (52 shorter events, 3.1 us)
Async XLA Ops:
  0.6 40.0 %copy-start.13 = (f32[16,17]{1,0:T(8,128)S(1)}, f32[16,17]{1,0:T(8,128)}, u32[]{:S(2)}) copy-start(f32[16,17]{1,0:T(8,128)} %param.14) | copy-start | bytes 3268
  2.3 0.7 copy-start.1
  3.0 19.4 %collective-permute-start = (f32[4,16,8,128]{3,2,1,0:T(8,128)S(1)}, f32[4,16,8,128]{3,2,1,0:T(8,128)S(1)}, u32[]{:S(2)}, u32[]{:S(2)}) collective-permute-start(f32[4,16,8,128]{3,2,1,0:T(8,128)S(1)} %get-tuple-element.40), channel_id=1, source_target_pairs={{0,1},{1,2},{2,3},{3,0},{4,5},{5,6},{6,7},{7,4},{8,9},{9,10},{10,1... | collective-permute-start | bytes 786440 | tf_op jit(solution)/shard_map/ppermute | solution.py:848
  3.5 19.0 %collective-permute-start.1 = (f32[4,16,8,128]{3,2,1,0:T(8,128)S(1)}, f32[4,16,8,128]{3,2,1,0:T(8,128)S(1)}, u32[]{:S(2)}, u32[]{:S(2)}) collective-permute-start(f32[4,16,8,128]{3,2,1,0:T(8,128)S(1)} %get-tuple-element.41), channel_id=1, source_target_pairs={{0,2},{1,3},{2,0},{3,1},{4,6},{5,7},{6,4},{7,5},{8,10},{9,11},{10,... | collective-permute-start | bytes 786440 | tf_op jit(solution)/shard_map/ppermute | solution.py:848
  6.0 16.4 %collective-permute-start.2 = (f32[4,16,8,128]{3,2,1,0:T(8,128)S(1)}, f32[4,16,8,128]{3,2,1,0:T(8,128)S(1)}, u32[]{:S(2)}, u32[]{:S(2)}) collective-permute-start(f32[4,16,8,128]{3,2,1,0:T(8,128)S(1)} %get-tuple-element.42), channel_id=1, source_target_pairs={{0,3},{1,0},{2,1},{3,2},{4,7},{5,4},{6,5},{7,6},{8,11},{9,8},{10,9... | collective-permute-start | bytes 786440 | tf_op jit(solution)/shard_map/ppermute | solution.py:848
  9.3 13.1 %all-to-all-start = ((f32[32,8,128]{2,1,0:T(8,128)}), f32[32,8,128]{2,1,0:T(8,128)S(1)}, u32[]{:S(2)}, u32[]{:S(2)}) async-start(f32[32,8,128]{2,1,0:T(8,128)} %get-tuple-element.39), calls=%async_computation | async-start | bytes 262144 | tf_op jit(solution)/shard_map/all_to_all | solution.py:787
  22.4 0.7 copy-start.5
  22.4 26.5 %copy-start.10 = (f32[4,16,8,128]{3,2,1,0:T(8,128)}, f32[4,16,8,128]{3,2,1,0:T(8,128)S(1)}, u32[]{:S(2)}) copy-start(f32[4,16,8,128]{3,2,1,0:T(8,128)S(1)} %collective-permute-done.refs_1_) | copy-start | bytes 786436
  22.4 26.4 %copy-start.11 = (f32[4,16,8,128]{3,2,1,0:T(8,128)}, f32[4,16,8,128]{3,2,1,0:T(8,128)S(1)}, u32[]{:S(2)}) copy-start(f32[4,16,8,128]{3,2,1,0:T(8,128)S(1)} %collective-permute-done.1.refs_2_) | copy-start | bytes 786436
  23.1 0.9 copy-start.2
  24.0 24.9 %copy-start.12 = (f32[4,16,8,128]{3,2,1,0:T(8,128)}, f32[4,16,8,128]{3,2,1,0:T(8,128)S(1)}, u32[]{:S(2)}) copy-start(f32[4,16,8,128]{3,2,1,0:T(8,128)S(1)} %collective-permute-done.2.refs_3_) | copy-start | bytes 786436
  33.8 1.5 collective-permute-start.3
  36.1 14.7 %all-to-all-start.1 = ((f32[16,4,8,128]{3,2,1,0:T(8,128)}), f32[16,4,8,128]{3,2,1,0:T(8,128)S(1)}, u32[]{:S(2)}, u32[]{:S(2)}) async-start(f32[16,4,8,128]{3,2,1,0:T(8,128)} %shard_map.124._.__), calls=%async_computation.1 | async-start | bytes 524288 | tf_op jit(solution)/shard_map/all_to_all | solution.py:787
  48.9 22.7 %copy-start.14 = (f32[17]{0:T(128)S(1)}, f32[17]{0:T(128)}, u32[]{:S(2)}) copy-start(f32[17]{0:T(128)} %param.15) | copy-start | bytes 208
  55.5 16.1 %all-to-all-start.2 = ((f32[16,4,8,128]{3,2,1,0:T(8,128)}), f32[16,4,8,128]{3,2,1,0:T(8,128)S(1)}, u32[]{:S(2)}, u32[]{:S(2)}) async-start(f32[16,4,8,128]{3,2,1,0:T(8,128)} %shard_map.126.__), calls=%async_computation.2 | async-start | bytes 524288 | tf_op jit(solution)/shard_map/all_to_all | solution.py:787
  60.5 19.2 %collective-permute-start.7 = (f32[4,256]{1,0:T(4,128)S(1)}, f32[4,256]{1,0:T(4,128)S(1)}, u32[]{:S(2)}, u32[]{:S(2)}) collective-permute-start(f32[4,256]{1,0:T(4,128)S(1)} %get-tuple-element.48), channel_id=1, source_target_pairs={{0,1},{1,2},{2,3},{3,0},{4,5},{5,6},{6,7},{7,4},{8,9},{9,10},{10,1... | collective-permute-start | bytes 12296 | tf_op jit(solution)/shard_map/ppermute | solution.py:804
  60.6 19.1 %collective-permute-start.8 = (f32[4,256]{1,0:T(4,128)S(1)}, f32[4,256]{1,0:T(4,128)S(1)}, u32[]{:S(2)}, u32[]{:S(2)}) collective-permute-start(f32[4,256]{1,0:T(4,128)S(1)} %get-tuple-element.49), channel_id=1, source_target_pairs={{1,0},{2,1},{3,2},{0,3},{5,4},{6,5},{7,6},{4,7},{9,8},{10,9},{11,1... | collective-permute-start | bytes 12296 | tf_op jit(solution)/shard_map/ppermute | solution.py:805
  62.3 17.4 %collective-permute-start.5 = (f32[128,256]{1,0:T(8,128)S(1)}, f32[128,256]{1,0:T(8,128)S(1)}, u32[]{:S(2)}, u32[]{:S(2)}) collective-permute-start(f32[128,256]{1,0:T(8,128)S(1)} %get-tuple-element.46), channel_id=1, source_target_pairs={{0,4},{4,8},{8,12},{12,16},{16,20},{20,24},{24,28},{28,0},{1,5},{5... | collective-permute-start | bytes 393224 | tf_op jit(solution)/shard_map/ppermute | solution.py:804
  64.2 15.5 %collective-permute-start.6 = (f32[128,256]{1,0:T(8,128)S(1)}, f32[128,256]{1,0:T(8,128)S(1)}, u32[]{:S(2)}, u32[]{:S(2)}) collective-permute-start(f32[128,256]{1,0:T(8,128)S(1)} %get-tuple-element.47), channel_id=1, source_target_pairs={{4,0},{8,4},{12,8},{16,12},{20,16},{24,20},{28,24},{0,28},{5,1},{9... | collective-permute-start | bytes 393224 | tf_op jit(solution)/shard_map/ppermute | solution.py:805
  71.6 8.2 %collective-permute-start.4 = (f32[16,4,8,128]{3,2,1,0:T(8,128)S(1)}, f32[16,4,8,128]{3,2,1,0:T(8,128)S(1)}, u32[]{:S(2)}, u32[]{:S(2)}) collective-permute-start(f32[16,4,8,128]{3,2,1,0:T(8,128)S(1)} %all-to-all-done.2.recv_ref), channel_id=1, source_target_pairs={{0,1},{1,0},{2,3},{3,2},{4,5},{5,4},{6,7},{7,6},{8,9},{9,8},{10,11... | collective-permute-start | bytes 786440 | tf_op jit(solution)/shard_map/ppermute | solution.py:791
  79.7 19.9 %copy-start.3 = (bf16[4,128,256]{2,1,0:T(8,128)(2,1)S(1)}, bf16[4,128,256]{2,1,0:T(8,128)(2,1)}, u32[]{:S(2)}) copy-start(bf16[4,128,256]{2,1,0:T(8,128)(2,1)} %perm_ref.9) | copy-start | bytes 786436
  79.7 19.9 %copy-start.8 = (f32[4,128,256]{2,1,0:T(8,128)S(1)}, f32[4,128,256]{2,1,0:T(8,128)}, u32[]{:S(2)}) copy-start(f32[4,128,256]{2,1,0:T(8,128)} %res_ref.3) | copy-start | bytes 1572868
  88.8 8.7 %collective-permute-start.9 = (f32[128,256]{1,0:T(8,128)S(1)}, f32[128,256]{1,0:T(8,128)S(1)}, u32[]{:S(2)}, u32[]{:S(2)}) collective-permute-start(f32[128,256]{1,0:T(8,128)S(1)} %get-tuple-element.51), channel_id=1, source_target_pairs={{0,4},{4,8},{8,12},{12,16},{16,20},{20,24},{24,28},{28,0},{1,5},{5... | collective-permute-start | bytes 393224 | tf_op jit(solution)/shard_map/ppermute | solution.py:804
  91.1 8.4 %collective-permute-start.10 = (f32[128,256]{1,0:T(8,128)S(1)}, f32[128,256]{1,0:T(8,128)S(1)}, u32[]{:S(2)}, u32[]{:S(2)}) collective-permute-start(f32[128,256]{1,0:T(8,128)S(1)} %get-tuple-element.52), channel_id=1, source_target_pairs={{4,0},{8,4},{12,8},{16,12},{20,16},{24,20},{28,24},{0,28},{5,1},{9... | collective-permute-start | bytes 393224 | tf_op jit(solution)/shard_map/ppermute | solution.py:805
  93.5 3.0 %collective-permute-start.11 = (f32[4,256]{1,0:T(4,128)S(1)}, f32[4,256]{1,0:T(4,128)S(1)}, u32[]{:S(2)}, u32[]{:S(2)}) collective-permute-start(f32[4,256]{1,0:T(4,128)S(1)} %get-tuple-element.53), channel_id=1, source_target_pairs={{0,1},{1,2},{2,3},{3,0},{4,5},{5,6},{6,7},{7,4},{8,9},{9,10},{10,1... | collective-permute-start | bytes 12296 | tf_op jit(solution)/shard_map/ppermute | solution.py:804
  93.5 3.1 %collective-permute-start.12 = (f32[4,256]{1,0:T(4,128)S(1)}, f32[4,256]{1,0:T(4,128)S(1)}, u32[]{:S(2)}, u32[]{:S(2)}) collective-permute-start(f32[4,256]{1,0:T(4,128)S(1)} %get-tuple-element.54), channel_id=1, source_target_pairs={{1,0},{2,1},{3,2},{0,3},{5,4},{6,5},{7,6},{4,7},{9,8},{10,9},{11,1... | collective-permute-start | bytes 12296 | tf_op jit(solution)/shard_map/ppermute | solution.py:805
  122.5 1.5 collective-permute-start.13
  124.8 14.0 %all-to-all-start.4 = ((f32[16,4,8,128]{3,2,1,0:T(8,128)}), f32[16,4,8,128]{3,2,1,0:T(8,128)S(1)}, u32[]{:S(2)}, u32[]{:S(2)}) async-start(f32[16,4,8,128]{3,2,1,0:T(8,128)} %shard_map.131._.__), calls=%async_computation.4 | async-start | bytes 524288 | tf_op jit(solution)/shard_map/all_to_all | solution.py:787
  142.8 14.4 %copy-start = (f32[16,4,8,128]{3,2,1,0:T(8,128)}, f32[16,4,8,128]{3,2,1,0:T(8,128)S(1)}, u32[]{:S(2)}) copy-start(f32[16,4,8,128]{3,2,1,0:T(8,128)S(1)} %shard_map.133.__) | copy-start | bytes 786436
  157.2 8.1 %collective-permute-start.14 = (f32[16,4,8,128]{3,2,1,0:T(8,128)S(1)}, f32[16,4,8,128]{3,2,1,0:T(8,128)S(1)}, u32[]{:S(2)}, u32[]{:S(2)}) collective-permute-start(f32[16,4,8,128]{3,2,1,0:T(8,128)S(1)} %all_to_all.36.recv_ref), channel_id=1, source_target_pairs={{0,1},{1,0},{2,3},{3,2},{4,5},{5,4},{6,7},{7,6},{8,9},{9,8},{10,11... | collective-permute-start | bytes 786440 | tf_op jit(solution)/shard_map/ppermute | solution.py:791
  165.3 19.1 %copy-start.4 = (bf16[4,128,256]{2,1,0:T(8,128)(2,1)S(1)}, bf16[4,128,256]{2,1,0:T(8,128)(2,1)}, u32[]{:S(2)}) copy-start(bf16[4,128,256]{2,1,0:T(8,128)(2,1)} %perm_ref.9) | copy-start | bytes 786436
  165.3 19.1 %copy-start.6 = (f32[32,8,128]{2,1,0:T(8,128)S(1)}, f32[32,8,128]{2,1,0:T(8,128)}, u32[]{:S(2)}) copy-start(f32[32,8,128]{2,1,0:T(8,128)} %copy-done.5) | copy-start | bytes 393220
  165.3 19.1 %copy-start.7 = (f32[32,8,128]{2,1,0:T(8,128)S(1)}, f32[32,8,128]{2,1,0:T(8,128)}, u32[]{:S(2)}) copy-start(f32[32,8,128]{2,1,0:T(8,128)} %all_to_all.35.sums_ref) | copy-start | bytes 393220
  165.3 19.1 %copy-start.9 = (f32[4,128,256]{2,1,0:T(8,128)S(1)}, f32[4,128,256]{2,1,0:T(8,128)}, u32[]{:S(2)}) copy-start(f32[4,128,256]{2,1,0:T(8,128)} %get-tuple-element.66.refs_12_.res_ref) | copy-start | bytes 1572868
  174.9 8.7 %collective-permute-start.15 = (f32[128,256]{1,0:T(8,128)S(1)}, f32[128,256]{1,0:T(8,128)S(1)}, u32[]{:S(2)}, u32[]{:S(2)}) collective-permute-start(f32[128,256]{1,0:T(8,128)S(1)} %get-tuple-element.62), channel_id=1, source_target_pairs={{0,4},{4,8},{8,12},{12,16},{16,20},{20,24},{24,28},{28,0},{1,5},{5... | collective-permute-start | bytes 393224 | tf_op jit(solution)/shard_map/ppermute | solution.py:804
  176.0 8.4 %collective-permute-start.16 = (f32[128,256]{1,0:T(8,128)S(1)}, f32[128,256]{1,0:T(8,128)S(1)}, u32[]{:S(2)}, u32[]{:S(2)}) collective-permute-start(f32[128,256]{1,0:T(8,128)S(1)} %get-tuple-element.63), channel_id=1, source_target_pairs={{4,0},{8,4},{12,8},{16,12},{20,16},{24,20},{28,24},{0,28},{5,1},{9... | collective-permute-start | bytes 393224 | tf_op jit(solution)/shard_map/ppermute | solution.py:805
  179.6 3.0 %collective-permute-start.17 = (f32[4,256]{1,0:T(4,128)S(1)}, f32[4,256]{1,0:T(4,128)S(1)}, u32[]{:S(2)}, u32[]{:S(2)}) collective-permute-start(f32[4,256]{1,0:T(4,128)S(1)} %get-tuple-element.64), channel_id=1, source_target_pairs={{0,1},{1,2},{2,3},{3,0},{4,5},{5,6},{6,7},{7,4},{8,9},{9,10},{10,1... | collective-permute-start | bytes 12296 | tf_op jit(solution)/shard_map/ppermute | solution.py:804
  179.6 3.1 %collective-permute-start.18 = (f32[4,256]{1,0:T(4,128)S(1)}, f32[4,256]{1,0:T(4,128)S(1)}, u32[]{:S(2)}, u32[]{:S(2)}) collective-permute-start(f32[4,256]{1,0:T(4,128)S(1)} %get-tuple-element.65), channel_id=1, source_target_pairs={{1,0},{2,1},{3,2},{0,3},{5,4},{6,5},{7,6},{4,7},{9,8},{10,9},{11,1... | collective-permute-start | bytes 12296 | tf_op jit(solution)/shard_map/ppermute | solution.py:805

commit v8 on v7

--- a/solution.py
+++ b/solution.py
@@ -228,6 +228,7 @@
 COL = ("y", "core")
 CHIPS = ("row", "y")
 BOTH = ("row", "y", "core")
+CHUNK = 32
 F32 = jnp.float32
 BF16 = jnp.bfloat16
 
@@ -290,6 +291,7 @@
         angle = angles(freqs, place * cols + np.arange(cols), n_col * cols)
         own = np.arange(KY).reshape(-1, 2, SUBLANES)[:, place % 2].reshape(-1)
         partner = np.arange(KY).reshape(-1, 2, SUBLANES)[:, 1 - place % 2].reshape(-1)
+        angle = angle[np.concatenate([own, partner])]
         both = np.concatenate([np.cos(angle), np.sin(angle)], 0)
         high, low = split_table(both)
         forward.append(
@@ -301,9 +303,6 @@
                 0,
             )
         )
-        angle = angle[np.concatenate([own, partner])]
-        both = np.concatenate([np.cos(angle), np.sin(angle)], 0)
-        high, low = split_table(both)
         back.append(
             np.concatenate(
                 [
@@ -441,17 +440,14 @@
     part = part[: 2 * KY] + part[2 * KY :]
     lane = lax.broadcasted_iota(jnp.int32, (KY, LANES), 1)
     sign = jnp.where(lane < LANES // 2, 1.0, -1.0).astype(F32)
-    n_col = KY // SUBLANES
-    core = lax.axis_index("core")
+    n_chip = KY // SUBLANES // 2
     for row in range(groups):
         lanes = slice(row * LANES, (row + 1) * LANES)
         block = part[:KY, lanes] + pltpu.roll(part[KY:, lanes], LANES // 2, 1) * sign
-        for place in range(n_col // 2):
-            start = 2 * place * SUBLANES
-            even = block[start : start + SUBLANES]
-            odd = block[start + SUBLANES : start + 2 * SUBLANES]
-            own_ref[row * n_col // 2 + place, 0] = jnp.where(core == 0, even, odd)
-            partner_ref[row * n_col // 2 + place, 0] = jnp.where(core == 0, odd, even)
+        for side, ref in enumerate((own_ref, partner_ref)):
+            for place in range(n_chip):
+                start = (side * n_chip + place) * SUBLANES
+                ref[row * n_chip + place, 0] = block[start : start + SUBLANES]
 
 
 def lift_first_body(cells, lift_ref, sums_ref, res_ref, perm_ref, deep_ref, col_ref, *refs):
@@ -464,6 +460,10 @@
 
 def join_body(own_ref, partner_ref, out_ref):
     out_ref[...] = own_ref[...] + partner_ref[...]
+
+
+def tie_body(*_):
+    pass
 
 
 def next_scalars(first_ref, sums_ref):
@@ -614,7 +614,7 @@
             store(places - place, even - odd)
 
 
-def back_transform(recv_ref, other_ref, point_ref, proj_ref, col_ref, deep_ref, wave_ref, scale):
+def back_transform(recv_ref, other_ref, point_ref, proj_ref, col_ref, deep_ref, wave_ref, total_ref, scale):
     groups = 2 * KZ * CHANNELS // LANES
     n_col = KY // SUBLANES
     cols = col_ref.shape[2] // 2
@@ -631,53 +631,74 @@
         pieces.append(jnp.concatenate(split_three(both), 0).T.astype(BF16))
     part = matmul(jnp.concatenate(pieces, 0), col_ref[lax.axis_index(COL)])
     wave_ref[...] = part[:, :cols] + part[:, cols:]
-    total = None
+
+    def waves(out):
+        both = [wave_ref[pl.ds(out + j, half, stride=CHANNELS), :] for j in range(2)]
+        high, middle, low = (
+            part.astype(BF16) for part in split_three(jnp.concatenate(both, 1))
+        )
+        return jnp.concatenate([high, middle, low, high], 0)
+
     for out in range(0, CHANNELS, 2):
-        waves = jnp.concatenate(
-            [wave_ref[pl.ds(out + j, half, stride=CHANNELS), :] for j in range(2)], 1
-        )
-        high, middle, low = (part.astype(BF16) for part in split_three(waves))
-        spatial = matmul(deep_ref[...], jnp.concatenate([high, middle, low, high], 0))
-        for j in range(2):
-            hidden = scaled_gelu(spatial[:, j * cols : (j + 1) * cols] + point_ref[0, out + j])
-            term = proj_ref[out + j] * hidden
-            total = term if total is None else total + term
-    return (scale * (total + proj_ref[CHANNELS])).T
-
-
-def put_edges(update, field_ref, low_ref, high_ref, left_ref, right_ref):
+        spatial = matmul(deep_ref[...], waves(out))
+        for start in range(0, spatial.shape[0], CHUNK):
+            lines = slice(start, start + CHUNK)
+            total = proj_ref[CHANNELS] if out == 0 else total_ref[lines]
+            for j in range(2):
+                value = spatial[lines, j * cols : (j + 1) * cols] + point_ref[0, out + j, lines]
+                total = total + proj_ref[out + j] * scaled_gelu(value)
+            total_ref[lines] = total
+    return (scale * total_ref[...]).T
+
+
+def put_lines(update, place, left_ref, right_ref):
+    left_ref[pl.ds(place, 1), :] = update[:1]
+    right_ref[pl.ds(place, 1), :] = update[update.shape[0] - 1 :]
+
+
+def back_outer(update, kept_ref, field_ref, low_ref, high_ref, left_ref, right_ref):
     step = pl.program_id(0)
+    kept_ref[0, 0] = update
     field_ref[0] = update
-    left_ref[pl.ds(step, 1), :] = update[:1]
-    right_ref[pl.ds(step, 1), :] = update[update.shape[0] - 1 :]
+    last = left_ref.shape[0] - 1
 
     @pl.when(step == 0)
     def _():
         low_ref[...] = update
-
-    @pl.when(step == pl.num_programs(0) - 1)
+        put_lines(update, 0, left_ref, right_ref)
+
+    @pl.when(step == 1)
     def _():
         high_ref[...] = update
-
-
-def back_first_body(cells, proj_ref, sums_ref, recv_ref, other_ref, point_ref, col_ref, deep_ref, *refs):
-    kept_ref, *edges, wave_ref = refs[4:]
-    scale = scale_of(gathered(sums_ref, 0), cells)
+        put_lines(update, last, left_ref, right_ref)
+
+
+def back_inner(update, left_in, right_in, kept_ref, field_ref, left_ref, right_ref):
+    step = pl.program_id(0)
+    kept_ref[0, 0] = update
+    field_ref[0] = update
+    last = left_ref.shape[0] - 1
+
+    @pl.when(step == 0)
+    def _():
+        for place in (0, last):
+            line = slice(place, place + 1)
+            left_ref[line] = left_in[line]
+            right_ref[line] = right_in[line]
+
+    put_lines(update, step + 1, left_ref, right_ref)
+
+
+def back_body(scale_from, scalars, waiting, inner, proj_ref, *refs):
+    scalar_refs, refs = refs[:scalars], refs[scalars:]
+    recv_ref, other_ref, point_ref, col_ref, deep_ref = refs[:5]
+    refs = refs[5 + waiting :]
+    *outs, wave_ref, total_ref = refs
     update = back_transform(
-        recv_ref, other_ref, point_ref, proj_ref, col_ref, deep_ref, wave_ref, scale
-    )
-    kept_ref[0, 0] = update
-    put_edges(update, *edges)
-
-
-def back_next_body(cells, proj_ref, first_ref, sums_ref, recv_ref, other_ref, point_ref, col_ref, deep_ref, _, kept_ref, *refs):
-    *edges, wave_ref = refs
-    _, _, total = next_scalars(first_ref, sums_ref)
-    update = back_transform(
-        recv_ref, other_ref, point_ref, proj_ref, col_ref, deep_ref, wave_ref, scale_of(total, cells)
-    )
-    kept_ref[0, 0] = update
-    put_edges(update, *edges)
+        recv_ref, other_ref, point_ref, proj_ref, col_ref, deep_ref, wave_ref, total_ref,
+        scale_from(*scalar_refs),
+    )
+    (back_inner if inner else back_outer)(update, *outs)
 
 
 def stencil(fields, perms):
@@ -795,15 +816,15 @@
     return exchange(partial, BOTH)
 
 
+def shift_planes(axis, first, last):
+    count = lax.axis_size(axis)
+    forward = [(i, (i + 1) % count) for i in range(count)]
+    backward = [(target, source) for source, target in forward]
+    return lax.ppermute(last, axis, forward), lax.ppermute(first, axis, backward)
+
+
 def neighbours(low, high, left, right):
-    found = []
-    for axis, first, last in (("row", low, high), (COL, left, right)):
-        count = lax.axis_size(axis)
-        forward = [(i, (i + 1) % count) for i in range(count)]
-        backward = [(target, source) for source, target in forward]
-        found.append(lax.ppermute(last, axis, forward))
-        found.append(lax.ppermute(first, axis, backward))
-    return found
+    return shift_planes("row", low, high) + shift_planes(COL, left, right)
 
 
 def tiled_local(right_side, permeability, lift_weight, spectral_weight, mix_weight, proj_weight):
@@ -903,7 +924,77 @@
         blocks = modes(received, point)
         received = exchange(blocks, CHIPS)
         point = points(lifted, 1, point, blocks)
+        received = pl.pallas_call(
+            tie_body,
+            out_shape=spectra,
+            in_specs=[anywhere, anywhere],
+            out_specs=anywhere,
+            input_output_aliases={0: 0},
+        )(received, point)
         return received, swap(received), point
+
+    def back(index, scale_from, scalars, fields, waiting):
+        def run(place_of, steps, inner, waiting, outs, out_specs, alias, loose):
+            count_in = 1 + len(scalars)
+            spectra_at = pl.BlockSpec(
+                (n_row * n_chip, 1, SUBLANES, LANES), lambda i: (0, place_of(i), 0, 0)
+            )
+            point_at = pl.BlockSpec(
+                (1, CHANNELS, depth, cols), lambda i: (place_of(i), 0, 0, 0)
+            )
+            kept_at = pl.BlockSpec((1, 1, cols, depth), lambda i: (index, place_of(i), 0, 0))
+            plane_at = pl.BlockSpec((1, cols, depth), lambda i: (place_of(i), 0, 0))
+            return call(
+                functools.partial(
+                    back_body,
+                    scale_from,
+                    len(scalars),
+                    2 if inner else len(waiting),
+                    inner,
+                ),
+                outs,
+                [smem]
+                + [vmem] * len(scalars)
+                + [spectra_at, spectra_at, point_at, vmem, vmem]
+                + ([anywhere, anywhere, vmem, vmem] if inner else [anywhere] * len(waiting)),
+                (kept_at, plane_at) + out_specs,
+                grid=(steps,),
+                scratch=[zt_scratch, pltpu.VMEM((depth, cols), F32)],
+                flops=back_flops / 2,
+                moved=9 * field_bytes,
+                alias={count_in + 5 + i: o for i, o in alias},
+                limit=12,
+                near=(count_in, count_in + 1)
+                + tuple(
+                    count_in + 5 + i
+                    for i, array in enumerate(waiting)
+                    if array.size != kept_shape.size
+                ),
+                loose=loose,
+            )(proj_weight, *scalars, *fields, col_back, deep_back, *waiting)
+
+        kept, field_out, low, high, left, right = run(
+            lambda i: i * (rows - 1),
+            2,
+            False,
+            waiting,
+            (kept_shape, field) + edge_shapes,
+            (vmem,) * 4,
+            [(0, 0)] if index else [],
+            (1,),
+        )
+        halo_rows = shift_planes("row", low, high)
+        kept, field_out, left, right = run(
+            lambda i: i + 1,
+            rows - 2,
+            True,
+            (kept, field_out, left, right),
+            (kept_shape, field) + edge_shapes[2:],
+            (vmem,) * 2,
+            [(0, 0), (1, 1)],
+            (1,),
+        )
+        return (kept, field_out) + halo_rows + shift_planes(COL, left, right)
 
     own, partner, lifted = call(
         functools.partial(lift_first_body, cells),
@@ -919,22 +1010,15 @@
         moved=2 * field_bytes + spectra_bytes,
     )(lift_weight, squares, right_side, permeability, deep_forward, col_forward, *weights)
     received, other, point = mixed_modes(own, partner, lifted)
-    kept, old, *edges = call(
-        functools.partial(back_first_body, cells),
-        (kept_shape, field) + edge_shapes,
-        [smem, vmem, spectra_block, spectra_block, point_block, vmem, vmem]
-        + [anywhere] * 4,
-        (pl.BlockSpec((1, 1, cols, depth), lambda i: (0, i, 0, 0)), plane) + (vmem,) * 4,
-        near=(2, 3, 7, 8, 9, 10),
-        loose=(1,),
-        grid=(rows,),
-        scratch=[zt_scratch],
-        limit=12,
-        flops=back_flops,
-        moved=18 * field_bytes,
-    )(proj_weight, squares, received, other, point, col_back, deep_back, *perm_halo)
-
-    old_halo = neighbours(*edges)
+    kept, old, *edges = back(
+        0,
+        lambda first_ref: scale_of(gathered(first_ref, 0), cells),
+        (squares,),
+        (received, other, point),
+        perm_halo,
+    )
+
+    old_halo = edges
     args = (old, permeability, *old_halo, *perm_halo, right_side)
     image, sums = call(
         operator_first_body,
@@ -963,22 +1047,15 @@
         moved=4 * field_bytes + spectra_bytes,
     )(lift_weight, squares, sums, right_side, image, permeability, deep_forward, col_forward)
     received, other, point = mixed_modes(own, partner, lifted)
-    kept, update, *edges = call(
-        functools.partial(back_next_body, cells),
-        (kept_shape, field) + edge_shapes,
-        [smem, vmem, vmem, spectra_block, spectra_block, point_block, vmem, vmem, anywhere],
-        (pl.BlockSpec((1, 1, cols, depth), lambda i: (1, i, 0, 0)), plane) + (vmem,) * 4,
-        near=(3, 4),
-        loose=(1,),
-        grid=(rows,),
-        limit=12,
-        scratch=[zt_scratch],
-        flops=back_flops,
-        moved=19 * field_bytes,
-        alias={8: 0},
-    )(proj_weight, squares, sums, received, other, point, col_back, deep_back, kept)
-
-    halo = neighbours(*edges)
+    kept, update, *edges = back(
+        1,
+        lambda first_ref, sums_ref: scale_of(next_scalars(first_ref, sums_ref)[2], cells),
+        (squares, sums),
+        (received, other, point),
+        (kept,),
+    )
+
+    halo = edges
     args = (squares, sums, update, old, permeability, *halo, *old_halo, *perm_halo, residual, image)
     way, last_image, later = call(
         functools.partial(operator_next_body, cells),
@@ -1017,6 +1094,8 @@
         and cols == LANES
         and depth % LANES == 0
         and rows * n_row >= KX
+        and rows > 2
+        and rows % 2 == 0
     )
 
 

time: 202 us -> 198 us (0.980)
  blocking collectives: 37.6 us -> 20.7 us
  Pallas kernels: 91 us -> 96.3 us
  starting transfers between devices: 42.3 us -> 47.1 us
  local copies, waits for them, and re-layouts: 2.33 us -> 5.6 us
    all_to_all x3 -> x2, blocking collectives: 37.6 us -> 20.7 us  [exchange(): return lax.all_to_all(blocks, axes, split_axis=0, concat_axis=0, tiled=True)]
    pallas_call x17 -> x19, Pallas kernels: 91 us -> 96.3 us  [wrapped(): found = run(*held)]
    all_to_all x4 -> x5, starting transfers between devices: 18 us -> 22.8 us  [exchange(): return lax.all_to_all(blocks, axes, split_axis=0, concat_axis=0, tiled=True)]
    unnamed x30 -> x36, local copies, waits for them, and re-layouts: 2.33 us -> 5.6 us
    all_to_all x4 -> x5, waiting for transfers between devices: 16.2 us -> 14.8 us  [exchange(): return lax.all_to_all(blocks, axes, split_axis=0, concat_axis=0, tiled=True)]
  transfers between devices with their start and end apart: 23 -> 24, of which waited for: 12 -> 12; matrix products, arithmetic and copies ran while one was open for 0% -> 0% of each run, Pallas kernels for 17% -> 23%
where the time goes in v8:
time: 198 us; the launch traced here: 197 us
  Pallas kernels  96.3 us (49%)
  starting transfers between devices  47.1 us (24%)
  waiting for transfers between devices  25.9 us (13%)
  blocking collectives  20.7 us (10%)
  local copies, waits for them, and re-layouts  5.6 us (3%)
    pallas_call x19, Pallas kernels, wrapped(): found = run(*held)  96.3 us
    all_to_all x5, starting transfers between devices, exchange(): return lax.all_to_all(blocks, axes, split_axis=0, concat_axis=0, tiled=True)  22.8 us
    all_to_all x2, blocking collectives, exchange(): return lax.all_to_all(blocks, axes, split_axis=0, concat_axis=0, tiled=True)  20.7 us
    ppermute x6, starting transfers between devices, shift_planes(): lax.ppermute(first, axis, backward)  16.7 us
    all_to_all x5, waiting for transfers between devices, exchange(): return lax.all_to_all(blocks, axes, split_axis=0, concat_axis=0, tiled=True)  14.8 us
    unnamed x36, local copies, waits for them, and re-layouts  5.6 us
    ppermute x6, waiting for transfers between devices, shift_planes(): lax.ppermute(last, axis, forward)  5.55 us
    ppermute x3, starting transfers between devices, tiled_local(): lax.ppermute(part, COL, [(i, (i + shift + 1) % n_col) for i in range(n_co...  4.45 us
  transfers between devices with their start and end apart: 24, of which 12 were waited for; matrix products, arithmetic and copies ran while one was open for 0% of the time, Pallas kernels for 23%

profile of v8, /device:TPU:0, one launch (start us, length us, event | category | flops | bytes accessed | tf_op | source)
XLA Modules:
  0.0 197.2 jit_solution(11234253057966265649)
XLA Ops:
  0.6 1.7 shard_map.121
  3.5 2.6 %collective-permute-start.1 = (f32[4,16,8,128]{3,2,1,0:T(8,128)S(1)}, f32[4,16,8,128]{3,2,1,0:T(8,128)S(1)}, u32[]{:S(2)}, u32[]{:S(2)}) collective-permute-start(f32[4,16,8,128]{3,2,1,0:T(8,128)S(1)} %get-tuple-element.49), channel_id=1, source_target_pairs={{0,2},{1,3},{2,0},{3,1},{4,6},{5,7},{6,4},{7,5},{8,10},{9,11},{10,... | collective-permute-start | bytes 786440 | tf_op jit(solution)/shard_map/ppermute | solution.py:869
  6.0 1.4 collective-permute-start.2
  7.5 1.8 shard_map.122
  9.3 4.9 %all-to-all-start = ((f32[32,8,128]{2,1,0:T(8,128)}), f32[32,8,128]{2,1,0:T(8,128)S(1)}, u32[]{:S(2)}, u32[]{:S(2)}) async-start(f32[32,8,128]{2,1,0:T(8,128)} %get-tuple-element.47), calls=%async_computation | async-start | bytes 262144 | tf_op jit(solution)/shard_map/all_to_all | solution.py:808
  14.9 7.5 %all-to-all-done.sums_ref.refs_0_.first_ref = f32[32,8,128]{2,1,0:T(8,128)S(1)} async-done(((f32[32,8,128]{2,1,0:T(8,128)}), f32[32,8,128]{2,1,0:T(8,128)S(1)}, u32[]{:S(2)}, u32[]{:S(2)}) %all-to-all-start) | async-done | bytes 131104 | tf_op jit(solution)/shard_map/all_to_all | solution.py:808
  24.0 9.8 %shard_map.123 = (f32[16,4,8,128]{3,2,1,0:T(8,128)S(1)}, f32[16,4,8,128]{3,2,1,0:T(8,128)S(1)}, f32[4,16,256,128]{3,2,1,0:T(8,128)}) custom-call(f32[3,16]{1,0:T(4,128)S(1)} %multiply_bitcast_fusion.lift_ref, f32[32,8,128]{2,1,0:T(8,128)} %copy-done, f32[4,128,256]{2,1,0:T(8,128)} %res_ref.3, bf16[4,128,256]{2,1,0:T(8,128)(2,1)} %perm_ref.9, ...), custom_call_target="tpu_custom_call" | custom-call | flops 2000000000 | bytes 1310720 | tf_op jit(solution)/shard_map/pallas_call | solution.py:355
  34.0 1.3 collective-permute-done.3.partner_ref
  36.1 4.5 %all-to-all-start.1 = ((f32[16,4,8,128]{3,2,1,0:T(8,128)}), f32[16,4,8,128]{3,2,1,0:T(8,128)S(1)}, u32[]{:S(2)}, u32[]{:S(2)}) async-start(f32[16,4,8,128]{3,2,1,0:T(8,128)} %shard_map.124._.__), calls=%async_computation.1 | async-start | bytes 524288 | tf_op jit(solution)/shard_map/all_to_all | solution.py:808
  40.6 8.2 %shard_map.125.refs_4_._ = f32[4,16,256,128]{3,2,1,0:T(8,128)} custom-call(f32[16,17]{1,0:T(8,128)S(1)} %broadcast_multiply_fusion.mix_ref, f32[4,16,256,128]{3,2,1,0:T(8,128)} %get-tuple-element.53.lifted_ref, f32[16,4,8,128]{3,2,1,0:T(8,128)} %shard_map.124._.__, f32[16,4,8,128]{3,2,1,0:T(8,128)} %shard_map.124._.__), custom_call_target="tpu_custom_call" | custom-call | flops 2500000000 | bytes 8388608 | tf_op jit(solution)/shard_map/pallas_call | solution.py:355
  48.9 1.9 all-to-all-done.1.recv_ref
  50.8 4.7 %shard_map.126.__ = f32[16,4,8,128]{3,2,1,0:T(8,128)} custom-call(f32[16,4,8,128]{3,2,1,0:T(8,128)S(1)} %all-to-all-done.1.recv_ref, f32[4,16,8,128]{3,2,1,0:T(8,128)} %copy-done.7, f32[4,16,8,128]{3,2,1,0:T(8,128)} %copy-done.13, f32[4,16,8,128]{3,2,1,0:T(8,128)} %copy-done.14, f32[4,16,8,128]{3,2,1,0:T(8,128)} %copy-done.15, ...), custom_call_target="tpu_custom_call" | custom-call | bytes 1572864 | tf_op jit(solution)/shard_map/pallas_call | solution.py:355
  55.4 5.0 %all-to-all-start.2 = ((f32[16,4,8,128]{3,2,1,0:T(8,128)}), f32[16,4,8,128]{3,2,1,0:T(8,128)S(1)}, u32[]{:S(2)}, u32[]{:S(2)}) async-start(f32[16,4,8,128]{3,2,1,0:T(8,128)} %shard_map.126.__), calls=%async_computation.2 | async-start | bytes 524288 | tf_op jit(solution)/shard_map/all_to_all | solution.py:808
  60.5 8.1 %shard_map.127.__1_.refs_3_ = f32[4,16,256,128]{3,2,1,0:T(8,128)} custom-call(f32[16,17]{1,0:T(8,128)S(1)} %broadcast_multiply_fusion.mix_ref, f32[4,16,256,128]{3,2,1,0:T(8,128)} %get-tuple-element.53.lifted_ref, f32[4,16,256,128]{3,2,1,0:T(8,128)} %shard_map.125.refs_4_._, f32[16,4,8,128]{3,2,1,0:T(8,128)} %shard_map.126.__), custom_call_target="tpu_custom_call", output_to_operand_aliasing={{}: (2, {})} | custom-call | flops 2500000000 | bytes 8388608 | tf_op jit(solution)/shard_map/pallas_call | solution.py:355
  68.6 1.5 all-to-all-done.2.__0_
  71.3 1.2 collective-permute-start.8
  72.5 1.1 collective-permute-start.5
  73.6 3.7 %collective-permute-start.6 = (f32[128,256]{1,0:T(8,128)S(1)}, f32[128,256]{1,0:T(8,128)S(1)}, u32[]{:S(2)}, u32[]{:S(2)}) collective-permute-start(f32[128,256]{1,0:T(8,128)S(1)} %get-tuple-element.55), channel_id=1, source_target_pairs={{4,0},{8,4},{12,8},{16,12},{20,16},{24,20},{28,24},{0,28},{5,1},{9... | collective-permute-start | bytes 393224 | tf_op jit(solution)/shard_map/ppermute | solution.py:823
  77.3 3.0 %collective-permute-done.5.refs_6_.refs_4_.refs_8_ = f32[128,256]{1,0:T(8,128)S(1)} collective-permute-done((f32[128,256]{1,0:T(8,128)S(1)}, f32[128,256]{1,0:T(8,128)S(1)}, u32[]{:S(2)}, u32[]{:S(2)}) %collective-permute-start.5) | collective-permute-done | bytes 131104 | tf_op jit(solution)/shard_map/ppermute | solution.py:823
  80.3 1.1 collective-permute-done.6.refs_7_.refs_5_.refs_9_
  81.3 0.9 copy-done.5
  82.3 5.8 %shard_map.129 = (f32[2,4,128,256]{3,2,1,0:T(8,128)}, f32[4,128,256]{2,1,0:T(8,128)S(1)}, f32[128,256]{1,0:T(8,128)S(1)}, f32[128,256]{1,0:T(8,128)S(1)}, f32[4,256]{1,0:T(4,128)S(1)}, /*index=5*/f32[4,256]{1,0:T(4,128)S(1)}) custom-call(f32[17]{0:T(128)S(1)} %fusion.proj_ref, f32[32,8,128]{2,1,0:T(8,128)} %copy-done, f32[16,4,8,128]{3,2,1,0:T(8,128)S(1)} %copy-done.5, ...), custom_call_target="tpu_custom_call" | custom-call | flops 1000000000 | bytes 4718592 | tf_op jit(solution)/shard_map/pallas_call | solution.py:355
  88.1 4.7 %collective-permute-start.10 = (f32[128,256]{1,0:T(8,128)S(1)}, f32[128,256]{1,0:T(8,128)S(1)}, u32[]{:S(2)}, u32[]{:S(2)}) collective-permute-start(f32[128,256]{1,0:T(8,128)S(1)} %get-tuple-element.64), channel_id=1, source_target_pairs={{4,0},{8,4},{12,8},{16,12},{20,16},{24,20},{28,24},{0,28},{5,1},{9... | collective-permute-start | bytes 393224 | tf_op jit(solution)/shard_map/ppermute | solution.py:823
  92.8 5.7 %shard_map.130 = (f32[2,4,128,256]{3,2,1,0:T(8,128)}, f32[4,128,256]{2,1,0:T(8,128)S(1)}, f32[4,256]{1,0:T(4,128)S(1)}, f32[4,256]{1,0:T(4,128)S(1)}) custom-call(f32[17]{0:T(128)S(1)} %fusion.proj_ref, f32[32,8,128]{2,1,0:T(8,128)} %copy-done, f32[16,4,8,128]{3,2,1,0:T(8,128)S(1)} %copy-done.5, ...), custom_call_target="tpu_custom_call", output_to_operand_aliasing={{0}: (7, {}), {1}: (8, {})} | custom-call | flops 1000000000 | bytes 4718592 | tf_op jit(solution)/shard_map/pallas_call | solution.py:355
  98.4 1.7 collective-permute-start.12
  100.2 1.3 collective-permute-done.11.refs_2_.refs_6_
  101.5 1.9 shard_map.131
  103.5 10.6 %all_to_all.35.sums_ref.refs_1_ = f32[32,8,128]{2,1,0:T(8,128)} all-to-all(f32[32,8,128]{2,1,0:T(8,128)S(1)} %get-tuple-element.67), channel_id=1, replica_groups=mesh['row'=8,'y'=2,'core'=2] {'row','y','core'}, dimensions={0} | all-to-all | bytes 262144 | tf_op jit(solution)/shard_map/all_to_all | solution.py:808
  114.1 10.0 %shard_map.132 = (f32[16,4,8,128]{3,2,1,0:T(8,128)S(1)}, f32[16,4,8,128]{3,2,1,0:T(8,128)S(1)}, f32[4,16,256,128]{3,2,1,0:T(8,128)}, f32[4,128,256]{2,1,0:T(8,128)}) custom-call(f32[3,16]{1,0:T(4,128)S(1)} %multiply_bitcast_fusion.lift_ref, f32[32,8,128]{2,1,0:T(8,128)} %copy-done, f32[32,8,128]{2,1,0:T(8,128)} %all_to_all.35.sums_ref.refs_1_, ...), custom_call_target="tpu_custom_call" | custom-call | flops 2000000000 | bytes 2359296 | tf_op jit(solution)/shard_map/pallas_call | solution.py:355
  124.3 1.3 collective-permute-done.13.partner_ref
  126.3 3.7 %all-to-all-start.4 = ((f32[16,4,8,128]{3,2,1,0:T(8,128)}), f32[16,4,8,128]{3,2,1,0:T(8,128)S(1)}, u32[]{:S(2)}, u32[]{:S(2)}) async-start(f32[16,4,8,128]{3,2,1,0:T(8,128)} %shard_map.133._.__), calls=%async_computation.4 | async-start | bytes 524288 | tf_op jit(solution)/shard_map/all_to_all | solution.py:808
  130.0 8.2 %shard_map.134.refs_4_._ = f32[4,16,256,128]{3,2,1,0:T(8,128)} custom-call(f32[16,17]{1,0:T(8,128)S(1)} %broadcast_multiply_fusion.mix_ref, f32[4,16,256,128]{3,2,1,0:T(8,128)} %get-tuple-element.71.lifted_ref, f32[16,4,8,128]{3,2,1,0:T(8,128)} %shard_map.133._.__, f32[16,4,8,128]{3,2,1,0:T(8,128)} %shard_map.133._.__), custom_call_target="tpu_custom_call" | custom-call | flops 2500000000 | bytes 8388608 | tf_op jit(solution)/shard_map/pallas_call | solution.py:355
  138.3 2.1 %all-to-all-done.4.recv_ref = f32[16,4,8,128]{3,2,1,0:T(8,128)S(1)} async-done(((f32[16,4,8,128]{3,2,1,0:T(8,128)}), f32[16,4,8,128]{3,2,1,0:T(8,128)S(1)}, u32[]{:S(2)}, u32[]{:S(2)}) %all-to-all-start.4) | async-done | bytes 262176 | tf_op jit(solution)/shard_map/all_to_all | solution.py:808
  140.3 4.7 %shard_map.135.__ = f32[16,4,8,128]{3,2,1,0:T(8,128)} custom-call(f32[16,4,8,128]{3,2,1,0:T(8,128)S(1)} %all-to-all-done.4.recv_ref, f32[4,16,8,128]{3,2,1,0:T(8,128)} %copy-done.7, f32[4,16,8,128]{3,2,1,0:T(8,128)} %copy-done.13, f32[4,16,8,128]{3,2,1,0:T(8,128)} %copy-done.14, f32[4,16,8,128]{3,2,1,0:T(8,128)} %copy-done.15, ...), custom_call_target="tpu_custom_call" | custom-call | bytes 1572864 | tf_op jit(solution)/shard_map/pallas_call | solution.py:355
  145.0 4.6 %all-to-all-start.5 = ((f32[16,4,8,128]{3,2,1,0:T(8,128)}), f32[16,4,8,128]{3,2,1,0:T(8,128)S(1)}, u32[]{:S(2)}, u32[]{:S(2)}) async-start(f32[16,4,8,128]{3,2,1,0:T(8,128)} %shard_map.135.__), calls=%async_computation.5 | async-start | bytes 524288 | tf_op jit(solution)/shard_map/all_to_all | solution.py:808
  149.6 8.1 %shard_map.136.__1_.refs_4_ = f32[4,16,256,128]{3,2,1,0:T(8,128)} custom-call(f32[16,17]{1,0:T(8,128)S(1)} %broadcast_multiply_fusion.mix_ref, f32[4,16,256,128]{3,2,1,0:T(8,128)} %get-tuple-element.71.lifted_ref, f32[4,16,256,128]{3,2,1,0:T(8,128)} %shard_map.134.refs_4_._, f32[16,4,8,128]{3,2,1,0:T(8,128)} %shard_map.135.__), custom_call_target="tpu_custom_call", output_to_operand_aliasing={{}: (2, {})} | custom-call | flops 2500000000 | bytes 8388608 | tf_op jit(solution)/shard_map/pallas_call | solution.py:355
  157.8 1.9 all-to-all-done.5.__0_
  160.3 1.7 collective-permute-done.14.refs_3_
  162.1 0.9 copy-done.3
  163.0 6.2 %shard_map.138 = (f32[2,4,128,256]{3,2,1,0:T(8,128)}, f32[4,128,256]{2,1,0:T(8,128)S(1)}, f32[128,256]{1,0:T(8,128)S(1)}, f32[128,256]{1,0:T(8,128)S(1)}, f32[4,256]{1,0:T(4,128)S(1)}, /*index=5*/f32[4,256]{1,0:T(4,128)S(1)}) custom-call(f32[17]{0:T(128)S(1)} %fusion.proj_ref, f32[32,8,128]{2,1,0:T(8,128)} %copy-done, ...), custom_call_target="tpu_custom_call", output_to_operand_aliasing={{0}: (8, {})} | custom-call | flops 1000000000 | bytes 4718592 | tf_op jit(solution)/shard_map/pallas_call | solution.py:355
  169.2 1.1 collective-permute-start.15
  170.3 3.7 %collective-permute-start.16 = (f32[128,256]{1,0:T(8,128)S(1)}, f32[128,256]{1,0:T(8,128)S(1)}, u32[]{:S(2)}, u32[]{:S(2)}) collective-permute-start(f32[128,256]{1,0:T(8,128)S(1)} %get-tuple-element.79), channel_id=1, source_target_pairs={{4,0},{8,4},{12,8},{16,12},{20,16},{24,20},{28,24},{0,28},{5,1},{9... | collective-permute-start | bytes 393224 | tf_op jit(solution)/shard_map/ppermute | solution.py:823
  173.9 5.7 %shard_map.139 = (f32[2,4,128,256]{3,2,1,0:T(8,128)}, f32[4,128,256]{2,1,0:T(8,128)S(1)}, f32[4,256]{1,0:T(4,128)S(1)}, f32[4,256]{1,0:T(4,128)S(1)}) custom-call(f32[17]{0:T(128)S(1)} %fusion.proj_ref, f32[32,8,128]{2,1,0:T(8,128)} %copy-done, f32[32,8,128]{2,1,0:T(8,128)} %all_to_all.35.sums_ref.refs_1_, ...), custom_call_target="tpu_custom_call", output_to_operand_aliasing={{0}: (8, {}), {1}: (9, {})} | custom-call | flops 1000000000 | bytes 4718592 | tf_op jit(solution)/shard_map/pallas_call | solution.py:355
  179.7 1.7 collective-permute-start.18
  181.4 1.3 collective-permute-done.17.refs_2_
  182.8 2.3 %shard_map.140 = (f32[4,128,256]{2,1,0:T(8,128)S(1)}, f32[4,128,256]{2,1,0:T(8,128)S(1)}, f32[32,8,128]{2,1,0:T(8,128)S(1)}) custom-call(f32[32,8,128]{2,1,0:T(8,128)S(1)} %copy-done.1, f32[32,8,128]{2,1,0:T(8,128)S(1)} %copy-done.6, f32[4,128,256]{2,1,0:T(8,128)S(1)} %get-tuple-element.77.field_ref, f32[4,128,256]{2,1,0:T(8,128)S(1)} %get-tuple-element.62.field_ref.old_ref, ...), custom_call_target="tpu_custom_call" | custom-call | bytes 5767168 | tf_op jit(solution)/shard_map/pallas_call | solution.py:355
  185.1 10.1 %all_to_all.36.later_ref = f32[32,8,128]{2,1,0:T(8,128)S(1)} all-to-all(f32[32,8,128]{2,1,0:T(8,128)S(1)} %get-tuple-element.83), channel_id=1, replica_groups=mesh['row'=8,'y'=2,'core'=2] {'row','y','core'}, dimensions={0} | all-to-all | bytes 262144 | tf_op jit(solution)/shard_map/all_to_all | solution.py:808
  195.2 2.0 %shard_map.141 = (f32[4,128,256]{2,1,0:T(8,128)}, f32[4,128,256]{2,1,0:T(8,128)}) custom-call(f32[32,8,128]{2,1,0:T(8,128)S(1)} %copy-done.6, f32[32,8,128]{2,1,0:T(8,128)S(1)} %all_to_all.36.later_ref, f32[4,128,256]{2,1,0:T(8,128)S(1)} %get-tuple-element.62.field_ref.old_ref, f32[4,128,256]{2,1,0:T(8,128)S(1)} %get-tuple-element.84.way_ref, ...), custom_call_target="tpu_custom_call" | custom-call | bytes 3145728 | tf_op jit(solution)/shard_map/pallas_call | solution.py:355
  (63 shorter events, 7.4 us)
Async XLA Ops:
  0.6 40.0 %copy-start.16 = (f32[16,17]{1,0:T(8,128)S(1)}, f32[16,17]{1,0:T(8,128)}, u32[]{:S(2)}) copy-start(f32[16,17]{1,0:T(8,128)} %param.14) | copy-start | bytes 3268
  2.3 0.7 copy-start.7
  3.0 19.4 %collective-permute-start = (f32[4,16,8,128]{3,2,1,0:T(8,128)S(1)}, f32[4,16,8,128]{3,2,1,0:T(8,128)S(1)}, u32[]{:S(2)}, u32[]{:S(2)}) collective-permute-start(f32[4,16,8,128]{3,2,1,0:T(8,128)S(1)} %get-tuple-element.48), channel_id=1, source_target_pairs={{0,1},{1,2},{2,3},{3,0},{4,5},{5,6},{6,7},{7,4},{8,9},{9,10},{10,1... | collective-permute-start | bytes 786440 | tf_op jit(solution)/shard_map/ppermute | solution.py:869
  3.5 19.0 %collective-permute-start.1 = (f32[4,16,8,128]{3,2,1,0:T(8,128)S(1)}, f32[4,16,8,128]{3,2,1,0:T(8,128)S(1)}, u32[]{:S(2)}, u32[]{:S(2)}) collective-permute-start(f32[4,16,8,128]{3,2,1,0:T(8,128)S(1)} %get-tuple-element.49), channel_id=1, source_target_pairs={{0,2},{1,3},{2,0},{3,1},{4,6},{5,7},{6,4},{7,5},{8,10},{9,11},{10,... | collective-permute-start | bytes 786440 | tf_op jit(solution)/shard_map/ppermute | solution.py:869
  6.0 16.4 %collective-permute-start.2 = (f32[4,16,8,128]{3,2,1,0:T(8,128)S(1)}, f32[4,16,8,128]{3,2,1,0:T(8,128)S(1)}, u32[]{:S(2)}, u32[]{:S(2)}) collective-permute-start(f32[4,16,8,128]{3,2,1,0:T(8,128)S(1)} %get-tuple-element.50), channel_id=1, source_target_pairs={{0,3},{1,0},{2,1},{3,2},{4,7},{5,4},{6,5},{7,6},{8,11},{9,8},{10,9... | collective-permute-start | bytes 786440 | tf_op jit(solution)/shard_map/ppermute | solution.py:869
  9.3 13.1 %all-to-all-start = ((f32[32,8,128]{2,1,0:T(8,128)}), f32[32,8,128]{2,1,0:T(8,128)S(1)}, u32[]{:S(2)}, u32[]{:S(2)}) async-start(f32[32,8,128]{2,1,0:T(8,128)} %get-tuple-element.47), calls=%async_computation | async-start | bytes 262144 | tf_op jit(solution)/shard_map/all_to_all | solution.py:808
  22.4 0.6 copy-start
  22.4 26.4 %copy-start.13 = (f32[4,16,8,128]{3,2,1,0:T(8,128)}, f32[4,16,8,128]{3,2,1,0:T(8,128)S(1)}, u32[]{:S(2)}) copy-start(f32[4,16,8,128]{3,2,1,0:T(8,128)S(1)} %collective-permute-done.refs_1_) | copy-start | bytes 786436
  22.4 26.4 %copy-start.14 = (f32[4,16,8,128]{3,2,1,0:T(8,128)}, f32[4,16,8,128]{3,2,1,0:T(8,128)S(1)}, u32[]{:S(2)}) copy-start(f32[4,16,8,128]{3,2,1,0:T(8,128)S(1)} %collective-permute-done.1.refs_2_) | copy-start | bytes 786436
  23.1 0.9 copy-start.8
  24.0 24.8 %copy-start.15 = (f32[4,16,8,128]{3,2,1,0:T(8,128)}, f32[4,16,8,128]{3,2,1,0:T(8,128)S(1)}, u32[]{:S(2)}) copy-start(f32[4,16,8,128]{3,2,1,0:T(8,128)S(1)} %collective-permute-done.2.refs_3_) | copy-start | bytes 786436
  33.8 1.5 collective-permute-start.3
  36.1 14.7 %all-to-all-start.1 = ((f32[16,4,8,128]{3,2,1,0:T(8,128)}), f32[16,4,8,128]{3,2,1,0:T(8,128)S(1)}, u32[]{:S(2)}, u32[]{:S(2)}) async-start(f32[16,4,8,128]{3,2,1,0:T(8,128)} %shard_map.124._.__), calls=%async_computation.1 | async-start | bytes 524288 | tf_op jit(solution)/shard_map/all_to_all | solution.py:808
  55.4 14.7 %all-to-all-start.2 = ((f32[16,4,8,128]{3,2,1,0:T(8,128)}), f32[16,4,8,128]{3,2,1,0:T(8,128)S(1)}, u32[]{:S(2)}, u32[]{:S(2)}) async-start(f32[16,4,8,128]{3,2,1,0:T(8,128)} %shard_map.126.__), calls=%async_computation.2 | async-start | bytes 524288 | tf_op jit(solution)/shard_map/all_to_all | solution.py:808
  68.6 8.7 %copy-start.17 = (f32[17]{0:T(128)S(1)}, f32[17]{0:T(128)}, u32[]{:S(2)}) copy-start(f32[17]{0:T(128)} %param.15) | copy-start | bytes 208
  70.1 0.7 copy-start.4
  70.8 10.5 %collective-permute-start.4 = (f32[16,4,8,128]{3,2,1,0:T(8,128)}, f32[16,4,8,128]{3,2,1,0:T(8,128)S(1)}, u32[]{:S(2)}, u32[]{:S(2)}) collective-permute-start(f32[16,4,8,128]{3,2,1,0:T(8,128)} %shard_map.128.refs_1_), channel_id=1, source_target_pairs={{0,1},{1,0},{2,3},{3,2},{4,5},{5,4},{6,7},{7,6},{8,9},{9,8},{10,11... | collective-permute-start | bytes 786440 | tf_op jit(solution)/shard_map/ppermute | solution.py:812
  70.8 6.5 %collective-permute-start.7 = (f32[4,256]{1,0:T(4,128)S(1)}, f32[4,256]{1,0:T(4,128)S(1)}, u32[]{:S(2)}, u32[]{:S(2)}) collective-permute-start(f32[4,256]{1,0:T(4,128)S(1)} %get-tuple-element.56), channel_id=1, source_target_pairs={{0,1},{1,2},{2,3},{3,0},{4,5},{5,6},{6,7},{7,4},{8,9},{9,10},{10,1... | collective-permute-start | bytes 12296 | tf_op jit(solution)/shard_map/ppermute | solution.py:823
  71.3 6.0 %collective-permute-start.8 = (f32[4,256]{1,0:T(4,128)S(1)}, f32[4,256]{1,0:T(4,128)S(1)}, u32[]{:S(2)}, u32[]{:S(2)}) collective-permute-start(f32[4,256]{1,0:T(4,128)S(1)} %get-tuple-element.57), channel_id=1, source_target_pairs={{1,0},{2,1},{3,2},{0,3},{5,4},{6,5},{7,6},{4,7},{9,8},{10,9},{11,1... | collective-permute-start | bytes 12296 | tf_op jit(solution)/shard_map/ppermute | solution.py:823
  72.5 7.7 %collective-permute-start.5 = (f32[128,256]{1,0:T(8,128)S(1)}, f32[128,256]{1,0:T(8,128)S(1)}, u32[]{:S(2)}, u32[]{:S(2)}) collective-permute-start(f32[128,256]{1,0:T(8,128)S(1)} %get-tuple-element.54), channel_id=1, source_target_pairs={{0,4},{4,8},{8,12},{12,16},{16,20},{20,24},{24,28},{28,0},{1,5},{5... | collective-permute-start | bytes 393224 | tf_op jit(solution)/shard_map/ppermute | solution.py:823
  73.6 7.7 %collective-permute-start.6 = (f32[128,256]{1,0:T(8,128)S(1)}, f32[128,256]{1,0:T(8,128)S(1)}, u32[]{:S(2)}, u32[]{:S(2)}) collective-permute-start(f32[128,256]{1,0:T(8,128)S(1)} %get-tuple-element.55), channel_id=1, source_target_pairs={{4,0},{8,4},{12,8},{16,12},{20,16},{24,20},{28,24},{0,28},{5,1},{9... | collective-permute-start | bytes 393224 | tf_op jit(solution)/shard_map/ppermute | solution.py:823
  81.3 1.0 copy-start.5
  82.3 19.2 %copy-start.9 = (bf16[4,128,256]{2,1,0:T(8,128)(2,1)S(1)}, bf16[4,128,256]{2,1,0:T(8,128)(2,1)}, u32[]{:S(2)}) copy-start(bf16[4,128,256]{2,1,0:T(8,128)(2,1)} %perm_ref.9) | copy-start | bytes 786436
  82.3 19.2 %copy-start.11 = (f32[4,128,256]{2,1,0:T(8,128)S(1)}, f32[4,128,256]{2,1,0:T(8,128)}, u32[]{:S(2)}) copy-start(f32[4,128,256]{2,1,0:T(8,128)} %res_ref.3) | copy-start | bytes 1572868
  88.0 13.5 %collective-permute-start.9 = (f32[128,256]{1,0:T(8,128)S(1)}, f32[128,256]{1,0:T(8,128)S(1)}, u32[]{:S(2)}, u32[]{:S(2)}) collective-permute-start(f32[128,256]{1,0:T(8,128)S(1)} %get-tuple-element.63), channel_id=1, source_target_pairs={{0,4},{4,8},{8,12},{12,16},{16,20},{20,24},{24,28},{28,0},{1,5},{5... | collective-permute-start | bytes 393224 | tf_op jit(solution)/shard_map/ppermute | solution.py:823
  88.1 13.4 %collective-permute-start.10 = (f32[128,256]{1,0:T(8,128)S(1)}, f32[128,256]{1,0:T(8,128)S(1)}, u32[]{:S(2)}, u32[]{:S(2)}) collective-permute-start(f32[128,256]{1,0:T(8,128)S(1)} %get-tuple-element.64), channel_id=1, source_target_pairs={{4,0},{8,4},{12,8},{16,12},{20,16},{24,20},{28,24},{0,28},{5,1},{9... | collective-permute-start | bytes 393224 | tf_op jit(solution)/shard_map/ppermute | solution.py:823
  98.4 3.0 %collective-permute-start.11 = (f32[4,256]{1,0:T(4,128)S(1)}, f32[4,256]{1,0:T(4,128)S(1)}, u32[]{:S(2)}, u32[]{:S(2)}) collective-permute-start(f32[4,256]{1,0:T(4,128)S(1)} %get-tuple-element.65), channel_id=1, source_target_pairs={{0,1},{1,2},{2,3},{3,0},{4,5},{5,6},{6,7},{7,4},{8,9},{9,10},{10,1... | collective-permute-start | bytes 12296 | tf_op jit(solution)/shard_map/ppermute | solution.py:823
  98.4 3.1 %collective-permute-start.12 = (f32[4,256]{1,0:T(4,128)S(1)}, f32[4,256]{1,0:T(4,128)S(1)}, u32[]{:S(2)}, u32[]{:S(2)}) collective-permute-start(f32[4,256]{1,0:T(4,128)S(1)} %get-tuple-element.66), channel_id=1, source_target_pairs={{1,0},{2,1},{3,2},{0,3},{5,4},{6,5},{7,6},{4,7},{9,8},{10,9},{11,1... | collective-permute-start | bytes 12296 | tf_op jit(solution)/shard_map/ppermute | solution.py:823
  124.0 1.5 collective-permute-start.13
  126.3 14.0 %all-to-all-start.4 = ((f32[16,4,8,128]{3,2,1,0:T(8,128)}), f32[16,4,8,128]{3,2,1,0:T(8,128)S(1)}, u32[]{:S(2)}, u32[]{:S(2)}) async-start(f32[16,4,8,128]{3,2,1,0:T(8,128)} %shard_map.133._.__), calls=%async_computation.4 | async-start | bytes 524288 | tf_op jit(solution)/shard_map/all_to_all | solution.py:808
  145.0 14.6 %all-to-all-start.5 = ((f32[16,4,8,128]{3,2,1,0:T(8,128)}), f32[16,4,8,128]{3,2,1,0:T(8,128)S(1)}, u32[]{:S(2)}, u32[]{:S(2)}) async-start(f32[16,4,8,128]{3,2,1,0:T(8,128)} %shard_map.135.__), calls=%async_computation.5 | async-start | bytes 524288 | tf_op jit(solution)/shard_map/all_to_all | solution.py:808
  159.6 0.7 copy-start.2
  160.3 1.7 collective-permute-start.14
  162.1 1.0 copy-start.3
  163.0 19.8 %copy-start.1 = (f32[32,8,128]{2,1,0:T(8,128)S(1)}, f32[32,8,128]{2,1,0:T(8,128)}, u32[]{:S(2)}) copy-start(f32[32,8,128]{2,1,0:T(8,128)} %copy-done) | copy-start | bytes 393220
  163.0 19.8 %copy-start.6 = (f32[32,8,128]{2,1,0:T(8,128)S(1)}, f32[32,8,128]{2,1,0:T(8,128)}, u32[]{:S(2)}) copy-start(f32[32,8,128]{2,1,0:T(8,128)} %all_to_all.35.sums_ref.refs_1_) | copy-start | bytes 393220
  163.0 19.8 %copy-start.10 = (bf16[4,128,256]{2,1,0:T(8,128)(2,1)S(1)}, bf16[4,128,256]{2,1,0:T(8,128)(2,1)}, u32[]{:S(2)}) copy-start(bf16[4,128,256]{2,1,0:T(8,128)(2,1)} %perm_ref.9) | copy-start | bytes 786436
  163.0 19.8 %copy-start.12 = (f32[4,128,256]{2,1,0:T(8,128)S(1)}, f32[4,128,256]{2,1,0:T(8,128)}, u32[]{:S(2)}) copy-start(f32[4,128,256]{2,1,0:T(8,128)} %get-tuple-element.82.refs_12_.res_ref) | copy-start | bytes 1572868
  169.2 13.5 %collective-permute-start.15 = (f32[128,256]{1,0:T(8,128)S(1)}, f32[128,256]{1,0:T(8,128)S(1)}, u32[]{:S(2)}, u32[]{:S(2)}) collective-permute-start(f32[128,256]{1,0:T(8,128)S(1)} %get-tuple-element.78), channel_id=1, source_target_pairs={{0,4},{4,8},{8,12},{12,16},{16,20},{20,24},{24,28},{28,0},{1,5},{5... | collective-permute-start | bytes 393224 | tf_op jit(solution)/shard_map/ppermute | solution.py:823
  170.3 12.5 %collective-permute-start.16 = (f32[128,256]{1,0:T(8,128)S(1)}, f32[128,256]{1,0:T(8,128)S(1)}, u32[]{:S(2)}, u32[]{:S(2)}) collective-permute-start(f32[128,256]{1,0:T(8,128)S(1)} %get-tuple-element.79), channel_id=1, source_target_pairs={{4,0},{8,4},{12,8},{16,12},{20,16},{24,20},{28,24},{0,28},{5,1},{9... | collective-permute-start | bytes 393224 | tf_op jit(solution)/shard_map/ppermute | solution.py:823
  179.7 3.0 %collective-permute-start.17 = (f32[4,256]{1,0:T(4,128)S(1)}, f32[4,256]{1,0:T(4,128)S(1)}, u32[]{:S(2)}, u32[]{:S(2)}) collective-permute-start(f32[4,256]{1,0:T(4,128)S(1)} %get-tuple-element.80), channel_id=1, source_target_pairs={{0,1},{1,2},{2,3},{3,0},{4,5},{5,6},{6,7},{7,4},{8,9},{9,10},{10,1... | collective-permute-start | bytes 12296 | tf_op jit(solution)/shard_map/ppermute | solution.py:823
  179.7 3.1 %collective-permute-start.18 = (f32[4,256]{1,0:T(4,128)S(1)}, f32[4,256]{1,0:T(4,128)S(1)}, u32[]{:S(2)}, u32[]{:S(2)}) collective-permute-start(f32[4,256]{1,0:T(4,128)S(1)} %get-tuple-element.81), channel_id=1, source_target_pairs={{1,0},{2,1},{3,2},{0,3},{5,4},{6,5},{7,6},{4,7},{9,8},{10,9},{11,1... | collective-permute-start | bytes 12296 | tf_op jit(solution)/shard_map/ppermute | solution.py:823

commit v9 on v8

--- a/solution.py
+++ b/solution.py
@@ -384,7 +384,7 @@
     return jnp.sum(total[row : row + 1], axis=1, keepdims=True)
 
 
-def squares_body(field_ref, perm_ref, _, out_ref, low_ref, high_ref, left_ref, right_ref):
+def squares_body(field_ref, perm_ref, out_ref, low_ref, high_ref, left_ref, right_ref):
     total = field_ref[0] * field_ref[0]
     for place in range(1, field_ref.shape[0]):
         total = total + field_ref[place] * field_ref[place]
@@ -873,10 +873,10 @@
     squares, *perm_edges = call(
         squares_body,
         (partial,) + edge_shapes,
-        [vmem, vmem, anywhere],
+        [vmem, vmem],
         (vmem,) * 5,
         moved=2 * field_bytes,
-    )(right_side, permeability, kept_weights)
+    )(right_side, permeability)
     squares = add_up(squares)
     perm_halo = neighbours(*perm_edges)
     acc_scratch = pltpu.VMEM((SUBLANES, LANES), F32)
@@ -917,7 +917,7 @@
             near=(0,),
         )(received, *weights, before)
 
-    def mixed_modes(own, partner, lifted):
+    def mixed_modes(own, partner, lifted, waiting):
         blocks = call(join_body, spectra, [vmem, vmem], vmem, near=(0, 1))(own, swap(partner))
         received = exchange(blocks, CHIPS)
         point = points(lifted, 0, blocks, blocks)
@@ -927,10 +927,10 @@
         received = pl.pallas_call(
             tie_body,
             out_shape=spectra,
-            in_specs=[anywhere, anywhere],
+            in_specs=[anywhere] * (2 + len(waiting)),
             out_specs=anywhere,
             input_output_aliases={0: 0},
-        )(received, point)
+        )(received, point, *waiting)
         return received, swap(received), point
 
     def back(index, scale_from, scalars, fields, waiting):
@@ -964,7 +964,7 @@
                 moved=9 * field_bytes,
                 alias={count_in + 5 + i: o for i, o in alias},
                 limit=12,
-                near=(count_in, count_in + 1)
+                near=(count_in + 1,)
                 + tuple(
                     count_in + 5 + i
                     for i, array in enumerate(waiting)
@@ -1009,13 +1009,13 @@
         flops=lift_flops,
         moved=2 * field_bytes + spectra_bytes,
     )(lift_weight, squares, right_side, permeability, deep_forward, col_forward, *weights)
-    received, other, point = mixed_modes(own, partner, lifted)
+    received, other, point = mixed_modes(own, partner, lifted, perm_halo)
     kept, old, *edges = back(
         0,
         lambda first_ref: scale_of(gathered(first_ref, 0), cells),
         (squares,),
         (received, other, point),
-        perm_halo,
+        (),
     )
 
     old_halo = edges
@@ -1046,7 +1046,7 @@
         flops=lift_flops,
         moved=4 * field_bytes + spectra_bytes,
     )(lift_weight, squares, sums, right_side, image, permeability, deep_forward, col_forward)
-    received, other, point = mixed_modes(own, partner, lifted)
+    received, other, point = mixed_modes(own, partner, lifted, ())
     kept, update, *edges = back(
         1,
         lambda first_ref, sums_ref: scale_of(next_scalars(first_ref, sums_ref)[2], cells),

time: 198 us -> 191 us (0.965)
  waiting for transfers between devices: 25.9 us -> 22.1 us
  local copies, waits for them, and re-layouts: 5.6 us -> 2.77 us
    ppermute x6, waiting for transfers between devices: 5.55 us -> 2.58 us  [shift_planes(): lax.ppermute(last, axis, forward)]
    unnamed x36 -> x46, local copies, waits for them, and re-layouts: 5.6 us -> 2.77 us
  transfers between devices with their start and end apart: 24 -> 24, of which waited for: 12 -> 10; matrix products, arithmetic and copies ran while one was open for 0% -> 0% of each run, Pallas kernels for 23% -> 24%
where the time goes in v9:
time: 191 us
  Pallas kernels  96.2 us (50%)
  starting transfers between devices  47.2 us (25%)
  waiting for transfers between devices  22.1 us (12%)
  blocking collectives  20.7 us (11%)
  local copies, waits for them, and re-layouts  2.77 us (1%)
    pallas_call x19, Pallas kernels, wrapped(): found = run(*held)  96.2 us
    all_to_all x5, starting transfers between devices, exchange(): return lax.all_to_all(blocks, axes, split_axis=0, concat_axis=0, tiled=True)  22.8 us
    all_to_all x2, blocking collectives, exchange(): return lax.all_to_all(blocks, axes, split_axis=0, concat_axis=0, tiled=True)  20.7 us
    ppermute x6, starting transfers between devices, shift_planes(): lax.ppermute(first, axis, backward)  16.5 us
    all_to_all x5, waiting for transfers between devices, exchange(): return lax.all_to_all(blocks, axes, split_axis=0, concat_axis=0, tiled=True)  13.3 us
    ppermute x4, waiting for transfers between devices, swap(): return lax.ppermute(blocks, 'core', [(0, 1), (1, 0)])  6.05 us
    ppermute x3, starting transfers between devices, tiled_local(): lax.ppermute(part, COL, [(i, (i + shift + 1) % n_col) for i in range(n_co...  4.5 us
  transfers between devices with their start and end apart: 24, of which 10 were waited for; matrix products, arithmetic and copies ran while one was open for 0% of the time, Pallas kernels for 24%

profile of v9, /device:TPU:0, one launch (start us, length us, event | category | flops | bytes accessed | tf_op | source)
XLA Modules:
  0.0 190.7 jit_solution(13284322780708832778)
XLA Ops:
  0.6 1.7 shard_map.122
  2.8 2.6 %collective-permute-start.1 = (f32[4,16,8,128]{3,2,1,0:T(8,128)S(1)}, f32[4,16,8,128]{3,2,1,0:T(8,128)S(1)}, u32[]{:S(2)}, u32[]{:S(2)}) collective-permute-start(f32[4,16,8,128]{3,2,1,0:T(8,128)S(1)} %get-tuple-element.49), channel_id=1, source_target_pairs={{0,2},{1,3},{2,0},{3,1},{4,6},{5,7},{6,4},{7,5},{8,10},{9,11},{10,... | collective-permute-start | bytes 786440 | tf_op jit(solution)/shard_map/ppermute | solution.py:869
  5.4 1.4 collective-permute-start.2
  6.8 1.8 shard_map.121
  8.7 4.9 %all-to-all-start = ((f32[32,8,128]{2,1,0:T(8,128)}), f32[32,8,128]{2,1,0:T(8,128)S(1)}, u32[]{:S(2)}, u32[]{:S(2)}) async-start(f32[32,8,128]{2,1,0:T(8,128)} %get-tuple-element.46), calls=%async_computation | async-start | bytes 262144 | tf_op jit(solution)/shard_map/all_to_all | solution.py:808
  14.2 7.5 %all-to-all-done.sums_ref.refs_0_.first_ref = f32[32,8,128]{2,1,0:T(8,128)S(1)} async-done(((f32[32,8,128]{2,1,0:T(8,128)}), f32[32,8,128]{2,1,0:T(8,128)S(1)}, u32[]{:S(2)}, u32[]{:S(2)}) %all-to-all-start) | async-done | bytes 131104 | tf_op jit(solution)/shard_map/all_to_all | solution.py:808
  22.4 9.7 %shard_map.123 = (f32[16,4,8,128]{3,2,1,0:T(8,128)S(1)}, f32[16,4,8,128]{3,2,1,0:T(8,128)S(1)}, f32[4,16,256,128]{3,2,1,0:T(8,128)}) custom-call(f32[3,16]{1,0:T(4,128)S(1)} %multiply_bitcast_fusion.lift_ref, f32[32,8,128]{2,1,0:T(8,128)} %copy-done, f32[4,128,256]{2,1,0:T(8,128)} %res_ref.3, bf16[4,128,256]{2,1,0:T(8,128)(2,1)} %perm_ref.9, ...), custom_call_target="tpu_custom_call" | custom-call | flops 2000000000 | bytes 1310720 | tf_op jit(solution)/shard_map/pallas_call | solution.py:355
  32.4 1.3 collective-permute-done.3.partner_ref
  33.7 0.7 shard_map.124._.__
  34.4 4.5 %all-to-all-start.1 = ((f32[16,4,8,128]{3,2,1,0:T(8,128)}), f32[16,4,8,128]{3,2,1,0:T(8,128)S(1)}, u32[]{:S(2)}, u32[]{:S(2)}) async-start(f32[16,4,8,128]{3,2,1,0:T(8,128)} %shard_map.124._.__), calls=%async_computation.1 | async-start | bytes 524288 | tf_op jit(solution)/shard_map/all_to_all | solution.py:808
  39.0 8.2 %shard_map.125.refs_4_._ = f32[4,16,256,128]{3,2,1,0:T(8,128)} custom-call(f32[16,17]{1,0:T(8,128)S(1)} %broadcast_multiply_fusion.mix_ref, f32[4,16,256,128]{3,2,1,0:T(8,128)} %get-tuple-element.53.lifted_ref, f32[16,4,8,128]{3,2,1,0:T(8,128)} %shard_map.124._.__, f32[16,4,8,128]{3,2,1,0:T(8,128)} %shard_map.124._.__), custom_call_target="tpu_custom_call" | custom-call | flops 2500000000 | bytes 8388608 | tf_op jit(solution)/shard_map/pallas_call | solution.py:355
  47.2 1.9 all-to-all-done.1.recv_ref
  49.1 4.7 %shard_map.126.__ = f32[16,4,8,128]{3,2,1,0:T(8,128)} custom-call(f32[16,4,8,128]{3,2,1,0:T(8,128)S(1)} %all-to-all-done.1.recv_ref, f32[4,16,8,128]{3,2,1,0:T(8,128)} %copy-done.11, f32[4,16,8,128]{3,2,1,0:T(8,128)} %copy-done.12, f32[4,16,8,128]{3,2,1,0:T(8,128)} %copy-done.13, f32[4,16,8,128]{3,2,1,0:T(8,128)} %copy-done.14, ...), custom_call_target="tpu_custom_call" | custom-call | bytes 1572864 | tf_op jit(solution)/shard_map/pallas_call | solution.py:355
  53.8 5.1 %all-to-all-start.2 = ((f32[16,4,8,128]{3,2,1,0:T(8,128)}), f32[16,4,8,128]{3,2,1,0:T(8,128)S(1)}, u32[]{:S(2)}, u32[]{:S(2)}) async-start(f32[16,4,8,128]{3,2,1,0:T(8,128)} %shard_map.126.__), calls=%async_computation.2 | async-start | bytes 524288 | tf_op jit(solution)/shard_map/all_to_all | solution.py:808
  58.9 1.7 collective-permute-start.7
  60.6 1.9 collective-permute-start.4
  62.5 2.8 %collective-permute-start.5 = (f32[128,256]{1,0:T(8,128)S(1)}, f32[128,256]{1,0:T(8,128)S(1)}, u32[]{:S(2)}, u32[]{:S(2)}) collective-permute-start(f32[128,256]{1,0:T(8,128)S(1)} %get-tuple-element.55), channel_id=1, source_target_pairs={{4,0},{8,4},{12,8},{16,12},{20,16},{24,20},{28,24},{0,28},{5,1},{9... | collective-permute-start | bytes 393224 | tf_op jit(solution)/shard_map/ppermute | solution.py:823
  65.4 8.1 %shard_map.127.__1_.refs_3_ = f32[4,16,256,128]{3,2,1,0:T(8,128)} custom-call(f32[16,17]{1,0:T(8,128)S(1)} %broadcast_multiply_fusion.mix_ref, f32[4,16,256,128]{3,2,1,0:T(8,128)} %get-tuple-element.53.lifted_ref, f32[4,16,256,128]{3,2,1,0:T(8,128)} %shard_map.125.refs_4_._, f32[16,4,8,128]{3,2,1,0:T(8,128)} %shard_map.126.__), custom_call_target="tpu_custom_call", output_to_operand_aliasing={{}: (2, {})} | custom-call | flops 2500000000 | bytes 8388608 | tf_op jit(solution)/shard_map/pallas_call | solution.py:355
  74.2 0.7 copy-done.20
  75.0 1.7 collective-permute-done.8.refs_2_
  76.7 5.7 %shard_map.129 = (f32[2,4,128,256]{3,2,1,0:T(8,128)}, f32[4,128,256]{2,1,0:T(8,128)S(1)}, f32[128,256]{1,0:T(8,128)S(1)}, f32[128,256]{1,0:T(8,128)S(1)}, f32[4,256]{1,0:T(4,128)S(1)}, /*index=5*/f32[4,256]{1,0:T(4,128)S(1)}) custom-call(f32[17]{0:T(128)S(1)} %fusion.proj_ref, f32[32,8,128]{2,1,0:T(8,128)} %copy-done, f32[16,4,8,128]{3,2,1,0:T(8,128)} %shard_map.128.refs_1_, ...), custom_call_target="tpu_custom_call" | custom-call | flops 1000000000 | bytes 4718592 | tf_op jit(solution)/shard_map/pallas_call | solution.py:355
  82.4 4.7 %collective-permute-start.10 = (f32[128,256]{1,0:T(8,128)S(1)}, f32[128,256]{1,0:T(8,128)S(1)}, u32[]{:S(2)}, u32[]{:S(2)}) collective-permute-start(f32[128,256]{1,0:T(8,128)S(1)} %get-tuple-element.64), channel_id=1, source_target_pairs={{4,0},{8,4},{12,8},{16,12},{20,16},{24,20},{28,24},{0,28},{5,1},{9... | collective-permute-start | bytes 393224 | tf_op jit(solution)/shard_map/ppermute | solution.py:823
  87.1 5.7 %shard_map.130 = (f32[2,4,128,256]{3,2,1,0:T(8,128)}, f32[4,128,256]{2,1,0:T(8,128)S(1)}, f32[4,256]{1,0:T(4,128)S(1)}, f32[4,256]{1,0:T(4,128)S(1)}) custom-call(f32[17]{0:T(128)S(1)} %fusion.proj_ref, f32[32,8,128]{2,1,0:T(8,128)} %copy-done, f32[16,4,8,128]{3,2,1,0:T(8,128)} %shard_map.128.refs_1_, ...), custom_call_target="tpu_custom_call", output_to_operand_aliasing={{0}: (7, {}), {1}: (8, {})} | custom-call | flops 1000000000 | bytes 4718592 | tf_op jit(solution)/shard_map/pallas_call | solution.py:355
  92.8 1.7 collective-permute-start.12
  94.5 1.3 collective-permute-done.11.refs_2_.refs_6_
  95.9 1.9 %shard_map.131 = (f32[4,128,256]{2,1,0:T(8,128)S(1)}, f32[32,8,128]{2,1,0:T(8,128)S(1)}) custom-call(f32[4,128,256]{2,1,0:T(8,128)S(1)} %get-tuple-element.62.field_ref.old_ref, bf16[4,128,256]{2,1,0:T(8,128)(2,1)S(1)} %copy-done.3, f32[128,256]{1,0:T(8,128)S(1)} %collective-permute-done.9.refs_0_.refs_4_, ...), custom_call_target="tpu_custom_call" | custom-call | bytes 4718592 | tf_op jit(solution)/shard_map/pallas_call | solution.py:355
  97.8 10.6 %all_to_all.35.sums_ref.refs_1_ = f32[32,8,128]{2,1,0:T(8,128)} all-to-all(f32[32,8,128]{2,1,0:T(8,128)S(1)} %get-tuple-element.67), channel_id=1, replica_groups=mesh['row'=8,'y'=2,'core'=2] {'row','y','core'}, dimensions={0} | all-to-all | bytes 262144 | tf_op jit(solution)/shard_map/all_to_all | solution.py:808
  108.5 10.0 %shard_map.132 = (f32[16,4,8,128]{3,2,1,0:T(8,128)S(1)}, f32[16,4,8,128]{3,2,1,0:T(8,128)S(1)}, f32[4,16,256,128]{3,2,1,0:T(8,128)}, f32[4,128,256]{2,1,0:T(8,128)}) custom-call(f32[3,16]{1,0:T(4,128)S(1)} %multiply_bitcast_fusion.lift_ref, f32[32,8,128]{2,1,0:T(8,128)} %copy-done, f32[32,8,128]{2,1,0:T(8,128)} %all_to_all.35.sums_ref.refs_1_, ...), custom_call_target="tpu_custom_call" | custom-call | flops 2000000000 | bytes 2359296 | tf_op jit(solution)/shard_map/pallas_call | solution.py:355
  118.7 1.3 collective-permute-done.13.partner_ref
  120.0 0.7 shard_map.133._.__
  120.7 3.7 %all-to-all-start.4 = ((f32[16,4,8,128]{3,2,1,0:T(8,128)}), f32[16,4,8,128]{3,2,1,0:T(8,128)S(1)}, u32[]{:S(2)}, u32[]{:S(2)}) async-start(f32[16,4,8,128]{3,2,1,0:T(8,128)} %shard_map.133._.__), calls=%async_computation.4 | async-start | bytes 524288 | tf_op jit(solution)/shard_map/all_to_all | solution.py:808
  124.4 8.2 %shard_map.134.refs_4_._ = f32[4,16,256,128]{3,2,1,0:T(8,128)} custom-call(f32[16,17]{1,0:T(8,128)S(1)} %broadcast_multiply_fusion.mix_ref, f32[4,16,256,128]{3,2,1,0:T(8,128)} %get-tuple-element.71.lifted_ref, f32[16,4,8,128]{3,2,1,0:T(8,128)} %shard_map.133._.__, f32[16,4,8,128]{3,2,1,0:T(8,128)} %shard_map.133._.__), custom_call_target="tpu_custom_call" | custom-call | flops 2500000000 | bytes 8388608 | tf_op jit(solution)/shard_map/pallas_call | solution.py:355
  132.7 2.1 %all-to-all-done.4.recv_ref = f32[16,4,8,128]{3,2,1,0:T(8,128)S(1)} async-done(((f32[16,4,8,128]{3,2,1,0:T(8,128)}), f32[16,4,8,128]{3,2,1,0:T(8,128)S(1)}, u32[]{:S(2)}, u32[]{:S(2)}) %all-to-all-start.4) | async-done | bytes 262176 | tf_op jit(solution)/shard_map/all_to_all | solution.py:808
  134.7 4.7 %shard_map.135.__ = f32[16,4,8,128]{3,2,1,0:T(8,128)} custom-call(f32[16,4,8,128]{3,2,1,0:T(8,128)S(1)} %all-to-all-done.4.recv_ref, f32[4,16,8,128]{3,2,1,0:T(8,128)} %copy-done.11, f32[4,16,8,128]{3,2,1,0:T(8,128)} %copy-done.12, f32[4,16,8,128]{3,2,1,0:T(8,128)} %copy-done.13, f32[4,16,8,128]{3,2,1,0:T(8,128)} %copy-done.14, ...), custom_call_target="tpu_custom_call" | custom-call | bytes 1572864 | tf_op jit(solution)/shard_map/pallas_call | solution.py:355
  139.4 4.7 %all-to-all-start.5 = ((f32[16,4,8,128]{3,2,1,0:T(8,128)}), f32[16,4,8,128]{3,2,1,0:T(8,128)S(1)}, u32[]{:S(2)}, u32[]{:S(2)}) async-start(f32[16,4,8,128]{3,2,1,0:T(8,128)} %shard_map.135.__), calls=%async_computation.5 | async-start | bytes 524288 | tf_op jit(solution)/shard_map/all_to_all | solution.py:808
  144.1 8.1 %shard_map.136.__1_.refs_4_ = f32[4,16,256,128]{3,2,1,0:T(8,128)} custom-call(f32[16,17]{1,0:T(8,128)S(1)} %broadcast_multiply_fusion.mix_ref, f32[4,16,256,128]{3,2,1,0:T(8,128)} %get-tuple-element.71.lifted_ref, f32[4,16,256,128]{3,2,1,0:T(8,128)} %shard_map.134.refs_4_._, f32[16,4,8,128]{3,2,1,0:T(8,128)} %shard_map.135.__), custom_call_target="tpu_custom_call", output_to_operand_aliasing={{}: (2, {})} | custom-call | flops 2500000000 | bytes 8388608 | tf_op jit(solution)/shard_map/pallas_call | solution.py:355
  152.2 1.8 all-to-all-done.5.__0_
  154.1 0.7 copy-done.19
  154.8 1.7 collective-permute-done.14.refs_3_
  156.5 6.3 %shard_map.138 = (f32[2,4,128,256]{3,2,1,0:T(8,128)}, f32[4,128,256]{2,1,0:T(8,128)S(1)}, f32[128,256]{1,0:T(8,128)S(1)}, f32[128,256]{1,0:T(8,128)S(1)}, f32[4,256]{1,0:T(4,128)S(1)}, /*index=5*/f32[4,256]{1,0:T(4,128)S(1)}) custom-call(f32[17]{0:T(128)S(1)} %fusion.proj_ref, f32[32,8,128]{2,1,0:T(8,128)} %copy-done, ...), custom_call_target="tpu_custom_call", output_to_operand_aliasing={{0}: (8, {})} | custom-call | flops 1000000000 | bytes 4718592 | tf_op jit(solution)/shard_map/pallas_call | solution.py:355
  162.8 1.1 collective-permute-start.15
  163.8 3.7 %collective-permute-start.16 = (f32[128,256]{1,0:T(8,128)S(1)}, f32[128,256]{1,0:T(8,128)S(1)}, u32[]{:S(2)}, u32[]{:S(2)}) collective-permute-start(f32[128,256]{1,0:T(8,128)S(1)} %get-tuple-element.79), channel_id=1, source_target_pairs={{4,0},{8,4},{12,8},{16,12},{20,16},{24,20},{28,24},{0,28},{5,1},{9... | collective-permute-start | bytes 393224 | tf_op jit(solution)/shard_map/ppermute | solution.py:823
  167.5 5.7 %shard_map.139 = (f32[2,4,128,256]{3,2,1,0:T(8,128)}, f32[4,128,256]{2,1,0:T(8,128)S(1)}, f32[4,256]{1,0:T(4,128)S(1)}, f32[4,256]{1,0:T(4,128)S(1)}) custom-call(f32[17]{0:T(128)S(1)} %fusion.proj_ref, f32[32,8,128]{2,1,0:T(8,128)} %copy-done, f32[32,8,128]{2,1,0:T(8,128)} %all_to_all.35.sums_ref.refs_1_, ...), custom_call_target="tpu_custom_call", output_to_operand_aliasing={{0}: (8, {}), {1}: (9, {})} | custom-call | flops 1000000000 | bytes 4718592 | tf_op jit(solution)/shard_map/pallas_call | solution.py:355
  173.2 1.7 collective-permute-start.18
  175.0 1.3 collective-permute-done.17.refs_2_
  176.4 2.3 %shard_map.140 = (f32[4,128,256]{2,1,0:T(8,128)S(1)}, f32[4,128,256]{2,1,0:T(8,128)S(1)}, f32[32,8,128]{2,1,0:T(8,128)S(1)}) custom-call(f32[32,8,128]{2,1,0:T(8,128)S(1)} %copy-done.1, f32[32,8,128]{2,1,0:T(8,128)S(1)} %copy-done.2, f32[4,128,256]{2,1,0:T(8,128)S(1)} %get-tuple-element.77.field_ref, f32[4,128,256]{2,1,0:T(8,128)S(1)} %get-tuple-element.62.field_ref.old_ref, ...), custom_call_target="tpu_custom_call" | custom-call | bytes 5767168 | tf_op jit(solution)/shard_map/pallas_call | solution.py:355
  178.6 10.1 %all_to_all.36.later_ref = f32[32,8,128]{2,1,0:T(8,128)S(1)} all-to-all(f32[32,8,128]{2,1,0:T(8,128)S(1)} %get-tuple-element.83), channel_id=1, replica_groups=mesh['row'=8,'y'=2,'core'=2] {'row','y','core'}, dimensions={0} | all-to-all | bytes 262144 | tf_op jit(solution)/shard_map/all_to_all | solution.py:808
  188.7 2.0 %shard_map.141 = (f32[4,128,256]{2,1,0:T(8,128)}, f32[4,128,256]{2,1,0:T(8,128)}) custom-call(f32[32,8,128]{2,1,0:T(8,128)S(1)} %copy-done.2, f32[32,8,128]{2,1,0:T(8,128)S(1)} %all_to_all.36.later_ref, f32[4,128,256]{2,1,0:T(8,128)S(1)} %get-tuple-element.62.field_ref.old_ref, f32[4,128,256]{2,1,0:T(8,128)S(1)} %get-tuple-element.84.way_ref, ...), custom_call_target="tpu_custom_call" | custom-call | bytes 3145728 | tf_op jit(solution)/shard_map/pallas_call | solution.py:355
  (73 shorter events, 3.2 us)
Async XLA Ops:
  0.6 38.3 %copy-start.21 = (f32[16,17]{1,0:T(8,128)S(1)}, f32[16,17]{1,0:T(8,128)}, u32[]{:S(2)}) copy-start(f32[16,17]{1,0:T(8,128)} %param.14) | copy-start | bytes 3268
  2.3 44.9 %copy-start.11 = (f32[4,16,8,128]{3,2,1,0:T(8,128)}, f32[4,16,8,128]{3,2,1,0:T(8,128)S(1)}, u32[]{:S(2)}) copy-start(f32[4,16,8,128]{3,2,1,0:T(8,128)S(1)} %get-tuple-element.47.refs_0_) | copy-start | bytes 786436
  2.3 19.5 %collective-permute-start = (f32[4,16,8,128]{3,2,1,0:T(8,128)S(1)}, f32[4,16,8,128]{3,2,1,0:T(8,128)S(1)}, u32[]{:S(2)}, u32[]{:S(2)}) collective-permute-start(f32[4,16,8,128]{3,2,1,0:T(8,128)S(1)} %get-tuple-element.48), channel_id=1, source_target_pairs={{0,1},{1,2},{2,3},{3,0},{4,5},{5,6},{6,7},{7,4},{8,9},{9,10},{10,1... | collective-permute-start | bytes 786440 | tf_op jit(solution)/shard_map/ppermute | solution.py:869
  2.8 19.0 %collective-permute-start.1 = (f32[4,16,8,128]{3,2,1,0:T(8,128)S(1)}, f32[4,16,8,128]{3,2,1,0:T(8,128)S(1)}, u32[]{:S(2)}, u32[]{:S(2)}) collective-permute-start(f32[4,16,8,128]{3,2,1,0:T(8,128)S(1)} %get-tuple-element.49), channel_id=1, source_target_pairs={{0,2},{1,3},{2,0},{3,1},{4,6},{5,7},{6,4},{7,5},{8,10},{9,11},{10,... | collective-permute-start | bytes 786440 | tf_op jit(solution)/shard_map/ppermute | solution.py:869
  5.4 16.4 %collective-permute-start.2 = (f32[4,16,8,128]{3,2,1,0:T(8,128)S(1)}, f32[4,16,8,128]{3,2,1,0:T(8,128)S(1)}, u32[]{:S(2)}, u32[]{:S(2)}) collective-permute-start(f32[4,16,8,128]{3,2,1,0:T(8,128)S(1)} %get-tuple-element.50), channel_id=1, source_target_pairs={{0,3},{1,0},{2,1},{3,2},{4,7},{5,4},{6,5},{7,6},{8,11},{9,8},{10,9... | collective-permute-start | bytes 786440 | tf_op jit(solution)/shard_map/ppermute | solution.py:869
  8.7 13.1 %all-to-all-start = ((f32[32,8,128]{2,1,0:T(8,128)}), f32[32,8,128]{2,1,0:T(8,128)S(1)}, u32[]{:S(2)}, u32[]{:S(2)}) async-start(f32[32,8,128]{2,1,0:T(8,128)} %get-tuple-element.46), calls=%async_computation | async-start | bytes 262144 | tf_op jit(solution)/shard_map/all_to_all | solution.py:808
  21.8 0.7 copy-start
  21.8 25.4 %copy-start.12 = (f32[4,16,8,128]{3,2,1,0:T(8,128)}, f32[4,16,8,128]{3,2,1,0:T(8,128)S(1)}, u32[]{:S(2)}) copy-start(f32[4,16,8,128]{3,2,1,0:T(8,128)S(1)} %collective-permute-done.refs_1_) | copy-start | bytes 786436
  21.8 25.4 %copy-start.13 = (f32[4,16,8,128]{3,2,1,0:T(8,128)}, f32[4,16,8,128]{3,2,1,0:T(8,128)S(1)}, u32[]{:S(2)}) copy-start(f32[4,16,8,128]{3,2,1,0:T(8,128)S(1)} %collective-permute-done.1.refs_2_) | copy-start | bytes 786436
  21.8 25.4 %copy-start.14 = (f32[4,16,8,128]{3,2,1,0:T(8,128)}, f32[4,16,8,128]{3,2,1,0:T(8,128)S(1)}, u32[]{:S(2)}) copy-start(f32[4,16,8,128]{3,2,1,0:T(8,128)S(1)} %collective-permute-done.2.refs_3_) | copy-start | bytes 786436
  32.2 1.5 collective-permute-start.3
  34.4 14.7 %all-to-all-start.1 = ((f32[16,4,8,128]{3,2,1,0:T(8,128)}), f32[16,4,8,128]{3,2,1,0:T(8,128)S(1)}, u32[]{:S(2)}, u32[]{:S(2)}) async-start(f32[16,4,8,128]{3,2,1,0:T(8,128)} %shard_map.124._.__), calls=%async_computation.1 | async-start | bytes 524288 | tf_op jit(solution)/shard_map/all_to_all | solution.py:808
  53.8 19.8 %all-to-all-start.2 = ((f32[16,4,8,128]{3,2,1,0:T(8,128)}), f32[16,4,8,128]{3,2,1,0:T(8,128)S(1)}, u32[]{:S(2)}, u32[]{:S(2)}) async-start(f32[16,4,8,128]{3,2,1,0:T(8,128)} %shard_map.126.__), calls=%async_computation.2 | async-start | bytes 524288 | tf_op jit(solution)/shard_map/all_to_all | solution.py:808
  58.8 14.6 %collective-permute-start.6 = (f32[4,256]{1,0:T(4,128)S(1)}, f32[4,256]{1,0:T(4,128)S(1)}, u32[]{:S(2)}, u32[]{:S(2)}) collective-permute-start(f32[4,256]{1,0:T(4,128)S(1)} %get-tuple-element.56), channel_id=1, source_target_pairs={{0,1},{1,2},{2,3},{3,0},{4,5},{5,6},{6,7},{7,4},{8,9},{9,10},{10,1... | collective-permute-start | bytes 12296 | tf_op jit(solution)/shard_map/ppermute | solution.py:823
  58.9 14.6 %collective-permute-start.7 = (f32[4,256]{1,0:T(4,128)S(1)}, f32[4,256]{1,0:T(4,128)S(1)}, u32[]{:S(2)}, u32[]{:S(2)}) collective-permute-start(f32[4,256]{1,0:T(4,128)S(1)} %get-tuple-element.57), channel_id=1, source_target_pairs={{1,0},{2,1},{3,2},{0,3},{5,4},{6,5},{7,6},{4,7},{9,8},{10,9},{11,1... | collective-permute-start | bytes 12296 | tf_op jit(solution)/shard_map/ppermute | solution.py:823
  60.6 12.9 %collective-permute-start.4 = (f32[128,256]{1,0:T(8,128)S(1)}, f32[128,256]{1,0:T(8,128)S(1)}, u32[]{:S(2)}, u32[]{:S(2)}) collective-permute-start(f32[128,256]{1,0:T(8,128)S(1)} %get-tuple-element.54), channel_id=1, source_target_pairs={{0,4},{4,8},{8,12},{12,16},{16,20},{20,24},{24,28},{28,0},{1,5},{5... | collective-permute-start | bytes 393224 | tf_op jit(solution)/shard_map/ppermute | solution.py:823
  62.5 11.0 %collective-permute-start.5 = (f32[128,256]{1,0:T(8,128)S(1)}, f32[128,256]{1,0:T(8,128)S(1)}, u32[]{:S(2)}, u32[]{:S(2)}) collective-permute-start(f32[128,256]{1,0:T(8,128)S(1)} %get-tuple-element.55), channel_id=1, source_target_pairs={{4,0},{8,4},{12,8},{16,12},{20,16},{24,20},{28,24},{0,28},{5,1},{9... | collective-permute-start | bytes 393224 | tf_op jit(solution)/shard_map/ppermute | solution.py:823
  73.5 1.5 copy-start.22
  73.5 0.6 copy-start.15
  73.5 0.6 copy-start.17
  73.5 0.6 copy-start.7
  73.5 0.7 copy-start.9
  74.2 0.7 copy-start.20
  74.9 1.7 collective-permute-start.8
  75.0 20.9 %copy-start.3 = (bf16[4,128,256]{2,1,0:T(8,128)(2,1)S(1)}, bf16[4,128,256]{2,1,0:T(8,128)(2,1)}, u32[]{:S(2)}) copy-start(bf16[4,128,256]{2,1,0:T(8,128)(2,1)} %perm_ref.9) | copy-start | bytes 786436
  75.0 20.9 %copy-start.5 = (f32[4,128,256]{2,1,0:T(8,128)S(1)}, f32[4,128,256]{2,1,0:T(8,128)}, u32[]{:S(2)}) copy-start(f32[4,128,256]{2,1,0:T(8,128)} %res_ref.3) | copy-start | bytes 1572868
  75.0 20.9 %copy-start.8 = (f32[128,256]{1,0:T(8,128)S(1)}, f32[128,256]{1,0:T(8,128)}, u32[]{:S(2)}) copy-start(f32[128,256]{1,0:T(8,128)} %copy-done.7) | copy-start | bytes 393220
  75.0 20.9 %copy-start.10 = (f32[128,256]{1,0:T(8,128)S(1)}, f32[128,256]{1,0:T(8,128)}, u32[]{:S(2)}) copy-start(f32[128,256]{1,0:T(8,128)} %copy-done.9) | copy-start | bytes 393220
  75.0 20.9 %copy-start.16 = (f32[4,256]{1,0:T(4,128)S(1)}, f32[4,256]{1,0:T(4,128)}, u32[]{:S(2)}) copy-start(f32[4,256]{1,0:T(4,128)} %copy-done.15) | copy-start | bytes 12292
  75.0 20.9 %copy-start.18 = (f32[4,256]{1,0:T(4,128)S(1)}, f32[4,256]{1,0:T(4,128)}, u32[]{:S(2)}) copy-start(f32[4,256]{1,0:T(4,128)} %copy-done.17) | copy-start | bytes 12292
  82.4 13.5 %collective-permute-start.9 = (f32[128,256]{1,0:T(8,128)S(1)}, f32[128,256]{1,0:T(8,128)S(1)}, u32[]{:S(2)}, u32[]{:S(2)}) collective-permute-start(f32[128,256]{1,0:T(8,128)S(1)} %get-tuple-element.63), channel_id=1, source_target_pairs={{0,4},{4,8},{8,12},{12,16},{16,20},{20,24},{24,28},{28,0},{1,5},{5... | collective-permute-start | bytes 393224 | tf_op jit(solution)/shard_map/ppermute | solution.py:823
  82.4 13.5 %collective-permute-start.10 = (f32[128,256]{1,0:T(8,128)S(1)}, f32[128,256]{1,0:T(8,128)S(1)}, u32[]{:S(2)}, u32[]{:S(2)}) collective-permute-start(f32[128,256]{1,0:T(8,128)S(1)} %get-tuple-element.64), channel_id=1, source_target_pairs={{4,0},{8,4},{12,8},{16,12},{20,16},{24,20},{28,24},{0,28},{5,1},{9... | collective-permute-start | bytes 393224 | tf_op jit(solution)/shard_map/ppermute | solution.py:823
  92.8 3.0 %collective-permute-start.11 = (f32[4,256]{1,0:T(4,128)S(1)}, f32[4,256]{1,0:T(4,128)S(1)}, u32[]{:S(2)}, u32[]{:S(2)}) collective-permute-start(f32[4,256]{1,0:T(4,128)S(1)} %get-tuple-element.65), channel_id=1, source_target_pairs={{0,1},{1,2},{2,3},{3,0},{4,5},{5,6},{6,7},{7,4},{8,9},{9,10},{10,1... | collective-permute-start | bytes 12296 | tf_op jit(solution)/shard_map/ppermute | solution.py:823
  92.8 3.1 %collective-permute-start.12 = (f32[4,256]{1,0:T(4,128)S(1)}, f32[4,256]{1,0:T(4,128)S(1)}, u32[]{:S(2)}, u32[]{:S(2)}) collective-permute-start(f32[4,256]{1,0:T(4,128)S(1)} %get-tuple-element.66), channel_id=1, source_target_pairs={{1,0},{2,1},{3,2},{0,3},{5,4},{6,5},{7,6},{4,7},{9,8},{10,9},{11,1... | collective-permute-start | bytes 12296 | tf_op jit(solution)/shard_map/ppermute | solution.py:823
  118.4 1.5 collective-permute-start.13
  120.7 14.0 %all-to-all-start.4 = ((f32[16,4,8,128]{3,2,1,0:T(8,128)}), f32[16,4,8,128]{3,2,1,0:T(8,128)S(1)}, u32[]{:S(2)}, u32[]{:S(2)}) async-start(f32[16,4,8,128]{3,2,1,0:T(8,128)} %shard_map.133._.__), calls=%async_computation.4 | async-start | bytes 524288 | tf_op jit(solution)/shard_map/all_to_all | solution.py:808
  139.4 14.6 %all-to-all-start.5 = ((f32[16,4,8,128]{3,2,1,0:T(8,128)}), f32[16,4,8,128]{3,2,1,0:T(8,128)S(1)}, u32[]{:S(2)}, u32[]{:S(2)}) async-start(f32[16,4,8,128]{3,2,1,0:T(8,128)} %shard_map.135.__), calls=%async_computation.5 | async-start | bytes 524288 | tf_op jit(solution)/shard_map/all_to_all | solution.py:808
  154.1 0.7 copy-start.19
  154.8 1.7 collective-permute-start.14
  156.5 19.8 %copy-start.1 = (f32[32,8,128]{2,1,0:T(8,128)S(1)}, f32[32,8,128]{2,1,0:T(8,128)}, u32[]{:S(2)}) copy-start(f32[32,8,128]{2,1,0:T(8,128)} %copy-done) | copy-start | bytes 393220
  156.5 19.8 %copy-start.2 = (f32[32,8,128]{2,1,0:T(8,128)S(1)}, f32[32,8,128]{2,1,0:T(8,128)}, u32[]{:S(2)}) copy-start(f32[32,8,128]{2,1,0:T(8,128)} %all_to_all.35.sums_ref.refs_1_) | copy-start | bytes 393220
  156.5 19.8 %copy-start.4 = (bf16[4,128,256]{2,1,0:T(8,128)(2,1)S(1)}, bf16[4,128,256]{2,1,0:T(8,128)(2,1)}, u32[]{:S(2)}) copy-start(bf16[4,128,256]{2,1,0:T(8,128)(2,1)} %perm_ref.9) | copy-start | bytes 786436
  156.5 19.8 %copy-start.6 = (f32[4,128,256]{2,1,0:T(8,128)S(1)}, f32[4,128,256]{2,1,0:T(8,128)}, u32[]{:S(2)}) copy-start(f32[4,128,256]{2,1,0:T(8,128)} %get-tuple-element.82.refs_12_.res_ref) | copy-start | bytes 1572868
  162.8 13.5 %collective-permute-start.15 = (f32[128,256]{1,0:T(8,128)S(1)}, f32[128,256]{1,0:T(8,128)S(1)}, u32[]{:S(2)}, u32[]{:S(2)}) collective-permute-start(f32[128,256]{1,0:T(8,128)S(1)} %get-tuple-element.78), channel_id=1, source_target_pairs={{0,4},{4,8},{8,12},{12,16},{16,20},{20,24},{24,28},{28,0},{1,5},{5... | collective-permute-start | bytes 393224 | tf_op jit(solution)/shard_map/ppermute | solution.py:823
  163.8 12.5 %collective-permute-start.16 = (f32[128,256]{1,0:T(8,128)S(1)}, f32[128,256]{1,0:T(8,128)S(1)}, u32[]{:S(2)}, u32[]{:S(2)}) collective-permute-start(f32[128,256]{1,0:T(8,128)S(1)} %get-tuple-element.79), channel_id=1, source_target_pairs={{4,0},{8,4},{12,8},{16,12},{20,16},{24,20},{28,24},{0,28},{5,1},{9... | collective-permute-start | bytes 393224 | tf_op jit(solution)/shard_map/ppermute | solution.py:823
  173.2 3.0 %collective-permute-start.17 = (f32[4,256]{1,0:T(4,128)S(1)}, f32[4,256]{1,0:T(4,128)S(1)}, u32[]{:S(2)}, u32[]{:S(2)}) collective-permute-start(f32[4,256]{1,0:T(4,128)S(1)} %get-tuple-element.80), channel_id=1, source_target_pairs={{0,1},{1,2},{2,3},{3,0},{4,5},{5,6},{6,7},{7,4},{8,9},{9,10},{10,1... | collective-permute-start | bytes 12296 | tf_op jit(solution)/shard_map/ppermute | solution.py:823
  173.2 3.1 %collective-permute-start.18 = (f32[4,256]{1,0:T(4,128)S(1)}, f32[4,256]{1,0:T(4,128)S(1)}, u32[]{:S(2)}, u32[]{:S(2)}) collective-permute-start(f32[4,256]{1,0:T(4,128)S(1)} %get-tuple-element.81), channel_id=1, source_target_pairs={{1,0},{2,1},{3,2},{0,3},{5,4},{6,5},{7,6},{4,7},{9,8},{10,9},{11,1... | collective-permute-start | bytes 12296 | tf_op jit(solution)/shard_map/ppermute | solution.py:823

commit v10 on v9

--- a/solution.py
+++ b/solution.py
@@ -884,13 +884,15 @@
 
     def points(lifted, part, before, after):
         first = part * rows // 2
-        half_block = pl.BlockSpec((1, CHANNELS, depth, cols), lambda i: (first + i, 0, 0, 0))
+        quarter = pl.BlockSpec(
+            (1, CHANNELS, depth // 4, cols), lambda i, j: (first + i, 0, j, 0)
+        )
         return call(
             point_body,
             channels,
-            [smem, half_block, anywhere, anywhere],
-            half_block,
-            grid=(rows // 2,),
+            [smem, quarter, anywhere, anywhere],
+            quarter,
+            grid=(rows // 2, 4),
             flops=2.5e9,
             moved=16 * field_bytes,
             alias={2: 0} if part else None,

time: 191 us -> 195 us (1.021)
  Pallas kernels: 96.2 us -> 99.8 us
  waiting for transfers between devices: 22.1 us -> 19.4 us
    pallas_call x19, Pallas kernels: 96.2 us -> 99.8 us  [wrapped(): found = run(*held)]
    all_to_all x5, waiting for transfers between devices: 13.3 us -> 10.7 us  [exchange(): return lax.all_to_all(blocks, axes, split_axis=0, concat_axis=0, tiled=True)]
  transfers between devices with their start and end apart: 24 -> 24, of which waited for: 10 -> 10; matrix products, arithmetic and copies ran while one was open for 0% -> 0% of each run, Pallas kernels for 24% -> 26%
where the time goes in v10:
time: 195 us; the launch traced here: 194 us
  Pallas kernels  99.8 us (51%)
  starting transfers between devices  48.9 us (25%)
  blocking collectives  21.2 us (11%)
  waiting for transfers between devices  19.4 us (10%)
  local copies, waits for them, and re-layouts  2.77 us (1%)
    pallas_call x19, Pallas kernels, wrapped(): found = run(*held)  99.8 us
    all_to_all x5, starting transfers between devices, exchange(): return lax.all_to_all(blocks, axes, split_axis=0, concat_axis=0, tiled=True)  24.5 us
    all_to_all x2, blocking collectives, exchange(): return lax.all_to_all(blocks, axes, split_axis=0, concat_axis=0, tiled=True)  21.2 us
    ppermute x6, starting transfers between devices, shift_planes(): lax.ppermute(first, axis, backward)  16.4 us
    all_to_all x5, waiting for transfers between devices, exchange(): return lax.all_to_all(blocks, axes, split_axis=0, concat_axis=0, tiled=True)  10.7 us
    ppermute x4, waiting for transfers between devices, swap(): return lax.ppermute(blocks, 'core', [(0, 1), (1, 0)])  6.05 us
    ppermute x3, starting transfers between devices, tiled_local(): lax.ppermute(part, COL, [(i, (i + shift + 1) % n_col) for i in range(n_co...  4.5 us
  transfers between devices with their start and end apart: 24, of which 10 were waited for; matrix products, arithmetic and copies ran while one was open for 0% of the time, Pallas kernels for 26%

profile of v10, /device:TPU:0, one launch (start us, length us, event | category | flops | bytes accessed | tf_op | source)
XLA Modules:
  0.0 193.8 jit_solution(15687948985753418976)
XLA Ops:
  0.6 1.7 shard_map.122
  2.8 2.6 %collective-permute-start.1 = (f32[4,16,8,128]{3,2,1,0:T(8,128)S(1)}, f32[4,16,8,128]{3,2,1,0:T(8,128)S(1)}, u32[]{:S(2)}, u32[]{:S(2)}) collective-permute-start(f32[4,16,8,128]{3,2,1,0:T(8,128)S(1)} %get-tuple-element.49), channel_id=1, source_target_pairs={{0,2},{1,3},{2,0},{3,1},{4,6},{5,7},{6,4},{7,5},{8,10},{9,11},{10,... | collective-permute-start | bytes 786440 | tf_op jit(solution)/shard_map/ppermute | solution.py:869
  5.4 1.4 collective-permute-start.2
  6.8 1.8 shard_map.121
  8.7 4.9 %all-to-all-start = ((f32[32,8,128]{2,1,0:T(8,128)}), f32[32,8,128]{2,1,0:T(8,128)S(1)}, u32[]{:S(2)}, u32[]{:S(2)}) async-start(f32[32,8,128]{2,1,0:T(8,128)} %get-tuple-element.46), calls=%async_computation | async-start | bytes 262144 | tf_op jit(solution)/shard_map/all_to_all | solution.py:808
  14.2 7.5 %all-to-all-done.sums_ref.refs_0_.first_ref = f32[32,8,128]{2,1,0:T(8,128)S(1)} async-done(((f32[32,8,128]{2,1,0:T(8,128)}), f32[32,8,128]{2,1,0:T(8,128)S(1)}, u32[]{:S(2)}, u32[]{:S(2)}) %all-to-all-start) | async-done | bytes 131104 | tf_op jit(solution)/shard_map/all_to_all | solution.py:808
  22.4 9.7 %shard_map.123 = (f32[16,4,8,128]{3,2,1,0:T(8,128)S(1)}, f32[16,4,8,128]{3,2,1,0:T(8,128)S(1)}, f32[4,16,256,128]{3,2,1,0:T(8,128)}) custom-call(f32[3,16]{1,0:T(4,128)S(1)} %multiply_bitcast_fusion.lift_ref, f32[32,8,128]{2,1,0:T(8,128)} %copy-done, f32[4,128,256]{2,1,0:T(8,128)} %res_ref.3, bf16[4,128,256]{2,1,0:T(8,128)(2,1)} %perm_ref.9, ...), custom_call_target="tpu_custom_call" | custom-call | flops 2000000000 | bytes 1310720 | tf_op jit(solution)/shard_map/pallas_call | solution.py:355
  32.4 1.3 collective-permute-done.3.partner_ref
  33.7 0.7 shard_map.124._.__
  34.4 4.5 %all-to-all-start.1 = ((f32[16,4,8,128]{3,2,1,0:T(8,128)}), f32[16,4,8,128]{3,2,1,0:T(8,128)S(1)}, u32[]{:S(2)}, u32[]{:S(2)}) async-start(f32[16,4,8,128]{3,2,1,0:T(8,128)} %shard_map.124._.__), calls=%async_computation.1 | async-start | bytes 524288 | tf_op jit(solution)/shard_map/all_to_all | solution.py:808
  39.0 9.1 %shard_map.125.refs_4_._ = f32[4,16,256,128]{3,2,1,0:T(8,128)} custom-call(f32[16,17]{1,0:T(8,128)S(1)} %broadcast_multiply_fusion.mix_ref, f32[4,16,256,128]{3,2,1,0:T(8,128)} %get-tuple-element.53.lifted_ref, f32[16,4,8,128]{3,2,1,0:T(8,128)} %shard_map.124._.__, f32[16,4,8,128]{3,2,1,0:T(8,128)} %shard_map.124._.__), custom_call_target="tpu_custom_call" | custom-call | flops 2500000000 | bytes 8388608 | tf_op jit(solution)/shard_map/pallas_call | solution.py:355
  48.1 1.0 all-to-all-done.1.recv_ref
  49.1 4.7 %shard_map.126.__ = f32[16,4,8,128]{3,2,1,0:T(8,128)} custom-call(f32[16,4,8,128]{3,2,1,0:T(8,128)S(1)} %all-to-all-done.1.recv_ref, f32[4,16,8,128]{3,2,1,0:T(8,128)} %copy-done.11, f32[4,16,8,128]{3,2,1,0:T(8,128)} %copy-done.12, f32[4,16,8,128]{3,2,1,0:T(8,128)} %copy-done.13, f32[4,16,8,128]{3,2,1,0:T(8,128)} %copy-done.14, ...), custom_call_target="tpu_custom_call" | custom-call | bytes 1572864 | tf_op jit(solution)/shard_map/pallas_call | solution.py:355
  53.8 5.9 %all-to-all-start.2 = ((f32[16,4,8,128]{3,2,1,0:T(8,128)}), f32[16,4,8,128]{3,2,1,0:T(8,128)S(1)}, u32[]{:S(2)}, u32[]{:S(2)}) async-start(f32[16,4,8,128]{3,2,1,0:T(8,128)} %shard_map.126.__), calls=%async_computation.2 | async-start | bytes 524288 | tf_op jit(solution)/shard_map/all_to_all | solution.py:808
  59.7 1.7 collective-permute-start.7
  61.5 1.9 collective-permute-start.4
  63.3 2.8 %collective-permute-start.5 = (f32[128,256]{1,0:T(8,128)S(1)}, f32[128,256]{1,0:T(8,128)S(1)}, u32[]{:S(2)}, u32[]{:S(2)}) collective-permute-start(f32[128,256]{1,0:T(8,128)S(1)} %get-tuple-element.55), channel_id=1, source_target_pairs={{4,0},{8,4},{12,8},{16,12},{20,16},{24,20},{28,24},{0,28},{5,1},{9... | collective-permute-start | bytes 393224 | tf_op jit(solution)/shard_map/ppermute | solution.py:823
  66.2 9.1 %shard_map.127.__1_.refs_3_ = f32[4,16,256,128]{3,2,1,0:T(8,128)} custom-call(f32[16,17]{1,0:T(8,128)S(1)} %broadcast_multiply_fusion.mix_ref, f32[4,16,256,128]{3,2,1,0:T(8,128)} %get-tuple-element.53.lifted_ref, f32[4,16,256,128]{3,2,1,0:T(8,128)} %shard_map.125.refs_4_._, f32[16,4,8,128]{3,2,1,0:T(8,128)} %shard_map.126.__), custom_call_target="tpu_custom_call", output_to_operand_aliasing={{}: (2, {})} | custom-call | flops 2500000000 | bytes 8388608 | tf_op jit(solution)/shard_map/pallas_call | solution.py:355
  76.0 0.7 copy-done.20
  76.8 1.7 collective-permute-done.8.refs_2_
  78.5 5.7 %shard_map.129 = (f32[2,4,128,256]{3,2,1,0:T(8,128)}, f32[4,128,256]{2,1,0:T(8,128)S(1)}, f32[128,256]{1,0:T(8,128)S(1)}, f32[128,256]{1,0:T(8,128)S(1)}, f32[4,256]{1,0:T(4,128)S(1)}, /*index=5*/f32[4,256]{1,0:T(4,128)S(1)}) custom-call(f32[17]{0:T(128)S(1)} %fusion.proj_ref, f32[32,8,128]{2,1,0:T(8,128)} %copy-done, f32[16,4,8,128]{3,2,1,0:T(8,128)} %shard_map.128.refs_1_, ...), custom_call_target="tpu_custom_call" | custom-call | flops 1000000000 | bytes 4718592 | tf_op jit(solution)/shard_map/pallas_call | solution.py:355
  84.1 4.7 %collective-permute-start.10 = (f32[128,256]{1,0:T(8,128)S(1)}, f32[128,256]{1,0:T(8,128)S(1)}, u32[]{:S(2)}, u32[]{:S(2)}) collective-permute-start(f32[128,256]{1,0:T(8,128)S(1)} %get-tuple-element.64), channel_id=1, source_target_pairs={{4,0},{8,4},{12,8},{16,12},{20,16},{24,20},{28,24},{0,28},{5,1},{9... | collective-permute-start | bytes 393224 | tf_op jit(solution)/shard_map/ppermute | solution.py:823
  88.9 5.7 %shard_map.130 = (f32[2,4,128,256]{3,2,1,0:T(8,128)}, f32[4,128,256]{2,1,0:T(8,128)S(1)}, f32[4,256]{1,0:T(4,128)S(1)}, f32[4,256]{1,0:T(4,128)S(1)}) custom-call(f32[17]{0:T(128)S(1)} %fusion.proj_ref, f32[32,8,128]{2,1,0:T(8,128)} %copy-done, f32[16,4,8,128]{3,2,1,0:T(8,128)} %shard_map.128.refs_1_, ...), custom_call_target="tpu_custom_call", output_to_operand_aliasing={{0}: (7, {}), {1}: (8, {})} | custom-call | flops 1000000000 | bytes 4718592 | tf_op jit(solution)/shard_map/pallas_call | solution.py:355
  94.5 1.7 collective-permute-start.12
  96.3 1.3 collective-permute-done.11.refs_2_.refs_6_
  97.7 1.9 %shard_map.131 = (f32[4,128,256]{2,1,0:T(8,128)S(1)}, f32[32,8,128]{2,1,0:T(8,128)S(1)}) custom-call(f32[4,128,256]{2,1,0:T(8,128)S(1)} %get-tuple-element.62.field_ref.old_ref, bf16[4,128,256]{2,1,0:T(8,128)(2,1)S(1)} %copy-done.3, f32[128,256]{1,0:T(8,128)S(1)} %collective-permute-done.9.refs_0_.refs_4_, ...), custom_call_target="tpu_custom_call" | custom-call | bytes 4718592 | tf_op jit(solution)/shard_map/pallas_call | solution.py:355
  99.6 10.6 %all_to_all.35.sums_ref.refs_1_ = f32[32,8,128]{2,1,0:T(8,128)} all-to-all(f32[32,8,128]{2,1,0:T(8,128)S(1)} %get-tuple-element.67), channel_id=1, replica_groups=mesh['row'=8,'y'=2,'core'=2] {'row','y','core'}, dimensions={0} | all-to-all | bytes 262144 | tf_op jit(solution)/shard_map/all_to_all | solution.py:808
  110.2 10.0 %shard_map.132 = (f32[16,4,8,128]{3,2,1,0:T(8,128)S(1)}, f32[16,4,8,128]{3,2,1,0:T(8,128)S(1)}, f32[4,16,256,128]{3,2,1,0:T(8,128)}, f32[4,128,256]{2,1,0:T(8,128)}) custom-call(f32[3,16]{1,0:T(4,128)S(1)} %multiply_bitcast_fusion.lift_ref, f32[32,8,128]{2,1,0:T(8,128)} %copy-done, f32[32,8,128]{2,1,0:T(8,128)} %all_to_all.35.sums_ref.refs_1_, ...), custom_call_target="tpu_custom_call" | custom-call | flops 2000000000 | bytes 2359296 | tf_op jit(solution)/shard_map/pallas_call | solution.py:355
  120.4 1.3 collective-permute-done.13.partner_ref
  121.8 0.7 shard_map.133._.__
  122.5 3.7 %all-to-all-start.4 = ((f32[16,4,8,128]{3,2,1,0:T(8,128)}), f32[16,4,8,128]{3,2,1,0:T(8,128)S(1)}, u32[]{:S(2)}, u32[]{:S(2)}) async-start(f32[16,4,8,128]{3,2,1,0:T(8,128)} %shard_map.133._.__), calls=%async_computation.4 | async-start | bytes 524288 | tf_op jit(solution)/shard_map/all_to_all | solution.py:808
  126.2 9.1 %shard_map.134.refs_4_._ = f32[4,16,256,128]{3,2,1,0:T(8,128)} custom-call(f32[16,17]{1,0:T(8,128)S(1)} %broadcast_multiply_fusion.mix_ref, f32[4,16,256,128]{3,2,1,0:T(8,128)} %get-tuple-element.71.lifted_ref, f32[16,4,8,128]{3,2,1,0:T(8,128)} %shard_map.133._.__, f32[16,4,8,128]{3,2,1,0:T(8,128)} %shard_map.133._.__), custom_call_target="tpu_custom_call" | custom-call | flops 2500000000 | bytes 8388608 | tf_op jit(solution)/shard_map/pallas_call | solution.py:355
  135.3 1.2 all-to-all-done.4.recv_ref
  136.5 4.7 %shard_map.135.__ = f32[16,4,8,128]{3,2,1,0:T(8,128)} custom-call(f32[16,4,8,128]{3,2,1,0:T(8,128)S(1)} %all-to-all-done.4.recv_ref, f32[4,16,8,128]{3,2,1,0:T(8,128)} %copy-done.11, f32[4,16,8,128]{3,2,1,0:T(8,128)} %copy-done.12, f32[4,16,8,128]{3,2,1,0:T(8,128)} %copy-done.13, f32[4,16,8,128]{3,2,1,0:T(8,128)} %copy-done.14, ...), custom_call_target="tpu_custom_call" | custom-call | bytes 1572864 | tf_op jit(solution)/shard_map/pallas_call | solution.py:355
  141.2 5.5 %all-to-all-start.5 = ((f32[16,4,8,128]{3,2,1,0:T(8,128)}), f32[16,4,8,128]{3,2,1,0:T(8,128)S(1)}, u32[]{:S(2)}, u32[]{:S(2)}) async-start(f32[16,4,8,128]{3,2,1,0:T(8,128)} %shard_map.135.__), calls=%async_computation.5 | async-start | bytes 524288 | tf_op jit(solution)/shard_map/all_to_all | solution.py:808
  146.7 9.1 %shard_map.136.__1_.refs_4_ = f32[4,16,256,128]{3,2,1,0:T(8,128)} custom-call(f32[16,17]{1,0:T(8,128)S(1)} %broadcast_multiply_fusion.mix_ref, f32[4,16,256,128]{3,2,1,0:T(8,128)} %get-tuple-element.71.lifted_ref, f32[4,16,256,128]{3,2,1,0:T(8,128)} %shard_map.134.refs_4_._, f32[16,4,8,128]{3,2,1,0:T(8,128)} %shard_map.135.__), custom_call_target="tpu_custom_call", output_to_operand_aliasing={{}: (2, {})} | custom-call | flops 2500000000 | bytes 8388608 | tf_op jit(solution)/shard_map/pallas_call | solution.py:355
  155.8 0.9 all-to-all-done.5.__0_
  156.7 0.7 copy-done.19
  157.4 1.7 collective-permute-done.14.refs_3_
  159.1 6.3 %shard_map.138 = (f32[2,4,128,256]{3,2,1,0:T(8,128)}, f32[4,128,256]{2,1,0:T(8,128)S(1)}, f32[128,256]{1,0:T(8,128)S(1)}, f32[128,256]{1,0:T(8,128)S(1)}, f32[4,256]{1,0:T(4,128)S(1)}, /*index=5*/f32[4,256]{1,0:T(4,128)S(1)}) custom-call(f32[17]{0:T(128)S(1)} %fusion.proj_ref, f32[32,8,128]{2,1,0:T(8,128)} %copy-done, ...), custom_call_target="tpu_custom_call", output_to_operand_aliasing={{0}: (8, {})} | custom-call | flops 1000000000 | bytes 4718592 | tf_op jit(solution)/shard_map/pallas_call | solution.py:355
  165.4 1.1 collective-permute-start.15
  166.5 3.7 %collective-permute-start.16 = (f32[128,256]{1,0:T(8,128)S(1)}, f32[128,256]{1,0:T(8,128)S(1)}, u32[]{:S(2)}, u32[]{:S(2)}) collective-permute-start(f32[128,256]{1,0:T(8,128)S(1)} %get-tuple-element.79), channel_id=1, source_target_pairs={{4,0},{8,4},{12,8},{16,12},{20,16},{24,20},{28,24},{0,28},{5,1},{9... | collective-permute-start | bytes 393224 | tf_op jit(solution)/shard_map/ppermute | solution.py:823
  170.1 5.7 %shard_map.139 = (f32[2,4,128,256]{3,2,1,0:T(8,128)}, f32[4,128,256]{2,1,0:T(8,128)S(1)}, f32[4,256]{1,0:T(4,128)S(1)}, f32[4,256]{1,0:T(4,128)S(1)}) custom-call(f32[17]{0:T(128)S(1)} %fusion.proj_ref, f32[32,8,128]{2,1,0:T(8,128)} %copy-done, f32[32,8,128]{2,1,0:T(8,128)} %all_to_all.35.sums_ref.refs_1_, ...), custom_call_target="tpu_custom_call", output_to_operand_aliasing={{0}: (8, {}), {1}: (9, {})} | custom-call | flops 1000000000 | bytes 4718592 | tf_op jit(solution)/shard_map/pallas_call | solution.py:355
  175.8 1.7 collective-permute-start.18
  177.6 1.3 collective-permute-done.17.refs_2_
  179.0 2.3 %shard_map.140 = (f32[4,128,256]{2,1,0:T(8,128)S(1)}, f32[4,128,256]{2,1,0:T(8,128)S(1)}, f32[32,8,128]{2,1,0:T(8,128)S(1)}) custom-call(f32[32,8,128]{2,1,0:T(8,128)S(1)} %copy-done.1, f32[32,8,128]{2,1,0:T(8,128)S(1)} %copy-done.2, f32[4,128,256]{2,1,0:T(8,128)S(1)} %get-tuple-element.77.field_ref, f32[4,128,256]{2,1,0:T(8,128)S(1)} %get-tuple-element.62.field_ref.old_ref, ...), custom_call_target="tpu_custom_call" | custom-call | bytes 5767168 | tf_op jit(solution)/shard_map/pallas_call | solution.py:355
  181.2 10.6 %all_to_all.36.later_ref = f32[32,8,128]{2,1,0:T(8,128)S(1)} all-to-all(f32[32,8,128]{2,1,0:T(8,128)S(1)} %get-tuple-element.83), channel_id=1, replica_groups=mesh['row'=8,'y'=2,'core'=2] {'row','y','core'}, dimensions={0} | all-to-all | bytes 262144 | tf_op jit(solution)/shard_map/all_to_all | solution.py:808
  191.8 2.0 %shard_map.141 = (f32[4,128,256]{2,1,0:T(8,128)}, f32[4,128,256]{2,1,0:T(8,128)}) custom-call(f32[32,8,128]{2,1,0:T(8,128)S(1)} %copy-done.2, f32[32,8,128]{2,1,0:T(8,128)S(1)} %all_to_all.36.later_ref, f32[4,128,256]{2,1,0:T(8,128)S(1)} %get-tuple-element.62.field_ref.old_ref, f32[4,128,256]{2,1,0:T(8,128)S(1)} %get-tuple-element.84.way_ref, ...), custom_call_target="tpu_custom_call" | custom-call | bytes 3145728 | tf_op jit(solution)/shard_map/pallas_call | solution.py:355
  (73 shorter events, 3.2 us)
Async XLA Ops:
  0.6 38.3 %copy-start.21 = (f32[16,17]{1,0:T(8,128)S(1)}, f32[16,17]{1,0:T(8,128)}, u32[]{:S(2)}) copy-start(f32[16,17]{1,0:T(8,128)} %param.14) | copy-start | bytes 3268
  2.3 45.7 %copy-start.11 = (f32[4,16,8,128]{3,2,1,0:T(8,128)}, f32[4,16,8,128]{3,2,1,0:T(8,128)S(1)}, u32[]{:S(2)}) copy-start(f32[4,16,8,128]{3,2,1,0:T(8,128)S(1)} %get-tuple-element.47.refs_0_) | copy-start | bytes 786436
  2.3 19.5 %collective-permute-start = (f32[4,16,8,128]{3,2,1,0:T(8,128)S(1)}, f32[4,16,8,128]{3,2,1,0:T(8,128)S(1)}, u32[]{:S(2)}, u32[]{:S(2)}) collective-permute-start(f32[4,16,8,128]{3,2,1,0:T(8,128)S(1)} %get-tuple-element.48), channel_id=1, source_target_pairs={{0,1},{1,2},{2,3},{3,0},{4,5},{5,6},{6,7},{7,4},{8,9},{9,10},{10,1... | collective-permute-start | bytes 786440 | tf_op jit(solution)/shard_map/ppermute | solution.py:869
  2.8 19.0 %collective-permute-start.1 = (f32[4,16,8,128]{3,2,1,0:T(8,128)S(1)}, f32[4,16,8,128]{3,2,1,0:T(8,128)S(1)}, u32[]{:S(2)}, u32[]{:S(2)}) collective-permute-start(f32[4,16,8,128]{3,2,1,0:T(8,128)S(1)} %get-tuple-element.49), channel_id=1, source_target_pairs={{0,2},{1,3},{2,0},{3,1},{4,6},{5,7},{6,4},{7,5},{8,10},{9,11},{10,... | collective-permute-start | bytes 786440 | tf_op jit(solution)/shard_map/ppermute | solution.py:869
  5.4 16.4 %collective-permute-start.2 = (f32[4,16,8,128]{3,2,1,0:T(8,128)S(1)}, f32[4,16,8,128]{3,2,1,0:T(8,128)S(1)}, u32[]{:S(2)}, u32[]{:S(2)}) collective-permute-start(f32[4,16,8,128]{3,2,1,0:T(8,128)S(1)} %get-tuple-element.50), channel_id=1, source_target_pairs={{0,3},{1,0},{2,1},{3,2},{4,7},{5,4},{6,5},{7,6},{8,11},{9,8},{10,9... | collective-permute-start | bytes 786440 | tf_op jit(solution)/shard_map/ppermute | solution.py:869
  8.7 13.1 %all-to-all-start = ((f32[32,8,128]{2,1,0:T(8,128)}), f32[32,8,128]{2,1,0:T(8,128)S(1)}, u32[]{:S(2)}, u32[]{:S(2)}) async-start(f32[32,8,128]{2,1,0:T(8,128)} %get-tuple-element.46), calls=%async_computation | async-start | bytes 262144 | tf_op jit(solution)/shard_map/all_to_all | solution.py:808
  21.8 0.7 copy-start
  21.8 26.2 %copy-start.12 = (f32[4,16,8,128]{3,2,1,0:T(8,128)}, f32[4,16,8,128]{3,2,1,0:T(8,128)S(1)}, u32[]{:S(2)}) copy-start(f32[4,16,8,128]{3,2,1,0:T(8,128)S(1)} %collective-permute-done.refs_1_) | copy-start | bytes 786436
  21.8 26.2 %copy-start.13 = (f32[4,16,8,128]{3,2,1,0:T(8,128)}, f32[4,16,8,128]{3,2,1,0:T(8,128)S(1)}, u32[]{:S(2)}) copy-start(f32[4,16,8,128]{3,2,1,0:T(8,128)S(1)} %collective-permute-done.1.refs_2_) | copy-start | bytes 786436
  21.8 26.2 %copy-start.14 = (f32[4,16,8,128]{3,2,1,0:T(8,128)}, f32[4,16,8,128]{3,2,1,0:T(8,128)S(1)}, u32[]{:S(2)}) copy-start(f32[4,16,8,128]{3,2,1,0:T(8,128)S(1)} %collective-permute-done.2.refs_3_) | copy-start | bytes 786436
  32.2 1.5 collective-permute-start.3
  34.4 14.7 %all-to-all-start.1 = ((f32[16,4,8,128]{3,2,1,0:T(8,128)}), f32[16,4,8,128]{3,2,1,0:T(8,128)S(1)}, u32[]{:S(2)}, u32[]{:S(2)}) async-start(f32[16,4,8,128]{3,2,1,0:T(8,128)} %shard_map.124._.__), calls=%async_computation.1 | async-start | bytes 524288 | tf_op jit(solution)/shard_map/all_to_all | solution.py:808
  53.8 21.5 %all-to-all-start.2 = ((f32[16,4,8,128]{3,2,1,0:T(8,128)}), f32[16,4,8,128]{3,2,1,0:T(8,128)S(1)}, u32[]{:S(2)}, u32[]{:S(2)}) async-start(f32[16,4,8,128]{3,2,1,0:T(8,128)} %shard_map.126.__), calls=%async_computation.2 | async-start | bytes 524288 | tf_op jit(solution)/shard_map/all_to_all | solution.py:808
  59.7 15.6 %collective-permute-start.6 = (f32[4,256]{1,0:T(4,128)S(1)}, f32[4,256]{1,0:T(4,128)S(1)}, u32[]{:S(2)}, u32[]{:S(2)}) collective-permute-start(f32[4,256]{1,0:T(4,128)S(1)} %get-tuple-element.56), channel_id=1, source_target_pairs={{0,1},{1,2},{2,3},{3,0},{4,5},{5,6},{6,7},{7,4},{8,9},{9,10},{10,1... | collective-permute-start | bytes 12296 | tf_op jit(solution)/shard_map/ppermute | solution.py:823
  59.7 15.5 %collective-permute-start.7 = (f32[4,256]{1,0:T(4,128)S(1)}, f32[4,256]{1,0:T(4,128)S(1)}, u32[]{:S(2)}, u32[]{:S(2)}) collective-permute-start(f32[4,256]{1,0:T(4,128)S(1)} %get-tuple-element.57), channel_id=1, source_target_pairs={{1,0},{2,1},{3,2},{0,3},{5,4},{6,5},{7,6},{4,7},{9,8},{10,9},{11,1... | collective-permute-start | bytes 12296 | tf_op jit(solution)/shard_map/ppermute | solution.py:823
  61.5 13.8 %collective-permute-start.4 = (f32[128,256]{1,0:T(8,128)S(1)}, f32[128,256]{1,0:T(8,128)S(1)}, u32[]{:S(2)}, u32[]{:S(2)}) collective-permute-start(f32[128,256]{1,0:T(8,128)S(1)} %get-tuple-element.54), channel_id=1, source_target_pairs={{0,4},{4,8},{8,12},{12,16},{16,20},{20,24},{24,28},{28,0},{1,5},{5... | collective-permute-start | bytes 393224 | tf_op jit(solution)/shard_map/ppermute | solution.py:823
  63.3 12.0 %collective-permute-start.5 = (f32[128,256]{1,0:T(8,128)S(1)}, f32[128,256]{1,0:T(8,128)S(1)}, u32[]{:S(2)}, u32[]{:S(2)}) collective-permute-start(f32[128,256]{1,0:T(8,128)S(1)} %get-tuple-element.55), channel_id=1, source_target_pairs={{4,0},{8,4},{12,8},{16,12},{20,16},{24,20},{28,24},{0,28},{5,1},{9... | collective-permute-start | bytes 393224 | tf_op jit(solution)/shard_map/ppermute | solution.py:823
  75.3 1.5 copy-start.22
  75.3 0.6 copy-start.15
  75.3 0.6 copy-start.17
  75.3 0.6 copy-start.7
  75.3 0.7 copy-start.9
  76.0 0.7 copy-start.20
  76.7 1.7 collective-permute-start.8
  76.7 20.9 %copy-start.3 = (bf16[4,128,256]{2,1,0:T(8,128)(2,1)S(1)}, bf16[4,128,256]{2,1,0:T(8,128)(2,1)}, u32[]{:S(2)}) copy-start(bf16[4,128,256]{2,1,0:T(8,128)(2,1)} %perm_ref.9) | copy-start | bytes 786436
  76.7 20.9 %copy-start.5 = (f32[4,128,256]{2,1,0:T(8,128)S(1)}, f32[4,128,256]{2,1,0:T(8,128)}, u32[]{:S(2)}) copy-start(f32[4,128,256]{2,1,0:T(8,128)} %res_ref.3) | copy-start | bytes 1572868
  76.8 20.9 %copy-start.8 = (f32[128,256]{1,0:T(8,128)S(1)}, f32[128,256]{1,0:T(8,128)}, u32[]{:S(2)}) copy-start(f32[128,256]{1,0:T(8,128)} %copy-done.7) | copy-start | bytes 393220
  76.8 20.9 %copy-start.10 = (f32[128,256]{1,0:T(8,128)S(1)}, f32[128,256]{1,0:T(8,128)}, u32[]{:S(2)}) copy-start(f32[128,256]{1,0:T(8,128)} %copy-done.9) | copy-start | bytes 393220
  76.8 20.9 %copy-start.16 = (f32[4,256]{1,0:T(4,128)S(1)}, f32[4,256]{1,0:T(4,128)}, u32[]{:S(2)}) copy-start(f32[4,256]{1,0:T(4,128)} %copy-done.15) | copy-start | bytes 12292
  76.8 20.9 %copy-start.18 = (f32[4,256]{1,0:T(4,128)S(1)}, f32[4,256]{1,0:T(4,128)}, u32[]{:S(2)}) copy-start(f32[4,256]{1,0:T(4,128)} %copy-done.17) | copy-start | bytes 12292
  84.1 13.5 %collective-permute-start.9 = (f32[128,256]{1,0:T(8,128)S(1)}, f32[128,256]{1,0:T(8,128)S(1)}, u32[]{:S(2)}, u32[]{:S(2)}) collective-permute-start(f32[128,256]{1,0:T(8,128)S(1)} %get-tuple-element.63), channel_id=1, source_target_pairs={{0,4},{4,8},{8,12},{12,16},{16,20},{20,24},{24,28},{28,0},{1,5},{5... | collective-permute-start | bytes 393224 | tf_op jit(solution)/shard_map/ppermute | solution.py:823
  84.1 13.5 %collective-permute-start.10 = (f32[128,256]{1,0:T(8,128)S(1)}, f32[128,256]{1,0:T(8,128)S(1)}, u32[]{:S(2)}, u32[]{:S(2)}) collective-permute-start(f32[128,256]{1,0:T(8,128)S(1)} %get-tuple-element.64), channel_id=1, source_target_pairs={{4,0},{8,4},{12,8},{16,12},{20,16},{24,20},{28,24},{0,28},{5,1},{9... | collective-permute-start | bytes 393224 | tf_op jit(solution)/shard_map/ppermute | solution.py:823
  94.5 3.0 %collective-permute-start.11 = (f32[4,256]{1,0:T(4,128)S(1)}, f32[4,256]{1,0:T(4,128)S(1)}, u32[]{:S(2)}, u32[]{:S(2)}) collective-permute-start(f32[4,256]{1,0:T(4,128)S(1)} %get-tuple-element.65), channel_id=1, source_target_pairs={{0,1},{1,2},{2,3},{3,0},{4,5},{5,6},{6,7},{7,4},{8,9},{9,10},{10,1... | collective-permute-start | bytes 12296 | tf_op jit(solution)/shard_map/ppermute | solution.py:823
  94.5 3.1 %collective-permute-start.12 = (f32[4,256]{1,0:T(4,128)S(1)}, f32[4,256]{1,0:T(4,128)S(1)}, u32[]{:S(2)}, u32[]{:S(2)}) collective-permute-start(f32[4,256]{1,0:T(4,128)S(1)} %get-tuple-element.66), channel_id=1, source_target_pairs={{1,0},{2,1},{3,2},{0,3},{5,4},{6,5},{7,6},{4,7},{9,8},{10,9},{11,1... | collective-permute-start | bytes 12296 | tf_op jit(solution)/shard_map/ppermute | solution.py:823
  120.2 1.5 collective-permute-start.13
  122.5 14.0 %all-to-all-start.4 = ((f32[16,4,8,128]{3,2,1,0:T(8,128)}), f32[16,4,8,128]{3,2,1,0:T(8,128)S(1)}, u32[]{:S(2)}, u32[]{:S(2)}) async-start(f32[16,4,8,128]{3,2,1,0:T(8,128)} %shard_map.133._.__), calls=%async_computation.4 | async-start | bytes 524288 | tf_op jit(solution)/shard_map/all_to_all | solution.py:808
  141.2 15.5 %all-to-all-start.5 = ((f32[16,4,8,128]{3,2,1,0:T(8,128)}), f32[16,4,8,128]{3,2,1,0:T(8,128)S(1)}, u32[]{:S(2)}, u32[]{:S(2)}) async-start(f32[16,4,8,128]{3,2,1,0:T(8,128)} %shard_map.135.__), calls=%async_computation.5 | async-start | bytes 524288 | tf_op jit(solution)/shard_map/all_to_all | solution.py:808
  156.7 0.7 copy-start.19
  157.4 1.7 collective-permute-start.14
  159.1 19.8 %copy-start.1 = (f32[32,8,128]{2,1,0:T(8,128)S(1)}, f32[32,8,128]{2,1,0:T(8,128)}, u32[]{:S(2)}) copy-start(f32[32,8,128]{2,1,0:T(8,128)} %copy-done) | copy-start | bytes 393220
  159.1 19.8 %copy-start.2 = (f32[32,8,128]{2,1,0:T(8,128)S(1)}, f32[32,8,128]{2,1,0:T(8,128)}, u32[]{:S(2)}) copy-start(f32[32,8,128]{2,1,0:T(8,128)} %all_to_all.35.sums_ref.refs_1_) | copy-start | bytes 393220
  159.1 19.8 %copy-start.4 = (bf16[4,128,256]{2,1,0:T(8,128)(2,1)S(1)}, bf16[4,128,256]{2,1,0:T(8,128)(2,1)}, u32[]{:S(2)}) copy-start(bf16[4,128,256]{2,1,0:T(8,128)(2,1)} %perm_ref.9) | copy-start | bytes 786436
  159.1 19.8 %copy-start.6 = (f32[4,128,256]{2,1,0:T(8,128)S(1)}, f32[4,128,256]{2,1,0:T(8,128)}, u32[]{:S(2)}) copy-start(f32[4,128,256]{2,1,0:T(8,128)} %get-tuple-element.82.refs_12_.res_ref) | copy-start | bytes 1572868
  165.4 13.5 %collective-permute-start.15 = (f32[128,256]{1,0:T(8,128)S(1)}, f32[128,256]{1,0:T(8,128)S(1)}, u32[]{:S(2)}, u32[]{:S(2)}) collective-permute-start(f32[128,256]{1,0:T(8,128)S(1)} %get-tuple-element.78), channel_id=1, source_target_pairs={{0,4},{4,8},{8,12},{12,16},{16,20},{20,24},{24,28},{28,0},{1,5},{5... | collective-permute-start | bytes 393224 | tf_op jit(solution)/shard_map/ppermute | solution.py:823
  166.5 12.5 %collective-permute-start.16 = (f32[128,256]{1,0:T(8,128)S(1)}, f32[128,256]{1,0:T(8,128)S(1)}, u32[]{:S(2)}, u32[]{:S(2)}) collective-permute-start(f32[128,256]{1,0:T(8,128)S(1)} %get-tuple-element.79), channel_id=1, source_target_pairs={{4,0},{8,4},{12,8},{16,12},{20,16},{24,20},{28,24},{0,28},{5,1},{9... | collective-permute-start | bytes 393224 | tf_op jit(solution)/shard_map/ppermute | solution.py:823
  175.8 3.0 %collective-permute-start.17 = (f32[4,256]{1,0:T(4,128)S(1)}, f32[4,256]{1,0:T(4,128)S(1)}, u32[]{:S(2)}, u32[]{:S(2)}) collective-permute-start(f32[4,256]{1,0:T(4,128)S(1)} %get-tuple-element.80), channel_id=1, source_target_pairs={{0,1},{1,2},{2,3},{3,0},{4,5},{5,6},{6,7},{7,4},{8,9},{9,10},{10,1... | collective-permute-start | bytes 12296 | tf_op jit(solution)/shard_map/ppermute | solution.py:823
  175.8 3.1 %collective-permute-start.18 = (f32[4,256]{1,0:T(4,128)S(1)}, f32[4,256]{1,0:T(4,128)S(1)}, u32[]{:S(2)}, u32[]{:S(2)}) collective-permute-start(f32[4,256]{1,0:T(4,128)S(1)} %get-tuple-element.81), channel_id=1, source_target_pairs={{1,0},{2,1},{3,2},{0,3},{5,4},{6,5},{7,6},{4,7},{9,8},{10,9},{11,1... | collective-permute-start | bytes 12296 | tf_op jit(solution)/shard_map/ppermute | solution.py:823

commit v11 on v9

--- a/solution.py
+++ b/solution.py
@@ -486,7 +486,7 @@
 
 
 def point_body(mix_ref, lifted_ref, _, __, point_ref):
-    size = 4 * SUBLANES
+    size = 8 * SUBLANES
     group = 4
 
     def step(index, carry):

time: 191 us -> 191 us (level)
  no operation moved by 1% of the time
where the time goes in v11:
time: 191 us; the launch traced here: 190 us
  Pallas kernels  95.3 us (50%)
  starting transfers between devices  46.7 us (24%)
  waiting for transfers between devices  22.9 us (12%)
  blocking collectives  20.7 us (11%)
  local copies, waits for them, and re-layouts  2.77 us (1%)
    pallas_call x19, Pallas kernels, wrapped(): found = run(*held)  95.3 us
    all_to_all x5, starting transfers between devices, exchange(): return lax.all_to_all(blocks, axes, split_axis=0, concat_axis=0, tiled=True)  22.4 us
    all_to_all x2, blocking collectives, exchange(): return lax.all_to_all(blocks, axes, split_axis=0, concat_axis=0, tiled=True)  20.7 us
    ppermute x6, starting transfers between devices, shift_planes(): lax.ppermute(first, axis, backward)  16.4 us
    all_to_all x5, waiting for transfers between devices, exchange(): return lax.all_to_all(blocks, axes, split_axis=0, concat_axis=0, tiled=True)  14.2 us
    ppermute x4, waiting for transfers between devices, swap(): return lax.ppermute(blocks, 'core', [(0, 1), (1, 0)])  6.05 us
    ppermute x3, starting transfers between devices, tiled_local(): lax.ppermute(part, COL, [(i, (i + shift + 1) % n_col) for i in range(n_co...  4.5 us
  transfers between devices with their start and end apart: 24, of which 10 were waited for; matrix products, arithmetic and copies ran while one was open for 0% of the time, Pallas kernels for 24%

profile of v11, /device:TPU:0, one launch (start us, length us, event | category | flops | bytes accessed | tf_op | source)
XLA Modules:
  0.0 190.2 jit_solution(10286993014745507846)
XLA Ops:
  0.6 1.7 shard_map.122
  2.8 2.6 %collective-permute-start.1 = (f32[4,16,8,128]{3,2,1,0:T(8,128)S(1)}, f32[4,16,8,128]{3,2,1,0:T(8,128)S(1)}, u32[]{:S(2)}, u32[]{:S(2)}) collective-permute-start(f32[4,16,8,128]{3,2,1,0:T(8,128)S(1)} %get-tuple-element.49), channel_id=1, source_target_pairs={{0,2},{1,3},{2,0},{3,1},{4,6},{5,7},{6,4},{7,5},{8,10},{9,11},{10,... | collective-permute-start | bytes 786440 | tf_op jit(solution)/shard_map/ppermute | solution.py:869
  5.4 1.4 collective-permute-start.2
  6.8 1.8 shard_map.121
  8.7 4.9 %all-to-all-start = ((f32[32,8,128]{2,1,0:T(8,128)}), f32[32,8,128]{2,1,0:T(8,128)S(1)}, u32[]{:S(2)}, u32[]{:S(2)}) async-start(f32[32,8,128]{2,1,0:T(8,128)} %get-tuple-element.46), calls=%async_computation | async-start | bytes 262144 | tf_op jit(solution)/shard_map/all_to_all | solution.py:808
  14.2 7.5 %all-to-all-done.sums_ref.refs_0_.first_ref = f32[32,8,128]{2,1,0:T(8,128)S(1)} async-done(((f32[32,8,128]{2,1,0:T(8,128)}), f32[32,8,128]{2,1,0:T(8,128)S(1)}, u32[]{:S(2)}, u32[]{:S(2)}) %all-to-all-start) | async-done | bytes 131104 | tf_op jit(solution)/shard_map/all_to_all | solution.py:808
  22.4 9.7 %shard_map.123 = (f32[16,4,8,128]{3,2,1,0:T(8,128)S(1)}, f32[16,4,8,128]{3,2,1,0:T(8,128)S(1)}, f32[4,16,256,128]{3,2,1,0:T(8,128)}) custom-call(f32[3,16]{1,0:T(4,128)S(1)} %multiply_bitcast_fusion.lift_ref, f32[32,8,128]{2,1,0:T(8,128)} %copy-done, f32[4,128,256]{2,1,0:T(8,128)} %res_ref.3, bf16[4,128,256]{2,1,0:T(8,128)(2,1)} %perm_ref.9, ...), custom_call_target="tpu_custom_call" | custom-call | flops 2000000000 | bytes 1310720 | tf_op jit(solution)/shard_map/pallas_call | solution.py:355
  32.4 1.3 collective-permute-done.3.partner_ref
  33.7 0.7 shard_map.124._.__
  34.4 4.5 %all-to-all-start.1 = ((f32[16,4,8,128]{3,2,1,0:T(8,128)}), f32[16,4,8,128]{3,2,1,0:T(8,128)S(1)}, u32[]{:S(2)}, u32[]{:S(2)}) async-start(f32[16,4,8,128]{3,2,1,0:T(8,128)} %shard_map.124._.__), calls=%async_computation.1 | async-start | bytes 524288 | tf_op jit(solution)/shard_map/all_to_all | solution.py:808
  39.0 8.0 %shard_map.125.refs_4_._ = f32[4,16,256,128]{3,2,1,0:T(8,128)} custom-call(f32[16,17]{1,0:T(8,128)S(1)} %broadcast_multiply_fusion.mix_ref, f32[4,16,256,128]{3,2,1,0:T(8,128)} %get-tuple-element.53.lifted_ref, f32[16,4,8,128]{3,2,1,0:T(8,128)} %shard_map.124._.__, f32[16,4,8,128]{3,2,1,0:T(8,128)} %shard_map.124._.__), custom_call_target="tpu_custom_call" | custom-call | flops 2500000000 | bytes 8388608 | tf_op jit(solution)/shard_map/pallas_call | solution.py:355
  47.0 2.1 %all-to-all-done.1.recv_ref = f32[16,4,8,128]{3,2,1,0:T(8,128)S(1)} async-done(((f32[16,4,8,128]{3,2,1,0:T(8,128)}), f32[16,4,8,128]{3,2,1,0:T(8,128)S(1)}, u32[]{:S(2)}, u32[]{:S(2)}) %all-to-all-start.1) | async-done | bytes 262176 | tf_op jit(solution)/shard_map/all_to_all | solution.py:808
  49.1 4.7 %shard_map.126.__ = f32[16,4,8,128]{3,2,1,0:T(8,128)} custom-call(f32[16,4,8,128]{3,2,1,0:T(8,128)S(1)} %all-to-all-done.1.recv_ref, f32[4,16,8,128]{3,2,1,0:T(8,128)} %copy-done.11, f32[4,16,8,128]{3,2,1,0:T(8,128)} %copy-done.12, f32[4,16,8,128]{3,2,1,0:T(8,128)} %copy-done.13, f32[4,16,8,128]{3,2,1,0:T(8,128)} %copy-done.14, ...), custom_call_target="tpu_custom_call" | custom-call | bytes 1572864 | tf_op jit(solution)/shard_map/pallas_call | solution.py:355
  53.8 4.8 %all-to-all-start.2 = ((f32[16,4,8,128]{3,2,1,0:T(8,128)}), f32[16,4,8,128]{3,2,1,0:T(8,128)S(1)}, u32[]{:S(2)}, u32[]{:S(2)}) async-start(f32[16,4,8,128]{3,2,1,0:T(8,128)} %shard_map.126.__), calls=%async_computation.2 | async-start | bytes 524288 | tf_op jit(solution)/shard_map/all_to_all | solution.py:808
  58.7 1.7 collective-permute-start.7
  60.4 1.9 collective-permute-start.4
  62.3 2.8 %collective-permute-start.5 = (f32[128,256]{1,0:T(8,128)S(1)}, f32[128,256]{1,0:T(8,128)S(1)}, u32[]{:S(2)}, u32[]{:S(2)}) collective-permute-start(f32[128,256]{1,0:T(8,128)S(1)} %get-tuple-element.55), channel_id=1, source_target_pairs={{4,0},{8,4},{12,8},{16,12},{20,16},{24,20},{28,24},{0,28},{5,1},{9... | collective-permute-start | bytes 393224 | tf_op jit(solution)/shard_map/ppermute | solution.py:823
  65.1 7.9 %shard_map.127.__1_.refs_3_ = f32[4,16,256,128]{3,2,1,0:T(8,128)} custom-call(f32[16,17]{1,0:T(8,128)S(1)} %broadcast_multiply_fusion.mix_ref, f32[4,16,256,128]{3,2,1,0:T(8,128)} %get-tuple-element.53.lifted_ref, f32[4,16,256,128]{3,2,1,0:T(8,128)} %shard_map.125.refs_4_._, f32[16,4,8,128]{3,2,1,0:T(8,128)} %shard_map.126.__), custom_call_target="tpu_custom_call", output_to_operand_aliasing={{}: (2, {})} | custom-call | flops 2500000000 | bytes 8388608 | tf_op jit(solution)/shard_map/pallas_call | solution.py:355
  73.8 0.7 copy-done.20
  74.6 1.7 collective-permute-done.8.refs_2_
  76.2 5.7 %shard_map.129 = (f32[2,4,128,256]{3,2,1,0:T(8,128)}, f32[4,128,256]{2,1,0:T(8,128)S(1)}, f32[128,256]{1,0:T(8,128)S(1)}, f32[128,256]{1,0:T(8,128)S(1)}, f32[4,256]{1,0:T(4,128)S(1)}, /*index=5*/f32[4,256]{1,0:T(4,128)S(1)}) custom-call(f32[17]{0:T(128)S(1)} %fusion.proj_ref, f32[32,8,128]{2,1,0:T(8,128)} %copy-done, f32[16,4,8,128]{3,2,1,0:T(8,128)} %shard_map.128.refs_1_, ...), custom_call_target="tpu_custom_call" | custom-call | flops 1000000000 | bytes 4718592 | tf_op jit(solution)/shard_map/pallas_call | solution.py:355
  81.9 4.7 %collective-permute-start.10 = (f32[128,256]{1,0:T(8,128)S(1)}, f32[128,256]{1,0:T(8,128)S(1)}, u32[]{:S(2)}, u32[]{:S(2)}) collective-permute-start(f32[128,256]{1,0:T(8,128)S(1)} %get-tuple-element.64), channel_id=1, source_target_pairs={{4,0},{8,4},{12,8},{16,12},{20,16},{24,20},{28,24},{0,28},{5,1},{9... | collective-permute-start | bytes 393224 | tf_op jit(solution)/shard_map/ppermute | solution.py:823
  86.6 5.7 %shard_map.130 = (f32[2,4,128,256]{3,2,1,0:T(8,128)}, f32[4,128,256]{2,1,0:T(8,128)S(1)}, f32[4,256]{1,0:T(4,128)S(1)}, f32[4,256]{1,0:T(4,128)S(1)}) custom-call(f32[17]{0:T(128)S(1)} %fusion.proj_ref, f32[32,8,128]{2,1,0:T(8,128)} %copy-done, f32[16,4,8,128]{3,2,1,0:T(8,128)} %shard_map.128.refs_1_, ...), custom_call_target="tpu_custom_call", output_to_operand_aliasing={{0}: (7, {}), {1}: (8, {})} | custom-call | flops 1000000000 | bytes 4718592 | tf_op jit(solution)/shard_map/pallas_call | solution.py:355
  92.3 1.7 collective-permute-start.12
  94.1 1.3 collective-permute-done.11.refs_2_.refs_6_
  95.4 1.9 %shard_map.131 = (f32[4,128,256]{2,1,0:T(8,128)S(1)}, f32[32,8,128]{2,1,0:T(8,128)S(1)}) custom-call(f32[4,128,256]{2,1,0:T(8,128)S(1)} %get-tuple-element.62.field_ref.old_ref, bf16[4,128,256]{2,1,0:T(8,128)(2,1)S(1)} %copy-done.3, f32[128,256]{1,0:T(8,128)S(1)} %collective-permute-done.9.refs_0_.refs_4_, ...), custom_call_target="tpu_custom_call" | custom-call | bytes 4718592 | tf_op jit(solution)/shard_map/pallas_call | solution.py:355
  97.4 10.6 %all_to_all.35.sums_ref.refs_1_ = f32[32,8,128]{2,1,0:T(8,128)} all-to-all(f32[32,8,128]{2,1,0:T(8,128)S(1)} %get-tuple-element.67), channel_id=1, replica_groups=mesh['row'=8,'y'=2,'core'=2] {'row','y','core'}, dimensions={0} | all-to-all | bytes 262144 | tf_op jit(solution)/shard_map/all_to_all | solution.py:808
  108.0 10.0 %shard_map.132 = (f32[16,4,8,128]{3,2,1,0:T(8,128)S(1)}, f32[16,4,8,128]{3,2,1,0:T(8,128)S(1)}, f32[4,16,256,128]{3,2,1,0:T(8,128)}, f32[4,128,256]{2,1,0:T(8,128)}) custom-call(f32[3,16]{1,0:T(4,128)S(1)} %multiply_bitcast_fusion.lift_ref, f32[32,8,128]{2,1,0:T(8,128)} %copy-done, f32[32,8,128]{2,1,0:T(8,128)} %all_to_all.35.sums_ref.refs_1_, ...), custom_call_target="tpu_custom_call" | custom-call | flops 2000000000 | bytes 2359296 | tf_op jit(solution)/shard_map/pallas_call | solution.py:355
  118.2 1.3 collective-permute-done.13.partner_ref
  119.5 0.7 shard_map.133._.__
  120.3 3.7 %all-to-all-start.4 = ((f32[16,4,8,128]{3,2,1,0:T(8,128)}), f32[16,4,8,128]{3,2,1,0:T(8,128)S(1)}, u32[]{:S(2)}, u32[]{:S(2)}) async-start(f32[16,4,8,128]{3,2,1,0:T(8,128)} %shard_map.133._.__), calls=%async_computation.4 | async-start | bytes 524288 | tf_op jit(solution)/shard_map/all_to_all | solution.py:808
  124.0 8.0 %shard_map.134.refs_4_._ = f32[4,16,256,128]{3,2,1,0:T(8,128)} custom-call(f32[16,17]{1,0:T(8,128)S(1)} %broadcast_multiply_fusion.mix_ref, f32[4,16,256,128]{3,2,1,0:T(8,128)} %get-tuple-element.71.lifted_ref, f32[16,4,8,128]{3,2,1,0:T(8,128)} %shard_map.133._.__, f32[16,4,8,128]{3,2,1,0:T(8,128)} %shard_map.133._.__), custom_call_target="tpu_custom_call" | custom-call | flops 2500000000 | bytes 8388608 | tf_op jit(solution)/shard_map/pallas_call | solution.py:355
  132.0 2.5 %all-to-all-done.4.recv_ref = f32[16,4,8,128]{3,2,1,0:T(8,128)S(1)} async-done(((f32[16,4,8,128]{3,2,1,0:T(8,128)}), f32[16,4,8,128]{3,2,1,0:T(8,128)S(1)}, u32[]{:S(2)}, u32[]{:S(2)}) %all-to-all-start.4) | async-done | bytes 262176 | tf_op jit(solution)/shard_map/all_to_all | solution.py:808
  134.5 4.7 %shard_map.135.__ = f32[16,4,8,128]{3,2,1,0:T(8,128)} custom-call(f32[16,4,8,128]{3,2,1,0:T(8,128)S(1)} %all-to-all-done.4.recv_ref, f32[4,16,8,128]{3,2,1,0:T(8,128)} %copy-done.11, f32[4,16,8,128]{3,2,1,0:T(8,128)} %copy-done.12, f32[4,16,8,128]{3,2,1,0:T(8,128)} %copy-done.13, f32[4,16,8,128]{3,2,1,0:T(8,128)} %copy-done.14, ...), custom_call_target="tpu_custom_call" | custom-call | bytes 1572864 | tf_op jit(solution)/shard_map/pallas_call | solution.py:355
  139.2 4.4 %all-to-all-start.5 = ((f32[16,4,8,128]{3,2,1,0:T(8,128)}), f32[16,4,8,128]{3,2,1,0:T(8,128)S(1)}, u32[]{:S(2)}, u32[]{:S(2)}) async-start(f32[16,4,8,128]{3,2,1,0:T(8,128)} %shard_map.135.__), calls=%async_computation.5 | async-start | bytes 524288 | tf_op jit(solution)/shard_map/all_to_all | solution.py:808
  143.6 7.9 %shard_map.136.__1_.refs_4_ = f32[4,16,256,128]{3,2,1,0:T(8,128)} custom-call(f32[16,17]{1,0:T(8,128)S(1)} %broadcast_multiply_fusion.mix_ref, f32[4,16,256,128]{3,2,1,0:T(8,128)} %get-tuple-element.71.lifted_ref, f32[4,16,256,128]{3,2,1,0:T(8,128)} %shard_map.134.refs_4_._, f32[16,4,8,128]{3,2,1,0:T(8,128)} %shard_map.135.__), custom_call_target="tpu_custom_call", output_to_operand_aliasing={{}: (2, {})} | custom-call | flops 2500000000 | bytes 8388608 | tf_op jit(solution)/shard_map/pallas_call | solution.py:355
  151.5 2.1 %all-to-all-done.5.__0_ = f32[16,4,8,128]{3,2,1,0:T(8,128)S(1)} async-done(((f32[16,4,8,128]{3,2,1,0:T(8,128)}), f32[16,4,8,128]{3,2,1,0:T(8,128)S(1)}, u32[]{:S(2)}, u32[]{:S(2)}) %all-to-all-start.5) | async-done | bytes 262176 | tf_op jit(solution)/shard_map/all_to_all | solution.py:808
  153.6 0.7 copy-done.19
  154.3 1.7 collective-permute-done.14.refs_3_
  156.0 6.3 %shard_map.138 = (f32[2,4,128,256]{3,2,1,0:T(8,128)}, f32[4,128,256]{2,1,0:T(8,128)S(1)}, f32[128,256]{1,0:T(8,128)S(1)}, f32[128,256]{1,0:T(8,128)S(1)}, f32[4,256]{1,0:T(4,128)S(1)}, /*index=5*/f32[4,256]{1,0:T(4,128)S(1)}) custom-call(f32[17]{0:T(128)S(1)} %fusion.proj_ref, f32[32,8,128]{2,1,0:T(8,128)} %copy-done, ...), custom_call_target="tpu_custom_call", output_to_operand_aliasing={{0}: (8, {})} | custom-call | flops 1000000000 | bytes 4718592 | tf_op jit(solution)/shard_map/pallas_call | solution.py:355
  162.3 1.1 collective-permute-start.15
  163.4 3.7 %collective-permute-start.16 = (f32[128,256]{1,0:T(8,128)S(1)}, f32[128,256]{1,0:T(8,128)S(1)}, u32[]{:S(2)}, u32[]{:S(2)}) collective-permute-start(f32[128,256]{1,0:T(8,128)S(1)} %get-tuple-element.79), channel_id=1, source_target_pairs={{4,0},{8,4},{12,8},{16,12},{20,16},{24,20},{28,24},{0,28},{5,1},{9... | collective-permute-start | bytes 393224 | tf_op jit(solution)/shard_map/ppermute | solution.py:823
  167.0 5.7 %shard_map.139 = (f32[2,4,128,256]{3,2,1,0:T(8,128)}, f32[4,128,256]{2,1,0:T(8,128)S(1)}, f32[4,256]{1,0:T(4,128)S(1)}, f32[4,256]{1,0:T(4,128)S(1)}) custom-call(f32[17]{0:T(128)S(1)} %fusion.proj_ref, f32[32,8,128]{2,1,0:T(8,128)} %copy-done, f32[32,8,128]{2,1,0:T(8,128)} %all_to_all.35.sums_ref.refs_1_, ...), custom_call_target="tpu_custom_call", output_to_operand_aliasing={{0}: (8, {}), {1}: (9, {})} | custom-call | flops 1000000000 | bytes 4718592 | tf_op jit(solution)/shard_map/pallas_call | solution.py:355
  172.7 1.7 collective-permute-start.18
  174.5 1.3 collective-permute-done.17.refs_2_
  175.9 2.3 %shard_map.140 = (f32[4,128,256]{2,1,0:T(8,128)S(1)}, f32[4,128,256]{2,1,0:T(8,128)S(1)}, f32[32,8,128]{2,1,0:T(8,128)S(1)}) custom-call(f32[32,8,128]{2,1,0:T(8,128)S(1)} %copy-done.1, f32[32,8,128]{2,1,0:T(8,128)S(1)} %copy-done.2, f32[4,128,256]{2,1,0:T(8,128)S(1)} %get-tuple-element.77.field_ref, f32[4,128,256]{2,1,0:T(8,128)S(1)} %get-tuple-element.62.field_ref.old_ref, ...), custom_call_target="tpu_custom_call" | custom-call | bytes 5767168 | tf_op jit(solution)/shard_map/pallas_call | solution.py:355
  178.1 10.1 %all_to_all.36.later_ref = f32[32,8,128]{2,1,0:T(8,128)S(1)} all-to-all(f32[32,8,128]{2,1,0:T(8,128)S(1)} %get-tuple-element.83), channel_id=1, replica_groups=mesh['row'=8,'y'=2,'core'=2] {'row','y','core'}, dimensions={0} | all-to-all | bytes 262144 | tf_op jit(solution)/shard_map/all_to_all | solution.py:808
  188.2 2.0 %shard_map.141 = (f32[4,128,256]{2,1,0:T(8,128)}, f32[4,128,256]{2,1,0:T(8,128)}) custom-call(f32[32,8,128]{2,1,0:T(8,128)S(1)} %copy-done.2, f32[32,8,128]{2,1,0:T(8,128)S(1)} %all_to_all.36.later_ref, f32[4,128,256]{2,1,0:T(8,128)S(1)} %get-tuple-element.62.field_ref.old_ref, f32[4,128,256]{2,1,0:T(8,128)S(1)} %get-tuple-element.84.way_ref, ...), custom_call_target="tpu_custom_call" | custom-call | bytes 3145728 | tf_op jit(solution)/shard_map/pallas_call | solution.py:355
  (73 shorter events, 3.2 us)
Async XLA Ops:
  0.6 38.3 %copy-start.21 = (f32[16,17]{1,0:T(8,128)S(1)}, f32[16,17]{1,0:T(8,128)}, u32[]{:S(2)}) copy-start(f32[16,17]{1,0:T(8,128)} %param.14) | copy-start | bytes 3268
  2.3 44.7 %copy-start.11 = (f32[4,16,8,128]{3,2,1,0:T(8,128)}, f32[4,16,8,128]{3,2,1,0:T(8,128)S(1)}, u32[]{:S(2)}) copy-start(f32[4,16,8,128]{3,2,1,0:T(8,128)S(1)} %get-tuple-element.47.refs_0_) | copy-start | bytes 786436
  2.3 19.5 %collective-permute-start = (f32[4,16,8,128]{3,2,1,0:T(8,128)S(1)}, f32[4,16,8,128]{3,2,1,0:T(8,128)S(1)}, u32[]{:S(2)}, u32[]{:S(2)}) collective-permute-start(f32[4,16,8,128]{3,2,1,0:T(8,128)S(1)} %get-tuple-element.48), channel_id=1, source_target_pairs={{0,1},{1,2},{2,3},{3,0},{4,5},{5,6},{6,7},{7,4},{8,9},{9,10},{10,1... | collective-permute-start | bytes 786440 | tf_op jit(solution)/shard_map/ppermute | solution.py:869
  2.8 19.0 %collective-permute-start.1 = (f32[4,16,8,128]{3,2,1,0:T(8,128)S(1)}, f32[4,16,8,128]{3,2,1,0:T(8,128)S(1)}, u32[]{:S(2)}, u32[]{:S(2)}) collective-permute-start(f32[4,16,8,128]{3,2,1,0:T(8,128)S(1)} %get-tuple-element.49), channel_id=1, source_target_pairs={{0,2},{1,3},{2,0},{3,1},{4,6},{5,7},{6,4},{7,5},{8,10},{9,11},{10,... | collective-permute-start | bytes 786440 | tf_op jit(solution)/shard_map/ppermute | solution.py:869
  5.4 16.4 %collective-permute-start.2 = (f32[4,16,8,128]{3,2,1,0:T(8,128)S(1)}, f32[4,16,8,128]{3,2,1,0:T(8,128)S(1)}, u32[]{:S(2)}, u32[]{:S(2)}) collective-permute-start(f32[4,16,8,128]{3,2,1,0:T(8,128)S(1)} %get-tuple-element.50), channel_id=1, source_target_pairs={{0,3},{1,0},{2,1},{3,2},{4,7},{5,4},{6,5},{7,6},{8,11},{9,8},{10,9... | collective-permute-start | bytes 786440 | tf_op jit(solution)/shard_map/ppermute | solution.py:869
  8.7 13.1 %all-to-all-start = ((f32[32,8,128]{2,1,0:T(8,128)}), f32[32,8,128]{2,1,0:T(8,128)S(1)}, u32[]{:S(2)}, u32[]{:S(2)}) async-start(f32[32,8,128]{2,1,0:T(8,128)} %get-tuple-element.46), calls=%async_computation | async-start | bytes 262144 | tf_op jit(solution)/shard_map/all_to_all | solution.py:808
  21.8 0.7 copy-start
  21.8 25.2 %copy-start.12 = (f32[4,16,8,128]{3,2,1,0:T(8,128)}, f32[4,16,8,128]{3,2,1,0:T(8,128)S(1)}, u32[]{:S(2)}) copy-start(f32[4,16,8,128]{3,2,1,0:T(8,128)S(1)} %collective-permute-done.refs_1_) | copy-start | bytes 786436
  21.8 25.2 %copy-start.13 = (f32[4,16,8,128]{3,2,1,0:T(8,128)}, f32[4,16,8,128]{3,2,1,0:T(8,128)S(1)}, u32[]{:S(2)}) copy-start(f32[4,16,8,128]{3,2,1,0:T(8,128)S(1)} %collective-permute-done.1.refs_2_) | copy-start | bytes 786436
  21.8 25.2 %copy-start.14 = (f32[4,16,8,128]{3,2,1,0:T(8,128)}, f32[4,16,8,128]{3,2,1,0:T(8,128)S(1)}, u32[]{:S(2)}) copy-start(f32[4,16,8,128]{3,2,1,0:T(8,128)S(1)} %collective-permute-done.2.refs_3_) | copy-start | bytes 786436
  32.2 1.5 collective-permute-start.3
  34.4 14.7 %all-to-all-start.1 = ((f32[16,4,8,128]{3,2,1,0:T(8,128)}), f32[16,4,8,128]{3,2,1,0:T(8,128)S(1)}, u32[]{:S(2)}, u32[]{:S(2)}) async-start(f32[16,4,8,128]{3,2,1,0:T(8,128)} %shard_map.124._.__), calls=%async_computation.1 | async-start | bytes 524288 | tf_op jit(solution)/shard_map/all_to_all | solution.py:808
  53.8 19.3 %all-to-all-start.2 = ((f32[16,4,8,128]{3,2,1,0:T(8,128)}), f32[16,4,8,128]{3,2,1,0:T(8,128)S(1)}, u32[]{:S(2)}, u32[]{:S(2)}) async-start(f32[16,4,8,128]{3,2,1,0:T(8,128)} %shard_map.126.__), calls=%async_computation.2 | async-start | bytes 524288 | tf_op jit(solution)/shard_map/all_to_all | solution.py:808
  58.6 14.4 %collective-permute-start.6 = (f32[4,256]{1,0:T(4,128)S(1)}, f32[4,256]{1,0:T(4,128)S(1)}, u32[]{:S(2)}, u32[]{:S(2)}) collective-permute-start(f32[4,256]{1,0:T(4,128)S(1)} %get-tuple-element.56), channel_id=1, source_target_pairs={{0,1},{1,2},{2,3},{3,0},{4,5},{5,6},{6,7},{7,4},{8,9},{9,10},{10,1... | collective-permute-start | bytes 12296 | tf_op jit(solution)/shard_map/ppermute | solution.py:823
  58.7 14.4 %collective-permute-start.7 = (f32[4,256]{1,0:T(4,128)S(1)}, f32[4,256]{1,0:T(4,128)S(1)}, u32[]{:S(2)}, u32[]{:S(2)}) collective-permute-start(f32[4,256]{1,0:T(4,128)S(1)} %get-tuple-element.57), channel_id=1, source_target_pairs={{1,0},{2,1},{3,2},{0,3},{5,4},{6,5},{7,6},{4,7},{9,8},{10,9},{11,1... | collective-permute-start | bytes 12296 | tf_op jit(solution)/shard_map/ppermute | solution.py:823
  60.4 12.6 %collective-permute-start.4 = (f32[128,256]{1,0:T(8,128)S(1)}, f32[128,256]{1,0:T(8,128)S(1)}, u32[]{:S(2)}, u32[]{:S(2)}) collective-permute-start(f32[128,256]{1,0:T(8,128)S(1)} %get-tuple-element.54), channel_id=1, source_target_pairs={{0,4},{4,8},{8,12},{12,16},{16,20},{20,24},{24,28},{28,0},{1,5},{5... | collective-permute-start | bytes 393224 | tf_op jit(solution)/shard_map/ppermute | solution.py:823
  62.3 10.8 %collective-permute-start.5 = (f32[128,256]{1,0:T(8,128)S(1)}, f32[128,256]{1,0:T(8,128)S(1)}, u32[]{:S(2)}, u32[]{:S(2)}) collective-permute-start(f32[128,256]{1,0:T(8,128)S(1)} %get-tuple-element.55), channel_id=1, source_target_pairs={{4,0},{8,4},{12,8},{16,12},{20,16},{24,20},{28,24},{0,28},{5,1},{9... | collective-permute-start | bytes 393224 | tf_op jit(solution)/shard_map/ppermute | solution.py:823
  73.0 1.5 copy-start.22
  73.0 0.6 copy-start.15
  73.1 0.6 copy-start.17
  73.1 0.6 copy-start.7
  73.1 0.7 copy-start.9
  73.8 0.7 copy-start.20
  74.5 1.7 collective-permute-start.8
  74.5 20.9 %copy-start.3 = (bf16[4,128,256]{2,1,0:T(8,128)(2,1)S(1)}, bf16[4,128,256]{2,1,0:T(8,128)(2,1)}, u32[]{:S(2)}) copy-start(bf16[4,128,256]{2,1,0:T(8,128)(2,1)} %perm_ref.9) | copy-start | bytes 786436
  74.5 20.9 %copy-start.5 = (f32[4,128,256]{2,1,0:T(8,128)S(1)}, f32[4,128,256]{2,1,0:T(8,128)}, u32[]{:S(2)}) copy-start(f32[4,128,256]{2,1,0:T(8,128)} %res_ref.3) | copy-start | bytes 1572868
  74.5 20.9 %copy-start.8 = (f32[128,256]{1,0:T(8,128)S(1)}, f32[128,256]{1,0:T(8,128)}, u32[]{:S(2)}) copy-start(f32[128,256]{1,0:T(8,128)} %copy-done.7) | copy-start | bytes 393220
  74.5 20.9 %copy-start.10 = (f32[128,256]{1,0:T(8,128)S(1)}, f32[128,256]{1,0:T(8,128)}, u32[]{:S(2)}) copy-start(f32[128,256]{1,0:T(8,128)} %copy-done.9) | copy-start | bytes 393220
  74.5 20.9 %copy-start.16 = (f32[4,256]{1,0:T(4,128)S(1)}, f32[4,256]{1,0:T(4,128)}, u32[]{:S(2)}) copy-start(f32[4,256]{1,0:T(4,128)} %copy-done.15) | copy-start | bytes 12292
  74.6 20.9 %copy-start.18 = (f32[4,256]{1,0:T(4,128)S(1)}, f32[4,256]{1,0:T(4,128)}, u32[]{:S(2)}) copy-start(f32[4,256]{1,0:T(4,128)} %copy-done.17) | copy-start | bytes 12292
  81.9 13.5 %collective-permute-start.9 = (f32[128,256]{1,0:T(8,128)S(1)}, f32[128,256]{1,0:T(8,128)S(1)}, u32[]{:S(2)}, u32[]{:S(2)}) collective-permute-start(f32[128,256]{1,0:T(8,128)S(1)} %get-tuple-element.63), channel_id=1, source_target_pairs={{0,4},{4,8},{8,12},{12,16},{16,20},{20,24},{24,28},{28,0},{1,5},{5... | collective-permute-start | bytes 393224 | tf_op jit(solution)/shard_map/ppermute | solution.py:823
  81.9 13.5 %collective-permute-start.10 = (f32[128,256]{1,0:T(8,128)S(1)}, f32[128,256]{1,0:T(8,128)S(1)}, u32[]{:S(2)}, u32[]{:S(2)}) collective-permute-start(f32[128,256]{1,0:T(8,128)S(1)} %get-tuple-element.64), channel_id=1, source_target_pairs={{4,0},{8,4},{12,8},{16,12},{20,16},{24,20},{28,24},{0,28},{5,1},{9... | collective-permute-start | bytes 393224 | tf_op jit(solution)/shard_map/ppermute | solution.py:823
  92.3 3.0 %collective-permute-start.11 = (f32[4,256]{1,0:T(4,128)S(1)}, f32[4,256]{1,0:T(4,128)S(1)}, u32[]{:S(2)}, u32[]{:S(2)}) collective-permute-start(f32[4,256]{1,0:T(4,128)S(1)} %get-tuple-element.65), channel_id=1, source_target_pairs={{0,1},{1,2},{2,3},{3,0},{4,5},{5,6},{6,7},{7,4},{8,9},{9,10},{10,1... | collective-permute-start | bytes 12296 | tf_op jit(solution)/shard_map/ppermute | solution.py:823
  92.3 3.1 %collective-permute-start.12 = (f32[4,256]{1,0:T(4,128)S(1)}, f32[4,256]{1,0:T(4,128)S(1)}, u32[]{:S(2)}, u32[]{:S(2)}) collective-permute-start(f32[4,256]{1,0:T(4,128)S(1)} %get-tuple-element.66), channel_id=1, source_target_pairs={{1,0},{2,1},{3,2},{0,3},{5,4},{6,5},{7,6},{4,7},{9,8},{10,9},{11,1... | collective-permute-start | bytes 12296 | tf_op jit(solution)/shard_map/ppermute | solution.py:823
  118.0 1.5 collective-permute-start.13
  120.3 14.2 %all-to-all-start.4 = ((f32[16,4,8,128]{3,2,1,0:T(8,128)}), f32[16,4,8,128]{3,2,1,0:T(8,128)S(1)}, u32[]{:S(2)}, u32[]{:S(2)}) async-start(f32[16,4,8,128]{3,2,1,0:T(8,128)} %shard_map.133._.__), calls=%async_computation.4 | async-start | bytes 524288 | tf_op jit(solution)/shard_map/all_to_all | solution.py:808
  139.2 14.4 %all-to-all-start.5 = ((f32[16,4,8,128]{3,2,1,0:T(8,128)}), f32[16,4,8,128]{3,2,1,0:T(8,128)S(1)}, u32[]{:S(2)}, u32[]{:S(2)}) async-start(f32[16,4,8,128]{3,2,1,0:T(8,128)} %shard_map.135.__), calls=%async_computation.5 | async-start | bytes 524288 | tf_op jit(solution)/shard_map/all_to_all | solution.py:808
  153.6 0.7 copy-start.19
  154.3 1.7 collective-permute-start.14
  156.0 19.8 %copy-start.1 = (f32[32,8,128]{2,1,0:T(8,128)S(1)}, f32[32,8,128]{2,1,0:T(8,128)}, u32[]{:S(2)}) copy-start(f32[32,8,128]{2,1,0:T(8,128)} %copy-done) | copy-start | bytes 393220
  156.0 19.8 %copy-start.2 = (f32[32,8,128]{2,1,0:T(8,128)S(1)}, f32[32,8,128]{2,1,0:T(8,128)}, u32[]{:S(2)}) copy-start(f32[32,8,128]{2,1,0:T(8,128)} %all_to_all.35.sums_ref.refs_1_) | copy-start | bytes 393220
  156.0 19.8 %copy-start.4 = (bf16[4,128,256]{2,1,0:T(8,128)(2,1)S(1)}, bf16[4,128,256]{2,1,0:T(8,128)(2,1)}, u32[]{:S(2)}) copy-start(bf16[4,128,256]{2,1,0:T(8,128)(2,1)} %perm_ref.9) | copy-start | bytes 786436
  156.0 19.8 %copy-start.6 = (f32[4,128,256]{2,1,0:T(8,128)S(1)}, f32[4,128,256]{2,1,0:T(8,128)}, u32[]{:S(2)}) copy-start(f32[4,128,256]{2,1,0:T(8,128)} %get-tuple-element.82.refs_12_.res_ref) | copy-start | bytes 1572868
  162.3 13.5 %collective-permute-start.15 = (f32[128,256]{1,0:T(8,128)S(1)}, f32[128,256]{1,0:T(8,128)S(1)}, u32[]{:S(2)}, u32[]{:S(2)}) collective-permute-start(f32[128,256]{1,0:T(8,128)S(1)} %get-tuple-element.78), channel_id=1, source_target_pairs={{0,4},{4,8},{8,12},{12,16},{16,20},{20,24},{24,28},{28,0},{1,5},{5... | collective-permute-start | bytes 393224 | tf_op jit(solution)/shard_map/ppermute | solution.py:823
  163.4 12.5 %collective-permute-start.16 = (f32[128,256]{1,0:T(8,128)S(1)}, f32[128,256]{1,0:T(8,128)S(1)}, u32[]{:S(2)}, u32[]{:S(2)}) collective-permute-start(f32[128,256]{1,0:T(8,128)S(1)} %get-tuple-element.79), channel_id=1, source_target_pairs={{4,0},{8,4},{12,8},{16,12},{20,16},{24,20},{28,24},{0,28},{5,1},{9... | collective-permute-start | bytes 393224 | tf_op jit(solution)/shard_map/ppermute | solution.py:823
  172.7 3.0 %collective-permute-start.17 = (f32[4,256]{1,0:T(4,128)S(1)}, f32[4,256]{1,0:T(4,128)S(1)}, u32[]{:S(2)}, u32[]{:S(2)}) collective-permute-start(f32[4,256]{1,0:T(4,128)S(1)} %get-tuple-element.80), channel_id=1, source_target_pairs={{0,1},{1,2},{2,3},{3,0},{4,5},{5,6},{6,7},{7,4},{8,9},{9,10},{10,1... | collective-permute-start | bytes 12296 | tf_op jit(solution)/shard_map/ppermute | solution.py:823
  172.7 3.1 %collective-permute-start.18 = (f32[4,256]{1,0:T(4,128)S(1)}, f32[4,256]{1,0:T(4,128)S(1)}, u32[]{:S(2)}, u32[]{:S(2)}) collective-permute-start(f32[4,256]{1,0:T(4,128)S(1)} %get-tuple-element.81), channel_id=1, source_target_pairs={{1,0},{2,1},{3,2},{0,3},{5,4},{6,5},{7,6},{4,7},{9,8},{10,9},{11,1... | collective-permute-start | bytes 12296 | tf_op jit(solution)/shard_map/ppermute | solution.py:823

commit v12 on v11

--- a/solution.py
+++ b/solution.py
@@ -486,8 +486,8 @@
 
 
 def point_body(mix_ref, lifted_ref, _, __, point_ref):
-    size = 8 * SUBLANES
-    group = 4
+    size = 16 * SUBLANES
+    group = 2
 
     def step(index, carry):
         lines = pl.ds(pl.multiple_of(index * size, size), size)

time: 191 us -> 189 us (0.990)
  transfers between devices with their start and end apart: 24 -> 24, of which waited for: 10 -> 10; matrix products, arithmetic and copies ran while one was open for 0% -> 0% of each run, Pallas kernels for 24% -> 23%
where the time goes in v12:
time: 189 us
  Pallas kernels  93.5 us (49%)
  starting transfers between devices  45.7 us (24%)
  waiting for transfers between devices  24.3 us (13%)
  blocking collectives  20.7 us (11%)
  local copies, waits for them, and re-layouts  2.77 us (1%)
    pallas_call x19, Pallas kernels, wrapped(): found = run(*held)  93.5 us
    all_to_all x5, starting transfers between devices, exchange(): return lax.all_to_all(blocks, axes, split_axis=0, concat_axis=0, tiled=True)  21.3 us
    all_to_all x2, blocking collectives, exchange(): return lax.all_to_all(blocks, axes, split_axis=0, concat_axis=0, tiled=True)  20.7 us
    ppermute x6, starting transfers between devices, shift_planes(): lax.ppermute(first, axis, backward)  16.4 us
    all_to_all x5, waiting for transfers between devices, exchange(): return lax.all_to_all(blocks, axes, split_axis=0, concat_axis=0, tiled=True)  15.5 us
    ppermute x4, waiting for transfers between devices, swap(): return lax.ppermute(blocks, 'core', [(0, 1), (1, 0)])  6.05 us
    ppermute x3, starting transfers between devices, tiled_local(): lax.ppermute(part, COL, [(i, (i + shift + 1) % n_col) for i in range(n_co...  4.5 us
  transfers between devices with their start and end apart: 24, of which 10 were waited for; matrix products, arithmetic and copies ran while one was open for 0% of the time, Pallas kernels for 23%

profile of v12, /device:TPU:0, one launch (start us, length us, event | category | flops | bytes accessed | tf_op | source)
XLA Modules:
  0.0 188.7 jit_solution(15677696002005754972)
XLA Ops:
  0.6 1.7 shard_map.122
  2.8 2.6 %collective-permute-start.1 = (f32[4,16,8,128]{3,2,1,0:T(8,128)S(1)}, f32[4,16,8,128]{3,2,1,0:T(8,128)S(1)}, u32[]{:S(2)}, u32[]{:S(2)}) collective-permute-start(f32[4,16,8,128]{3,2,1,0:T(8,128)S(1)} %get-tuple-element.49), channel_id=1, source_target_pairs={{0,2},{1,3},{2,0},{3,1},{4,6},{5,7},{6,4},{7,5},{8,10},{9,11},{10,... | collective-permute-start | bytes 786440 | tf_op jit(solution)/shard_map/ppermute | solution.py:869
  5.4 1.4 collective-permute-start.2
  6.8 1.8 shard_map.121
  8.7 4.9 %all-to-all-start = ((f32[32,8,128]{2,1,0:T(8,128)}), f32[32,8,128]{2,1,0:T(8,128)S(1)}, u32[]{:S(2)}, u32[]{:S(2)}) async-start(f32[32,8,128]{2,1,0:T(8,128)} %get-tuple-element.46), calls=%async_computation | async-start | bytes 262144 | tf_op jit(solution)/shard_map/all_to_all | solution.py:808
  14.2 7.5 %all-to-all-done.sums_ref.refs_0_.first_ref = f32[32,8,128]{2,1,0:T(8,128)S(1)} async-done(((f32[32,8,128]{2,1,0:T(8,128)}), f32[32,8,128]{2,1,0:T(8,128)S(1)}, u32[]{:S(2)}, u32[]{:S(2)}) %all-to-all-start) | async-done | bytes 131104 | tf_op jit(solution)/shard_map/all_to_all | solution.py:808
  22.4 9.7 %shard_map.123 = (f32[16,4,8,128]{3,2,1,0:T(8,128)S(1)}, f32[16,4,8,128]{3,2,1,0:T(8,128)S(1)}, f32[4,16,256,128]{3,2,1,0:T(8,128)}) custom-call(f32[3,16]{1,0:T(4,128)S(1)} %multiply_bitcast_fusion.lift_ref, f32[32,8,128]{2,1,0:T(8,128)} %copy-done, f32[4,128,256]{2,1,0:T(8,128)} %res_ref.3, bf16[4,128,256]{2,1,0:T(8,128)(2,1)} %perm_ref.9, ...), custom_call_target="tpu_custom_call" | custom-call | flops 2000000000 | bytes 1310720 | tf_op jit(solution)/shard_map/pallas_call | solution.py:355
  32.4 1.3 collective-permute-done.3.partner_ref
  33.7 0.7 shard_map.124._.__
  34.4 4.5 %all-to-all-start.1 = ((f32[16,4,8,128]{3,2,1,0:T(8,128)}), f32[16,4,8,128]{3,2,1,0:T(8,128)S(1)}, u32[]{:S(2)}, u32[]{:S(2)}) async-start(f32[16,4,8,128]{3,2,1,0:T(8,128)} %shard_map.124._.__), calls=%async_computation.1 | async-start | bytes 524288 | tf_op jit(solution)/shard_map/all_to_all | solution.py:808
  39.0 7.6 %shard_map.125.refs_4_._ = f32[4,16,256,128]{3,2,1,0:T(8,128)} custom-call(f32[16,17]{1,0:T(8,128)S(1)} %broadcast_multiply_fusion.mix_ref, f32[4,16,256,128]{3,2,1,0:T(8,128)} %get-tuple-element.53.lifted_ref, f32[16,4,8,128]{3,2,1,0:T(8,128)} %shard_map.124._.__, f32[16,4,8,128]{3,2,1,0:T(8,128)} %shard_map.124._.__), custom_call_target="tpu_custom_call" | custom-call | flops 2500000000 | bytes 8388608 | tf_op jit(solution)/shard_map/pallas_call | solution.py:355
  46.6 2.5 %all-to-all-done.1.recv_ref = f32[16,4,8,128]{3,2,1,0:T(8,128)S(1)} async-done(((f32[16,4,8,128]{3,2,1,0:T(8,128)}), f32[16,4,8,128]{3,2,1,0:T(8,128)S(1)}, u32[]{:S(2)}, u32[]{:S(2)}) %all-to-all-start.1) | async-done | bytes 262176 | tf_op jit(solution)/shard_map/all_to_all | solution.py:808
  49.1 4.7 %shard_map.126.__ = f32[16,4,8,128]{3,2,1,0:T(8,128)} custom-call(f32[16,4,8,128]{3,2,1,0:T(8,128)S(1)} %all-to-all-done.1.recv_ref, f32[4,16,8,128]{3,2,1,0:T(8,128)} %copy-done.11, f32[4,16,8,128]{3,2,1,0:T(8,128)} %copy-done.12, f32[4,16,8,128]{3,2,1,0:T(8,128)} %copy-done.13, f32[4,16,8,128]{3,2,1,0:T(8,128)} %copy-done.14, ...), custom_call_target="tpu_custom_call" | custom-call | bytes 1572864 | tf_op jit(solution)/shard_map/pallas_call | solution.py:355
  53.8 4.4 %all-to-all-start.2 = ((f32[16,4,8,128]{3,2,1,0:T(8,128)}), f32[16,4,8,128]{3,2,1,0:T(8,128)S(1)}, u32[]{:S(2)}, u32[]{:S(2)}) async-start(f32[16,4,8,128]{3,2,1,0:T(8,128)} %shard_map.126.__), calls=%async_computation.2 | async-start | bytes 524288 | tf_op jit(solution)/shard_map/all_to_all | solution.py:808
  58.2 1.7 collective-permute-start.7
  60.0 1.9 collective-permute-start.4
  61.8 2.8 %collective-permute-start.5 = (f32[128,256]{1,0:T(8,128)S(1)}, f32[128,256]{1,0:T(8,128)S(1)}, u32[]{:S(2)}, u32[]{:S(2)}) collective-permute-start(f32[128,256]{1,0:T(8,128)S(1)} %get-tuple-element.55), channel_id=1, source_target_pairs={{4,0},{8,4},{12,8},{16,12},{20,16},{24,20},{28,24},{0,28},{5,1},{9... | collective-permute-start | bytes 393224 | tf_op jit(solution)/shard_map/ppermute | solution.py:823
  64.7 7.4 %shard_map.127.__1_.refs_3_ = f32[4,16,256,128]{3,2,1,0:T(8,128)} custom-call(f32[16,17]{1,0:T(8,128)S(1)} %broadcast_multiply_fusion.mix_ref, f32[4,16,256,128]{3,2,1,0:T(8,128)} %get-tuple-element.53.lifted_ref, f32[4,16,256,128]{3,2,1,0:T(8,128)} %shard_map.125.refs_4_._, f32[16,4,8,128]{3,2,1,0:T(8,128)} %shard_map.126.__), custom_call_target="tpu_custom_call", output_to_operand_aliasing={{}: (2, {})} | custom-call | flops 2500000000 | bytes 8388608 | tf_op jit(solution)/shard_map/pallas_call | solution.py:355
  72.9 0.7 copy-done.20
  73.7 1.7 collective-permute-done.8.refs_2_
  75.3 5.7 %shard_map.129 = (f32[2,4,128,256]{3,2,1,0:T(8,128)}, f32[4,128,256]{2,1,0:T(8,128)S(1)}, f32[128,256]{1,0:T(8,128)S(1)}, f32[128,256]{1,0:T(8,128)S(1)}, f32[4,256]{1,0:T(4,128)S(1)}, /*index=5*/f32[4,256]{1,0:T(4,128)S(1)}) custom-call(f32[17]{0:T(128)S(1)} %fusion.proj_ref, f32[32,8,128]{2,1,0:T(8,128)} %copy-done, f32[16,4,8,128]{3,2,1,0:T(8,128)} %shard_map.128.refs_1_, ...), custom_call_target="tpu_custom_call" | custom-call | flops 1000000000 | bytes 4718592 | tf_op jit(solution)/shard_map/pallas_call | solution.py:355
  81.0 4.7 %collective-permute-start.10 = (f32[128,256]{1,0:T(8,128)S(1)}, f32[128,256]{1,0:T(8,128)S(1)}, u32[]{:S(2)}, u32[]{:S(2)}) collective-permute-start(f32[128,256]{1,0:T(8,128)S(1)} %get-tuple-element.64), channel_id=1, source_target_pairs={{4,0},{8,4},{12,8},{16,12},{20,16},{24,20},{28,24},{0,28},{5,1},{9... | collective-permute-start | bytes 393224 | tf_op jit(solution)/shard_map/ppermute | solution.py:823
  85.7 5.7 %shard_map.130 = (f32[2,4,128,256]{3,2,1,0:T(8,128)}, f32[4,128,256]{2,1,0:T(8,128)S(1)}, f32[4,256]{1,0:T(4,128)S(1)}, f32[4,256]{1,0:T(4,128)S(1)}) custom-call(f32[17]{0:T(128)S(1)} %fusion.proj_ref, f32[32,8,128]{2,1,0:T(8,128)} %copy-done, f32[16,4,8,128]{3,2,1,0:T(8,128)} %shard_map.128.refs_1_, ...), custom_call_target="tpu_custom_call", output_to_operand_aliasing={{0}: (7, {}), {1}: (8, {})} | custom-call | flops 1000000000 | bytes 4718592 | tf_op jit(solution)/shard_map/pallas_call | solution.py:355
  91.4 1.7 collective-permute-start.12
  93.2 1.3 collective-permute-done.11.refs_2_.refs_6_
  94.6 1.9 %shard_map.131 = (f32[4,128,256]{2,1,0:T(8,128)S(1)}, f32[32,8,128]{2,1,0:T(8,128)S(1)}) custom-call(f32[4,128,256]{2,1,0:T(8,128)S(1)} %get-tuple-element.62.field_ref.old_ref, bf16[4,128,256]{2,1,0:T(8,128)(2,1)S(1)} %copy-done.3, f32[128,256]{1,0:T(8,128)S(1)} %collective-permute-done.9.refs_0_.refs_4_, ...), custom_call_target="tpu_custom_call" | custom-call | bytes 4718592 | tf_op jit(solution)/shard_map/pallas_call | solution.py:355
  96.5 10.6 %all_to_all.35.sums_ref.refs_1_ = f32[32,8,128]{2,1,0:T(8,128)} all-to-all(f32[32,8,128]{2,1,0:T(8,128)S(1)} %get-tuple-element.67), channel_id=1, replica_groups=mesh['row'=8,'y'=2,'core'=2] {'row','y','core'}, dimensions={0} | all-to-all | bytes 262144 | tf_op jit(solution)/shard_map/all_to_all | solution.py:808
  107.1 10.0 %shard_map.132 = (f32[16,4,8,128]{3,2,1,0:T(8,128)S(1)}, f32[16,4,8,128]{3,2,1,0:T(8,128)S(1)}, f32[4,16,256,128]{3,2,1,0:T(8,128)}, f32[4,128,256]{2,1,0:T(8,128)}) custom-call(f32[3,16]{1,0:T(4,128)S(1)} %multiply_bitcast_fusion.lift_ref, f32[32,8,128]{2,1,0:T(8,128)} %copy-done, f32[32,8,128]{2,1,0:T(8,128)} %all_to_all.35.sums_ref.refs_1_, ...), custom_call_target="tpu_custom_call" | custom-call | flops 2000000000 | bytes 2359296 | tf_op jit(solution)/shard_map/pallas_call | solution.py:355
  117.3 1.3 collective-permute-done.13.partner_ref
  118.6 0.7 shard_map.133._.__
  119.4 3.5 %all-to-all-start.4 = ((f32[16,4,8,128]{3,2,1,0:T(8,128)}), f32[16,4,8,128]{3,2,1,0:T(8,128)S(1)}, u32[]{:S(2)}, u32[]{:S(2)}) async-start(f32[16,4,8,128]{3,2,1,0:T(8,128)} %shard_map.133._.__), calls=%async_computation.4 | async-start | bytes 524288 | tf_op jit(solution)/shard_map/all_to_all | solution.py:808
  122.9 7.6 %shard_map.134.refs_4_._ = f32[4,16,256,128]{3,2,1,0:T(8,128)} custom-call(f32[16,17]{1,0:T(8,128)S(1)} %broadcast_multiply_fusion.mix_ref, f32[4,16,256,128]{3,2,1,0:T(8,128)} %get-tuple-element.71.lifted_ref, f32[16,4,8,128]{3,2,1,0:T(8,128)} %shard_map.133._.__, f32[16,4,8,128]{3,2,1,0:T(8,128)} %shard_map.133._.__), custom_call_target="tpu_custom_call" | custom-call | flops 2500000000 | bytes 8388608 | tf_op jit(solution)/shard_map/pallas_call | solution.py:355
  130.5 2.9 %all-to-all-done.4.recv_ref = f32[16,4,8,128]{3,2,1,0:T(8,128)S(1)} async-done(((f32[16,4,8,128]{3,2,1,0:T(8,128)}), f32[16,4,8,128]{3,2,1,0:T(8,128)S(1)}, u32[]{:S(2)}, u32[]{:S(2)}) %all-to-all-start.4) | async-done | bytes 262176 | tf_op jit(solution)/shard_map/all_to_all | solution.py:808
  133.4 4.7 %shard_map.135.__ = f32[16,4,8,128]{3,2,1,0:T(8,128)} custom-call(f32[16,4,8,128]{3,2,1,0:T(8,128)S(1)} %all-to-all-done.4.recv_ref, f32[4,16,8,128]{3,2,1,0:T(8,128)} %copy-done.11, f32[4,16,8,128]{3,2,1,0:T(8,128)} %copy-done.12, f32[4,16,8,128]{3,2,1,0:T(8,128)} %copy-done.13, f32[4,16,8,128]{3,2,1,0:T(8,128)} %copy-done.14, ...), custom_call_target="tpu_custom_call" | custom-call | bytes 1572864 | tf_op jit(solution)/shard_map/pallas_call | solution.py:355
  138.1 4.0 %all-to-all-start.5 = ((f32[16,4,8,128]{3,2,1,0:T(8,128)}), f32[16,4,8,128]{3,2,1,0:T(8,128)S(1)}, u32[]{:S(2)}, u32[]{:S(2)}) async-start(f32[16,4,8,128]{3,2,1,0:T(8,128)} %shard_map.135.__), calls=%async_computation.5 | async-start | bytes 524288 | tf_op jit(solution)/shard_map/all_to_all | solution.py:808
  142.1 7.5 %shard_map.136.__1_.refs_4_ = f32[4,16,256,128]{3,2,1,0:T(8,128)} custom-call(f32[16,17]{1,0:T(8,128)S(1)} %broadcast_multiply_fusion.mix_ref, f32[4,16,256,128]{3,2,1,0:T(8,128)} %get-tuple-element.71.lifted_ref, f32[4,16,256,128]{3,2,1,0:T(8,128)} %shard_map.134.refs_4_._, f32[16,4,8,128]{3,2,1,0:T(8,128)} %shard_map.135.__), custom_call_target="tpu_custom_call", output_to_operand_aliasing={{}: (2, {})} | custom-call | flops 2500000000 | bytes 8388608 | tf_op jit(solution)/shard_map/pallas_call | solution.py:355
  149.5 2.5 %all-to-all-done.5.__0_ = f32[16,4,8,128]{3,2,1,0:T(8,128)S(1)} async-done(((f32[16,4,8,128]{3,2,1,0:T(8,128)}), f32[16,4,8,128]{3,2,1,0:T(8,128)S(1)}, u32[]{:S(2)}, u32[]{:S(2)}) %all-to-all-start.5) | async-done | bytes 262176 | tf_op jit(solution)/shard_map/all_to_all | solution.py:808
  152.0 0.7 copy-done.19
  152.7 1.7 collective-permute-done.14.refs_3_
  154.5 6.3 %shard_map.138 = (f32[2,4,128,256]{3,2,1,0:T(8,128)}, f32[4,128,256]{2,1,0:T(8,128)S(1)}, f32[128,256]{1,0:T(8,128)S(1)}, f32[128,256]{1,0:T(8,128)S(1)}, f32[4,256]{1,0:T(4,128)S(1)}, /*index=5*/f32[4,256]{1,0:T(4,128)S(1)}) custom-call(f32[17]{0:T(128)S(1)} %fusion.proj_ref, f32[32,8,128]{2,1,0:T(8,128)} %copy-done, ...), custom_call_target="tpu_custom_call", output_to_operand_aliasing={{0}: (8, {})} | custom-call | flops 1000000000 | bytes 4718592 | tf_op jit(solution)/shard_map/pallas_call | solution.py:355
  160.8 1.1 collective-permute-start.15
  161.8 3.7 %collective-permute-start.16 = (f32[128,256]{1,0:T(8,128)S(1)}, f32[128,256]{1,0:T(8,128)S(1)}, u32[]{:S(2)}, u32[]{:S(2)}) collective-permute-start(f32[128,256]{1,0:T(8,128)S(1)} %get-tuple-element.79), channel_id=1, source_target_pairs={{4,0},{8,4},{12,8},{16,12},{20,16},{24,20},{28,24},{0,28},{5,1},{9... | collective-permute-start | bytes 393224 | tf_op jit(solution)/shard_map/ppermute | solution.py:823
  165.5 5.7 %shard_map.139 = (f32[2,4,128,256]{3,2,1,0:T(8,128)}, f32[4,128,256]{2,1,0:T(8,128)S(1)}, f32[4,256]{1,0:T(4,128)S(1)}, f32[4,256]{1,0:T(4,128)S(1)}) custom-call(f32[17]{0:T(128)S(1)} %fusion.proj_ref, f32[32,8,128]{2,1,0:T(8,128)} %copy-done, f32[32,8,128]{2,1,0:T(8,128)} %all_to_all.35.sums_ref.refs_1_, ...), custom_call_target="tpu_custom_call", output_to_operand_aliasing={{0}: (8, {}), {1}: (9, {})} | custom-call | flops 1000000000 | bytes 4718592 | tf_op jit(solution)/shard_map/pallas_call | solution.py:355
  171.2 1.7 collective-permute-start.18
  173.0 1.3 collective-permute-done.17.refs_2_
  174.3 2.3 %shard_map.140 = (f32[4,128,256]{2,1,0:T(8,128)S(1)}, f32[4,128,256]{2,1,0:T(8,128)S(1)}, f32[32,8,128]{2,1,0:T(8,128)S(1)}) custom-call(f32[32,8,128]{2,1,0:T(8,128)S(1)} %copy-done.1, f32[32,8,128]{2,1,0:T(8,128)S(1)} %copy-done.2, f32[4,128,256]{2,1,0:T(8,128)S(1)} %get-tuple-element.77.field_ref, f32[4,128,256]{2,1,0:T(8,128)S(1)} %get-tuple-element.62.field_ref.old_ref, ...), custom_call_target="tpu_custom_call" | custom-call | bytes 5767168 | tf_op jit(solution)/shard_map/pallas_call | solution.py:355
  176.6 10.1 %all_to_all.36.later_ref = f32[32,8,128]{2,1,0:T(8,128)S(1)} all-to-all(f32[32,8,128]{2,1,0:T(8,128)S(1)} %get-tuple-element.83), channel_id=1, replica_groups=mesh['row'=8,'y'=2,'core'=2] {'row','y','core'}, dimensions={0} | all-to-all | bytes 262144 | tf_op jit(solution)/shard_map/all_to_all | solution.py:808
  186.7 2.0 %shard_map.141 = (f32[4,128,256]{2,1,0:T(8,128)}, f32[4,128,256]{2,1,0:T(8,128)}) custom-call(f32[32,8,128]{2,1,0:T(8,128)S(1)} %copy-done.2, f32[32,8,128]{2,1,0:T(8,128)S(1)} %all_to_all.36.later_ref, f32[4,128,256]{2,1,0:T(8,128)S(1)} %get-tuple-element.62.field_ref.old_ref, f32[4,128,256]{2,1,0:T(8,128)S(1)} %get-tuple-element.84.way_ref, ...), custom_call_target="tpu_custom_call" | custom-call | bytes 3145728 | tf_op jit(solution)/shard_map/pallas_call | solution.py:355
  (73 shorter events, 3.2 us)
Async XLA Ops:
  0.6 38.3 %copy-start.21 = (f32[16,17]{1,0:T(8,128)S(1)}, f32[16,17]{1,0:T(8,128)}, u32[]{:S(2)}) copy-start(f32[16,17]{1,0:T(8,128)} %param.14) | copy-start | bytes 3268
  2.3 44.2 %copy-start.11 = (f32[4,16,8,128]{3,2,1,0:T(8,128)}, f32[4,16,8,128]{3,2,1,0:T(8,128)S(1)}, u32[]{:S(2)}) copy-start(f32[4,16,8,128]{3,2,1,0:T(8,128)S(1)} %get-tuple-element.47.refs_0_) | copy-start | bytes 786436
  2.3 19.5 %collective-permute-start = (f32[4,16,8,128]{3,2,1,0:T(8,128)S(1)}, f32[4,16,8,128]{3,2,1,0:T(8,128)S(1)}, u32[]{:S(2)}, u32[]{:S(2)}) collective-permute-start(f32[4,16,8,128]{3,2,1,0:T(8,128)S(1)} %get-tuple-element.48), channel_id=1, source_target_pairs={{0,1},{1,2},{2,3},{3,0},{4,5},{5,6},{6,7},{7,4},{8,9},{9,10},{10,1... | collective-permute-start | bytes 786440 | tf_op jit(solution)/shard_map/ppermute | solution.py:869
  2.8 19.0 %collective-permute-start.1 = (f32[4,16,8,128]{3,2,1,0:T(8,128)S(1)}, f32[4,16,8,128]{3,2,1,0:T(8,128)S(1)}, u32[]{:S(2)}, u32[]{:S(2)}) collective-permute-start(f32[4,16,8,128]{3,2,1,0:T(8,128)S(1)} %get-tuple-element.49), channel_id=1, source_target_pairs={{0,2},{1,3},{2,0},{3,1},{4,6},{5,7},{6,4},{7,5},{8,10},{9,11},{10,... | collective-permute-start | bytes 786440 | tf_op jit(solution)/shard_map/ppermute | solution.py:869
  5.4 16.4 %collective-permute-start.2 = (f32[4,16,8,128]{3,2,1,0:T(8,128)S(1)}, f32[4,16,8,128]{3,2,1,0:T(8,128)S(1)}, u32[]{:S(2)}, u32[]{:S(2)}) collective-permute-start(f32[4,16,8,128]{3,2,1,0:T(8,128)S(1)} %get-tuple-element.50), channel_id=1, source_target_pairs={{0,3},{1,0},{2,1},{3,2},{4,7},{5,4},{6,5},{7,6},{8,11},{9,8},{10,9... | collective-permute-start | bytes 786440 | tf_op jit(solution)/shard_map/ppermute | solution.py:869
  8.7 13.1 %all-to-all-start = ((f32[32,8,128]{2,1,0:T(8,128)}), f32[32,8,128]{2,1,0:T(8,128)S(1)}, u32[]{:S(2)}, u32[]{:S(2)}) async-start(f32[32,8,128]{2,1,0:T(8,128)} %get-tuple-element.46), calls=%async_computation | async-start | bytes 262144 | tf_op jit(solution)/shard_map/all_to_all | solution.py:808
  21.8 0.7 copy-start
  21.8 24.7 %copy-start.12 = (f32[4,16,8,128]{3,2,1,0:T(8,128)}, f32[4,16,8,128]{3,2,1,0:T(8,128)S(1)}, u32[]{:S(2)}) copy-start(f32[4,16,8,128]{3,2,1,0:T(8,128)S(1)} %collective-permute-done.refs_1_) | copy-start | bytes 786436
  21.8 24.7 %copy-start.13 = (f32[4,16,8,128]{3,2,1,0:T(8,128)}, f32[4,16,8,128]{3,2,1,0:T(8,128)S(1)}, u32[]{:S(2)}) copy-start(f32[4,16,8,128]{3,2,1,0:T(8,128)S(1)} %collective-permute-done.1.refs_2_) | copy-start | bytes 786436
  21.8 24.7 %copy-start.14 = (f32[4,16,8,128]{3,2,1,0:T(8,128)}, f32[4,16,8,128]{3,2,1,0:T(8,128)S(1)}, u32[]{:S(2)}) copy-start(f32[4,16,8,128]{3,2,1,0:T(8,128)S(1)} %collective-permute-done.2.refs_3_) | copy-start | bytes 786436
  32.2 1.5 collective-permute-start.3
  34.4 14.7 %all-to-all-start.1 = ((f32[16,4,8,128]{3,2,1,0:T(8,128)}), f32[16,4,8,128]{3,2,1,0:T(8,128)S(1)}, u32[]{:S(2)}, u32[]{:S(2)}) async-start(f32[16,4,8,128]{3,2,1,0:T(8,128)} %shard_map.124._.__), calls=%async_computation.1 | async-start | bytes 524288 | tf_op jit(solution)/shard_map/all_to_all | solution.py:808
  53.8 18.4 %all-to-all-start.2 = ((f32[16,4,8,128]{3,2,1,0:T(8,128)}), f32[16,4,8,128]{3,2,1,0:T(8,128)S(1)}, u32[]{:S(2)}, u32[]{:S(2)}) async-start(f32[16,4,8,128]{3,2,1,0:T(8,128)} %shard_map.126.__), calls=%async_computation.2 | async-start | bytes 524288 | tf_op jit(solution)/shard_map/all_to_all | solution.py:808
  58.2 14.0 %collective-permute-start.6 = (f32[4,256]{1,0:T(4,128)S(1)}, f32[4,256]{1,0:T(4,128)S(1)}, u32[]{:S(2)}, u32[]{:S(2)}) collective-permute-start(f32[4,256]{1,0:T(4,128)S(1)} %get-tuple-element.56), channel_id=1, source_target_pairs={{0,1},{1,2},{2,3},{3,0},{4,5},{5,6},{6,7},{7,4},{8,9},{9,10},{10,1... | collective-permute-start | bytes 12296 | tf_op jit(solution)/shard_map/ppermute | solution.py:823
  58.2 13.9 %collective-permute-start.7 = (f32[4,256]{1,0:T(4,128)S(1)}, f32[4,256]{1,0:T(4,128)S(1)}, u32[]{:S(2)}, u32[]{:S(2)}) collective-permute-start(f32[4,256]{1,0:T(4,128)S(1)} %get-tuple-element.57), channel_id=1, source_target_pairs={{1,0},{2,1},{3,2},{0,3},{5,4},{6,5},{7,6},{4,7},{9,8},{10,9},{11,1... | collective-permute-start | bytes 12296 | tf_op jit(solution)/shard_map/ppermute | solution.py:823
  60.0 12.2 %collective-permute-start.4 = (f32[128,256]{1,0:T(8,128)S(1)}, f32[128,256]{1,0:T(8,128)S(1)}, u32[]{:S(2)}, u32[]{:S(2)}) collective-permute-start(f32[128,256]{1,0:T(8,128)S(1)} %get-tuple-element.54), channel_id=1, source_target_pairs={{0,4},{4,8},{8,12},{12,16},{16,20},{20,24},{24,28},{28,0},{1,5},{5... | collective-permute-start | bytes 393224 | tf_op jit(solution)/shard_map/ppermute | solution.py:823
  61.8 10.3 %collective-permute-start.5 = (f32[128,256]{1,0:T(8,128)S(1)}, f32[128,256]{1,0:T(8,128)S(1)}, u32[]{:S(2)}, u32[]{:S(2)}) collective-permute-start(f32[128,256]{1,0:T(8,128)S(1)} %get-tuple-element.55), channel_id=1, source_target_pairs={{4,0},{8,4},{12,8},{16,12},{20,16},{24,20},{28,24},{0,28},{5,1},{9... | collective-permute-start | bytes 393224 | tf_op jit(solution)/shard_map/ppermute | solution.py:823
  72.1 1.5 copy-start.22
  72.1 0.6 copy-start.15
  72.2 0.6 copy-start.17
  72.2 0.6 copy-start.7
  72.2 0.7 copy-start.9
  72.9 0.7 copy-start.20
  73.6 1.7 collective-permute-start.8
  73.6 20.9 %copy-start.3 = (bf16[4,128,256]{2,1,0:T(8,128)(2,1)S(1)}, bf16[4,128,256]{2,1,0:T(8,128)(2,1)}, u32[]{:S(2)}) copy-start(bf16[4,128,256]{2,1,0:T(8,128)(2,1)} %perm_ref.9) | copy-start | bytes 786436
  73.6 20.9 %copy-start.5 = (f32[4,128,256]{2,1,0:T(8,128)S(1)}, f32[4,128,256]{2,1,0:T(8,128)}, u32[]{:S(2)}) copy-start(f32[4,128,256]{2,1,0:T(8,128)} %res_ref.3) | copy-start | bytes 1572868
  73.6 20.9 %copy-start.8 = (f32[128,256]{1,0:T(8,128)S(1)}, f32[128,256]{1,0:T(8,128)}, u32[]{:S(2)}) copy-start(f32[128,256]{1,0:T(8,128)} %copy-done.7) | copy-start | bytes 393220
  73.6 20.9 %copy-start.10 = (f32[128,256]{1,0:T(8,128)S(1)}, f32[128,256]{1,0:T(8,128)}, u32[]{:S(2)}) copy-start(f32[128,256]{1,0:T(8,128)} %copy-done.9) | copy-start | bytes 393220
  73.7 20.9 %copy-start.16 = (f32[4,256]{1,0:T(4,128)S(1)}, f32[4,256]{1,0:T(4,128)}, u32[]{:S(2)}) copy-start(f32[4,256]{1,0:T(4,128)} %copy-done.15) | copy-start | bytes 12292
  73.7 20.9 %copy-start.18 = (f32[4,256]{1,0:T(4,128)S(1)}, f32[4,256]{1,0:T(4,128)}, u32[]{:S(2)}) copy-start(f32[4,256]{1,0:T(4,128)} %copy-done.17) | copy-start | bytes 12292
  81.0 13.5 %collective-permute-start.9 = (f32[128,256]{1,0:T(8,128)S(1)}, f32[128,256]{1,0:T(8,128)S(1)}, u32[]{:S(2)}, u32[]{:S(2)}) collective-permute-start(f32[128,256]{1,0:T(8,128)S(1)} %get-tuple-element.63), channel_id=1, source_target_pairs={{0,4},{4,8},{8,12},{12,16},{16,20},{20,24},{24,28},{28,0},{1,5},{5... | collective-permute-start | bytes 393224 | tf_op jit(solution)/shard_map/ppermute | solution.py:823
  81.0 13.5 %collective-permute-start.10 = (f32[128,256]{1,0:T(8,128)S(1)}, f32[128,256]{1,0:T(8,128)S(1)}, u32[]{:S(2)}, u32[]{:S(2)}) collective-permute-start(f32[128,256]{1,0:T(8,128)S(1)} %get-tuple-element.64), channel_id=1, source_target_pairs={{4,0},{8,4},{12,8},{16,12},{20,16},{24,20},{28,24},{0,28},{5,1},{9... | collective-permute-start | bytes 393224 | tf_op jit(solution)/shard_map/ppermute | solution.py:823
  91.4 3.0 %collective-permute-start.11 = (f32[4,256]{1,0:T(4,128)S(1)}, f32[4,256]{1,0:T(4,128)S(1)}, u32[]{:S(2)}, u32[]{:S(2)}) collective-permute-start(f32[4,256]{1,0:T(4,128)S(1)} %get-tuple-element.65), channel_id=1, source_target_pairs={{0,1},{1,2},{2,3},{3,0},{4,5},{5,6},{6,7},{7,4},{8,9},{9,10},{10,1... | collective-permute-start | bytes 12296 | tf_op jit(solution)/shard_map/ppermute | solution.py:823
  91.4 3.1 %collective-permute-start.12 = (f32[4,256]{1,0:T(4,128)S(1)}, f32[4,256]{1,0:T(4,128)S(1)}, u32[]{:S(2)}, u32[]{:S(2)}) collective-permute-start(f32[4,256]{1,0:T(4,128)S(1)} %get-tuple-element.66), channel_id=1, source_target_pairs={{1,0},{2,1},{3,2},{0,3},{5,4},{6,5},{7,6},{4,7},{9,8},{10,9},{11,1... | collective-permute-start | bytes 12296 | tf_op jit(solution)/shard_map/ppermute | solution.py:823
  117.1 1.5 collective-permute-start.13
  119.4 14.0 %all-to-all-start.4 = ((f32[16,4,8,128]{3,2,1,0:T(8,128)}), f32[16,4,8,128]{3,2,1,0:T(8,128)S(1)}, u32[]{:S(2)}, u32[]{:S(2)}) async-start(f32[16,4,8,128]{3,2,1,0:T(8,128)} %shard_map.133._.__), calls=%async_computation.4 | async-start | bytes 524288 | tf_op jit(solution)/shard_map/all_to_all | solution.py:808
  138.1 14.0 %all-to-all-start.5 = ((f32[16,4,8,128]{3,2,1,0:T(8,128)}), f32[16,4,8,128]{3,2,1,0:T(8,128)S(1)}, u32[]{:S(2)}, u32[]{:S(2)}) async-start(f32[16,4,8,128]{3,2,1,0:T(8,128)} %shard_map.135.__), calls=%async_computation.5 | async-start | bytes 524288 | tf_op jit(solution)/shard_map/all_to_all | solution.py:808
  152.0 0.7 copy-start.19
  152.7 1.7 collective-permute-start.14
  154.5 19.8 %copy-start.1 = (f32[32,8,128]{2,1,0:T(8,128)S(1)}, f32[32,8,128]{2,1,0:T(8,128)}, u32[]{:S(2)}) copy-start(f32[32,8,128]{2,1,0:T(8,128)} %copy-done) | copy-start | bytes 393220
  154.5 19.8 %copy-start.2 = (f32[32,8,128]{2,1,0:T(8,128)S(1)}, f32[32,8,128]{2,1,0:T(8,128)}, u32[]{:S(2)}) copy-start(f32[32,8,128]{2,1,0:T(8,128)} %all_to_all.35.sums_ref.refs_1_) | copy-start | bytes 393220
  154.5 19.8 %copy-start.4 = (bf16[4,128,256]{2,1,0:T(8,128)(2,1)S(1)}, bf16[4,128,256]{2,1,0:T(8,128)(2,1)}, u32[]{:S(2)}) copy-start(bf16[4,128,256]{2,1,0:T(8,128)(2,1)} %perm_ref.9) | copy-start | bytes 786436
  154.5 19.8 %copy-start.6 = (f32[4,128,256]{2,1,0:T(8,128)S(1)}, f32[4,128,256]{2,1,0:T(8,128)}, u32[]{:S(2)}) copy-start(f32[4,128,256]{2,1,0:T(8,128)} %get-tuple-element.82.refs_12_.res_ref) | copy-start | bytes 1572868
  160.8 13.5 %collective-permute-start.15 = (f32[128,256]{1,0:T(8,128)S(1)}, f32[128,256]{1,0:T(8,128)S(1)}, u32[]{:S(2)}, u32[]{:S(2)}) collective-permute-start(f32[128,256]{1,0:T(8,128)S(1)} %get-tuple-element.78), channel_id=1, source_target_pairs={{0,4},{4,8},{8,12},{12,16},{16,20},{20,24},{24,28},{28,0},{1,5},{5... | collective-permute-start | bytes 393224 | tf_op jit(solution)/shard_map/ppermute | solution.py:823
  161.8 12.5 %collective-permute-start.16 = (f32[128,256]{1,0:T(8,128)S(1)}, f32[128,256]{1,0:T(8,128)S(1)}, u32[]{:S(2)}, u32[]{:S(2)}) collective-permute-start(f32[128,256]{1,0:T(8,128)S(1)} %get-tuple-element.79), channel_id=1, source_target_pairs={{4,0},{8,4},{12,8},{16,12},{20,16},{24,20},{28,24},{0,28},{5,1},{9... | collective-permute-start | bytes 393224 | tf_op jit(solution)/shard_map/ppermute | solution.py:823
  171.2 3.0 %collective-permute-start.17 = (f32[4,256]{1,0:T(4,128)S(1)}, f32[4,256]{1,0:T(4,128)S(1)}, u32[]{:S(2)}, u32[]{:S(2)}) collective-permute-start(f32[4,256]{1,0:T(4,128)S(1)} %get-tuple-element.80), channel_id=1, source_target_pairs={{0,1},{1,2},{2,3},{3,0},{4,5},{5,6},{6,7},{7,4},{8,9},{9,10},{10,1... | collective-permute-start | bytes 12296 | tf_op jit(solution)/shard_map/ppermute | solution.py:823
  171.2 3.1 %collective-permute-start.18 = (f32[4,256]{1,0:T(4,128)S(1)}, f32[4,256]{1,0:T(4,128)S(1)}, u32[]{:S(2)}, u32[]{:S(2)}) collective-permute-start(f32[4,256]{1,0:T(4,128)S(1)} %get-tuple-element.81), channel_id=1, source_target_pairs={{1,0},{2,1},{3,2},{0,3},{5,4},{6,5},{7,6},{4,7},{9,8},{10,9},{11,1... | collective-permute-start | bytes 12296 | tf_op jit(solution)/shard_map/ppermute | solution.py:823
